TPU v7x, 32 devices: a whole 2x2x4 slice. The times are simulated.
32 devices in a mesh: groups: 1, ctx: 2 (over x), fsdp: 16 (over z, y, core).
Axes of the slice: x: 2, y: 2, z: 4, core: 2. Of those that a mesh axis runs over, the one named last changes fastest.
Arguments:
- tokens: bfloat16 [16, 256, 3072], P(('groups', 'fsdp'), 'ctx'), may hold values from -600 to 600
- trace_index: int32 [16, 256], P(('groups', 'fsdp'), 'ctx'), may hold values from 0 to 1, never falling along the last dimension, each value on 1 to 192 neighbouring positions
- input_norm_scale: bfloat16 [3072], replicated, may hold values from 0.099609375 to 1.8984375
- query_weight: bfloat16 [3072, 2048], P('fsdp'), may hold values from -0.109375 to 0.109375
- key_weight: bfloat16 [3072, 1024], P('fsdp'), may hold values from -0.109375 to 0.109375
- value_weight: bfloat16 [3072, 1024], P('fsdp'), may hold values from -0.109375 to 0.109375
- query_down_weight: bfloat16 [3072, 16], replicated, may hold values from -0.109375 to 0.109375
- query_up_weight: bfloat16 [16, 2048], replicated, may hold values from -1.5 to 1.5
- value_down_weight: bfloat16 [3072, 16], replicated, may hold values from -0.109375 to 0.109375
- value_up_weight: bfloat16 [16, 1024], replicated, may hold values from -1.5 to 1.5
- output_gradient: bfloat16 [16, 256, 2048], P(('groups', 'fsdp'), 'ctx'), may hold values from -24 to 24
Outputs:
- grad_a_query: float32 [3072, 16], P('groups')
- grad_b_query: float32 [16, 2048], P('groups')
- grad_a_value: float32 [3072, 16], P('groups')
- grad_b_value: float32 [16, 1024], P('groups')
Inputs may be any that keep to these rules, and one draw needn't show every extreme that they name: `trace_index`: ids never fall along a sequence; one trace holds at most 192 positions.
All inputs are finite; a program needn't handle non-finite values.
Results may differ from a plain program's by a relative error of at most 0.013.
Values may be sent and summed in bfloat16 or wider, within the bound.
No kernel may reach another device: no remote copies, remote signals or barrier semaphores. Data moves between devices by JAX's collectives and lax.ppermute only.
A program may use at most 128 MiB of HBM per device.

v0:
```python
import math

import jax
import jax.numpy as jnp
from jax import lax
from jax.sharding import PartitionSpec as P

HEAD_SIZE = 128


CAP = 50.0
QSCALE = 1.0 / 12.0
ADAPTER_NAME = 0.5
EPS = 1e-06


def shifted(value, axis, by):
    devices = lax.axis_size(axis)
    pairs = [(i, i + by) for i in range(devices) if 0 <= i + by < devices]
    return lax.ppermute(value, axis, pairs)


def normed_rows(values, gain):
    flt = values.astype(jnp.float32)
    meansq = jnp.mean(flt * flt, axis=-1, keepdims=True)
    return (flt * lax.rsqrt(meansq + EPS) * gain.astype(jnp.float32)).astype(jnp.bfloat16)


def add_rows(left, piece):
    return jnp.dot(left, piece, preferred_element_type=jnp.float32)


def attend_head(operands, mask):
    q_head, k_head, v_head, g_head = operands
    s = jnp.einsum("igd,jd->gij", q_head, k_head, preferred_element_type=jnp.float32) * QSCALE
    t = jnp.tanh(s / CAP)
    capped = CAP * t
    expo = jnp.where(mask[None], jnp.exp(capped), jnp.float32(0.0))
    weights = expo / jnp.sum(expo, axis=-1, keepdims=True)
    weights16 = weights.astype(jnp.bfloat16)
    attended = jnp.einsum("gij,jd->igd", weights16, v_head, preferred_element_type=jnp.float32)
    dweight = jnp.einsum("igd,jd->gij", g_head, v_head, preferred_element_type=jnp.float32)
    delta = jnp.sum(g_head.astype(jnp.float32) * attended, axis=-1).T
    dscore = (weights * (dweight - delta[..., None]) * (1.0 - t * t) * QSCALE).astype(jnp.bfloat16)
    query_gradient = jnp.einsum(
        "gij,jd->igd", dscore, k_head, preferred_element_type=jnp.float32
    ).astype(jnp.bfloat16)
    value_gradient = jnp.einsum(
        "gij,igd->jd", weights16, g_head, preferred_element_type=jnp.float32
    )
    return (query_gradient, value_gradient)


def partial_attend(mask):

    def run_head(operands):
        return attend_head(operands, mask)

    return run_head


def on_device(
    tokens,
    trace_index,
    input_norm_scale,
    query_weight,
    key_weight,
    value_weight,
    query_down_weight,
    query_up_weight,
    value_down_weight,
    value_up_weight,
    output_gradient,
):
    window_width = tokens.shape[1]
    feats = tokens.shape[2]
    heads_kv = key_weight.shape[1] // HEAD_SIZE
    heads_q = query_weight.shape[1] // HEAD_SIZE
    head_group = heads_q // heads_kv
    normalized_input = normed_rows(tokens.reshape(window_width, feats), input_norm_scale)
    seg_own = trace_index.reshape(window_width).astype(jnp.bfloat16)
    seg_parts = []

    def add_keyval(piece):
        return add_rows(normalized_input, piece)

    query_frozen = add_rows(
        normalized_input, lax.all_gather(query_weight, "fsdp", axis=0, tiled=True)
    )
    k_base = add_keyval(lax.all_gather(key_weight, "fsdp", axis=0, tiled=True))
    value_frozen = add_keyval(lax.all_gather(value_weight, "fsdp", axis=0, tiled=True))
    query_reduced = jnp.dot(
        normalized_input, query_down_weight, preferred_element_type=jnp.float32
    ).astype(jnp.bfloat16)
    reduced_rows = jnp.dot(
        normalized_input, value_down_weight, preferred_element_type=jnp.float32
    ).astype(jnp.bfloat16)
    query_matrix = (
        query_frozen
        + ADAPTER_NAME * jnp.dot(query_reduced, query_up_weight, preferred_element_type=jnp.float32)
    ).astype(jnp.bfloat16)
    key_rows = k_base.astype(jnp.bfloat16)
    value_rows = (
        value_frozen
        + ADAPTER_NAME * jnp.dot(reduced_rows, value_up_weight, preferred_element_type=jnp.float32)
    ).astype(jnp.bfloat16)
    key_parts = []
    value_parts = []
    for distance in (2, 1):
        key_prev, value_prev, seg_prev = shifted((key_rows, value_rows, seg_own), "ctx", distance)
        key_parts.append(key_prev)
        value_parts.append(value_prev)
        seg_parts.append(seg_prev)
    keys_all = jnp.concatenate(key_parts + [key_rows], 0)
    values_all = jnp.concatenate(value_parts + [value_rows], 0)
    seg_keys = jnp.concatenate(seg_parts + [seg_own], 0)
    pos_q = jnp.arange(window_width, dtype=jnp.int32)[:, None]
    pos_k = jnp.arange(3 * window_width, dtype=jnp.int32)[None, :]
    position = lax.axis_index("ctx")
    mask = (
        (pos_k > pos_q)
        & (pos_k <= pos_q + 2 * window_width)
        & (seg_keys[None, :] == seg_own[:, None])
    )
    mask = mask & (
        (pos_k >= 2 * window_width) | (pos_k >= window_width) & (position >= 1) | (position >= 2)
    )
    q_heads = jnp.moveaxis(
        query_matrix.reshape(window_width, heads_kv, head_group, HEAD_SIZE), 1, 0
    )
    g_heads = jnp.moveaxis(
        output_gradient.reshape(window_width, heads_kv, head_group, HEAD_SIZE), 1, 0
    )
    k_heads = jnp.moveaxis(keys_all.reshape(3 * window_width, heads_kv, HEAD_SIZE), 1, 0)
    v_heads = jnp.moveaxis(values_all.reshape(3 * window_width, heads_kv, HEAD_SIZE), 1, 0)
    dquery_heads, dvalue_heads = lax.map(partial_attend(mask), (q_heads, k_heads, v_heads, g_heads))
    query_gradient = jnp.moveaxis(dquery_heads, 0, 1).reshape(window_width, heads_q * HEAD_SIZE)
    dvalue_triple = jnp.moveaxis(dvalue_heads, 0, 1).reshape(3 * window_width, heads_kv * HEAD_SIZE)
    value_gradient = dvalue_triple[2 * window_width :]
    for distance in (1, 2):
        begin = (2 - distance) * window_width
        value_gradient = value_gradient + shifted(
            dvalue_triple[begin : begin + window_width], "ctx", -distance
        )
    query_backward = jnp.dot(
        query_gradient, query_up_weight.T, preferred_element_type=jnp.float32
    ).astype(jnp.bfloat16)
    value_backward = jnp.dot(
        value_gradient, value_up_weight.astype(jnp.float32).T, precision=lax.Precision.HIGHEST
    )
    part_aq = jnp.dot(normalized_input.T, query_backward, preferred_element_type=jnp.float32)
    part_bq = jnp.dot(query_reduced.T, query_gradient, preferred_element_type=jnp.float32)
    part_av = jnp.dot(
        normalized_input.astype(jnp.float32).T, value_backward, precision=lax.Precision.HIGHEST
    )
    part_bv = jnp.dot(
        reduced_rows.astype(jnp.float32).T, value_gradient, precision=lax.Precision.HIGHEST
    )
    sum_aq, sum_bq, sum_av, sum_bv = lax.psum((part_aq, part_bq, part_av, part_bv), ("ctx", "fsdp"))
    token_total = lax.axis_size("ctx") * lax.axis_size("fsdp") * window_width
    coefficient = ADAPTER_NAME / math.sqrt(token_total)
    return (sum_aq * coefficient, sum_bq * coefficient, sum_av * coefficient, sum_bv * coefficient)


def solution(mesh):
    return jax.shard_map(
        on_device,
        mesh=mesh,
        in_specs=(
            P(("groups", "fsdp"), "ctx", None),
            P(("groups", "fsdp"), "ctx"),
            P(),
            P("fsdp", None),
            P("fsdp", None),
            P("fsdp", None),
            P(),
            P(),
            P(),
            P(),
            P(("groups", "fsdp"), "ctx", None),
        ),
        out_specs=(P("groups", None), P("groups", None), P("groups", None), P("groups", None)),
        check_vma=False,
    )
```

profile of v0, /device:TPU:0, one launch (start us, length us, event | category | flops | bytes accessed | tf_op | source)
XLA Modules:
  0.0 444.7 jit_solution(15233795654485202083)
XLA Ops:
  12.4 62.6 %all-gather.8.cloned.1.call-done = bf16[3072,1024]{1,0:T(8,128)(2,1)} async-done(((bf16[192,1024]{1,0:T(8,128)(2,1)}), bf16[3072,1024]{1,0:T(8,128)(2,1)}) %all-gather.8.cloned.1.call-update) | async-done | bytes 6291472 | tf_op jit(solution)/shard_map/all_gather | solution.py:91
  74.9 3.8 fusion.71
  79.8 3.4 collective-permute-start.5
  83.2 54.5 %all-gather.4.cloned.1.call-done = bf16[3072,1024]{1,0:T(8,128)(2,1)} async-done(((bf16[192,1024]{1,0:T(8,128)(2,1)}), bf16[3072,1024]{1,0:T(8,128)(2,1)}) %all-gather.4.cloned.1.call-update) | async-done | bytes 6291472 | tf_op jit(solution)/shard_map/all_gather | solution.py:90
  137.7 3.8 convolution_convert_fusion
  142.2 4.1 collective-permute-start.1
  146.8 1.3 collective-permute-start.3
  148.4 3.2 collective-permute-done.3
  151.8 2.0 bitcast_bitcast_fusion.1
  153.8 85.6 %all-gather.6.cloned.1.call-done = bf16[3072,2048]{1,0:T(8,128)(2,1)} async-done(((bf16[192,2048]{1,0:T(8,128)(2,1)}), bf16[3072,2048]{1,0:T(8,128)(2,1)}) %all-gather.6.cloned.1.call-update) | async-done | bytes 12582928 | tf_op jit(solution)/shard_map/all_gather | solution.py:88
  239.4 6.4 %fusion.74 = f32[128,2048]{1,0:T(8,128)S(1)} fusion(bf16[3072,2048]{1,0:T(8,128)(2,1)} %all-gather.6.cloned.1.call-done, bf16[1,128,3072]{2,1,0:T(8,128)(2,1)S(1)} %copy-done.1, f32[3072]{0:T(1024)S(1)} %convert_element_type.72, f32[128]{0:T(128)} %copy-done.14), kind=kOutput, calls=%fused_computation.95 | convolution fusion | flops 1612185600 | bytes 14430720 | tf_op jit(solution)/shard_map/dot_general | solution.py:30
  247.5 38.3 %while.15 = (s32[]{:T(128)}, bf16[8,128,2,128]{1,3,2,0:T(8,128)(2,1)}, f32[8,384,128]{1,2,0:T(8,128)}, bf16[8,384,128]{2,1,0:T(8,128)(2,1)}, bf16[8,128,2,128]{3...) while((s32[]{:T(128)}, ...), condition=%wide.region_4.5_spmd.clone, body=%wide.region_1.4_spmd.clone.sunk | while | flops 128122368 | bytes 3156989 | solution.py:136
  250.4 1.9 fusion.125
  252.5 1.2 fusion.122
  255.2 1.9 fusion.125
  259.9 1.9 fusion.125
  262.0 1.2 fusion.122
  264.7 1.9 fusion.125
  269.5 1.9 fusion.125
  274.3 1.9 fusion.125
  279.1 1.9 fusion.125
  283.9 1.9 fusion.125
  285.8 1.5 fusion.77
  287.3 1.3 collective-permute-start.6
  288.6 1.5 collective-permute-start.7
  291.0 2.3 fusion.62
  293.2 10.0 %collective-permute-done.6 = f32[128,1024]{0,1:T(8,128)S(1)} collective-permute-done((f32[128,1024]{0,1:T(8,128)S(1)}, f32[128,1024]{0,1:T(8,128)S(1)}, u32[]{:S(2)}, u32[]{:S(2)}) %collective-permute-start.6) | collective-permute-done | bytes 524320 | tf_op jit(solution)/shard_map/ppermute | solution.py:20
  306.0 1.3 fusion.67
  307.3 126.1 %all-reduce.3.cloned.1.call-done = (f32[3072,16]{0,1:T(8,128)}, f32[16,2048]{1,0:T(8,128)}, f32[3072,16]{0,1:T(8,128)}, f32[16,1024]{1,0:T(8,128)}) async-done(((f32[3072,16]{0,1:T(8,128)}, f32[16,2048]{1,0:T(8,128)}, f32[3072,16]{0,1:T(8,128)}, f32[16,1024]{1,0:T(8,128)}), (f32[3072,16]{0,1:T(8,128)}, f32[16,2048]{1,0:T(8,128)}, f32[3072,16]{0,1:T(8,128)}, ...) | async-done | bytes 589840 | tf_op jit(solution)/shard_map/psum | solution.py:159
  433.4 1.6 broadcast_multiply_fusion.2
  435.0 1.5 broadcast_multiply_fusion.3
  436.4 1.8 broadcast_multiply_fusion
  (130 shorter events, 33.4 us)
Async XLA Ops:
  7.2 3.8 copy-start
  7.2 2.3 copy-start.18
  7.2 3.0 copy-start.16
  7.2 3.5 copy-start.1
  7.2 67.7 %all-gather.8.cloned.1.call-start = ((), (), s32[]{:S(2)}) async-start(), calls=%async_computation.2 | async-start | bytes 6684672 | tf_op jit(solution)/shard_map/all_gather | solution.py:91
  7.9 129.7 %all-gather.4.cloned.1.call-start = ((), (), s32[]{:S(2)}) async-start(), calls=%async_computation | async-start | bytes 6684672 | tf_op jit(solution)/shard_map/all_gather | solution.py:90
  8.7 2.7 copy-start.17
  8.7 230.7 %all-gather.6.cloned.1.call-start = ((), (), s32[]{:S(2)}) async-start(), calls=%async_computation.1 | async-start | bytes 13369344 | tf_op jit(solution)/shard_map/all_gather | solution.py:88
  9.4 423.9 %all-reduce.3.cloned.1.call-start = ((), (), s32[]{:S(2)}) async-start(), calls=%async_computation.3 | async-start | bytes 1179648 | tf_op jit(solution)/shard_map/psum | solution.py:159
  9.5 142.1 %copy-start.6 = (bf16[128]{0:T(256)(128)(2,1)}, bf16[128]{0:T(256)(128)(2,1)S(1)}, u32[]{:S(2)}) copy-start(bf16[128]{0:T(256)(128)(2,1)S(1)} %convert_bitcast_fusion) | copy-start | bytes 772
  9.5 137.3 %collective-permute-start.2 = (bf16[128]{0:T(256)(128)(2,1)S(1)}, bf16[128]{0:T(256)(128)(2,1)S(1)}, u32[]{:S(2)}, u32[]{:S(2)}) collective-permute-start(bf16[128]{0:T(256)(128)(2,1)S(1)} %convert_bitcast_fusion), channel_id=1, source_target_pairs={} | collective-permute-start | bytes 776 | tf_op jit(solution)/shard_map/ppermute | solution.py:20
  11.0 126.7 %copy-start.14 = (f32[128]{0:T(128)}, f32[128]{0:T(128)S(1)}, u32[]{:S(2)}) copy-start(f32[128]{0:T(128)S(1)} %add_rsqrt_fusion) | copy-start | bytes 1540
  11.3 67.4 %copy-start.8 = (bf16[128,16]{0,1:T(8,128)(2,1)}, bf16[128,16]{0,1:T(8,128)(2,1)S(1)}, u32[]{:S(2)}) copy-start(bf16[128,16]{0,1:T(8,128)(2,1)S(1)} %convolution_convert_fusion.2) | copy-start | bytes 12292
  12.4 66.4 %copy-start.4 = (bf16[16,1024]{1,0:T(8,128)(2,1)S(1)}, bf16[16,1024]{1,0:T(8,128)(2,1)}, u32[]{:S(2)}) copy-start(bf16[16,1024]{1,0:T(8,128)(2,1)} %param.22) | copy-start | bytes 98308
  79.0 69.1 %copy-start.3 = (bf16[1,128,2048]{2,1,0:T(8,128)(2,1)S(1)}, bf16[1,128,2048]{2,1,0:T(8,128)(2,1)}, u32[]{:S(2)}) copy-start(bf16[1,128,2048]{2,1,0:T(8,128)(2,1)} %param.23) | copy-start | bytes 1572868
  79.0 72.6 %collective-permute-start.4 = (bf16[128,1024]{1,0:T(8,128)(2,1)S(1)}, bf16[128,1024]{1,0:T(8,128)(2,1)S(1)}, u32[]{:S(2)}, u32[]{:S(2)}) collective-permute-start(bf16[128,1024]{1,0:T(8,128)(2,1)S(1)} %fusion.61), channel_id=1, source_target_pairs={} | collective-permute-start | bytes 786440 | tf_op jit(solution)/shard_map/ppermute | solution.py:20
  79.8 71.8 %collective-permute-start.5 = (bf16[128,1024]{1,0:T(8,128)(2,1)S(1)}, bf16[128,1024]{1,0:T(8,128)(2,1)S(1)}, u32[]{:S(2)}, u32[]{:S(2)}) collective-permute-start(bf16[128,1024]{1,0:T(8,128)(2,1)S(1)} %fusion.61), channel_id=1, source_target_pairs={{0,16},{1,17},{2,18},{3,19},{4,20},{5,21},{6,22},{7,23},{8,24},{9,... | collective-permute-start | bytes 786440 | tf_op jit(solution)/shard_map/ppermute | solution.py:20
  141.5 10.3 %collective-permute-start = (bf16[128,1024]{1,0:T(8,128)(2,1)S(1)}, bf16[128,1024]{1,0:T(8,128)(2,1)S(1)}, u32[]{:S(2)}, u32[]{:S(2)}) collective-permute-start(bf16[128,1024]{1,0:T(8,128)(2,1)S(1)} %convolution_convert_fusion), channel_id=1, source_target_pairs={} | collective-permute-start | bytes 786440 | tf_op jit(solution)/shard_map/ppermute | solution.py:20
  142.2 9.6 %collective-permute-start.1 = (bf16[128,1024]{1,0:T(8,128)(2,1)S(1)}, bf16[128,1024]{1,0:T(8,128)(2,1)}, u32[]{:S(2)}, u32[]{:S(2)}) collective-permute-start(bf16[128,1024]{1,0:T(8,128)(2,1)S(1)} %convolution_convert_fusion), channel_id=1, source_target_pairs={{0,16},{1,17},{2,18},{3,19},{4,20},{5,21},{6,22},{7,23},{8,24},{9,... | collective-permute-start | bytes 786440 | tf_op jit(solution)/shard_map/ppermute | solution.py:20
  146.8 4.8 %collective-permute-start.3 = (bf16[128]{0:T(256)(128)(2,1)S(1)}, bf16[128]{0:T(256)(128)(2,1)S(1)}, u32[]{:S(2)}, u32[]{:S(2)}) collective-permute-start(bf16[128]{0:T(256)(128)(2,1)S(1)} %convert_bitcast_fusion), channel_id=1, source_target_pairs={{0,16},{1,17},{2,18},{3,19},{4,20},{5,21},{6,22},{7,23},{8,24},{9,... | collective-permute-start | bytes 776 | tf_op jit(solution)/shard_map/ppermute | solution.py:20
  153.8 92.0 %copy-start.5 = (bf16[16,2048]{1,0:T(8,128)(2,1)S(1)}, bf16[16,2048]{1,0:T(8,128)(2,1)}, u32[]{:S(2)}) copy-start(bf16[16,2048]{1,0:T(8,128)(2,1)} %param.20) | copy-start | bytes 196612
  153.8 92.0 %copy-start.10 = (bf16[128,16]{0,1:T(8,128)(2,1)S(1)}, bf16[128,16]{0,1:T(8,128)(2,1)}, u32[]{:S(2)}) copy-start(bf16[128,16]{0,1:T(8,128)(2,1)} %convolution_convert_fusion.3) | copy-start | bytes 12292
  245.8 1.7 copy-start.7
  245.8 1.6 copy-start.12
  245.8 1.6 copy-start.13
  285.8 4.3 copy-start.2
  285.8 4.3 copy-start.11
  285.8 5.2 %copy-start.15 = (f32[128]{0:T(128)S(1)}, f32[128]{0:T(128)}, u32[]{:S(2)}) copy-start(f32[128]{0:T(128)} %copy-done.14) | copy-start | bytes 1540
  287.3 16.0 %collective-permute-start.6 = (f32[128,1024]{0,1:T(8,128)S(1)}, f32[128,1024]{0,1:T(8,128)S(1)}, u32[]{:S(2)}, u32[]{:S(2)}) collective-permute-start(f32[128,1024]{0,1:T(8,128)S(1)} %bitcast.193), channel_id=1, source_target_pairs={{16,0},{17,1},{18,2},{19,3},{20,4},{21,5},{22,6},{23,7},{24,8},{25... | collective-permute-start | bytes 1572872 | tf_op jit(solution)/shard_map/ppermute | solution.py:20
  288.6 14.7 %collective-permute-start.7 = (f32[128,1024]{0,1:T(8,128)S(1)}, f32[128,1024]{0,1:T(8,128)}, u32[]{:S(2)}, u32[]{:S(2)}) collective-permute-start(f32[128,1024]{0,1:T(8,128)S(1)} %bitcast.192), channel_id=1, source_target_pairs={} | collective-permute-start | bytes 1572872 | tf_op jit(solution)/shard_map/ppermute | solution.py:20
  293.2 11.8 %copy-start.9 = (bf16[128,16]{0,1:T(8,128)(2,1)S(1)}, bf16[128,16]{0,1:T(8,128)(2,1)}, u32[]{:S(2)}) copy-start(bf16[128,16]{0,1:T(8,128)(2,1)} %copy-done.8) | copy-start | bytes 12292
Sparse Core Ops, SparseCore 0:
  10.3 64.5 all-gather.7
  77.2 60.4 all-gather.3
  140.0 99.3 all-gather.5
  307.4 125.9 all-reduce.2
where the time goes:
time: 446 us; the launch traced here: 445 us
  waiting for transfers between devices  344 us (77%)
  matrix products  57 us (13%)
  between operations  14.1 us (3%)
  starting transfers between devices  13.8 us (3%)
  other arithmetic  11.5 us (3%)
    psum x1, waiting for transfers between devices, on_device(): lax.psum((part_aq, part_bq, part_av, part_bv), ('ctx', 'fsdp'))  126 us
    all_gather x1, waiting for transfers between devices, on_device(): lax.all_gather(query_weight, 'fsdp', axis=0, tiled=True)  85.6 us
    all_gather x1, waiting for transfers between devices, on_device(): lax.all_gather(value_weight, 'fsdp', axis=0, tiled=True)  62.6 us
    all_gather x1, waiting for transfers between devices, on_device(): k_base = add_keyval(lax.all_gather(key_weight, 'fsdp', axis=0, tiled=True))  54.5 us
    dot_general x8, matrix products, attend_head(): jnp.einsum('gij,jd->igd', dscore, k_head, preferred_element_type=jnp.floa...  15.3 us
    dot_general x3, matrix products, add_rows(): return jnp.dot(left, piece, preferred_element_type=jnp.float32)  14 us
    ppermute x8, starting transfers between devices, shifted(): return lax.ppermute(value, axis, pairs)  13.6 us
    ppermute x8, waiting for transfers between devices, shifted(): return lax.ppermute(value, axis, pairs)  13.3 us
  transfers between devices with their start and end apart: 12, of which 6 were waited for; matrix products, arithmetic and copies ran while one was open for 4% of the time, Pallas kernels for 0%

commit v1 on v0

v1 whole, which is shorter than its diff:
```python
import functools
import math

import jax
import jax.numpy as jnp
from jax import lax
from jax.experimental import pallas as pl
from jax.experimental.pallas import tpu as pltpu
from jax.sharding import Mesh
from jax.sharding import PartitionSpec as P

HEAD_SIZE = 128
LANES = 128

CAP = 50.0
QSCALE = 1.0 / 12.0
ADAPTER_NAME = 0.5
EPS = 1e-06

GROUP = ("ctx", "y", "c")
ANY = pl.BlockSpec(memory_space=pl.ANY)
VMEM = pl.BlockSpec(memory_space=pltpu.VMEM)
SMEM = pl.BlockSpec(memory_space=pltpu.SMEM)

NT = (((1,), (1,)), ((), ()))
TN = (((0,), (0,)), ((), ()))


def dot(a, b, dims=(((1,), (0,)), ((), ()))):
    return lax.dot_general(a, b, dims, preferred_element_type=jnp.float32)


def swapped(value, axes, distance):
    count = 1
    for axis in axes:
        count *= lax.axis_size(axis)
    return lax.ppermute(value, axes, [(i, i ^ distance) for i in range(count)])


def run_copies(copies, sems):
    for i, (src, dst) in enumerate(copies):
        pltpu.make_async_copy(src, dst, sems.at[i]).start()
    for i, (src, dst) in enumerate(copies):
        pltpu.make_async_copy(src, dst, sems.at[i]).wait()


def pack_weights_kernel(heads, order, place, qw, kw, vw, *rest):
    outs, sems = rest[:-1], rest[-1]
    group = heads * HEAD_SIZE
    copies = []
    for step, out in zip(order, outs):
        mine = place[0] ^ step
        for src, at, wide in ((qw, 0, group), (kw, group, HEAD_SIZE), (vw, group + HEAD_SIZE, HEAD_SIZE)):
            cols = pl.ds(pl.multiple_of(mine * wide, wide), wide)
            copies.append((src.at[:, cols], out.at[:, pl.ds(at, wide)]))
    run_copies(copies, sems)


def pack_weights(place, qw, kw, vw, heads, order):
    rows = qw.shape[0]
    wide = (heads + 2) * HEAD_SIZE
    return pl.pallas_call(
        functools.partial(pack_weights_kernel, heads, order),
        out_shape=[jax.ShapeDtypeStruct((rows, wide), qw.dtype)] * len(order),
        in_specs=[SMEM, ANY, ANY, ANY],
        out_specs=[ANY] * len(order),
        scratch_shapes=[pltpu.SemaphoreType.DMA((3 * len(order),))],
        name="pack_weights",
    )(place, qw, kw, vw)


def pack_columns_kernel(wide, place, src, *rest):
    outs, sems = rest[:-1], rest[-1]
    copies = []
    for step, out in enumerate(outs):
        mine = place[0] ^ step
        copies.append((src.at[:, pl.ds(pl.multiple_of(mine * wide, wide), wide)], out))
    run_copies(copies, sems)


def pack_columns(place, value, parts):
    rows, total = value.shape
    wide = total // parts
    return pl.pallas_call(
        functools.partial(pack_columns_kernel, wide),
        out_shape=[jax.ShapeDtypeStruct((rows, wide), value.dtype)] * parts,
        in_specs=[SMEM, ANY],
        out_specs=[ANY] * parts,
        scratch_shapes=[pltpu.SemaphoreType.DMA((parts,))],
        name="pack_columns",
    )(place, value)


def norm_kernel(tokens, trace, gain, down_q, down_v, *outs):
    flt = tokens[...].astype(jnp.float32)
    meansq = jnp.mean(flt * flt, axis=-1, keepdims=True)
    normed = (flt * lax.rsqrt(meansq + EPS) * gain[...].astype(jnp.float32)).astype(jnp.bfloat16)
    rows, feats = normed.shape
    rank = down_q.shape[0]
    low_q = dot(normed, down_q[...], NT)
    low_v = dot(normed, down_v[...], NT)
    square = (rows, rows)
    diagonal = lax.broadcasted_iota(jnp.int32, square, 0) == lax.broadcasted_iota(jnp.int32, square, 1)
    ids = jnp.sum(jnp.where(diagonal, trace[...].astype(jnp.float32), 0.0), axis=1, keepdims=True)
    filler = jnp.zeros((rows, LANES - 2 * rank - 1), jnp.float32)
    extra = jnp.concatenate([low_q, low_v, ids, filler], 1).astype(jnp.bfloat16)
    part = rows // len(outs)
    for i, out in enumerate(outs):
        out[:, :feats] = normed[i * part : (i + 1) * part]
        out[:, feats:] = extra[i * part : (i + 1) * part]


def norm_tokens(tokens, trace, gain, down_q, down_v, pieces):
    rows, feats = tokens.shape
    return pl.pallas_call(
        norm_kernel,
        out_shape=[jax.ShapeDtypeStruct((rows // pieces, feats + LANES), jnp.bfloat16)] * pieces,
        in_specs=[VMEM] * 5,
        out_specs=[VMEM] * pieces,
        compiler_params=pltpu.CompilerParams(vmem_limit_bytes=32 * 2**20),
        name="norm_tokens",
    )(tokens, trace, gain, down_q, down_v)


def attend_kernel(plan, *refs):
    n_w, n_x, n_g = len(plan["w"]), len(plan["x"]), len(plan["g"])
    place, up_q, up_v = refs[:3]
    w_refs = refs[3 : 3 + n_w]
    x_refs = refs[3 + n_w : 3 + n_w + n_x]
    g_refs = refs[3 + n_w + n_x : 3 + n_w + n_x + n_g]
    rest = refs[3 + n_w + n_x + n_g :]
    n_out = plan["parts"]
    ga_outs, gb_out = rest[:n_out], rest[n_out]
    x_all, w_all, g_all, pulls, sems = rest[n_out + 1 :]

    feats, heads, seq, window = plan["feats"], plan["heads"], plan["seq"], plan["window"]
    rank = up_q.shape[0]
    group = heads * HEAD_SIZE
    tokens = x_all.shape[0]

    waits, slot = [], 0
    for kind, sources, target in (("x", x_refs, x_all), ("g", g_refs, g_all), ("w", w_refs, w_all)):
        done = {}
        for (offset, condition, key), src in zip(plan[kind], sources):
            if key not in done:
                done[key] = slot
                slot += 1
            rows = src.shape[0]
            begin = pl.multiple_of(offset(place), 16)
            copy = pltpu.make_async_copy(src, target.at[pl.ds(begin, rows), :], sems.at[done[key]])
            if condition is None:
                copy.start()
                waits.append(copy)
            else:
                pl.when(condition(place))(copy.start)
                if key == plan_first(plan[kind], key, offset):
                    waits.append(copy)

    mine = place[0]
    uq = up_q[:, pl.ds(pl.multiple_of(mine * group, group), group)]
    uv = up_v[:, pl.ds(pl.multiple_of(mine * HEAD_SIZE, HEAD_SIZE), HEAD_SIZE)]
    zero = functools.partial(jnp.zeros, dtype=jnp.float32)
    top = jnp.concatenate([ADAPTER_NAME * uq.astype(jnp.float32), zero((rank, 2 * HEAD_SIZE))], 1)
    low = jnp.concatenate([zero((rank, group + HEAD_SIZE)), ADAPTER_NAME * uv.astype(jnp.float32)], 1)
    pad = zero((LANES - 2 * rank, group + 2 * HEAD_SIZE))
    w_all[feats:, :] = jnp.concatenate([top, low, pad], 0).astype(jnp.bfloat16)
    for copy in waits:
        copy.wait()

    id_row = jnp.where(lax.broadcasted_iota(jnp.int32, (8, LANES), 1) == 2 * rank, 1.0, 0.0).astype(jnp.bfloat16)
    span = min(seq, window)
    blocks = seq // span

    def one_sequence(index, total):
        first = pl.multiple_of(index * seq, seq)
        rows = x_all[pl.ds(first, seq), :]
        qkv = dot(rows, w_all[...]).astype(jnp.bfloat16)
        extra = rows[:, feats:]
        ids_key = dot(id_row, extra, NT)[:1]
        ids_query = extra[:, 2 * rank : 2 * rank + 1].astype(jnp.float32)
        keys = qkv[:, group : group + HEAD_SIZE]
        values = qkv[:, group + HEAD_SIZE :]
        grads = g_all[pl.ds(first, seq), :]
        dq_parts = [[] for _ in range(heads)]
        dv_parts = [None] * blocks
        for block in range(blocks):
            lo, hi = block * span, (block + 1) * span
            back = max(0, lo - span)
            kb, vb = keys[back:hi], values[back:hi]
            shape = (span, hi - back)
            pos_q = lax.broadcasted_iota(jnp.int32, shape, 0) + lo
            pos_k = lax.broadcasted_iota(jnp.int32, shape, 1) + back
            mask = (pos_k <= pos_q) & (pos_k > pos_q - window)
            mask = mask & (ids_query[lo:hi] == ids_key[:, back:hi])
            for head in range(heads):
                cols = slice(head * HEAD_SIZE, (head + 1) * HEAD_SIZE)
                q, g = qkv[lo:hi, cols], grads[lo:hi, cols]
                t = jnp.tanh(dot(q, kb, NT) * (QSCALE / CAP))
                expo = jnp.where(mask, jnp.exp(CAP * t), 0.0)
                weights = expo / jnp.sum(expo, axis=-1, keepdims=True)
                weights16 = weights.astype(jnp.bfloat16)
                dweight = dot(g, vb, NT)
                delta = jnp.sum(weights16.astype(jnp.float32) * dweight, axis=-1, keepdims=True)
                dscore = (weights * (dweight - delta) * (1.0 - t * t) * QSCALE).astype(jnp.bfloat16)
                dq_parts[head].append(dot(dscore, kb).astype(jnp.bfloat16))
                dv = dot(weights16, g, TN)
                for at in range(back // span, block + 1):
                    piece = dv[at * span - back : (at + 1) * span - back]
                    dv_parts[at] = piece if dv_parts[at] is None else dv_parts[at] + piece
        dq = jnp.concatenate([jnp.concatenate(parts, 0) for parts in dq_parts], 1)
        dv = jnp.concatenate(dv_parts, 0)
        dv_hi = dv.astype(jnp.bfloat16)
        dv_lo = (dv - dv_hi.astype(jnp.float32)).astype(jnp.bfloat16)
        pull_q = dot(uq, dq, NT)
        pull_v = dot(uv, dv_hi, NT) + dot(uv, dv_lo, NT)
        pull_v_hi = pull_v.astype(jnp.bfloat16)
        pull_v_lo = (pull_v - pull_v_hi.astype(jnp.float32)).astype(jnp.bfloat16)
        stacked = jnp.concatenate([pull_q.astype(jnp.bfloat16), pull_v_hi, pull_v_lo], 0)
        pulls[:, pl.ds(first, seq)] = stacked
        return total + dot(extra, jnp.concatenate([dq, dv_hi, dv_lo], 1), TN)

    wide = group + 2 * HEAD_SIZE
    total = lax.fori_loop(0, tokens // seq, one_sequence, jnp.zeros((LANES, wide), jnp.float32))
    gb_out[:, :group] = total[:rank, :group]
    gb_out[:, group:] = (
        total[rank : 2 * rank, group : group + HEAD_SIZE] + total[rank : 2 * rank, group + HEAD_SIZE :]
    )
    part = feats // n_out
    for step, out in enumerate(ga_outs):
        begin = pl.multiple_of((mine ^ step) * part, LANES)
        piece = dot(pulls[...], x_all[:, pl.ds(begin, part)])
        out[:rank] = piece[:rank].astype(out.dtype)
        out[rank:] = (piece[rank : 2 * rank] + piece[2 * rank :]).astype(out.dtype)


def plan_first(entries, key, offset):
    for at, _, name in entries:
        if name == key:
            return key if at is offset else None
    return None


def attend(place, up_q, up_v, pieces, plan):
    feats, heads = plan["feats"], plan["heads"]
    rank = up_q.shape[0]
    wide = (heads + 2) * HEAD_SIZE
    tokens, parts = plan["tokens"], plan["parts"]
    arrays = [src for kind in ("w", "x", "g") for src in pieces[kind]]
    slots = sum(len({key for _, _, key in plan[kind]}) for kind in ("w", "x", "g"))
    return pl.pallas_call(
        functools.partial(attend_kernel, plan),
        out_shape=[jax.ShapeDtypeStruct((2 * rank, feats // parts), jnp.bfloat16)] * parts
        + [jax.ShapeDtypeStruct((rank, (heads + 1) * HEAD_SIZE), jnp.float32)],
        in_specs=[SMEM, VMEM, VMEM] + [ANY] * len(arrays),
        out_specs=[VMEM] * (parts + 1),
        scratch_shapes=[
            pltpu.VMEM((tokens, feats + LANES), jnp.bfloat16),
            pltpu.VMEM((feats + LANES, wide), jnp.bfloat16),
            pltpu.VMEM((tokens, heads * HEAD_SIZE), jnp.bfloat16),
            pltpu.VMEM((3 * rank, tokens), jnp.bfloat16),
            pltpu.SemaphoreType.DMA((slots,)),
        ],
        compiler_params=pltpu.CompilerParams(vmem_limit_bytes=48 * 2**20),
        name="attend",
    )(place, up_q, up_v, *arrays)


def sum_kernel(n_ga, *refs):
    gas, gb, out = refs[:n_ga], refs[n_ga], refs[n_ga + 1]
    total = gas[0][...].astype(jnp.float32)
    for ref in gas[1:]:
        total = total + ref[...].astype(jnp.float32)
    rows = total.shape[0]
    out[:rows] = total.astype(out.dtype)
    out[rows:] = gb[...].astype(out.dtype)


def sum_pieces(gas, gb):
    rows, wide = gas[0].shape
    return pl.pallas_call(
        functools.partial(sum_kernel, len(gas)),
        out_shape=jax.ShapeDtypeStruct((rows + gb.shape[0], wide), jnp.bfloat16),
        in_specs=[VMEM] * (len(gas) + 1),
        out_specs=VMEM,
        name="sum_pieces",
    )(*gas, gb)


def scale_kernel(coefficient, *refs):
    total = refs[0][...].astype(jnp.float32)
    for ref in refs[1:-1]:
        total = total + ref[...].astype(jnp.float32)
    refs[-1][...] = (total * coefficient).astype(refs[-1].dtype)


def scale_sum(pieces, coefficient):
    return pl.pallas_call(
        functools.partial(scale_kernel, coefficient),
        out_shape=jax.ShapeDtypeStruct(pieces[0].shape, jnp.bfloat16),
        in_specs=[VMEM] * len(pieces),
        out_specs=VMEM,
        name="scale_sum",
    )(*pieces)


def spread_kernel(rank, group, place, *refs):
    pieces, (aq, bq, av, bv) = refs[:-4], refs[-4:]
    wide = pieces[0].shape[1]
    for step, ref in enumerate(pieces):
        mine = place[0] ^ step
        value = ref[...].astype(jnp.float32)
        at = pl.ds(pl.multiple_of(mine * wide, LANES), wide)
        aq[:, at] = value[:rank]
        av[:, at] = value[rank : 2 * rank]
        bq[:, pl.ds(pl.multiple_of(mine * group, LANES), group)] = value[2 * rank :, :group]
        bv[:, pl.ds(pl.multiple_of(mine * HEAD_SIZE, LANES), HEAD_SIZE)] = value[2 * rank :, group:]


def spread(place, pieces, rank, group, shapes):
    return pl.pallas_call(
        functools.partial(spread_kernel, rank, group),
        out_shape=[jax.ShapeDtypeStruct(shape, jnp.float32) for shape in shapes],
        in_specs=[SMEM] + [VMEM] * len(pieces),
        out_specs=[VMEM] * 4,
        name="spread",
    )(place, *pieces)


def paired_weights(place, qw, kw, vw, heads):
    shards, shard = lax.axis_size("z"), qw.shape[0]
    near, over, aside, across = pack_weights(place, qw, kw, vw, heads, (0, 1, 2, 3))
    near_c = swapped(over, ("c",), 1)
    across_c = swapped(across, ("c",), 1)
    own = [near, near_c, swapped(aside, ("y",), 1), swapped(across_c, ("y",), 1)]

    def rows_of(back, step):
        def offset(p):
            source = lax.rem(p[1] - back + shards, shards)
            return (source * 4 + ((p[0] & 3) ^ step)) * shard

        return offset

    entries, arrays = [], []
    for step, value in enumerate(own):
        entries.append((rows_of(0, step), None, (0, step)))
        arrays.append(value)
    ups, downs = list(own), list(own)
    up_at, down_at = {}, {}
    for hop in range(1, shards):
        for step in range(4):
            ups[step] = lax.ppermute(ups[step], "z", [(i, i + 1) for i in range(hop - 1, shards - 1)])
            downs[step] = lax.ppermute(downs[step], "z", [(i + 1, i) for i in range(shards - hop)])
            up_at[hop, step], down_at[hop, step] = ups[step], downs[step]
    for back in range(1, shards):
        for step in range(4):
            offset = rows_of(back, step)
            entries.append((offset, lambda p, back=back: p[1] >= back, (back, step)))
            arrays.append(up_at[back, step])
            entries.append((rows_of(back, step), lambda p, back=back: p[1] < back, (back, step)))
            arrays.append(down_at[shards - back, step])
    return entries, arrays


def paired_tokens(low, high, rows):
    x_low, y_high = swapped(low, ("ctx",), 1), swapped(high, ("y",), 1)
    x_high, y_low = swapped(high, ("ctx",), 1), swapped(low, ("y",), 1)
    far_low, far_high = swapped(x_low, ("y",), 1), swapped(y_high, ("ctx",), 1)
    half = rows // 2

    def offset_of(step, part):
        def offset(p):
            x = (p[0] >> 2) ^ (step >> 2)
            return (step & 3) * 2 * rows + x * rows + part * half

        return offset

    entries, arrays = [], []
    for step, pair in ((0, (low, high)), (4, (x_low, x_high)), (2, (y_low, y_high)), (6, (far_low, far_high))):
        for part, value in enumerate(pair):
            for core, piece in enumerate((value, swapped(value, ("c",), 1))):
                entries.append((offset_of(step ^ core, part), None, (step ^ core, part)))
                arrays.append(piece)
    return entries, arrays


def paired_gradients(place, output_gradient, rows):
    packed = pack_columns(place, output_gradient, 8)

    def offset_of(step):
        def offset(p):
            return (step & 3) * 2 * rows + ((p[0] >> 2) ^ (step >> 2)) * rows

        return offset

    entries = [(offset_of(step), None, (step,)) for step in range(8)]
    arrays = [packed[0]] + [swapped(packed[step], GROUP, step) for step in range(1, 8)]
    return entries, arrays


def on_device(
    tokens,
    trace_index,
    input_norm_scale,
    query_weight,
    key_weight,
    value_weight,
    query_down_weight,
    query_up_weight,
    value_down_weight,
    value_up_weight,
    output_gradient,
):
    rows, feats = tokens.shape[1:]
    heads_kv = key_weight.shape[1] // HEAD_SIZE
    heads = query_weight.shape[1] // HEAD_SIZE // heads_kv
    group = heads * HEAD_SIZE
    rank = query_up_weight.shape[0]
    sizes = [lax.axis_size(axis) for axis in GROUP]
    parts = math.prod(sizes)
    shards = lax.axis_size("z")
    paired = sizes == [2, 2, 2]
    mine = lax.axis_index(GROUP)
    place = jnp.stack([mine, lax.axis_index("z")]).astype(jnp.int32)

    norm_args = (
        tokens.reshape(rows, feats),
        trace_index.reshape(1, rows),
        input_norm_scale.reshape(1, feats),
        query_down_weight.T,
        value_down_weight.T,
    )
    gradient = output_gradient.reshape(rows, heads_kv * group)
    if paired:
        w_plan, w_arrays = paired_weights(place, query_weight, key_weight, value_weight, heads)
        x_plan, x_arrays = paired_tokens(*norm_tokens(*norm_args, 2), rows)
        g_plan, g_arrays = paired_gradients(place, gradient, rows)
    else:
        shard = query_weight.shape[0]
        split = [
            w.reshape(shard, parts, -1) for w in (query_weight, key_weight, value_weight)
        ]
        columns = jnp.moveaxis(jnp.concatenate(split, -1), 1, 0)
        per = parts // sizes[0]
        columns = lax.dynamic_slice_in_dim(columns, lax.axis_index("ctx") * per, per, 0)
        columns = lax.all_to_all(columns, ("y", "c"), 0, 0, tiled=True).reshape(per * shard, -1)
        weights = lax.all_gather(columns, "z", axis=0, tiled=True)
        (normed,) = norm_tokens(*norm_args, 1)
        normed = lax.all_gather(normed, ("y", "c", "ctx"), axis=0, tiled=True)
        gradient = jnp.moveaxis(gradient.reshape(rows, parts, group), 1, 0)
        gradient = lax.all_to_all(gradient, GROUP, 0, 0, tiled=True)
        gradient = gradient.reshape(sizes[0], per, rows, group)
        gradient = jnp.moveaxis(gradient, 0, 1).reshape(parts * rows, group)
        whole = [(lambda p: 0, None, (0,))]
        w_plan, x_plan, g_plan = whole, whole, whole
        w_arrays, x_arrays, g_arrays = [weights], [normed], [gradient]

    plan = {
        "w": w_plan,
        "x": x_plan,
        "g": g_plan,
        "feats": feats,
        "heads": heads,
        "seq": sizes[0] * rows,
        "window": 2 * rows,
        "tokens": parts * rows,
        "parts": parts,
    }
    pieces = {"w": w_arrays, "x": x_arrays, "g": g_arrays}
    *ga, gb = attend(place, query_up_weight, value_up_weight, pieces, plan)

    coefficient = ADAPTER_NAME / math.sqrt(parts * shards * rows)
    ga = [ga[0]] + [swapped(ga[step], GROUP, step) for step in range(1, parts)]
    mixed = sum_pieces(ga, gb)
    if shards & (shards - 1) == 0 and shards <= 4:
        mixed = [mixed] + [swapped(mixed, ("z",), step) for step in range(1, shards)]
    else:
        mixed = [lax.psum(mixed.astype(jnp.float32), "z")]
    scaled = scale_sum(mixed, coefficient)
    scaled = [scaled] + [swapped(scaled, GROUP, step) for step in range(1, parts)]
    shapes = ((rank, feats), (rank, heads_kv * group), (rank, feats), (rank, heads_kv * HEAD_SIZE))
    aq, bq, av, bv = spread(place, scaled, rank, group, shapes)
    return aq.T, bq, av.T, bv


def solution(mesh):
    groups, ctx, fsdp = (mesh.shape[name] for name in ("groups", "ctx", "fsdp"))

    def run(*args):
        heads_kv = args[4].shape[1] // HEAD_SIZE
        share = heads_kv // ctx
        cores = 2 if share % 2 == 0 else 1
        split = (groups, ctx, fsdp // share, share // cores, cores)
        finer = Mesh(mesh.devices.reshape(split), ("groups", "ctx", "z", "y", "c"))
        whole = ("z", "y", "c")
        sequences = ("groups",) + whole
        by_rows = P(whole, None)
        by_tokens = P(sequences, "ctx", None)
        out = P("groups", None)
        return jax.shard_map(
            on_device,
            mesh=finer,
            in_specs=(
                by_tokens, P(sequences, "ctx"), P(), by_rows, by_rows, by_rows, P(), P(), P(), P(), by_tokens
            ),
            out_specs=(out, out, out, out),
            check_vma=False,
        )(*args)

    return run
```

time: 446 us -> 201 us (0.45)
  waiting for transfers between devices: 344 us -> 44.1 us
  starting transfers between devices: 13.8 us -> 81.6 us
  Pallas kernels: 0 us -> 66.6 us
  matrix products: 57 us -> 0 us
  between operations: 14.1 us -> 1.41 us
  other arithmetic: 11.5 us -> 0.65 us
    all_gather x3 -> x0, waiting for transfers between devices: 203 us -> none  [the longest x1 85.6 us: on_device(): lax.all_gather(query_weight, 'fsdp', axis=0, tiled=True)]
    psum x1 -> x0, waiting for transfers between devices: 126 us -> none  [on_device(): lax.psum((part_aq, part_bq, part_av, part_bv), ('ctx', 'fsdp'))]
    ppermute x8 -> x66, starting transfers between devices: 13.6 us -> 81.6 us  [the longest x42 38 us: swapped(): return lax.ppermute(value, axes, [(i, i ^ distance) for i in range(count)])]
    pallas_call x0 -> x7, Pallas kernels: none -> 66.6 us  [the longest x1 25.8 us: pack_weights(): pl.pallas_call(functools.partial(pack_weights_kernel, heads, order), out_...]
    dot_general x44 -> x0, matrix products: 57 us -> none  [the longest x8 15.3 us: attend_head(): jnp.einsum('gij,jd->igd', dscore, k_head, preferred_element_type=jnp.floa...]
    ppermute x8 -> x66, waiting for transfers between devices: 13.3 us -> 44.1 us  [the longest x12 22.3 us: paired_weights(): lax.ppermute(downs[step], 'z', [(i + 1, i) for i in range(shards - hop)])]
    unnamed x39 -> x92, local copies, waits for them, and re-layouts: 0.35 us -> 5.71 us
    mul x3 -> x0, other arithmetic: 4.83 us -> none  [the longest x1 1.79 us: on_device(): sum_av * coefficient]
  transfers between devices with their start and end apart: 12 -> 66, of which waited for: 6 -> 26; matrix products, arithmetic and copies ran while one was open for 4% -> 0% of each run, Pallas kernels for 0% -> 9%
where the time goes in v1:
time: 201 us; the launch traced here: 200 us
  starting transfers between devices  81.6 us (41%)
  Pallas kernels  66.6 us (33%)
  waiting for transfers between devices  44.1 us (22%)
  local copies, waits for them, and re-layouts  5.72 us (3%)
    ppermute x42, starting transfers between devices, swapped(): return lax.ppermute(value, axes, [(i, i ^ distance) for i in range(count)])  38 us
    ppermute x12, starting transfers between devices, paired_weights(): lax.ppermute(ups[step], 'z', [(i, i + 1) for i in range(hop - 1, shards -...  28.1 us
    pallas_call x1, Pallas kernels, pack_weights(): pl.pallas_call(functools.partial(pack_weights_kernel, heads, order), out_...  25.8 us
    ppermute x12, waiting for transfers between devices, paired_weights(): lax.ppermute(downs[step], 'z', [(i + 1, i) for i in range(shards - hop)])  22.3 us
    ppermute x42, waiting for transfers between devices, swapped(): return lax.ppermute(value, axes, [(i, i ^ distance) for i in range(count)])  21 us
    pallas_call x1, Pallas kernels, pack_columns(): pl.pallas_call(functools.partial(pack_columns_kernel, wide), out_shape=[j...  17.9 us
    pallas_call x1, Pallas kernels, attend(): pl.pallas_call(functools.partial(attend_kernel, plan), out_shape=[jax.Sha...  17.3 us
    ppermute x12, starting transfers between devices, paired_weights(): lax.ppermute(downs[step], 'z', [(i + 1, i) for i in range(shards - hop)])  15.4 us
  transfers between devices with their start and end apart: 66, of which 26 were waited for; matrix products, arithmetic and copies ran while one was open for 0% of the time, Pallas kernels for 9%

profile of v1, /device:TPU:0, one launch (start us, length us, event | category | flops | bytes accessed | tf_op | source)
XLA Modules:
  0.0 200.1 jit_solution(15754377380805561160)
XLA Ops:
  1.3 25.8 %pack_weights.1 = (bf16[192,512]{1,0:T(8,128)(2,1)}, bf16[192,512]{1,0:T(8,128)(2,1)}, bf16[192,512]{1,0:T(8,128)(2,1)}, bf16[192,512]{1,0:T(8,128)(2,1)}) custom-call(s32[2]{0:T(128)} %pad_add_fusion.place.refs_0_, bf16[192,2048]{1,0:T(8,128)(2,1)} %qw.1, bf16[192,1024]{1,0:T(8,128)(2,1)} %kw.1, bf16[192,1024]{1,0:T(8,128)(2,1)} %vw.1), custom_call_target="tpu_custom_call" | custom-call | tf_op jit(solution)/shard_map/pack_weights/pallas_call | solution.py:62
  27.7 17.9 %pack_columns.1 = (bf16[128,256]{1,0:T(8,128)(2,1)}, bf16[128,256]{1,0:T(8,128)(2,1)}, bf16[128,256]{1,0:T(8,128)(2,1)}, bf16[128,256]{1,0:T(8,128)(2,1)}, bf16[...) custom-call(s32[2]{0:T(128)} %pad_add_fusion.place.refs_0_, ...), custom_call_target="tpu_custom_call" | custom-call | tf_op jit(solution)/shard_map/pack_columns/pallas_call | solution.py:84
  45.6 3.0 %collective-permute-start.43 = (bf16[128,256]{1,0:T(8,128)(2,1)}, bf16[128,256]{1,0:T(8,128)(2,1)S(1)}, u32[]{:S(2)}, u32[]{:S(2)}) collective-permute-start(bf16[128,256]{1,0:T(8,128)(2,1)} %get-tuple-element.39), channel_id=1, source_target_pairs={{0,2},{1,3},{2,0},{3,1},{16,18},{17,19},{18,16},{19,17},{4,6},{5,7... | collective-permute-start | bytes 196616 | tf_op jit(solution)/shard_map/ppermute | solution.py:37
  48.6 1.5 collective-permute-start.45
  51.2 3.4 %collective-permute-start.47 = (bf16[128,256]{1,0:T(8,128)(2,1)}, bf16[128,256]{1,0:T(8,128)(2,1)S(1)}, u32[]{:S(2)}, u32[]{:S(2)}) collective-permute-start(bf16[128,256]{1,0:T(8,128)(2,1)} %get-tuple-element.43), channel_id=1, source_target_pairs={{0,18},{1,19},{2,16},{3,17},{16,2},{17,3},{18,0},{19,1},{4,22},{5,... | collective-permute-start | bytes 196616 | tf_op jit(solution)/shard_map/ppermute | solution.py:37
  59.5 3.6 %collective-permute-start.4 = (bf16[192,512]{1,0:T(8,128)(2,1)S(1)}, bf16[192,512]{1,0:T(8,128)(2,1)S(1)}, u32[]{:S(2)}, u32[]{:S(2)}) collective-permute-start(bf16[192,512]{1,0:T(8,128)(2,1)S(1)} %copy-done.3), channel_id=1, source_target_pairs={{0,4},{4,8},{8,12},{1,5},{5,9},{9,13},{2,6},{6,10},{10,14},{3,7},{... | collective-permute-start | bytes 589832 | tf_op jit(solution)/shard_map/ppermute | solution.py:351
  66.0 2.3 %collective-permute-start.34 = (bf16[64,3200]{1,0:T(8,128)(2,1)S(1)}, bf16[64,3200]{1,0:T(8,128)(2,1)S(1)}, u32[]{:S(2)}, u32[]{:S(2)}) collective-permute-start(bf16[64,3200]{1,0:T(8,128)(2,1)S(1)} %get-tuple-element.35.refs_31_), channel_id=1, source_target_pairs={{0,2},{2,0},{1,3},{3,1},{4,6},{6,4},{5,7},{7,5},{8,10},{10,8},{9,1... | collective-permute-start | bytes 1228808 | tf_op jit(solution)/shard_map/ppermute | solution.py:37
  68.2 4.5 %collective-permute-start.8 = (bf16[192,512]{1,0:T(8,128)(2,1)S(1)}, bf16[192,512]{1,0:T(8,128)(2,1)S(1)}, u32[]{:S(2)}, u32[]{:S(2)}) collective-permute-start(bf16[192,512]{1,0:T(8,128)(2,1)S(1)} %collective-permute-done.refs_4_), channel_id=1, source_target_pairs={{0,4},{4,8},{8,12},{1,5},{5,9},{9,13},{2,6},{6,10},{10,14},{3,7},{... | collective-permute-start | bytes 589832 | tf_op jit(solution)/shard_map/ppermute | solution.py:351
  74.1 4.6 %collective-permute-start.12 = (bf16[192,512]{1,0:T(8,128)(2,1)S(1)}, bf16[192,512]{1,0:T(8,128)(2,1)S(1)}, u32[]{:S(2)}, u32[]{:S(2)}) collective-permute-start(bf16[192,512]{1,0:T(8,128)(2,1)S(1)} %collective-permute-done.1.refs_5_), channel_id=1, source_target_pairs={{0,4},{4,8},{8,12},{1,5},{5,9},{9,13},{2,6},{6,10},{10,14},{3,7},{... | collective-permute-start | bytes 589832 | tf_op jit(solution)/shard_map/ppermute | solution.py:351
  84.4 1.9 collective-permute-done.6.refs_16_
  86.4 2.0 collective-permute-start.36
  88.4 1.4 collective-permute-start.32
  89.7 2.2 %collective-permute-done.30.refs_35_ = bf16[64,3200]{1,0:T(8,128)(2,1)S(1)} collective-permute-done((bf16[64,3200]{1,0:T(8,128)(2,1)S(1)}, bf16[64,3200]{1,0:T(8,128)(2,1)S(1)}, u32[]{:S(2)}, u32[]{:S(2)}) %collective-permute-start.30) | collective-permute-done | bytes 409632 | tf_op jit(solution)/shard_map/ppermute | solution.py:37
  93.9 2.4 %collective-permute-done.36.refs_41_ = bf16[64,3200]{1,0:T(8,128)(2,1)S(1)} collective-permute-done((bf16[64,3200]{1,0:T(8,128)(2,1)S(1)}, bf16[64,3200]{1,0:T(8,128)(2,1)S(1)}, u32[]{:S(2)}, u32[]{:S(2)}) %collective-permute-start.36) | collective-permute-done | bytes 409632 | tf_op jit(solution)/shard_map/ppermute | solution.py:37
  101.8 10.1 %collective-permute-start.16 = (bf16[192,512]{1,0:T(8,128)(2,1)S(1)}, bf16[192,512]{1,0:T(8,128)(2,1)S(1)}, u32[]{:S(2)}, u32[]{:S(2)}) collective-permute-start(bf16[192,512]{1,0:T(8,128)(2,1)S(1)} %collective-permute-done.3.refs_6_), channel_id=1, source_target_pairs={{0,4},{4,8},{8,12},{1,5},{5,9},{9,13},{2,6},{6,10},{10,14},{3,7},{... | collective-permute-start | bytes 589832 | tf_op jit(solution)/shard_map/ppermute | solution.py:351
  117.3 4.4 %collective-permute-done.7.refs_8_ = bf16[192,512]{1,0:T(8,128)(2,1)S(1)} collective-permute-done((bf16[192,512]{1,0:T(8,128)(2,1)S(1)}, bf16[192,512]{1,0:T(8,128)(2,1)S(1)}, u32[]{:S(2)}, u32[]{:S(2)}) %collective-permute-start.7) | collective-permute-done | bytes 196640 | tf_op jit(solution)/shard_map/ppermute | solution.py:352
  122.5 1.7 collective-permute-done.11.refs_10_
  124.2 2.7 %collective-permute-start.38 = (bf16[64,3200]{1,0:T(8,128)(2,1)S(1)}, bf16[64,3200]{1,0:T(8,128)(2,1)S(1)}, u32[]{:S(2)}, u32[]{:S(2)}) collective-permute-start(bf16[64,3200]{1,0:T(8,128)(2,1)S(1)} %collective-permute-done.30.refs_35_), channel_id=1, source_target_pairs={{0,2},{2,0},{1,3},{3,1},{4,6},{6,4},{5,7},{7,5},{8,10},{10,8},{9,1... | collective-permute-start | bytes 1228808 | tf_op jit(solution)/shard_map/ppermute | solution.py:37
  129.3 5.6 %collective-permute-done.18.refs_22_ = bf16[192,512]{1,0:T(8,128)(2,1)S(1)} collective-permute-done((bf16[192,512]{1,0:T(8,128)(2,1)S(1)}, bf16[192,512]{1,0:T(8,128)(2,1)S(1)}, u32[]{:S(2)}, u32[]{:S(2)}) %collective-permute-start.18) | collective-permute-done | bytes 196640 | tf_op jit(solution)/shard_map/ppermute | solution.py:352
  139.2 7.2 %collective-permute-done.19.refs_14_ = bf16[192,512]{1,0:T(8,128)(2,1)S(1)} collective-permute-done((bf16[192,512]{1,0:T(8,128)(2,1)S(1)}, bf16[192,512]{1,0:T(8,128)(2,1)S(1)}, u32[]{:S(2)}, u32[]{:S(2)}) %collective-permute-start.19) | collective-permute-done | bytes 196640 | tf_op jit(solution)/shard_map/ppermute | solution.py:352
  147.3 17.3 %attend.1 = (bf16[32,384]{1,0:T(8,128)(2,1)S(1)}, bf16[32,384]{1,0:T(8,128)(2,1)S(1)}, bf16[32,384]{1,0:T(8,128)(2,1)S(1)}, bf16[32,384]{1,0:T(8,128)(2,1)S(1)},...) custom-call(s32[2]{0:T(128)S(1)} %copy-done.11, ...), custom_call_target="tpu_custom_call" | custom-call | tf_op jit(solution)/shard_map/attend/pallas_call | solution.py:250
  170.1 2.1 %collective-permute-start.55 = (bf16[32,384]{1,0:T(8,128)(2,1)S(1)}, bf16[32,384]{1,0:T(8,128)(2,1)S(1)}, u32[]{:S(2)}, u32[]{:S(2)}) collective-permute-start(bf16[32,384]{1,0:T(8,128)(2,1)S(1)} %get-tuple-element.52), channel_id=1, source_target_pairs={{0,19},{1,18},{2,17},{3,16},{16,3},{17,2},{18,1},{19,0},{4,23},{5,... | collective-permute-start | bytes 73736 | tf_op jit(solution)/shard_map/ppermute | solution.py:37
  172.2 2.1 %collective-permute-done.54.refs_6_ = bf16[32,384]{1,0:T(8,128)(2,1)S(1)} collective-permute-done((bf16[32,384]{1,0:T(8,128)(2,1)S(1)}, bf16[32,384]{1,0:T(8,128)(2,1)S(1)}, u32[]{:S(2)}, u32[]{:S(2)}) %collective-permute-start.54) | collective-permute-done | bytes 24608 | tf_op jit(solution)/shard_map/ppermute | solution.py:37
  175.0 1.5 sum_pieces.1.refs_0_
  176.6 4.0 %collective-permute-start.58 = (bf16[48,384]{1,0:T(8,128)(2,1)}, bf16[48,384]{1,0:T(8,128)(2,1)S(1)}, u32[]{:S(2)}, u32[]{:S(2)}) collective-permute-start(bf16[48,384]{1,0:T(8,128)(2,1)} %sum_pieces.1.refs_0_), channel_id=1, source_target_pairs={{0,12},{4,8},{8,4},{12,0},{1,13},{5,9},{9,5},{13,1},{2,14},{6,10},... | collective-permute-start | bytes 110600 | tf_op jit(solution)/shard_map/ppermute | solution.py:37
  181.2 1.6 collective-permute-done.58.refs_3_
  182.7 2.9 %collective-permute-done.57.refs_2_ = bf16[48,384]{1,0:T(8,128)(2,1)S(1)} collective-permute-done((bf16[48,384]{1,0:T(8,128)(2,1)}, bf16[48,384]{1,0:T(8,128)(2,1)S(1)}, u32[]{:S(2)}, u32[]{:S(2)}) %collective-permute-start.57) | collective-permute-done | bytes 36896 | tf_op jit(solution)/shard_map/ppermute | solution.py:37
  186.9 1.5 scale_sum.1.refs_0_
  188.4 1.4 collective-permute-start.64
  189.8 1.4 collective-permute-start.63
  191.2 1.5 collective-permute-start.62
  198.4 1.7 spread.1
  (201 shorter events, 51.4 us)
Async XLA Ops:
  27.1 35.9 %collective-permute-start = (bf16[192,512]{1,0:T(8,128)(2,1)}, bf16[192,512]{1,0:T(8,128)(2,1)S(1)}, u32[]{:S(2)}, u32[]{:S(2)}) collective-permute-start(bf16[192,512]{1,0:T(8,128)(2,1)} %get-tuple-element.32), channel_id=1, source_target_pairs={{0,1},{1,0},{2,3},{3,2},{4,5},{5,4},{6,7},{7,6},{8,9},{9,8},{10,11... | collective-permute-start | bytes 589832 | tf_op jit(solution)/shard_map/ppermute | solution.py:37
  55.1 10.9 %collective-permute-start.1 = (bf16[192,512]{1,0:T(8,128)(2,1)}, bf16[192,512]{1,0:T(8,128)(2,1)S(1)}, u32[]{:S(2)}, u32[]{:S(2)}) collective-permute-start(bf16[192,512]{1,0:T(8,128)(2,1)} %get-tuple-element.33), channel_id=1, source_target_pairs={{0,2},{2,0},{1,3},{3,1},{4,6},{6,4},{5,7},{7,5},{8,10},{10,8},{9,1... | collective-permute-start | bytes 589832 | tf_op jit(solution)/shard_map/ppermute | solution.py:37
  55.8 12.4 %collective-permute-start.2 = (bf16[192,512]{1,0:T(8,128)(2,1)}, bf16[192,512]{1,0:T(8,128)(2,1)S(1)}, u32[]{:S(2)}, u32[]{:S(2)}) collective-permute-start(bf16[192,512]{1,0:T(8,128)(2,1)} %get-tuple-element.34), channel_id=1, source_target_pairs={{0,1},{1,0},{2,3},{3,2},{4,5},{5,4},{6,7},{7,6},{8,9},{9,8},{10,11... | collective-permute-start | bytes 589832 | tf_op jit(solution)/shard_map/ppermute | solution.py:37
  57.2 15.6 %collective-permute-start.5 = (bf16[192,512]{1,0:T(8,128)(2,1)S(1)}, bf16[192,512]{1,0:T(8,128)(2,1)S(1)}, u32[]{:S(2)}, u32[]{:S(2)}) collective-permute-start(bf16[192,512]{1,0:T(8,128)(2,1)S(1)} %copy-done.3), channel_id=1, source_target_pairs={{4,0},{8,4},{12,8},{5,1},{9,5},{13,9},{6,2},{10,6},{14,10},{7,3},{... | collective-permute-start | bytes 589832 | tf_op jit(solution)/shard_map/ppermute | solution.py:352
  59.5 14.6 %collective-permute-start.4 = (bf16[192,512]{1,0:T(8,128)(2,1)S(1)}, bf16[192,512]{1,0:T(8,128)(2,1)S(1)}, u32[]{:S(2)}, u32[]{:S(2)}) collective-permute-start(bf16[192,512]{1,0:T(8,128)(2,1)S(1)} %copy-done.3), channel_id=1, source_target_pairs={{0,4},{4,8},{8,12},{1,5},{5,9},{9,13},{2,6},{6,10},{10,14},{3,7},{... | collective-permute-start | bytes 589832 | tf_op jit(solution)/shard_map/ppermute | solution.py:351
  63.1 15.6 %collective-permute-start.9 = (bf16[192,512]{1,0:T(8,128)(2,1)S(1)}, bf16[192,512]{1,0:T(8,128)(2,1)S(1)}, u32[]{:S(2)}, u32[]{:S(2)}) collective-permute-start(bf16[192,512]{1,0:T(8,128)(2,1)S(1)} %collective-permute-done.refs_4_), channel_id=1, source_target_pairs={{4,0},{8,4},{12,8},{5,1},{9,5},{13,9},{6,2},{10,6},{14,10},{7,3},{... | collective-permute-start | bytes 589832 | tf_op jit(solution)/shard_map/ppermute | solution.py:352
  66.0 23.7 %collective-permute-start.34 = (bf16[64,3200]{1,0:T(8,128)(2,1)S(1)}, bf16[64,3200]{1,0:T(8,128)(2,1)S(1)}, u32[]{:S(2)}, u32[]{:S(2)}) collective-permute-start(bf16[64,3200]{1,0:T(8,128)(2,1)S(1)} %get-tuple-element.35.refs_31_), channel_id=1, source_target_pairs={{0,2},{2,0},{1,3},{3,1},{4,6},{6,4},{5,7},{7,5},{8,10},{10,8},{9,1... | collective-permute-start | bytes 1228808 | tf_op jit(solution)/shard_map/ppermute | solution.py:37
  68.2 10.6 %collective-permute-start.8 = (bf16[192,512]{1,0:T(8,128)(2,1)S(1)}, bf16[192,512]{1,0:T(8,128)(2,1)S(1)}, u32[]{:S(2)}, u32[]{:S(2)}) collective-permute-start(bf16[192,512]{1,0:T(8,128)(2,1)S(1)} %collective-permute-done.refs_4_), channel_id=1, source_target_pairs={{0,4},{4,8},{8,12},{1,5},{5,9},{9,13},{2,6},{6,10},{10,14},{3,7},{... | collective-permute-start | bytes 589832 | tf_op jit(solution)/shard_map/ppermute | solution.py:351
  80.4 7.9 %collective-permute-start.20 = (bf16[192,512]{1,0:T(8,128)(2,1)S(1)}, bf16[192,512]{1,0:T(8,128)(2,1)S(1)}, u32[]{:S(2)}, u32[]{:S(2)}) collective-permute-start(bf16[192,512]{1,0:T(8,128)(2,1)S(1)} %collective-permute-done.4.refs_7_), channel_id=1, source_target_pairs={{4,8},{8,12},{5,9},{9,13},{6,10},{10,14},{7,11},{11,15},{20,24},{2... | collective-permute-start | bytes 589832 | tf_op jit(solution)/shard_map/ppermute | solution.py:351
  81.8 10.1 %collective-permute-start.30 = (bf16[64,3200]{1,0:T(8,128)(2,1)S(1)}, bf16[64,3200]{1,0:T(8,128)(2,1)S(1)}, u32[]{:S(2)}, u32[]{:S(2)}) collective-permute-start(bf16[64,3200]{1,0:T(8,128)(2,1)S(1)} %get-tuple-element.35.refs_31_), channel_id=1, source_target_pairs={{0,16},{16,0},{1,17},{17,1},{2,18},{18,2},{3,19},{19,3},{4,20},{20... | collective-permute-start | bytes 1228808 | tf_op jit(solution)/shard_map/ppermute | solution.py:37
  84.4 8.8 %collective-permute-start.28 = (bf16[64,3200]{1,0:T(8,128)(2,1)S(1)}, bf16[64,3200]{1,0:T(8,128)(2,1)S(1)}, u32[]{:S(2)}, u32[]{:S(2)}) collective-permute-start(bf16[64,3200]{1,0:T(8,128)(2,1)S(1)} %get-tuple-element.35.refs_31_), channel_id=1, source_target_pairs={{0,1},{1,0},{2,3},{3,2},{4,5},{5,4},{6,7},{7,6},{8,9},{9,8},{10,11... | collective-permute-start | bytes 1228808 | tf_op jit(solution)/shard_map/ppermute | solution.py:37
  86.4 10.0 %collective-permute-start.36 = (bf16[64,3200]{1,0:T(8,128)(2,1)S(1)}, bf16[64,3200]{1,0:T(8,128)(2,1)S(1)}, u32[]{:S(2)}, u32[]{:S(2)}) collective-permute-start(bf16[64,3200]{1,0:T(8,128)(2,1)S(1)} %get-tuple-element.36.refs_33_), channel_id=1, source_target_pairs={{0,2},{2,0},{1,3},{3,1},{4,6},{6,4},{5,7},{7,5},{8,10},{10,8},{9,1... | collective-permute-start | bytes 1228808 | tf_op jit(solution)/shard_map/ppermute | solution.py:37
  88.4 10.2 %collective-permute-start.32 = (bf16[64,3200]{1,0:T(8,128)(2,1)S(1)}, bf16[64,3200]{1,0:T(8,128)(2,1)S(1)}, u32[]{:S(2)}, u32[]{:S(2)}) collective-permute-start(bf16[64,3200]{1,0:T(8,128)(2,1)S(1)} %get-tuple-element.36.refs_33_), channel_id=1, source_target_pairs={{0,16},{16,0},{1,17},{17,1},{2,18},{18,2},{3,19},{19,3},{4,20},{20... | collective-permute-start | bytes 1228808 | tf_op jit(solution)/shard_map/ppermute | solution.py:37
  89.7 9.5 %collective-permute-start.29 = (bf16[64,3200]{1,0:T(8,128)(2,1)S(1)}, bf16[64,3200]{1,0:T(8,128)(2,1)S(1)}, u32[]{:S(2)}, u32[]{:S(2)}) collective-permute-start(bf16[64,3200]{1,0:T(8,128)(2,1)S(1)} %get-tuple-element.36.refs_33_), channel_id=1, source_target_pairs={{0,1},{1,0},{2,3},{3,2},{4,5},{5,4},{6,7},{7,6},{8,9},{9,8},{10,11... | collective-permute-start | bytes 1228808 | tf_op jit(solution)/shard_map/ppermute | solution.py:37
  91.9 9.9 %collective-permute-start.10 = (bf16[192,512]{1,0:T(8,128)(2,1)S(1)}, bf16[192,512]{1,0:T(8,128)(2,1)S(1)}, u32[]{:S(2)}, u32[]{:S(2)}) collective-permute-start(bf16[192,512]{1,0:T(8,128)(2,1)S(1)} %collective-permute-done.9.refs_26_), channel_id=1, source_target_pairs={{4,0},{8,4},{5,1},{9,5},{6,2},{10,6},{7,3},{11,7},{20,16},{24,20},... | collective-permute-start | bytes 589832 | tf_op jit(solution)/shard_map/ppermute | solution.py:352
  93.2 18.7 %collective-permute-start.21 = (bf16[192,512]{1,0:T(8,128)(2,1)S(1)}, bf16[192,512]{1,0:T(8,128)(2,1)S(1)}, u32[]{:S(2)}, u32[]{:S(2)}) collective-permute-start(bf16[192,512]{1,0:T(8,128)(2,1)S(1)} %collective-permute-done.8.refs_9_), channel_id=1, source_target_pairs={{4,8},{8,12},{5,9},{9,13},{6,10},{10,14},{7,11},{11,15},{20,24},{2... | collective-permute-start | bytes 589832 | tf_op jit(solution)/shard_map/ppermute | solution.py:351
  96.3 16.9 %collective-permute-start.14 = (bf16[192,512]{1,0:T(8,128)(2,1)S(1)}, bf16[192,512]{1,0:T(8,128)(2,1)S(1)}, u32[]{:S(2)}, u32[]{:S(2)}) collective-permute-start(bf16[192,512]{1,0:T(8,128)(2,1)S(1)} %collective-permute-done.13.refs_28_), channel_id=1, source_target_pairs={{4,0},{8,4},{5,1},{9,5},{6,2},{10,6},{7,3},{11,7},{20,16},{24,20},... | collective-permute-start | bytes 589832 | tf_op jit(solution)/shard_map/ppermute | solution.py:352
  98.6 15.4 %collective-permute-start.22 = (bf16[192,512]{1,0:T(8,128)(2,1)S(1)}, bf16[192,512]{1,0:T(8,128)(2,1)S(1)}, u32[]{:S(2)}, u32[]{:S(2)}) collective-permute-start(bf16[192,512]{1,0:T(8,128)(2,1)S(1)} %collective-permute-done.12.refs_11_), channel_id=1, source_target_pairs={{4,8},{8,12},{5,9},{9,13},{6,10},{10,14},{7,11},{11,15},{20,24},{2... | collective-permute-start | bytes 589832 | tf_op jit(solution)/shard_map/ppermute | solution.py:351
  99.3 16.0 %collective-permute-start.17 = (bf16[192,512]{1,0:T(8,128)(2,1)S(1)}, bf16[192,512]{1,0:T(8,128)(2,1)S(1)}, u32[]{:S(2)}, u32[]{:S(2)}) collective-permute-start(bf16[192,512]{1,0:T(8,128)(2,1)S(1)} %collective-permute-done.3.refs_6_), channel_id=1, source_target_pairs={{4,0},{8,4},{12,8},{5,1},{9,5},{13,9},{6,2},{10,6},{14,10},{7,3},{... | collective-permute-start | bytes 589832 | tf_op jit(solution)/shard_map/ppermute | solution.py:352
  101.8 14.2 %collective-permute-start.16 = (bf16[192,512]{1,0:T(8,128)(2,1)S(1)}, bf16[192,512]{1,0:T(8,128)(2,1)S(1)}, u32[]{:S(2)}, u32[]{:S(2)}) collective-permute-start(bf16[192,512]{1,0:T(8,128)(2,1)S(1)} %collective-permute-done.3.refs_6_), channel_id=1, source_target_pairs={{0,4},{4,8},{8,12},{1,5},{5,9},{9,13},{2,6},{6,10},{10,14},{3,7},{... | collective-permute-start | bytes 589832 | tf_op jit(solution)/shard_map/ppermute | solution.py:351
  111.9 9.8 %collective-permute-start.7 = (bf16[192,512]{1,0:T(8,128)(2,1)S(1)}, bf16[192,512]{1,0:T(8,128)(2,1)S(1)}, u32[]{:S(2)}, u32[]{:S(2)}) collective-permute-start(bf16[192,512]{1,0:T(8,128)(2,1)S(1)} %collective-permute-done.6.refs_16_), channel_id=1, source_target_pairs={{4,0},{5,1},{6,2},{7,3},{20,16},{21,17},{22,18},{23,19}} | collective-permute-start | bytes 589832 | tf_op jit(solution)/shard_map/ppermute | solution.py:352
  113.3 9.1 %collective-permute-start.24 = (bf16[192,512]{1,0:T(8,128)(2,1)S(1)}, bf16[192,512]{1,0:T(8,128)(2,1)S(1)}, u32[]{:S(2)}, u32[]{:S(2)}) collective-permute-start(bf16[192,512]{1,0:T(8,128)(2,1)S(1)} %collective-permute-done.20.refs_15_), channel_id=1, source_target_pairs={{8,12},{9,13},{10,14},{11,15},{24,28},{25,29},{26,30},{27,31}} | collective-permute-start | bytes 589832 | tf_op jit(solution)/shard_map/ppermute | solution.py:351
  113.9 10.2 %collective-permute-start.11 = (bf16[192,512]{1,0:T(8,128)(2,1)S(1)}, bf16[192,512]{1,0:T(8,128)(2,1)S(1)}, u32[]{:S(2)}, u32[]{:S(2)}) collective-permute-start(bf16[192,512]{1,0:T(8,128)(2,1)S(1)} %collective-permute-done.10.refs_18_), channel_id=1, source_target_pairs={{4,0},{5,1},{6,2},{7,3},{20,16},{21,17},{22,18},{23,19}} | collective-permute-start | bytes 589832 | tf_op jit(solution)/shard_map/ppermute | solution.py:352
  115.3 11.6 %collective-permute-start.25 = (bf16[192,512]{1,0:T(8,128)(2,1)S(1)}, bf16[192,512]{1,0:T(8,128)(2,1)S(1)}, u32[]{:S(2)}, u32[]{:S(2)}) collective-permute-start(bf16[192,512]{1,0:T(8,128)(2,1)S(1)} %collective-permute-done.21.refs_17_), channel_id=1, source_target_pairs={{8,12},{9,13},{10,14},{11,15},{24,28},{25,29},{26,30},{27,31}} | collective-permute-start | bytes 589832 | tf_op jit(solution)/shard_map/ppermute | solution.py:351
  116.0 11.3 %collective-permute-start.15 = (bf16[192,512]{1,0:T(8,128)(2,1)S(1)}, bf16[192,512]{1,0:T(8,128)(2,1)S(1)}, u32[]{:S(2)}, u32[]{:S(2)}) collective-permute-start(bf16[192,512]{1,0:T(8,128)(2,1)S(1)} %collective-permute-done.14.refs_20_), channel_id=1, source_target_pairs={{4,0},{5,1},{6,2},{7,3},{20,16},{21,17},{22,18},{23,19}} | collective-permute-start | bytes 589832 | tf_op jit(solution)/shard_map/ppermute | solution.py:352
  122.4 13.0 %collective-permute-start.35 = (bf16[64,3200]{1,0:T(8,128)(2,1)S(1)}, bf16[64,3200]{1,0:T(8,128)(2,1)S(1)}, u32[]{:S(2)}, u32[]{:S(2)}) collective-permute-start(bf16[64,3200]{1,0:T(8,128)(2,1)S(1)} %collective-permute-done.34.refs_39_), channel_id=1, source_target_pairs={{0,1},{1,0},{2,3},{3,2},{4,5},{5,4},{6,7},{7,6},{8,9},{9,8},{10,11... | collective-permute-start | bytes 1228808 | tf_op jit(solution)/shard_map/ppermute | solution.py:37
  124.2 11.5 %collective-permute-start.38 = (bf16[64,3200]{1,0:T(8,128)(2,1)S(1)}, bf16[64,3200]{1,0:T(8,128)(2,1)S(1)}, u32[]{:S(2)}, u32[]{:S(2)}) collective-permute-start(bf16[64,3200]{1,0:T(8,128)(2,1)S(1)} %collective-permute-done.30.refs_35_), channel_id=1, source_target_pairs={{0,2},{2,0},{1,3},{3,1},{4,6},{6,4},{5,7},{7,5},{8,10},{10,8},{9,1... | collective-permute-start | bytes 1228808 | tf_op jit(solution)/shard_map/ppermute | solution.py:37
  126.9 10.2 %collective-permute-start.40 = (bf16[64,3200]{1,0:T(8,128)(2,1)S(1)}, bf16[64,3200]{1,0:T(8,128)(2,1)S(1)}, u32[]{:S(2)}, u32[]{:S(2)}) collective-permute-start(bf16[64,3200]{1,0:T(8,128)(2,1)S(1)} %collective-permute-done.36.refs_41_), channel_id=1, source_target_pairs={{0,16},{16,0},{1,17},{17,1},{2,18},{18,2},{3,19},{19,3},{4,20},{20... | collective-permute-start | bytes 1228808 | tf_op jit(solution)/shard_map/ppermute | solution.py:37
  135.7 10.7 %collective-permute-start.39 = (bf16[64,3200]{1,0:T(8,128)(2,1)S(1)}, bf16[64,3200]{1,0:T(8,128)(2,1)S(1)}, u32[]{:S(2)}, u32[]{:S(2)}) collective-permute-start(bf16[64,3200]{1,0:T(8,128)(2,1)S(1)} %collective-permute-done.38.refs_43_), channel_id=1, source_target_pairs={{0,1},{1,0},{2,3},{3,2},{4,5},{5,4},{6,7},{7,6},{8,9},{9,8},{10,11... | collective-permute-start | bytes 1228808 | tf_op jit(solution)/shard_map/ppermute | solution.py:37
  137.1 9.2 %collective-permute-start.41 = (bf16[64,3200]{1,0:T(8,128)(2,1)S(1)}, bf16[64,3200]{1,0:T(8,128)(2,1)S(1)}, u32[]{:S(2)}, u32[]{:S(2)}) collective-permute-start(bf16[64,3200]{1,0:T(8,128)(2,1)S(1)} %collective-permute-done.40.refs_45_), channel_id=1, source_target_pairs={{0,1},{1,0},{2,3},{3,2},{4,5},{5,4},{6,7},{7,6},{8,9},{9,8},{10,11... | collective-permute-start | bytes 1228808 | tf_op jit(solution)/shard_map/ppermute | solution.py:37
  137.2 9.2 %collective-permute-start.19 = (bf16[192,512]{1,0:T(8,128)(2,1)S(1)}, bf16[192,512]{1,0:T(8,128)(2,1)S(1)}, u32[]{:S(2)}, u32[]{:S(2)}) collective-permute-start(bf16[192,512]{1,0:T(8,128)(2,1)S(1)} %collective-permute-done.18.refs_22_), channel_id=1, source_target_pairs={{4,0},{5,1},{6,2},{7,3},{20,16},{21,17},{22,18},{23,19}} | collective-permute-start | bytes 589832 | tf_op jit(solution)/shard_map/ppermute | solution.py:352
  138.5 7.9 %collective-permute-start.27 = (bf16[192,512]{1,0:T(8,128)(2,1)S(1)}, bf16[192,512]{1,0:T(8,128)(2,1)S(1)}, u32[]{:S(2)}, u32[]{:S(2)}) collective-permute-start(bf16[192,512]{1,0:T(8,128)(2,1)S(1)} %collective-permute-done.23.refs_21_), channel_id=1, source_target_pairs={{8,12},{9,13},{10,14},{11,15},{24,28},{25,29},{26,30},{27,31}} | collective-permute-start | bytes 589832 | tf_op jit(solution)/shard_map/ppermute | solution.py:351
  (80 other events, 1261.9 us)

commit v2 on v1

v2 whole, which is shorter than its diff:
```python
import functools
import math

import jax
import jax.numpy as jnp
from jax import lax
from jax.experimental import pallas as pl
from jax.experimental.pallas import tpu as pltpu
from jax.sharding import Mesh
from jax.sharding import PartitionSpec as P

HEAD_SIZE = 128
LANES = 128

CAP = 50.0
QSCALE = 1.0 / 12.0
ADAPTER_NAME = 0.5
EPS = 1e-06

GROUP = ("ctx", "y", "c")
ANY = pl.BlockSpec(memory_space=pl.ANY)
VMEM = pl.BlockSpec(memory_space=pltpu.VMEM)
SMEM = pl.BlockSpec(memory_space=pltpu.SMEM)

NT = (((1,), (1,)), ((), ()))
TN = (((0,), (0,)), ((), ()))


def dot(a, b, dims=(((1,), (0,)), ((), ()))):
    return lax.dot_general(a, b, dims, preferred_element_type=jnp.float32)


def swapped(value, axes, distance):
    count = 1
    for axis in axes:
        count *= lax.axis_size(axis)
    return lax.ppermute(value, axes, [(i, i ^ distance) for i in range(count)])


def pack_weights_kernel(heads, place, qw, kw, vw, out):
    group = heads * HEAD_SIZE
    for index in range(out.shape[0]):
        mine = (place[0] // 4) * 4 + index
        for src, at, wide in ((qw, 0, group), (kw, group, HEAD_SIZE), (vw, group + HEAD_SIZE, HEAD_SIZE)):
            out[index, :, at : at + wide] = src[:, pl.ds(pl.multiple_of(mine * wide, wide), wide)]


def pack_weights(place, qw, kw, vw, heads):
    return pl.pallas_call(
        functools.partial(pack_weights_kernel, heads),
        out_shape=jax.ShapeDtypeStruct((4, qw.shape[0], (heads + 2) * HEAD_SIZE), qw.dtype),
        in_specs=[SMEM, VMEM, VMEM, VMEM],
        out_specs=VMEM,
        name="pack_weights",
    )(place, qw, kw, vw)


def fence_kernel(*refs):
    pass


def fence(values, *earlier):
    count = len(values)
    return pl.pallas_call(
        fence_kernel,
        out_shape=[jax.ShapeDtypeStruct(value.shape, value.dtype) for value in values],
        in_specs=[ANY] * (count + len(earlier)),
        out_specs=[ANY] * count,
        input_output_aliases={i: i for i in range(count)},
        name="fence",
    )(*values, *earlier)


def norm_kernel(tokens, trace, gain, down_q, down_v, *rest):
    out = rest[-1]
    flt = tokens[...].astype(jnp.float32)
    meansq = jnp.mean(flt * flt, axis=-1, keepdims=True)
    normed = (flt * lax.rsqrt(meansq + EPS) * gain[...].astype(jnp.float32)[None, :]).astype(jnp.bfloat16)
    rows, feats = normed.shape
    rank = down_q.shape[0]
    low_q = dot(normed, down_q[...], NT)
    low_v = dot(normed, down_v[...], NT)
    square = (rows, rows)
    diagonal = lax.broadcasted_iota(jnp.int32, square, 0) == lax.broadcasted_iota(jnp.int32, square, 1)
    ids = jnp.sum(jnp.where(diagonal, trace[...].astype(jnp.float32), 0.0), axis=1, keepdims=True)
    filler = jnp.zeros((rows, LANES - 2 * rank - 1), jnp.float32)
    extra = jnp.concatenate([low_q, low_v, ids, filler], 1).astype(jnp.bfloat16)
    out[:, :feats] = normed
    out[:, feats:] = extra


def norm_tokens(tokens, trace, gain, down_q, down_v, *earlier):
    rows, feats = tokens.shape
    return pl.pallas_call(
        norm_kernel,
        out_shape=jax.ShapeDtypeStruct((rows, feats + LANES), jnp.bfloat16),
        in_specs=[VMEM] * 5 + [ANY] * len(earlier),
        out_specs=VMEM,
        compiler_params=pltpu.CompilerParams(vmem_limit_bytes=32 * 2**20),
        name="norm_tokens",
    )(tokens, trace, gain, down_q, down_v, *earlier)


class Loads:
    def __init__(self, sems):
        self.sems, self.count, self.waits = sems, 0, []

    def add(self, place, pieces, target):
        for piece, src in pieces:
            offset, sequence, choice = piece
            begin = pl.multiple_of(offset(place), 16)
            rows = src.shape[-2]
            if choice is not None and len(src.shape) == 3:
                src = src.at[choice(place)]
            copy = pltpu.make_async_copy(src, target.at[pl.ds(begin, rows), :], self.sems.at[self.count])
            copy.start()
            self.waits.append((sequence, copy))
            self.count += 1

    def add_either(self, condition, first, second, target):
        copies = [pltpu.make_async_copy(src, target, self.sems.at[self.count]) for src in (first, second)]
        pl.when(condition)(copies[0].start)
        pl.when(jnp.logical_not(condition))(copies[1].start)
        self.waits.append((0, copies[0]))
        self.count += 1

    def wait(self, sequence):
        for needed, copy in self.waits:
            if needed == sequence:
                copy.wait()


def project_kernel(plan, *refs):
    n_x, shards = len(plan["x"]), plan["shards"]
    place, up_q, up_v = refs[:3]
    x_refs, w_refs, rest = refs[3 : 3 + n_x], refs[3 + n_x : -4], refs[-4:]
    out, x_all, w_all, sems = rest
    feats, heads, seq = plan["feats"], plan["heads"], plan["seq"]
    rank, group = up_q.shape[0], heads * HEAD_SIZE
    depth = plan["depth"]

    loads, at = Loads(sems), 0
    for index, (_, condition, sources) in enumerate(shards):
        target = w_all.at[pl.ds(index * depth, depth), :]
        if condition is None:
            loads.add(place, [((lambda p, i=index: i * depth, 0, None), w_refs[at])], w_all)
        else:
            loads.add_either(condition(place), w_refs[at], w_refs[at + 1], target)
        at += len(sources)
    loads.add(place, list(zip(plan["x"], x_refs)), x_all)

    mine = place[0]
    uq = up_q[:, pl.ds(pl.multiple_of(mine * group, group), group)]
    uv = up_v[:, pl.ds(pl.multiple_of(mine * HEAD_SIZE, HEAD_SIZE), HEAD_SIZE)]
    zero = functools.partial(jnp.zeros, dtype=jnp.float32)
    top = jnp.concatenate([ADAPTER_NAME * uq.astype(jnp.float32), zero((rank, 2 * HEAD_SIZE))], 1)
    low = jnp.concatenate([zero((rank, group + HEAD_SIZE)), ADAPTER_NAME * uv.astype(jnp.float32)], 1)
    pad = zero((LANES - 2 * rank, group + 2 * HEAD_SIZE))
    ups = jnp.concatenate([top, low, pad], 0).astype(jnp.bfloat16)

    for index in range(x_all.shape[0] // seq):
        loads.wait(index)
        rows = pl.ds(index * seq, seq)
        total = dot(x_all[rows, feats:], ups)
        for number, (offset, _, _) in enumerate(shards):
            columns = pl.ds(pl.multiple_of(offset(place), LANES), depth)
            total = total + dot(x_all[rows, columns], w_all[number * depth : (number + 1) * depth])
        out[rows, :] = total


def attend_kernel(plan, *refs):
    n_x, n_g, last = len(plan["x"]), len(plan["g"]), plan["last"]
    place, up_q, up_v, base = refs[:4]
    x_refs, g_refs = refs[4 : 4 + n_x], refs[4 + n_x : 4 + n_x + n_g]
    w_refs, rest = refs[4 + n_x + n_g : -8], refs[-8:]
    ga_out, gb_out, x_all, g_all, w_all, base_all, pulls, sems = rest

    feats, heads, seq, window, depth = (plan[k] for k in ("feats", "heads", "seq", "window", "depth"))
    rank, parts = up_q.shape[0], plan["parts"]
    group = heads * HEAD_SIZE
    tokens = x_all.shape[0]
    sequences = tokens // seq

    loads = Loads(sems)
    if last is not None:
        offset, condition = last
        copy = pltpu.make_async_copy(w_refs[0], w_all, sems.at[loads.count])
        loads.count += 1
        pl.when(condition(place))(copy.start)
    for index in range(sequences):
        rows = pl.ds(index * seq, seq)
        copy_base = pltpu.make_async_copy(base.at[rows, :], base_all.at[rows, :], sems.at[loads.count])
        copy_base.start()
        loads.waits.append((index, copy_base))
        loads.count += 1
        for pieces, sources, target in ((plan["x"], x_refs, x_all), (plan["g"], g_refs, g_all)):
            chosen = [(piece, src) for piece, src in zip(pieces, sources) if piece[1] == index]
            loads.add(place, chosen, target)
    if last is not None:

        @pl.when(jnp.logical_not(condition(place)))
        def _():
            w_all[...] = w_refs[1][...]

        pl.when(condition(place))(copy.wait)

    mine = place[0]
    uq = up_q[:, pl.ds(pl.multiple_of(mine * group, group), group)]
    uv = up_v[:, pl.ds(pl.multiple_of(mine * HEAD_SIZE, HEAD_SIZE), HEAD_SIZE)]
    id_row = jnp.where(lax.broadcasted_iota(jnp.int32, (8, LANES), 1) == 2 * rank, 1.0, 0.0).astype(jnp.bfloat16)
    span = min(seq, window)
    blocks = seq // span
    sums = jnp.zeros((LANES, group + 2 * HEAD_SIZE), jnp.float32)

    for index in range(sequences):
        loads.wait(index)
        rows = pl.ds(index * seq, seq)
        qkv = base_all[rows, :]
        if last is not None:
            columns = pl.ds(pl.multiple_of(offset(place), LANES), depth)
            qkv = qkv + dot(x_all[rows, columns], w_all[...])
        qkv = qkv.astype(jnp.bfloat16)
        extra = x_all[rows, feats:]
        ids_key = dot(id_row, extra, NT)[:1]
        ids_query = extra[:, 2 * rank : 2 * rank + 1].astype(jnp.float32)
        keys = qkv[:, group : group + HEAD_SIZE]
        values = qkv[:, group + HEAD_SIZE :]
        grads = g_all[rows, :]
        dq_parts = [[] for _ in range(heads)]
        dv_parts = [None] * blocks
        for block in range(blocks):
            lo, hi = block * span, (block + 1) * span
            back = max(0, lo - span)
            kb, vb = keys[back:hi], values[back:hi]
            shape = (span, hi - back)
            pos_q = lax.broadcasted_iota(jnp.int32, shape, 0) + lo
            pos_k = lax.broadcasted_iota(jnp.int32, shape, 1) + back
            mask = (pos_k <= pos_q) & (pos_k > pos_q - window)
            mask = mask & (ids_query[lo:hi] == ids_key[:, back:hi])
            for head in range(heads):
                cols = slice(head * HEAD_SIZE, (head + 1) * HEAD_SIZE)
                q, g = qkv[lo:hi, cols], grads[lo:hi, cols]
                t = jnp.tanh(dot(q, kb, NT) * (QSCALE / CAP))
                expo = jnp.where(mask, jnp.exp(CAP * t), 0.0)
                weights = expo / jnp.sum(expo, axis=-1, keepdims=True)
                weights16 = weights.astype(jnp.bfloat16)
                dweight = dot(g, vb, NT)
                delta = jnp.sum(weights16.astype(jnp.float32) * dweight, axis=-1, keepdims=True)
                dscore = (weights * (dweight - delta) * (1.0 - t * t) * QSCALE).astype(jnp.bfloat16)
                dq_parts[head].append(dot(dscore, kb).astype(jnp.bfloat16))
                dv = dot(weights16, g, TN)
                for at in range(back // span, block + 1):
                    piece = dv[at * span - back : (at + 1) * span - back]
                    dv_parts[at] = piece if dv_parts[at] is None else dv_parts[at] + piece
        dq = jnp.concatenate([jnp.concatenate(some, 0) for some in dq_parts], 1)
        dv = jnp.concatenate(dv_parts, 0)
        dv_hi = dv.astype(jnp.bfloat16)
        dv_lo = (dv - dv_hi.astype(jnp.float32)).astype(jnp.bfloat16)
        pull_q = dot(uq, dq, NT)
        pull_v = dot(uv, dv_hi, NT) + dot(uv, dv_lo, NT)
        pull_v_hi = pull_v.astype(jnp.bfloat16)
        pull_v_lo = (pull_v - pull_v_hi.astype(jnp.float32)).astype(jnp.bfloat16)
        pulls[:, rows] = jnp.concatenate([pull_q.astype(jnp.bfloat16), pull_v_hi, pull_v_lo], 0)
        sums = sums + dot(extra, jnp.concatenate([dq, dv_hi, dv_lo], 1), TN)

    gb_out[:, :group] = sums[:rank, :group]
    gb_out[:, group:] = sums[rank : 2 * rank, group : group + HEAD_SIZE] + sums[rank : 2 * rank, group + HEAD_SIZE :]
    part = feats // parts
    for index in range(parts):
        piece = dot(pulls[...], x_all[:, index * part : (index + 1) * part])
        ga_out[index, :rank] = piece[:rank].astype(ga_out.dtype)
        ga_out[index, rank:] = (piece[rank : 2 * rank] + piece[2 * rank :]).astype(ga_out.dtype)


def attend(place, up_q, up_v, gathered, plan):
    feats, heads, tokens, parts, seq = (plan[k] for k in ("feats", "heads", "tokens", "parts", "seq"))
    rank = up_q.shape[0]
    wide = (heads + 2) * HEAD_SIZE
    x_plan, x_arrays = zip(*gathered["x"])
    g_plan, g_arrays = zip(*gathered["g"])
    shards = gathered["w"]
    w_arrays = [array for _, _, sources in shards for array in sources]
    depth = w_arrays[0].shape[0]
    plan = dict(plan, x=x_plan, g=g_plan, shards=shards, depth=depth)
    params = pltpu.CompilerParams(vmem_limit_bytes=60 * 2**20)
    base = pl.pallas_call(
        functools.partial(project_kernel, plan),
        out_shape=jax.ShapeDtypeStruct((tokens, wide), jnp.float32),
        in_specs=[SMEM, VMEM, VMEM] + [ANY] * (len(x_arrays) + len(w_arrays)),
        out_specs=VMEM,
        scratch_shapes=[
            pltpu.VMEM((tokens, feats + LANES), jnp.bfloat16),
            pltpu.VMEM((len(shards) * depth, wide), jnp.bfloat16),
            pltpu.SemaphoreType.DMA((len(x_arrays) + len(shards),)),
        ],
        compiler_params=params,
        cost_estimate=pl.CostEstimate(
            flops=2 * tokens * len(shards) * depth * wide,
            bytes_accessed=2 * tokens * feats + 2 * len(shards) * depth * wide + 4 * tokens * wide,
            transcendentals=0,
        ),
        name="project",
    )(place, up_q, up_v, *x_arrays, *w_arrays)

    offset, condition, sources = gathered["last"] or (None, None, [])
    plan["last"] = None if offset is None else (offset, condition)
    return pl.pallas_call(
        functools.partial(attend_kernel, plan),
        out_shape=[
            jax.ShapeDtypeStruct((parts, 2 * rank, feats // parts), jnp.bfloat16),
            jax.ShapeDtypeStruct((rank, (heads + 1) * HEAD_SIZE), jnp.float32),
        ],
        in_specs=[SMEM, VMEM, VMEM]
        + [ANY] * (1 + len(x_arrays) + len(g_arrays))
        + [ANY, VMEM][: len(sources)],
        out_specs=[VMEM] * 2,
        scratch_shapes=[
            pltpu.VMEM((tokens, feats + LANES), jnp.bfloat16),
            pltpu.VMEM((tokens, heads * HEAD_SIZE), jnp.bfloat16),
            pltpu.VMEM((depth, wide) if sources else (16, LANES), jnp.bfloat16),
            pltpu.VMEM((tokens, wide), jnp.float32),
            pltpu.VMEM((3 * rank, tokens), jnp.bfloat16),
            pltpu.SemaphoreType.DMA((1 + tokens // seq + len(x_arrays) + len(g_arrays),)),
        ],
        compiler_params=params,
        name="attend",
    )(place, up_q, up_v, base, *x_arrays, *g_arrays, *sources)


def sum_kernel(gas, gb, out):
    total = gas[0].astype(jnp.float32)
    for index in range(1, gas.shape[0]):
        total = total + gas[index].astype(jnp.float32)
    rows = total.shape[0]
    out[:rows] = total.astype(out.dtype)
    out[rows:] = gb[...].astype(out.dtype)


def sum_pieces(gas, gb):
    _, rows, wide = gas.shape
    return pl.pallas_call(
        sum_kernel,
        out_shape=jax.ShapeDtypeStruct((rows + gb.shape[0], wide), jnp.bfloat16),
        in_specs=[VMEM] * 2,
        out_specs=VMEM,
        name="sum_pieces",
    )(gas, gb)


def scale_kernel(coefficient, *refs):
    total = refs[0][...].astype(jnp.float32)
    for ref in refs[1:-1]:
        total = total + ref[...].astype(jnp.float32)
    refs[-1][...] = (total * coefficient).astype(refs[-1].dtype)


def scale_sum(pieces, coefficient):
    return pl.pallas_call(
        functools.partial(scale_kernel, coefficient),
        out_shape=jax.ShapeDtypeStruct(pieces[0].shape, jnp.bfloat16),
        in_specs=[VMEM] * len(pieces),
        out_specs=VMEM,
        name="scale_sum",
    )(*pieces)


def spread_kernel(rank, group, place, *refs):
    pieces, (aq, bq, av, bv) = refs[:-4], refs[-4:]
    wide = pieces[0].shape[1]
    for step, ref in enumerate(pieces):
        mine = place[0] ^ step
        value = ref[...].astype(jnp.float32)
        at = pl.ds(pl.multiple_of(mine * wide, LANES), wide)
        aq[:, at] = value[:rank]
        av[:, at] = value[rank : 2 * rank]
        bq[:, pl.ds(pl.multiple_of(mine * group, LANES), group)] = value[2 * rank :, :group]
        bv[:, pl.ds(pl.multiple_of(mine * HEAD_SIZE, LANES), HEAD_SIZE)] = value[2 * rank :, group:]


def spread(place, pieces, rank, group, shapes):
    return pl.pallas_call(
        functools.partial(spread_kernel, rank, group),
        out_shape=[jax.ShapeDtypeStruct(shape, jnp.float32) for shape in shapes],
        in_specs=[SMEM] + [VMEM] * len(pieces),
        out_specs=[VMEM] * 4,
        name="spread",
    )(place, *pieces)


def outer_pairs(value):
    return lax.ppermute(value, "z", [(0, 1), (1, 0), (2, 3), (3, 2)])


def inner_pairs(value):
    return lax.ppermute(value, "z", [(0, 0), (1, 2), (2, 1), (3, 3)])


def is_inner(p):
    return (p[1] == 1) | (p[1] == 2)


def is_outer(p):
    return (p[1] == 0) | (p[1] == 3)


def paired_gather(place, qw, kw, vw, heads, norm_args, gradient):
    shard, rows = qw.shape[0], norm_args[0].shape[0]
    packed = pack_weights(place, qw, kw, vw, heads)
    own = lax.all_to_all(packed, ("y", "c"), 0, 0, tiled=True).reshape(4 * shard, -1)
    normed = norm_tokens(*norm_args, packed)

    c_tokens = swapped(normed, ("c",), 1)
    x_tokens = swapped(normed, ("ctx",), 1)
    (later,) = fence((norm_tokens(*norm_args, normed),), own, c_tokens)
    y_tokens = swapped(later, ("y",), 1)
    hop_2, hop_1 = inner_pairs(own), outer_pairs(own)
    xc_tokens, xy_tokens = swapped(x_tokens, ("c",), 1), swapped(x_tokens, ("y",), 1)

    hop_4, hop_3 = inner_pairs(hop_1), outer_pairs(hop_2)
    (gradient,) = fence((gradient,), hop_1, xc_tokens)
    gradient = lax.all_to_all(gradient, GROUP, 0, 0, tiled=True)
    yc_tokens = swapped(y_tokens, ("c",), 1)

    hop_5 = outer_pairs(hop_4)
    (xy_tokens,) = fence((xy_tokens,), hop_3, hop_4, yc_tokens)
    xyc_tokens = swapped(xy_tokens, ("c",), 1)

    def weight_columns(back):
        return lambda p: (p[1] ^ back) * 4 * shard

    def token_rows(step):
        return lambda p: (step & 3) * 2 * rows + ((p[0] >> 2) ^ (step >> 2)) * rows

    def source(step):
        return lambda p: p[0] ^ step

    tokens = (normed, c_tokens, y_tokens, yc_tokens, x_tokens, xc_tokens, xy_tokens, xyc_tokens)
    return {
        "w": [
            (weight_columns(0), None, [own]),
            (weight_columns(1), None, [hop_1]),
            (weight_columns(2), is_inner, [hop_4, hop_3]),
        ],
        "last": (weight_columns(3), is_inner, [hop_2, hop_5]),
        "x": [((token_rows(step), step & 3, None), value) for step, value in enumerate(tokens)],
        "g": [((token_rows(step), step & 3, source(step)), gradient) for step in range(8)],
    }


def on_device(
    tokens,
    trace_index,
    input_norm_scale,
    query_weight,
    key_weight,
    value_weight,
    query_down_weight,
    query_up_weight,
    value_down_weight,
    value_up_weight,
    output_gradient,
):
    rows, feats = tokens.shape[1:]
    heads_kv = key_weight.shape[1] // HEAD_SIZE
    heads = query_weight.shape[1] // HEAD_SIZE // heads_kv
    group = heads * HEAD_SIZE
    rank = query_up_weight.shape[0]
    sizes = [lax.axis_size(axis) for axis in GROUP]
    parts = math.prod(sizes)
    shards = lax.axis_size("z")
    paired = sizes == [2, 2, 2] and shards == 4
    mine = lax.axis_index(GROUP)
    place = jnp.stack([mine, lax.axis_index("z")]).astype(jnp.int32)

    norm_args = (
        tokens.reshape(rows, feats),
        trace_index.reshape(1, rows),
        input_norm_scale,
        query_down_weight.T,
        value_down_weight.T,
    )
    gradient = jnp.moveaxis(output_gradient.reshape(rows, parts, group), 1, 0)
    if paired:
        gathered = paired_gather(
            place, query_weight, key_weight, value_weight, heads, norm_args, gradient
        )
    else:
        shard = query_weight.shape[0]
        split = [w.reshape(shard, parts, -1) for w in (query_weight, key_weight, value_weight)]
        columns = jnp.moveaxis(jnp.concatenate(split, -1), 1, 0)
        per = parts // sizes[0]
        columns = lax.dynamic_slice_in_dim(columns, lax.axis_index("ctx") * per, per, 0)
        columns = lax.all_to_all(columns, ("y", "c"), 0, 0, tiled=True).reshape(per * shard, -1)
        weights = lax.all_gather(columns, "z", axis=0, tiled=True)
        normed = lax.all_gather(norm_tokens(*norm_args), ("y", "c", "ctx"), axis=0, tiled=True)
        gradient = lax.all_to_all(gradient, GROUP, 0, 0, tiled=True)
        gradient = gradient.reshape(sizes[0], per, rows, group)
        gradient = jnp.moveaxis(gradient, 0, 1).reshape(parts * rows, group)
        gathered = {
            "w": [(lambda p: 0, None, [weights])],
            "last": None,
            "x": [((lambda p: 0, 0, None), normed)],
            "g": [((lambda p: 0, 0, None), gradient)],
        }

    plan = {
        "feats": feats,
        "heads": heads,
        "seq": sizes[0] * rows,
        "window": 2 * rows,
        "tokens": parts * rows,
        "parts": parts,
    }
    ga, gb = attend(place, query_up_weight, value_up_weight, gathered, plan)

    coefficient = ADAPTER_NAME / math.sqrt(parts * shards * rows)
    mixed = sum_pieces(lax.all_to_all(ga, GROUP, 0, 0, tiled=True), gb)
    if shards & (shards - 1) == 0 and shards <= 4:
        mixed = [mixed] + [swapped(mixed, ("z",), step) for step in range(1, shards)]
    else:
        mixed = [lax.psum(mixed.astype(jnp.float32), "z")]
    scaled = scale_sum(mixed, coefficient)
    scaled = [scaled] + [swapped(scaled, GROUP, step) for step in range(1, parts)]
    shapes = ((rank, feats), (rank, heads_kv * group), (rank, feats), (rank, heads_kv * HEAD_SIZE))
    aq, bq, av, bv = spread(place, scaled, rank, group, shapes)
    return aq.T, bq, av.T, bv


def solution(mesh):
    groups, ctx, fsdp = (mesh.shape[name] for name in ("groups", "ctx", "fsdp"))

    def run(*args):
        heads_kv = args[4].shape[1] // HEAD_SIZE
        share = heads_kv // ctx
        cores = 2 if share % 2 == 0 else 1
        split = (groups, ctx, fsdp // share, share // cores, cores)
        finer = Mesh(mesh.devices.reshape(split), ("groups", "ctx", "z", "y", "c"))
        whole = ("z", "y", "c")
        sequences = ("groups",) + whole
        by_rows = P(whole, None)
        by_tokens = P(sequences, "ctx", None)
        out = P("groups", None)
        return jax.shard_map(
            on_device,
            mesh=finer,
            in_specs=(
                by_tokens, P(sequences, "ctx"), P(), by_rows, by_rows, by_rows, P(), P(), P(), P(), by_tokens
            ),
            out_specs=(out, out, out, out),
            check_vma=False,
        )(*args)

    return run
```

time: 201 us -> 134 us (0.67)
  starting transfers between devices: 81.6 us -> 33.4 us
  Pallas kernels: 66.6 us -> 28 us
  blocking collectives: 0 us -> 9.68 us
  waiting for transfers between devices: 44.1 us -> 50.9 us
  local copies, waits for them, and re-layouts: 5.72 us -> 9.35 us
    ppermute x24 -> x5, starting transfers between devices: 43.6 us -> 10.9 us  [the longest x3 8.45 us: outer_pairs(): return lax.ppermute(value, 'z', [(0, 1), (1, 0), (2, 3), (3, 2)])]
    pallas_call x4 -> x8, Pallas kernels: 46.1 us -> 14.2 us  [the longest x1 8.53 us: attend(): pl.pallas_call(functools.partial(project_kernel, plan), out_shape=jax.Sha...]
    ppermute x42 -> x17, starting transfers between devices: 38 us -> 15.1 us  [swapped(): return lax.ppermute(value, axes, [(i, i ^ distance) for i in range(count)])]
    ppermute x24 -> x5, waiting for transfers between devices: 23.1 us -> 8.93 us  [the longest x3 8.93 us: outer_pairs(): return lax.ppermute(value, 'z', [(0, 1), (1, 0), (2, 3), (3, 2)])]
    ppermute x42 -> x17, waiting for transfers between devices: 21 us -> 33.9 us  [swapped(): return lax.ppermute(value, axes, [(i, i ^ distance) for i in range(count)])]
    all_to_all x0 -> x1, blocking collectives: none -> 9.68 us  [on_device(): mixed = sum_pieces(lax.all_to_all(ga, GROUP, 0, 0, tiled=True), gb)]
    all_to_all x0 -> x2, waiting for transfers between devices: none -> 8.08 us  [the longest x1 8.08 us: paired_gather(): lax.all_to_all(packed, ('y', 'c'), 0, 0, tiled=True).reshape(4 * shard, -1)]
    all_to_all x0 -> x2, starting transfers between devices: none -> 7.39 us  [the longest x1 3.9 us: paired_gather(): lax.all_to_all(packed, ('y', 'c'), 0, 0, tiled=True).reshape(4 * shard, -1)]
  transfers between devices with their start and end apart: 66 -> 24, of which waited for: 26 -> 11; matrix products, arithmetic and copies ran while one was open for 0% -> 2% of each run, Pallas kernels for 9% -> 7%
where the time goes in v2:
time: 134 us; the launch traced here: 133 us
  waiting for transfers between devices  50.9 us (38%)
  starting transfers between devices  33.4 us (25%)
  Pallas kernels  28 us (21%)
  blocking collectives  9.68 us (7%)
  local copies, waits for them, and re-layouts  9.35 us (7%)
    ppermute x17, waiting for transfers between devices, swapped(): return lax.ppermute(value, axes, [(i, i ^ distance) for i in range(count)])  33.9 us
    ppermute x17, starting transfers between devices, swapped(): return lax.ppermute(value, axes, [(i, i ^ distance) for i in range(count)])  15.1 us
    pallas_call x1, Pallas kernels, attend(): pl.pallas_call(functools.partial(attend_kernel, plan), out_shape=[jax.Sha...  10.5 us
    all_to_all x1, blocking collectives, on_device(): mixed = sum_pieces(lax.all_to_all(ga, GROUP, 0, 0, tiled=True), gb)  9.68 us
    ppermute x3, waiting for transfers between devices, outer_pairs(): return lax.ppermute(value, 'z', [(0, 1), (1, 0), (2, 3), (3, 2)])  8.93 us
    pallas_call x1, Pallas kernels, attend(): pl.pallas_call(functools.partial(project_kernel, plan), out_shape=jax.Sha...  8.53 us
    ppermute x3, starting transfers between devices, outer_pairs(): return lax.ppermute(value, 'z', [(0, 1), (1, 0), (2, 3), (3, 2)])  8.45 us
    unnamed x59, local copies, waits for them, and re-layouts  8.36 us
  transfers between devices with their start and end apart: 24, of which 11 were waited for; matrix products, arithmetic and copies ran while one was open for 2% of the time, Pallas kernels for 7%

profile of v2, /device:TPU:0, one launch (start us, length us, event | category | flops | bytes accessed | tf_op | source)
XLA Modules:
  0.0 132.9 jit_solution(4294638563516904018)
XLA Ops:
  1.4 2.4 %pack_weights.1.rest_0_ = bf16[4,192,512]{2,1,0:T(8,128)(2,1)} custom-call(s32[2]{0:T(128)} %pad_add_fusion.place.refs_0_, bf16[192,2048]{1,0:T(8,128)(2,1)} %qw.1, bf16[192,1024]{1,0:T(8,128)(2,1)} %kw.1, bf16[192,1024]{1,0:T(8,128)(2,1)} %vw.1), custom_call_target="tpu_custom_call" | custom-call | tf_op jit(solution)/shard_map/pack_weights/pallas_call | solution.py:49
  5.2 3.9 %all-to-all-start = ((bf16[4,192,512]{2,1,0:T(8,128)(2,1)}), bf16[4,192,512]{2,1,0:T(8,128)(2,1)S(1)}, u32[]{:S(2)}, u32[]{:S(2)}) async-start(bf16[4,192,512]{2,1,0:T(8,128)(2,1)} %pack_weights.1.rest_0_), calls=%async_computation | async-start | bytes 1572864 | tf_op jit(solution)/shard_map/all_to_all | solution.py:409
  9.1 2.2 %collective-permute-start.3 = (bf16[128,3200]{1,0:T(8,128)(2,1)S(1)}, bf16[128,3200]{1,0:T(8,128)(2,1)}, u32[]{:S(2)}, u32[]{:S(2)}) collective-permute-start(bf16[128,3200]{1,0:T(8,128)(2,1)S(1)} %norm_tokens.2.rest_0_.refs_3_.refs_4_), channel_id=1, source_target_pairs={{0,16},{16,0},{1,17},{17,1},{2,18},{18,2},{3,19},{19,3},{4,20},{20... | collective-permute-start | bytes 2457608 | tf_op jit(solution)/shard_map/ppermute | solution.py:37
  13.1 8.1 %all-to-all-done = bf16[4,192,512]{2,1,0:T(8,128)(2,1)S(1)} async-done(((bf16[4,192,512]{2,1,0:T(8,128)(2,1)}), bf16[4,192,512]{2,1,0:T(8,128)(2,1)S(1)}, u32[]{:S(2)}, u32[]{:S(2)}) %all-to-all-start) | async-done | bytes 786464 | tf_op jit(solution)/shard_map/all_to_all | solution.py:409
  22.3 2.1 %collective-permute-start.8 = (bf16[768,512]{1,0:T(8,128)(2,1)}, bf16[768,512]{1,0:T(8,128)(2,1)S(1)}, u32[]{:S(2)}, u32[]{:S(2)}) collective-permute-start(bf16[768,512]{1,0:T(8,128)(2,1)} %bitcast.17), channel_id=1, source_target_pairs={{0,4},{4,0},{8,12},{12,8},{1,5},{5,1},{9,13},{13,9},{2,6},{6,2},{1... | collective-permute-start | bytes 2359304 | tf_op jit(solution)/shard_map/ppermute | solution.py:391
  24.4 1.8 %collective-permute-start.6 = (bf16[768,512]{1,0:T(8,128)(2,1)}, bf16[768,512]{1,0:T(8,128)(2,1)S(1)}, u32[]{:S(2)}, u32[]{:S(2)}) collective-permute-start(bf16[768,512]{1,0:T(8,128)(2,1)} %bitcast.18), channel_id=1, source_target_pairs={{0,0},{4,8},{8,4},{12,12},{1,1},{5,9},{9,5},{13,13},{2,2},{6,10},{... | collective-permute-start | bytes 2359304 | tf_op jit(solution)/shard_map/ppermute | solution.py:395
  26.2 4.0 %collective-permute-done.3.refs_7_.refs_8_ = bf16[128,3200]{1,0:T(8,128)(2,1)} collective-permute-done((bf16[128,3200]{1,0:T(8,128)(2,1)S(1)}, bf16[128,3200]{1,0:T(8,128)(2,1)}, u32[]{:S(2)}, u32[]{:S(2)}) %collective-permute-start.3) | collective-permute-done | bytes 819232 | tf_op jit(solution)/shard_map/ppermute | solution.py:37
  30.3 1.8 %collective-permute-start.5 = (bf16[128,3200]{1,0:T(8,128)(2,1)}, bf16[128,3200]{1,0:T(8,128)(2,1)S(1)}, u32[]{:S(2)}, u32[]{:S(2)}) collective-permute-start(bf16[128,3200]{1,0:T(8,128)(2,1)} %collective-permute-done.3.refs_7_.refs_8_), channel_id=1, source_target_pairs={{0,2},{2,0},{1,3},{3,1},{4,6},{6,4},{5,7},{7,5},{8,10},{10,8},{9,1... | collective-permute-start | bytes 2457608 | tf_op jit(solution)/shard_map/ppermute | solution.py:37
  32.0 11.6 %collective-permute-done.1.refs_5_.refs_6_ = bf16[128,3200]{1,0:T(8,128)(2,1)S(1)} collective-permute-done((bf16[128,3200]{1,0:T(8,128)(2,1)}, bf16[128,3200]{1,0:T(8,128)(2,1)S(1)}, u32[]{:S(2)}, u32[]{:S(2)}) %collective-permute-start.1) | collective-permute-done | bytes 819232 | tf_op jit(solution)/shard_map/ppermute | solution.py:37
  44.4 4.6 %collective-permute-start.7 = (bf16[768,512]{1,0:T(8,128)(2,1)S(1)}, bf16[768,512]{1,0:T(8,128)(2,1)S(1)}, u32[]{:S(2)}, u32[]{:S(2)}) collective-permute-start(bf16[768,512]{1,0:T(8,128)(2,1)S(1)} %collective-permute-done.6.refs_20_), channel_id=1, source_target_pairs={{0,4},{4,0},{8,12},{12,8},{1,5},{5,1},{9,13},{13,9},{2,6},{6,2},{1... | collective-permute-start | bytes 2359304 | tf_op jit(solution)/shard_map/ppermute | solution.py:391
  49.0 11.2 %collective-permute-done.5.refs_0_ = bf16[128,3200]{1,0:T(8,128)(2,1)S(1)} collective-permute-done((bf16[128,3200]{1,0:T(8,128)(2,1)}, bf16[128,3200]{1,0:T(8,128)(2,1)S(1)}, u32[]{:S(2)}, u32[]{:S(2)}) %collective-permute-start.5) | collective-permute-done | bytes 819232 | tf_op jit(solution)/shard_map/ppermute | solution.py:37
  60.3 6.7 %collective-permute-done.7.refs_1_.refs_14_ = bf16[768,512]{1,0:T(8,128)(2,1)S(1)} collective-permute-done((bf16[768,512]{1,0:T(8,128)(2,1)S(1)}, bf16[768,512]{1,0:T(8,128)(2,1)S(1)}, u32[]{:S(2)}, u32[]{:S(2)}) %collective-permute-start.7) | collective-permute-done | bytes 786464 | tf_op jit(solution)/shard_map/ppermute | solution.py:391
  68.7 1.7 %collective-permute-start.11 = (bf16[768,512]{1,0:T(8,128)(2,1)}, bf16[768,512]{1,0:T(8,128)(2,1)}, u32[]{:S(2)}, u32[]{:S(2)}) collective-permute-start(bf16[768,512]{1,0:T(8,128)(2,1)} %copy-done.16), channel_id=1, source_target_pairs={{0,4},{4,0},{8,12},{12,8},{1,5},{5,1},{9,13},{13,9},{2,6},{6,2},{1... | collective-permute-start | bytes 2359304 | tf_op jit(solution)/shard_map/ppermute | solution.py:391
  70.5 1.3 copy.18
  71.8 1.0 copy.19
  73.7 3.5 %all-to-all-start.1 = ((bf16[8,128,256]{2,1,0:T(8,128)(2,1)}), bf16[8,128,256]{2,1,0:T(8,128)(2,1)S(1)}, u32[]{:S(2)}, u32[]{:S(2)}) async-start(bf16[8,128,256]{2,1,0:T(8,128)(2,1)} %fence.5), calls=%async_computation.1 | async-start | bytes 1048576 | tf_op jit(solution)/shard_map/all_to_all | solution.py:421
  78.2 8.5 %project.1.refs_3_ = f32[1024,512]{1,0:T(8,128)} custom-call(s32[2]{0:T(128)} %pad_add_fusion.place.refs_0_, bf16[16,2048]{1,0:T(8,128)(2,1)} %refs_1_.3, bf16[16,1024]{1,0:T(8,128)(2,1)} %refs_2_.3, bf16[128,3200]{1,0:T(8,128)(2,1)} %copy-done, bf16[128,3200]{1,0:T(8,128)(2,1)} %copy-done.8, bf16[128,3200]{1,0:T(8,128)(2,1)} %copy-done.13, ...), custom_call_target="tpu_custom_call" | custom-call | flops 2415919104 | bytes 10747904 | tf_op jit(solution)/shard_map/project/pallas_call | solution.py:286
  86.8 2.3 %collective-permute-done.11.refs_21_ = bf16[768,512]{1,0:T(8,128)(2,1)} collective-permute-done((bf16[768,512]{1,0:T(8,128)(2,1)}, bf16[768,512]{1,0:T(8,128)(2,1)}, u32[]{:S(2)}, u32[]{:S(2)}) %collective-permute-start.11) | collective-permute-done | bytes 786464 | tf_op jit(solution)/shard_map/ppermute | solution.py:391
  89.0 10.5 %attend.1 = (bf16[8,32,384]{2,1,0:T(8,128)(2,1)}, f32[16,384]{1,0:T(8,128)}) custom-call(s32[2]{0:T(128)} %pad_add_fusion.place.refs_0_, bf16[16,2048]{1,0:T(8,128)(2,1)} %refs_1_.3, bf16[16,1024]{1,0:T(8,128)(2,1)} %refs_2_.3, f32[1024,512]{1,0:T(8,128)} %project.1.refs_3_, bf16[128,3200]{1,0:T(8,128)(2,1)} %copy-done, bf16[128,3200]{1,0:T(8,128)(2,1)} %copy-done.8, ...), custom_call_target="tpu_custom_call" | custom-call | tf_op jit(solution)/shard_map/attend/pallas_call | solution.py:307
  99.5 9.7 %all_to_all.15.gas = bf16[8,32,384]{2,1,0:T(8,128)(2,1)} all-to-all(bf16[8,32,384]{2,1,0:T(8,128)(2,1)} %get-tuple-element.10), channel_id=1, replica_groups=mesh['groups'=1,'ctx'=2,'z'=4,'y'=2,'c'=2] {'ctx','y','c'}, dimensions={0} | all-to-all | bytes 393216 | tf_op jit(solution)/shard_map/all_to_all | solution.py:517
  109.2 1.6 %sum_pieces.1.refs_0_ = bf16[48,384]{1,0:T(8,128)(2,1)} custom-call(bf16[8,32,384]{2,1,0:T(8,128)(2,1)} %all_to_all.15.gas, f32[16,384]{1,0:T(8,128)} %get-tuple-element.11.gb), custom_call_target="tpu_custom_call" | custom-call | tf_op jit(solution)/shard_map/sum_pieces/pallas_call | solution.py:341
  110.8 2.0 %collective-permute-start.12 = (bf16[48,384]{1,0:T(8,128)(2,1)}, bf16[48,384]{1,0:T(8,128)(2,1)S(1)}, u32[]{:S(2)}, u32[]{:S(2)}) collective-permute-start(bf16[48,384]{1,0:T(8,128)(2,1)} %sum_pieces.1.refs_0_), channel_id=1, source_target_pairs={{0,4},{4,0},{8,12},{12,8},{1,5},{5,1},{9,13},{13,9},{2,6},{6,2},{1... | collective-permute-start | bytes 110600 | tf_op jit(solution)/shard_map/ppermute | solution.py:37
  113.3 1.9 %collective-permute-start.14 = (bf16[48,384]{1,0:T(8,128)(2,1)}, bf16[48,384]{1,0:T(8,128)(2,1)S(1)}, u32[]{:S(2)}, u32[]{:S(2)}) collective-permute-start(bf16[48,384]{1,0:T(8,128)(2,1)} %sum_pieces.1.refs_0_), channel_id=1, source_target_pairs={{0,12},{4,8},{8,4},{12,0},{1,13},{5,9},{9,5},{13,1},{2,14},{6,10},... | collective-permute-start | bytes 110600 | tf_op jit(solution)/shard_map/ppermute | solution.py:37
  115.2 3.0 %collective-permute-done.13.refs_2_ = bf16[48,384]{1,0:T(8,128)(2,1)S(1)} collective-permute-done((bf16[48,384]{1,0:T(8,128)(2,1)}, bf16[48,384]{1,0:T(8,128)(2,1)S(1)}, u32[]{:S(2)}, u32[]{:S(2)}) %collective-permute-start.13) | collective-permute-done | bytes 36896 | tf_op jit(solution)/shard_map/ppermute | solution.py:37
  118.2 1.1 collective-permute-done.14.refs_3_
  119.9 1.5 %scale_sum.1.refs_0_ = bf16[48,384]{1,0:T(8,128)(2,1)} custom-call(bf16[48,384]{1,0:T(8,128)(2,1)} %sum_pieces.1.refs_0_, bf16[48,384]{1,0:T(8,128)(2,1)} %copy-done.26, bf16[48,384]{1,0:T(8,128)(2,1)} %copy-done.27, bf16[48,384]{1,0:T(8,128)(2,1)} %copy-done.28), custom_call_target="tpu_custom_call" | custom-call | tf_op jit(solution)/shard_map/scale_sum/pallas_call | solution.py:358
  121.4 1.1 collective-permute-start.16
  123.3 1.1 collective-permute-start.18
  124.9 1.1 collective-permute-start.20
  126.0 1.6 %collective-permute-start.21 = (bf16[48,384]{1,0:T(8,128)(2,1)}, bf16[48,384]{1,0:T(8,128)(2,1)S(1)}, u32[]{:S(2)}, u32[]{:S(2)}) collective-permute-start(bf16[48,384]{1,0:T(8,128)(2,1)} %scale_sum.1.refs_0_), channel_id=1, source_target_pairs={{0,19},{1,18},{2,17},{3,16},{16,3},{17,2},{18,1},{19,0},{4,23},{5,... | collective-permute-start | bytes 110600 | tf_op jit(solution)/shard_map/ppermute | solution.py:37
  128.2 1.8 %collective-permute-done.20.refs_6_ = bf16[48,384]{1,0:T(8,128)(2,1)S(1)} collective-permute-done((bf16[48,384]{1,0:T(8,128)(2,1)}, bf16[48,384]{1,0:T(8,128)(2,1)S(1)}, u32[]{:S(2)}, u32[]{:S(2)}) %collective-permute-start.20) | collective-permute-done | bytes 36896 | tf_op jit(solution)/shard_map/ppermute | solution.py:37
  131.2 1.7 %spread.1 = (f32[16,3072]{1,0:T(8,128)}, f32[16,2048]{1,0:T(8,128)}, f32[16,3072]{1,0:T(8,128)}, f32[16,1024]{1,0:T(8,128)}) custom-call(s32[2]{0:T(128)} %pad_add_fusion.place.refs_0_, bf16[48,384]{1,0:T(8,128)(2,1)} %scale_sum.1.refs_0_, bf16[48,384]{1,0:T(8,128)(2,1)} %copy-done.19, bf16[48,384]{1,0:T(8,128)(2,1)} %copy-done.20, ...), custom_call_target="tpu_custom_call" | custom-call | tf_op jit(solution)/shard_map/spread/pallas_call | solution.py:381
  (89 shorter events, 13.6 us)
Async XLA Ops:
  4.7 7.5 %copy-start = (bf16[128,3200]{1,0:T(8,128)(2,1)}, bf16[128,3200]{1,0:T(8,128)(2,1)S(1)}, u32[]{:S(2)}) copy-start(bf16[128,3200]{1,0:T(8,128)(2,1)S(1)} %norm_tokens.2.rest_0_.refs_3_.refs_4_) | copy-start | bytes 2457604
  4.7 16.5 %collective-permute-start = (bf16[128,3200]{1,0:T(8,128)(2,1)S(1)}, bf16[128,3200]{1,0:T(8,128)(2,1)S(1)}, u32[]{:S(2)}, u32[]{:S(2)}) collective-permute-start(bf16[128,3200]{1,0:T(8,128)(2,1)S(1)} %norm_tokens.2.rest_0_.refs_3_.refs_4_), channel_id=1, source_target_pairs={{0,1},{1,0},{2,3},{3,2},{4,5},{5,4},{6,7},{7,6},{8,9},{9,8},{10,11... | collective-permute-start | bytes 2457608 | tf_op jit(solution)/shard_map/ppermute | solution.py:37
  5.2 16.0 %all-to-all-start = ((bf16[4,192,512]{2,1,0:T(8,128)(2,1)}), bf16[4,192,512]{2,1,0:T(8,128)(2,1)S(1)}, u32[]{:S(2)}, u32[]{:S(2)}) async-start(bf16[4,192,512]{2,1,0:T(8,128)(2,1)} %pack_weights.1.rest_0_), calls=%async_computation | async-start | bytes 1572864 | tf_op jit(solution)/shard_map/all_to_all | solution.py:409
  9.1 21.2 %collective-permute-start.3 = (bf16[128,3200]{1,0:T(8,128)(2,1)S(1)}, bf16[128,3200]{1,0:T(8,128)(2,1)}, u32[]{:S(2)}, u32[]{:S(2)}) collective-permute-start(bf16[128,3200]{1,0:T(8,128)(2,1)S(1)} %norm_tokens.2.rest_0_.refs_3_.refs_4_), channel_id=1, source_target_pairs={{0,16},{16,0},{1,17},{17,1},{2,18},{18,2},{3,19},{19,3},{4,20},{20... | collective-permute-start | bytes 2457608 | tf_op jit(solution)/shard_map/ppermute | solution.py:37
  22.3 21.3 %collective-permute-start.1 = (bf16[128,3200]{1,0:T(8,128)(2,1)}, bf16[128,3200]{1,0:T(8,128)(2,1)S(1)}, u32[]{:S(2)}, u32[]{:S(2)}) collective-permute-start(bf16[128,3200]{1,0:T(8,128)(2,1)} %fence.3), channel_id=1, source_target_pairs={{0,2},{2,0},{1,3},{3,1},{4,6},{6,4},{5,7},{7,5},{8,10},{10,8},{9,1... | collective-permute-start | bytes 2457608 | tf_op jit(solution)/shard_map/ppermute | solution.py:37
  22.3 21.3 %collective-permute-start.8 = (bf16[768,512]{1,0:T(8,128)(2,1)}, bf16[768,512]{1,0:T(8,128)(2,1)S(1)}, u32[]{:S(2)}, u32[]{:S(2)}) collective-permute-start(bf16[768,512]{1,0:T(8,128)(2,1)} %bitcast.17), channel_id=1, source_target_pairs={{0,4},{4,0},{8,12},{12,8},{1,5},{5,1},{9,13},{13,9},{2,6},{6,2},{1... | collective-permute-start | bytes 2359304 | tf_op jit(solution)/shard_map/ppermute | solution.py:391
  24.4 20.0 %collective-permute-start.6 = (bf16[768,512]{1,0:T(8,128)(2,1)}, bf16[768,512]{1,0:T(8,128)(2,1)S(1)}, u32[]{:S(2)}, u32[]{:S(2)}) collective-permute-start(bf16[768,512]{1,0:T(8,128)(2,1)} %bitcast.18), channel_id=1, source_target_pairs={{0,0},{4,8},{8,4},{12,12},{1,1},{5,9},{9,5},{13,13},{2,2},{6,10},{... | collective-permute-start | bytes 2359304 | tf_op jit(solution)/shard_map/ppermute | solution.py:395
  30.3 30.0 %collective-permute-start.5 = (bf16[128,3200]{1,0:T(8,128)(2,1)}, bf16[128,3200]{1,0:T(8,128)(2,1)S(1)}, u32[]{:S(2)}, u32[]{:S(2)}) collective-permute-start(bf16[128,3200]{1,0:T(8,128)(2,1)} %collective-permute-done.3.refs_7_.refs_8_), channel_id=1, source_target_pairs={{0,2},{2,0},{1,3},{3,1},{4,6},{6,4},{5,7},{7,5},{8,10},{10,8},{9,1... | collective-permute-start | bytes 2457608 | tf_op jit(solution)/shard_map/ppermute | solution.py:37
  43.7 33.6 %copy-start.13 = (bf16[128,3200]{1,0:T(8,128)(2,1)}, bf16[128,3200]{1,0:T(8,128)(2,1)S(1)}, u32[]{:S(2)}) copy-start(bf16[128,3200]{1,0:T(8,128)(2,1)S(1)} %collective-permute-done.1.refs_5_.refs_6_) | copy-start | bytes 2457604
  43.7 24.2 %collective-permute-start.2 = (bf16[128,3200]{1,0:T(8,128)(2,1)S(1)}, bf16[128,3200]{1,0:T(8,128)(2,1)S(1)}, u32[]{:S(2)}, u32[]{:S(2)}) collective-permute-start(bf16[128,3200]{1,0:T(8,128)(2,1)S(1)} %collective-permute-done.1.refs_5_.refs_6_), channel_id=1, source_target_pairs={{0,1},{1,0},{2,3},{3,2},{4,5},{5,4},{6,7},{7,6},{8,9},{9,8},{10,11... | collective-permute-start | bytes 2457608 | tf_op jit(solution)/shard_map/ppermute | solution.py:37
  43.7 16.6 %copy-start.15 = (bf16[768,512]{1,0:T(8,128)(2,1)}, bf16[768,512]{1,0:T(8,128)(2,1)S(1)}, u32[]{:S(2)}) copy-start(bf16[768,512]{1,0:T(8,128)(2,1)S(1)} %collective-permute-done.8.refs_12_.refs_1_) | copy-start | bytes 2359300
  43.7 16.6 %collective-permute-start.9 = (bf16[768,512]{1,0:T(8,128)(2,1)S(1)}, bf16[768,512]{1,0:T(8,128)(2,1)S(1)}, u32[]{:S(2)}, u32[]{:S(2)}) collective-permute-start(bf16[768,512]{1,0:T(8,128)(2,1)S(1)} %collective-permute-done.8.refs_12_.refs_1_), channel_id=1, source_target_pairs={{0,0},{4,8},{8,4},{12,12},{1,1},{5,9},{9,5},{13,13},{2,2},{6,10},{... | collective-permute-start | bytes 2359304 | tf_op jit(solution)/shard_map/ppermute | solution.py:395
  44.4 22.5 %copy-start.18 = (bf16[768,512]{1,0:T(8,128)(2,1)}, bf16[768,512]{1,0:T(8,128)(2,1)S(1)}, u32[]{:S(2)}) copy-start(bf16[768,512]{1,0:T(8,128)(2,1)S(1)} %collective-permute-done.6.refs_20_) | copy-start | bytes 2359300
  44.4 22.5 %collective-permute-start.7 = (bf16[768,512]{1,0:T(8,128)(2,1)S(1)}, bf16[768,512]{1,0:T(8,128)(2,1)S(1)}, u32[]{:S(2)}, u32[]{:S(2)}) collective-permute-start(bf16[768,512]{1,0:T(8,128)(2,1)S(1)} %collective-permute-done.6.refs_20_), channel_id=1, source_target_pairs={{0,4},{4,0},{8,12},{12,8},{1,5},{5,1},{9,13},{13,9},{2,6},{6,2},{1... | collective-permute-start | bytes 2359304 | tf_op jit(solution)/shard_map/ppermute | solution.py:391
  49.0 23.8 %collective-permute-start.4 = (bf16[128,3200]{1,0:T(8,128)(2,1)}, bf16[128,3200]{1,0:T(8,128)(2,1)S(1)}, u32[]{:S(2)}, u32[]{:S(2)}) collective-permute-start(bf16[128,3200]{1,0:T(8,128)(2,1)} %collective-permute-done.3.refs_7_.refs_8_), channel_id=1, source_target_pairs={{0,1},{1,0},{2,3},{3,2},{4,5},{5,4},{6,7},{7,6},{8,9},{9,8},{10,11... | collective-permute-start | bytes 2457608 | tf_op jit(solution)/shard_map/ppermute | solution.py:37
  60.3 7.6 %copy-start.11 = (bf16[128,3200]{1,0:T(8,128)(2,1)}, bf16[128,3200]{1,0:T(8,128)(2,1)S(1)}, u32[]{:S(2)}) copy-start(bf16[128,3200]{1,0:T(8,128)(2,1)S(1)} %collective-permute-done.5.refs_0_) | copy-start | bytes 2457604
  60.3 6.7 %copy-start.16 = (bf16[768,512]{1,0:T(8,128)(2,1)}, bf16[768,512]{1,0:T(8,128)(2,1)S(1)}, u32[]{:S(2)}) copy-start(bf16[768,512]{1,0:T(8,128)(2,1)S(1)} %collective-permute-done.9.refs_2_.refs_13_) | copy-start | bytes 2359300
  68.7 8.5 %collective-permute-start.10 = (bf16[128,3200]{1,0:T(8,128)(2,1)}, bf16[128,3200]{1,0:T(8,128)(2,1)S(1)}, u32[]{:S(2)}, u32[]{:S(2)}) collective-permute-start(bf16[128,3200]{1,0:T(8,128)(2,1)} %fence.4.refs_9_.refs_10_), channel_id=1, source_target_pairs={{0,1},{1,0},{2,3},{3,2},{4,5},{5,4},{6,7},{7,6},{8,9},{9,8},{10,11... | collective-permute-start | bytes 2457608 | tf_op jit(solution)/shard_map/ppermute | solution.py:37
  68.7 20.3 %collective-permute-start.11 = (bf16[768,512]{1,0:T(8,128)(2,1)}, bf16[768,512]{1,0:T(8,128)(2,1)}, u32[]{:S(2)}, u32[]{:S(2)}) collective-permute-start(bf16[768,512]{1,0:T(8,128)(2,1)} %copy-done.16), channel_id=1, source_target_pairs={{0,4},{4,0},{8,12},{12,8},{1,5},{5,1},{9,13},{13,9},{2,6},{6,2},{1... | collective-permute-start | bytes 2359304 | tf_op jit(solution)/shard_map/ppermute | solution.py:391
  73.7 13.0 %all-to-all-start.1 = ((bf16[8,128,256]{2,1,0:T(8,128)(2,1)}), bf16[8,128,256]{2,1,0:T(8,128)(2,1)S(1)}, u32[]{:S(2)}, u32[]{:S(2)}) async-start(bf16[8,128,256]{2,1,0:T(8,128)(2,1)} %fence.5), calls=%async_computation.1 | async-start | bytes 1048576 | tf_op jit(solution)/shard_map/all_to_all | solution.py:421
  110.8 4.4 %collective-permute-start.12 = (bf16[48,384]{1,0:T(8,128)(2,1)}, bf16[48,384]{1,0:T(8,128)(2,1)S(1)}, u32[]{:S(2)}, u32[]{:S(2)}) collective-permute-start(bf16[48,384]{1,0:T(8,128)(2,1)} %sum_pieces.1.refs_0_), channel_id=1, source_target_pairs={{0,4},{4,0},{8,12},{12,8},{1,5},{5,1},{9,13},{13,9},{2,6},{6,2},{1... | collective-permute-start | bytes 110600 | tf_op jit(solution)/shard_map/ppermute | solution.py:37
  112.8 5.4 %collective-permute-start.13 = (bf16[48,384]{1,0:T(8,128)(2,1)}, bf16[48,384]{1,0:T(8,128)(2,1)S(1)}, u32[]{:S(2)}, u32[]{:S(2)}) collective-permute-start(bf16[48,384]{1,0:T(8,128)(2,1)} %sum_pieces.1.refs_0_), channel_id=1, source_target_pairs={{0,8},{4,12},{8,0},{12,4},{1,9},{5,13},{9,1},{13,5},{2,10},{6,14},... | collective-permute-start | bytes 110600 | tf_op jit(solution)/shard_map/ppermute | solution.py:37
  113.3 6.0 %collective-permute-start.14 = (bf16[48,384]{1,0:T(8,128)(2,1)}, bf16[48,384]{1,0:T(8,128)(2,1)S(1)}, u32[]{:S(2)}, u32[]{:S(2)}) collective-permute-start(bf16[48,384]{1,0:T(8,128)(2,1)} %sum_pieces.1.refs_0_), channel_id=1, source_target_pairs={{0,12},{4,8},{8,4},{12,0},{1,13},{5,9},{9,5},{13,1},{2,14},{6,10},... | collective-permute-start | bytes 110600 | tf_op jit(solution)/shard_map/ppermute | solution.py:37
  121.4 3.5 %collective-permute-start.15 = (bf16[48,384]{1,0:T(8,128)(2,1)}, bf16[48,384]{1,0:T(8,128)(2,1)S(1)}, u32[]{:S(2)}, u32[]{:S(2)}) collective-permute-start(bf16[48,384]{1,0:T(8,128)(2,1)} %scale_sum.1.refs_0_), channel_id=1, source_target_pairs={{0,1},{1,0},{2,3},{3,2},{16,17},{17,16},{18,19},{19,18},{4,5},{5,4... | collective-permute-start | bytes 110600 | tf_op jit(solution)/shard_map/ppermute | solution.py:37
  121.4 4.6 %collective-permute-start.16 = (bf16[48,384]{1,0:T(8,128)(2,1)}, bf16[48,384]{1,0:T(8,128)(2,1)S(1)}, u32[]{:S(2)}, u32[]{:S(2)}) collective-permute-start(bf16[48,384]{1,0:T(8,128)(2,1)} %scale_sum.1.refs_0_), channel_id=1, source_target_pairs={{0,2},{1,3},{2,0},{3,1},{16,18},{17,19},{18,16},{19,17},{4,6},{5,7... | collective-permute-start | bytes 110600 | tf_op jit(solution)/shard_map/ppermute | solution.py:37
  122.5 5.1 %collective-permute-start.17 = (bf16[48,384]{1,0:T(8,128)(2,1)}, bf16[48,384]{1,0:T(8,128)(2,1)S(1)}, u32[]{:S(2)}, u32[]{:S(2)}) collective-permute-start(bf16[48,384]{1,0:T(8,128)(2,1)} %scale_sum.1.refs_0_), channel_id=1, source_target_pairs={{0,3},{1,2},{2,1},{3,0},{16,19},{17,18},{18,17},{19,16},{4,7},{5,6... | collective-permute-start | bytes 110600 | tf_op jit(solution)/shard_map/ppermute | solution.py:37
  123.3 4.4 %collective-permute-start.18 = (bf16[48,384]{1,0:T(8,128)(2,1)}, bf16[48,384]{1,0:T(8,128)(2,1)S(1)}, u32[]{:S(2)}, u32[]{:S(2)}) collective-permute-start(bf16[48,384]{1,0:T(8,128)(2,1)} %scale_sum.1.refs_0_), channel_id=1, source_target_pairs={{0,16},{1,17},{2,18},{3,19},{16,0},{17,1},{18,2},{19,3},{4,20},{5,... | collective-permute-start | bytes 110600 | tf_op jit(solution)/shard_map/ppermute | solution.py:37
  124.4 3.8 %collective-permute-start.19 = (bf16[48,384]{1,0:T(8,128)(2,1)}, bf16[48,384]{1,0:T(8,128)(2,1)S(1)}, u32[]{:S(2)}, u32[]{:S(2)}) collective-permute-start(bf16[48,384]{1,0:T(8,128)(2,1)} %scale_sum.1.refs_0_), channel_id=1, source_target_pairs={{0,17},{1,16},{2,19},{3,18},{16,1},{17,0},{18,3},{19,2},{4,21},{5,... | collective-permute-start | bytes 110600 | tf_op jit(solution)/shard_map/ppermute | solution.py:37
  124.9 5.6 %copy-start.19 = (bf16[48,384]{1,0:T(8,128)(2,1)}, bf16[48,384]{1,0:T(8,128)(2,1)S(1)}, u32[]{:S(2)}) copy-start(bf16[48,384]{1,0:T(8,128)(2,1)S(1)} %collective-permute-done.15.refs_1_) | copy-start | bytes 110596
  124.9 5.1 %collective-permute-start.20 = (bf16[48,384]{1,0:T(8,128)(2,1)}, bf16[48,384]{1,0:T(8,128)(2,1)S(1)}, u32[]{:S(2)}, u32[]{:S(2)}) collective-permute-start(bf16[48,384]{1,0:T(8,128)(2,1)} %scale_sum.1.refs_0_), channel_id=1, source_target_pairs={{0,18},{1,19},{2,16},{3,17},{16,2},{17,3},{18,0},{19,1},{4,22},{5,... | collective-permute-start | bytes 110600 | tf_op jit(solution)/shard_map/ppermute | solution.py:37
  126.0 4.5 %copy-start.20 = (bf16[48,384]{1,0:T(8,128)(2,1)}, bf16[48,384]{1,0:T(8,128)(2,1)S(1)}, u32[]{:S(2)}) copy-start(bf16[48,384]{1,0:T(8,128)(2,1)S(1)} %collective-permute-done.16.refs_2_) | copy-start | bytes 110596
  126.0 4.5 %collective-permute-start.21 = (bf16[48,384]{1,0:T(8,128)(2,1)}, bf16[48,384]{1,0:T(8,128)(2,1)S(1)}, u32[]{:S(2)}, u32[]{:S(2)}) collective-permute-start(bf16[48,384]{1,0:T(8,128)(2,1)} %scale_sum.1.refs_0_), channel_id=1, source_target_pairs={{0,19},{1,18},{2,17},{3,16},{16,3},{17,2},{18,1},{19,0},{4,23},{5,... | collective-permute-start | bytes 110600 | tf_op jit(solution)/shard_map/ppermute | solution.py:37
  (21 other events, 39.7 us)

commit v3 on v2

--- a/solution.py
+++ b/solution.py
@@ -21,6 +21,7 @@
 ANY = pl.BlockSpec(memory_space=pl.ANY)
 VMEM = pl.BlockSpec(memory_space=pltpu.VMEM)
 SMEM = pl.BlockSpec(memory_space=pltpu.SMEM)
+PARAMS = pltpu.CompilerParams(vmem_limit_bytes=60 * 2**20)
 
 NT = (((1,), (1,)), ((), ()))
 TN = (((0,), (0,)), ((), ()))
@@ -37,22 +38,65 @@
     return lax.ppermute(value, axes, [(i, i ^ distance) for i in range(count)])
 
 
-def pack_weights_kernel(heads, place, qw, kw, vw, out):
+def pack_weights_kernel(heads, qw, kw, vw, *outs):
     group = heads * HEAD_SIZE
-    for index in range(out.shape[0]):
-        mine = (place[0] // 4) * 4 + index
-        for src, at, wide in ((qw, 0, group), (kw, group, HEAD_SIZE), (vw, group + HEAD_SIZE, HEAD_SIZE)):
-            out[index, :, at : at + wide] = src[:, pl.ds(pl.multiple_of(mine * wide, wide), wide)]
-
-
-def pack_weights(place, qw, kw, vw, heads):
+    for core, out in enumerate(outs):
+        for chip in range(out.shape[0]):
+            mine = lax.axis_index(GROUP) ^ (2 * chip + core)
+            for src, at, wide in ((qw, 0, group), (kw, group, HEAD_SIZE), (vw, group + HEAD_SIZE, HEAD_SIZE)):
+                out[chip, :, at : at + wide] = src[:, pl.ds(pl.multiple_of(mine * wide, wide), wide)]
+
+
+def pack_weights(qw, kw, vw, heads):
+    shape = (2, qw.shape[0], (heads + 2) * HEAD_SIZE)
     return pl.pallas_call(
         functools.partial(pack_weights_kernel, heads),
-        out_shape=jax.ShapeDtypeStruct((4, qw.shape[0], (heads + 2) * HEAD_SIZE), qw.dtype),
-        in_specs=[SMEM, VMEM, VMEM, VMEM],
-        out_specs=VMEM,
+        out_shape=[jax.ShapeDtypeStruct(shape, qw.dtype)] * 2,
+        in_specs=[VMEM] * 3,
+        out_specs=[VMEM] * 2,
+        compiler_params=PARAMS,
         name="pack_weights",
-    )(place, qw, kw, vw)
+    )(qw, kw, vw)
+
+
+def join_rows_kernel(place, kept, got, near, far):
+    rows = kept.shape[1]
+    core = place[0] & 1
+    for chip, out in enumerate((near, far)):
+        out[pl.ds(pl.multiple_of(core * rows, 16), rows), :] = kept[chip]
+        out[pl.ds(pl.multiple_of((1 - core) * rows, 16), rows), :] = got[chip]
+
+
+def join_rows(place, kept, got):
+    _, rows, wide = kept.shape
+    return pl.pallas_call(
+        join_rows_kernel,
+        out_shape=[jax.ShapeDtypeStruct((2 * rows, wide), kept.dtype)] * 2,
+        in_specs=[SMEM, VMEM, VMEM],
+        out_specs=[VMEM] * 2,
+        compiler_params=PARAMS,
+        name="join_rows",
+    )(place, kept, got)
+
+
+def join_pairs_kernel(*refs):
+    count = len(refs) // 3
+    for first, second, out in zip(refs[:count], refs[count : 2 * count], refs[2 * count :]):
+        rows = first.shape[0]
+        out[:rows] = first[...]
+        out[rows:] = second[...]
+
+
+def join_pairs(first, second):
+    rows, wide = first[0].shape
+    return pl.pallas_call(
+        join_pairs_kernel,
+        out_shape=[jax.ShapeDtypeStruct((2 * rows, wide), first[0].dtype)] * len(first),
+        in_specs=[VMEM] * (2 * len(first)),
+        out_specs=[VMEM] * len(first),
+        compiler_params=PARAMS,
+        name="join_pairs",
+    )(*first, *second)
 
 
 def fence_kernel(*refs):
@@ -67,12 +111,12 @@
         in_specs=[ANY] * (count + len(earlier)),
         out_specs=[ANY] * count,
         input_output_aliases={i: i for i in range(count)},
+        compiler_params=PARAMS,
         name="fence",
     )(*values, *earlier)
 
 
-def norm_kernel(tokens, trace, gain, down_q, down_v, *rest):
-    out = rest[-1]
+def norm_kernel(copies, tokens, trace, gain, down_q, down_v, *rest):
     flt = tokens[...].astype(jnp.float32)
     meansq = jnp.mean(flt * flt, axis=-1, keepdims=True)
     normed = (flt * lax.rsqrt(meansq + EPS) * gain[...].astype(jnp.float32)[None, :]).astype(jnp.bfloat16)
@@ -85,18 +129,19 @@
     ids = jnp.sum(jnp.where(diagonal, trace[...].astype(jnp.float32), 0.0), axis=1, keepdims=True)
     filler = jnp.zeros((rows, LANES - 2 * rank - 1), jnp.float32)
     extra = jnp.concatenate([low_q, low_v, ids, filler], 1).astype(jnp.bfloat16)
-    out[:, :feats] = normed
-    out[:, feats:] = extra
-
-
-def norm_tokens(tokens, trace, gain, down_q, down_v, *earlier):
+    for out in rest[-copies:]:
+        out[:, :feats] = normed
+        out[:, feats:] = extra
+
+
+def norm_tokens(tokens, trace, gain, down_q, down_v, copies, *earlier):
     rows, feats = tokens.shape
     return pl.pallas_call(
-        norm_kernel,
-        out_shape=jax.ShapeDtypeStruct((rows, feats + LANES), jnp.bfloat16),
+        functools.partial(norm_kernel, copies),
+        out_shape=[jax.ShapeDtypeStruct((rows, feats + LANES), jnp.bfloat16)] * copies,
         in_specs=[VMEM] * 5 + [ANY] * len(earlier),
-        out_specs=VMEM,
-        compiler_params=pltpu.CompilerParams(vmem_limit_bytes=32 * 2**20),
+        out_specs=[VMEM] * copies,
+        compiler_params=pltpu.CompilerParams(vmem_limit_bytes=16 * 2**20),
         name="norm_tokens",
     )(tokens, trace, gain, down_q, down_v, *earlier)
 
@@ -117,12 +162,24 @@
             self.waits.append((sequence, copy))
             self.count += 1
 
-    def add_either(self, condition, first, second, target):
-        copies = [pltpu.make_async_copy(src, target, self.sems.at[self.count]) for src in (first, second)]
-        pl.when(condition)(copies[0].start)
-        pl.when(jnp.logical_not(condition))(copies[1].start)
-        self.waits.append((0, copies[0]))
-        self.count += 1
+    def add_shard(self, place, condition, sources, target, at):
+        copies = []
+        for chunks in sources:
+            some = []
+            for number, (src, part, offset) in enumerate(chunks):
+                begin = pl.multiple_of(at + offset(place), 16)
+                src = src.at[part]
+                to = target.at[pl.ds(begin, src.shape[0]), :]
+                some.append(pltpu.make_async_copy(src, to, self.sems.at[self.count + number]))
+            copies.append(some)
+        for number, copy in enumerate(copies[0]):
+            if condition is None:
+                copy.start()
+            else:
+                pl.when(condition)(copy.start)
+                pl.when(jnp.logical_not(condition))(copies[1][number].start)
+            self.waits.append((0, copy))
+            self.count += 1
 
     def wait(self, sequence):
         for needed, copy in self.waits:
@@ -139,14 +196,11 @@
     rank, group = up_q.shape[0], heads * HEAD_SIZE
     depth = plan["depth"]
 
-    loads, at = Loads(sems), 0
+    loads = Loads(sems)
     for index, (_, condition, sources) in enumerate(shards):
-        target = w_all.at[pl.ds(index * depth, depth), :]
-        if condition is None:
-            loads.add(place, [((lambda p, i=index: i * depth, 0, None), w_refs[at])], w_all)
-        else:
-            loads.add_either(condition(place), w_refs[at], w_refs[at + 1], target)
-        at += len(sources)
+        chosen = None if condition is None else condition(place)
+        sources = [[(w_refs[at], part, offset) for at, part, offset in chunks] for chunks in sources]
+        loads.add_shard(place, chosen, sources, w_all, index * depth)
     loads.add(place, list(zip(plan["x"], x_refs)), x_all)
 
     mine = place[0]
@@ -183,10 +237,15 @@
 
     loads = Loads(sems)
     if last is not None:
-        offset, condition = last
-        copy = pltpu.make_async_copy(w_refs[0], w_all, sems.at[loads.count])
-        loads.count += 1
-        pl.when(condition(place))(copy.start)
+        offset, condition, chunks = last
+        inner = condition(place)
+        here = []
+        for part, chunk_offset in chunks:
+            src = w_refs[0].at[part]
+            to = w_all.at[pl.ds(pl.multiple_of(chunk_offset(place), 16), src.shape[0]), :]
+            here.append(pltpu.make_async_copy(src, to, sems.at[loads.count]))
+            pl.when(inner)(here[-1].start)
+            loads.count += 1
     for index in range(sequences):
         rows = pl.ds(index * seq, seq)
         copy_base = pltpu.make_async_copy(base.at[rows, :], base_all.at[rows, :], sems.at[loads.count])
@@ -198,11 +257,14 @@
             loads.add(place, chosen, target)
     if last is not None:
 
-        @pl.when(jnp.logical_not(condition(place)))
+        @pl.when(jnp.logical_not(inner))
         def _():
-            w_all[...] = w_refs[1][...]
-
-        pl.when(condition(place))(copy.wait)
+            for part, chunk_offset in chunks:
+                value = w_refs[1][part, :]
+                w_all[pl.ds(pl.multiple_of(chunk_offset(place), 16), value.shape[0]), :] = value
+
+        for copy in here:
+            pl.when(inner)(copy.wait)
 
     mine = place[0]
     uq = up_q[:, pl.ds(pl.multiple_of(mine * group, group), group)]
@@ -278,11 +340,17 @@
     wide = (heads + 2) * HEAD_SIZE
     x_plan, x_arrays = zip(*gathered["x"])
     g_plan, g_arrays = zip(*gathered["g"])
-    shards = gathered["w"]
-    w_arrays = [array for _, _, sources in shards for array in sources]
-    depth = w_arrays[0].shape[0]
+    w_arrays, shards = [], []
+    for offset, condition, sources in gathered["w"]:
+        shards.append((offset, condition, []))
+        for chunks in sources:
+            shards[-1][2].append([])
+            for array, part, at in chunks:
+                index = next((i for i, known in enumerate(w_arrays) if known is array), len(w_arrays))
+                w_arrays += [array] if index == len(w_arrays) else []
+                shards[-1][2][-1].append((index, part, at))
+    depth = w_arrays[-1].shape[0]
     plan = dict(plan, x=x_plan, g=g_plan, shards=shards, depth=depth)
-    params = pltpu.CompilerParams(vmem_limit_bytes=60 * 2**20)
     base = pl.pallas_call(
         functools.partial(project_kernel, plan),
         out_shape=jax.ShapeDtypeStruct((tokens, wide), jnp.float32),
@@ -291,19 +359,20 @@
         scratch_shapes=[
             pltpu.VMEM((tokens, feats + LANES), jnp.bfloat16),
             pltpu.VMEM((len(shards) * depth, wide), jnp.bfloat16),
-            pltpu.SemaphoreType.DMA((len(x_arrays) + len(shards),)),
+            pltpu.SemaphoreType.DMA((len(x_arrays) + sum(len(sources[0]) for _, _, sources in shards),)),
         ],
-        compiler_params=params,
         cost_estimate=pl.CostEstimate(
             flops=2 * tokens * len(shards) * depth * wide,
             bytes_accessed=2 * tokens * feats + 2 * len(shards) * depth * wide + 4 * tokens * wide,
             transcendentals=0,
         ),
+        compiler_params=PARAMS,
         name="project",
     )(place, up_q, up_v, *x_arrays, *w_arrays)
 
     offset, condition, sources = gathered["last"] or (None, None, [])
-    plan["last"] = None if offset is None else (offset, condition)
+    plan["last"] = None if offset is None else (offset, condition, [chunk[1:] for chunk in sources[0]])
+    last = [chunks[0][0] for chunks in sources]
     return pl.pallas_call(
         functools.partial(attend_kernel, plan),
         out_shape=[
@@ -312,19 +381,19 @@
         ],
         in_specs=[SMEM, VMEM, VMEM]
         + [ANY] * (1 + len(x_arrays) + len(g_arrays))
-        + [ANY, VMEM][: len(sources)],
+        + [ANY, VMEM][: len(last)],
         out_specs=[VMEM] * 2,
         scratch_shapes=[
             pltpu.VMEM((tokens, feats + LANES), jnp.bfloat16),
             pltpu.VMEM((tokens, heads * HEAD_SIZE), jnp.bfloat16),
-            pltpu.VMEM((depth, wide) if sources else (16, LANES), jnp.bfloat16),
+            pltpu.VMEM((depth, wide) if last else (16, LANES), jnp.bfloat16),
             pltpu.VMEM((tokens, wide), jnp.float32),
             pltpu.VMEM((3 * rank, tokens), jnp.bfloat16),
-            pltpu.SemaphoreType.DMA((1 + tokens // seq + len(x_arrays) + len(g_arrays),)),
+            pltpu.SemaphoreType.DMA((len(last) + tokens // seq + len(x_arrays) + len(g_arrays),)),
         ],
-        compiler_params=params,
+        compiler_params=PARAMS,
         name="attend",
-    )(place, up_q, up_v, base, *x_arrays, *g_arrays, *sources)
+    )(place, up_q, up_v, base, *x_arrays, *g_arrays, *last)
 
 
 def sum_kernel(gas, gb, out):
@@ -343,6 +412,7 @@
         out_shape=jax.ShapeDtypeStruct((rows + gb.shape[0], wide), jnp.bfloat16),
         in_specs=[VMEM] * 2,
         out_specs=VMEM,
+        compiler_params=PARAMS,
         name="sum_pieces",
     )(gas, gb)
 
@@ -360,6 +430,7 @@
         out_shape=jax.ShapeDtypeStruct(pieces[0].shape, jnp.bfloat16),
         in_specs=[VMEM] * len(pieces),
         out_specs=VMEM,
+        compiler_params=PARAMS,
         name="scale_sum",
     )(*pieces)
 
@@ -383,6 +454,7 @@
         out_shape=[jax.ShapeDtypeStruct(shape, jnp.float32) for shape in shapes],
         in_specs=[SMEM] + [VMEM] * len(pieces),
         out_specs=[VMEM] * 4,
+        compiler_params=PARAMS,
         name="spread",
     )(place, *pieces)
 
@@ -405,44 +477,60 @@
 
 def paired_gather(place, qw, kw, vw, heads, norm_args, gradient):
     shard, rows = qw.shape[0], norm_args[0].shape[0]
-    packed = pack_weights(place, qw, kw, vw, heads)
-    own = lax.all_to_all(packed, ("y", "c"), 0, 0, tiled=True).reshape(4 * shard, -1)
-    normed = norm_tokens(*norm_args, packed)
-
-    c_tokens = swapped(normed, ("c",), 1)
-    x_tokens = swapped(normed, ("ctx",), 1)
-    (later,) = fence((norm_tokens(*norm_args, normed),), own, c_tokens)
+    kept, given = pack_weights(qw, kw, vw, heads)
+    near, beside = join_rows(place, kept, swapped(given, ("c",), 1))
+    far = swapped(beside, ("y",), 1)
+    normed, later = norm_tokens(*norm_args, 2, beside)
+    c_tokens, x_tokens = swapped(normed, ("c",), 1), swapped(normed, ("ctx",), 1)
+    hop_1, hop_2 = outer_pairs(near), inner_pairs(near)
+    (later,) = fence((later,), far, hop_1, hop_2)
     y_tokens = swapped(later, ("y",), 1)
-    hop_2, hop_1 = inner_pairs(own), outer_pairs(own)
-    xc_tokens, xy_tokens = swapped(x_tokens, ("c",), 1), swapped(x_tokens, ("y",), 1)
+    hop_1, hop_2 = join_pairs((hop_1, hop_2), (outer_pairs(far), inner_pairs(far)))
 
     hop_4, hop_3 = inner_pairs(hop_1), outer_pairs(hop_2)
+    half = rows // 2
+    far_low, far_high = swapped(x_tokens[:half], ("y",), 1), swapped(y_tokens[half:], ("ctx",), 1)
+    xc_tokens = swapped(x_tokens, ("c",), 1)
     (gradient,) = fence((gradient,), hop_1, xc_tokens)
     gradient = lax.all_to_all(gradient, GROUP, 0, 0, tiled=True)
-    yc_tokens = swapped(y_tokens, ("c",), 1)
-
+
+    (hop_4,) = fence((hop_4,), hop_3)
     hop_5 = outer_pairs(hop_4)
-    (xy_tokens,) = fence((xy_tokens,), hop_3, hop_4, yc_tokens)
-    xyc_tokens = swapped(xy_tokens, ("c",), 1)
+    y_tokens, far_low, far_high = fence((y_tokens, far_low, far_high), hop_4)
+    yc_tokens, farc_low, farc_high = (swapped(value, ("c",), 1) for value in (y_tokens, far_low, far_high))
 
     def weight_columns(back):
         return lambda p: (p[1] ^ back) * 4 * shard
 
-    def token_rows(step):
-        return lambda p: (step & 3) * 2 * rows + ((p[0] >> 2) ^ (step >> 2)) * rows
+    def token_rows(step, skip=0):
+        return lambda p: (step & 3) * 2 * rows + ((p[0] >> 2) ^ (step >> 2)) * rows + skip
 
     def source(step):
         return lambda p: p[0] ^ step
 
-    tokens = (normed, c_tokens, y_tokens, yc_tokens, x_tokens, xc_tokens, xy_tokens, xyc_tokens)
+    size = 2 * shard
+
+    def ordered(value, other=None):
+        def own_chip(p):
+            return ((p[0] >> 1) & 1) * size
+
+        def chip_beside(p):
+            return (1 - ((p[0] >> 1) & 1)) * size
+
+        if other is not None:
+            return [(value, slice(0, size), own_chip), (other, slice(0, size), chip_beside)]
+        return [(value, slice(0, size), own_chip), (value, slice(size, 2 * size), chip_beside)]
+
+    pieces = [(0, 0, normed), (1, 0, c_tokens), (2, 0, y_tokens), (3, 0, yc_tokens), (4, 0, x_tokens)]
+    pieces += [(5, 0, xc_tokens), (6, 0, far_low), (6, half, far_high), (7, 0, farc_low), (7, half, farc_high)]
     return {
         "w": [
-            (weight_columns(0), None, [own]),
-            (weight_columns(1), None, [hop_1]),
-            (weight_columns(2), is_inner, [hop_4, hop_3]),
+            (weight_columns(0), None, [ordered(near, far)]),
+            (weight_columns(1), None, [ordered(hop_1)]),
+            (weight_columns(2), is_inner, [ordered(hop_4), ordered(hop_3)]),
         ],
-        "last": (weight_columns(3), is_inner, [hop_2, hop_5]),
-        "x": [((token_rows(step), step & 3, None), value) for step, value in enumerate(tokens)],
+        "last": (weight_columns(3), is_inner, [ordered(hop_2), ordered(hop_5)]),
+        "x": [((token_rows(step, skip), step & 3, None), value) for step, skip, value in pieces],
         "g": [((token_rows(step), step & 3, source(step)), gradient) for step in range(8)],
     }
 
@@ -492,12 +580,12 @@
         columns = lax.dynamic_slice_in_dim(columns, lax.axis_index("ctx") * per, per, 0)
         columns = lax.all_to_all(columns, ("y", "c"), 0, 0, tiled=True).reshape(per * shard, -1)
         weights = lax.all_gather(columns, "z", axis=0, tiled=True)
-        normed = lax.all_gather(norm_tokens(*norm_args), ("y", "c", "ctx"), axis=0, tiled=True)
+        normed = lax.all_gather(norm_tokens(*norm_args, 1)[0], ("y", "c", "ctx"), axis=0, tiled=True)
         gradient = lax.all_to_all(gradient, GROUP, 0, 0, tiled=True)
         gradient = gradient.reshape(sizes[0], per, rows, group)
         gradient = jnp.moveaxis(gradient, 0, 1).reshape(parts * rows, group)
         gathered = {
-            "w": [(lambda p: 0, None, [weights])],
+            "w": [(lambda p: 0, None, [[(weights, slice(None), lambda p: 0)]])],
             "last": None,
             "x": [((lambda p: 0, 0, None), normed)],
             "g": [((lambda p: 0, 0, None), gradient)],

time: 134 us -> 127 us (0.948)
  waiting for transfers between devices: 50.9 us -> 29 us
  starting transfers between devices: 33.4 us -> 43.6 us
  Pallas kernels: 28 us -> 32 us
    ppermute x17 -> x21, waiting for transfers between devices: 33.9 us -> 8.17 us  [swapped(): return lax.ppermute(value, axes, [(i, i ^ distance) for i in range(count)])]
    ppermute x3 -> x4, waiting for transfers between devices: 8.93 us -> 20.6 us  [outer_pairs(): return lax.ppermute(value, 'z', [(0, 1), (1, 0), (2, 3), (3, 2)])]
    all_to_all x1 -> x0, waiting for transfers between devices: 8.08 us -> none  [paired_gather(): lax.all_to_all(packed, ('y', 'c'), 0, 0, tiled=True).reshape(4 * shard, -1)]
    ppermute x2 -> x3, starting transfers between devices: 2.49 us -> 7.9 us  [inner_pairs(): return lax.ppermute(value, 'z', [(0, 0), (1, 2), (2, 1), (3, 3)])]
    ppermute x17 -> x21, starting transfers between devices: 15.1 us -> 19.7 us  [swapped(): return lax.ppermute(value, axes, [(i, i ^ distance) for i in range(count)])]
    pallas_call x3 -> x4, Pallas kernels: 4.13 us -> 8.06 us  [the longest x1 2.64 us: join_pairs(): pl.pallas_call(join_pairs_kernel, out_shape=[jax.ShapeDtypeStruct((2 * ro...]
    all_to_all x1 -> x0, starting transfers between devices: 3.9 us -> none  [paired_gather(): lax.all_to_all(packed, ('y', 'c'), 0, 0, tiled=True).reshape(4 * shard, -1)]
    ppermute x3 -> x4, starting transfers between devices: 8.45 us -> 12.3 us  [outer_pairs(): return lax.ppermute(value, 'z', [(0, 1), (1, 0), (2, 3), (3, 2)])]
  transfers between devices with their start and end apart: 24 -> 29, of which waited for: 11 -> 12; matrix products, arithmetic and copies ran while one was open for 2% -> 4% of each run, Pallas kernels for 7% -> 10%
where the time goes in v3:
time: 127 us; the launch traced here: 126 us
  starting transfers between devices  43.6 us (34%)
  Pallas kernels  32 us (25%)
  waiting for transfers between devices  29 us (23%)
  local copies, waits for them, and re-layouts  10.6 us (8%)
  blocking collectives  9.69 us (8%)
    ppermute x4, waiting for transfers between devices, outer_pairs(): return lax.ppermute(value, 'z', [(0, 1), (1, 0), (2, 3), (3, 2)])  20.6 us
    ppermute x21, starting transfers between devices, swapped(): return lax.ppermute(value, axes, [(i, i ^ distance) for i in range(count)])  19.7 us
    ppermute x4, starting transfers between devices, outer_pairs(): return lax.ppermute(value, 'z', [(0, 1), (1, 0), (2, 3), (3, 2)])  12.3 us
    pallas_call x1, Pallas kernels, attend(): pl.pallas_call(functools.partial(attend_kernel, plan), out_shape=[jax.Sha...  10.6 us
    all_to_all x1, blocking collectives, on_device(): mixed = sum_pieces(lax.all_to_all(ga, GROUP, 0, 0, tiled=True), gb)  9.69 us
    pallas_call x1, Pallas kernels, attend(): pl.pallas_call(functools.partial(project_kernel, plan), out_shape=jax.Sha...  8.59 us
    ppermute x21, waiting for transfers between devices, swapped(): return lax.ppermute(value, axes, [(i, i ^ distance) for i in range(count)])  8.17 us
    ppermute x3, starting transfers between devices, inner_pairs(): return lax.ppermute(value, 'z', [(0, 0), (1, 2), (2, 1), (3, 3)])  7.9 us
  transfers between devices with their start and end apart: 29, of which 12 were waited for; matrix products, arithmetic and copies ran while one was open for 4% of the time, Pallas kernels for 10%

profile of v3, /device:TPU:0, one launch (start us, length us, event | category | flops | bytes accessed | tf_op | source)
XLA Modules:
  0.0 126.4 jit_solution(13546214347809063111)
XLA Ops:
  0.7 2.5 %pack_weights.1 = (bf16[2,192,512]{2,1,0:T(8,128)(2,1)}, bf16[2,192,512]{2,1,0:T(8,128)(2,1)}) custom-call(bf16[192,2048]{1,0:T(8,128)(2,1)} %qw.1, bf16[192,1024]{1,0:T(8,128)(2,1)} %kw.1, bf16[192,1024]{1,0:T(8,128)(2,1)} %vw.1), custom_call_target="tpu_custom_call" | custom-call | tf_op jit(solution)/shard_map/pack_weights/pallas_call | solution.py:52
  5.9 2.1 %join_rows.1 = (bf16[384,512]{1,0:T(8,128)(2,1)}, bf16[384,512]{1,0:T(8,128)(2,1)}) custom-call(s32[2]{0:T(128)} %pad_add_fusion.place.refs_0_, bf16[2,192,512]{2,1,0:T(8,128)(2,1)} %get-tuple-element.21.kept, bf16[2,192,512]{2,1,0:T(8,128)(2,1)} %copy-done.17), custom_call_target="tpu_custom_call" | custom-call | tf_op jit(solution)/shard_map/join_rows/pallas_call | solution.py:72
  8.0 2.9 %collective-permute-start.2 = (bf16[384,512]{1,0:T(8,128)(2,1)}, bf16[384,512]{1,0:T(8,128)(2,1)S(1)}, u32[]{:S(2)}, u32[]{:S(2)}) collective-permute-start(bf16[384,512]{1,0:T(8,128)(2,1)} %get-tuple-element.23.rest_0_), channel_id=1, source_target_pairs={{0,2},{2,0},{1,3},{3,1},{4,6},{6,4},{5,7},{7,5},{8,10},{10,8},{9,1... | collective-permute-start | bytes 1179656 | tf_op jit(solution)/shard_map/ppermute | solution.py:38
  10.9 1.6 %collective-permute-start.3 = (bf16[384,512]{1,0:T(8,128)(2,1)}, bf16[384,512]{1,0:T(8,128)(2,1)S(1)}, u32[]{:S(2)}, u32[]{:S(2)}) collective-permute-start(bf16[384,512]{1,0:T(8,128)(2,1)} %get-tuple-element.26.refs_13_), channel_id=1, source_target_pairs={{0,4},{4,0},{8,12},{12,8},{1,5},{5,1},{9,13},{13,9},{2,6},{6,2},{1... | collective-permute-start | bytes 1179656 | tf_op jit(solution)/shard_map/ppermute | solution.py:463
  12.5 4.5 %collective-permute-start.4 = (bf16[384,512]{1,0:T(8,128)(2,1)}, bf16[384,512]{1,0:T(8,128)(2,1)}, u32[]{:S(2)}, u32[]{:S(2)}) collective-permute-start(bf16[384,512]{1,0:T(8,128)(2,1)} %get-tuple-element.26.refs_13_), channel_id=1, source_target_pairs={{0,0},{4,8},{8,4},{12,12},{1,1},{5,9},{9,5},{13,13},{2,2},{6,10},{... | collective-permute-start | bytes 1179656 | tf_op jit(solution)/shard_map/ppermute | solution.py:467
  19.8 1.5 %collective-permute-start.6 = (bf16[128,3200]{1,0:T(8,128)(2,1)S(1)}, bf16[128,3200]{1,0:T(8,128)(2,1)S(1)}, u32[]{:S(2)}, u32[]{:S(2)}) collective-permute-start(bf16[128,3200]{1,0:T(8,128)(2,1)S(1)} %get-tuple-element.24.refs_3_.refs_4_), channel_id=1, source_target_pairs={{0,16},{16,0},{1,17},{17,1},{2,18},{18,2},{3,19},{19,3},{4,20},{20... | collective-permute-start | bytes 2457608 | tf_op jit(solution)/shard_map/ppermute | solution.py:38
  23.2 1.6 %collective-permute-start.10 = (bf16[384,512]{1,0:T(8,128)(2,1)}, bf16[384,512]{1,0:T(8,128)(2,1)S(1)}, u32[]{:S(2)}, u32[]{:S(2)}) collective-permute-start(bf16[384,512]{1,0:T(8,128)(2,1)} %copy-done.15), channel_id=1, source_target_pairs={{0,0},{4,8},{8,4},{12,12},{1,1},{5,9},{9,5},{13,13},{2,2},{6,10},{... | collective-permute-start | bytes 1179656 | tf_op jit(solution)/shard_map/ppermute | solution.py:467
  24.8 6.1 %collective-permute-start.9 = (bf16[384,512]{1,0:T(8,128)(2,1)}, bf16[384,512]{1,0:T(8,128)(2,1)S(1)}, u32[]{:S(2)}, u32[]{:S(2)}) collective-permute-start(bf16[384,512]{1,0:T(8,128)(2,1)} %copy-done.15), channel_id=1, source_target_pairs={{0,4},{4,0},{8,12},{12,8},{1,5},{5,1},{9,13},{13,9},{2,6},{6,2},{1... | collective-permute-start | bytes 1179656 | tf_op jit(solution)/shard_map/ppermute | solution.py:463
  30.9 7.6 %collective-permute-done.9.refs_2_ = bf16[384,512]{1,0:T(8,128)(2,1)S(1)} collective-permute-done((bf16[384,512]{1,0:T(8,128)(2,1)}, bf16[384,512]{1,0:T(8,128)(2,1)S(1)}, u32[]{:S(2)}, u32[]{:S(2)}) %collective-permute-start.9) | collective-permute-done | bytes 393248 | tf_op jit(solution)/shard_map/ppermute | solution.py:463
  39.3 2.6 %join_pairs.1 = (bf16[768,512]{1,0:T(8,128)(2,1)}, bf16[768,512]{1,0:T(8,128)(2,1)}) custom-call(bf16[384,512]{1,0:T(8,128)(2,1)} %copy-done.16, bf16[384,512]{1,0:T(8,128)(2,1)} %collective-permute-done.4.refs_3_.refs_1_, bf16[384,512]{1,0:T(8,128)(2,1)} %copy-done.19, bf16[384,512]{1,0:T(8,128)(2,1)} %copy-done.18), custom_call_target="tpu_custom_call" | custom-call | tf_op jit(solution)/shard_map/join_pairs/pallas_call | solution.py:92
  41.9 1.8 %collective-permute-start.11 = (bf16[768,512]{1,0:T(8,128)(2,1)}, bf16[768,512]{1,0:T(8,128)(2,1)S(1)}, u32[]{:S(2)}, u32[]{:S(2)}) collective-permute-start(bf16[768,512]{1,0:T(8,128)(2,1)} %get-tuple-element.27.refs_15_.refs_1_), channel_id=1, source_target_pairs={{0,0},{4,8},{8,4},{12,12},{1,1},{5,9},{9,5},{13,13},{2,2},{6,10},{... | collective-permute-start | bytes 2359304 | tf_op jit(solution)/shard_map/ppermute | solution.py:467
  43.7 2.9 %collective-permute-start.12 = (bf16[768,512]{1,0:T(8,128)(2,1)}, bf16[768,512]{1,0:T(8,128)(2,1)}, u32[]{:S(2)}, u32[]{:S(2)}) collective-permute-start(bf16[768,512]{1,0:T(8,128)(2,1)} %get-tuple-element.28.refs_22_), channel_id=1, source_target_pairs={{0,4},{4,0},{8,12},{12,8},{1,5},{5,1},{9,13},{13,9},{2,6},{6,2},{1... | collective-permute-start | bytes 2359304 | tf_op jit(solution)/shard_map/ppermute | solution.py:463
  47.6 1.5 %collective-permute-start.7 = (bf16[64,3200]{1,0:T(8,128)(2,1)}, bf16[64,3200]{1,0:T(8,128)(2,1)S(1)}, u32[]{:S(2)}, u32[]{:S(2)}) collective-permute-start(bf16[64,3200]{1,0:T(8,128)(2,1)} %slice.8), channel_id=1, source_target_pairs={{0,2},{2,0},{1,3},{3,1},{4,6},{6,4},{5,7},{7,5},{8,10},{10,8},{9,1... | collective-permute-start | bytes 1228808 | tf_op jit(solution)/shard_map/ppermute | solution.py:38
  49.9 1.5 %collective-permute-start.8 = (bf16[64,3200]{1,0:T(8,128)(2,1)}, bf16[64,3200]{1,0:T(8,128)(2,1)}, u32[]{:S(2)}, u32[]{:S(2)}) collective-permute-start(bf16[64,3200]{1,0:T(8,128)(2,1)} %slice.9), channel_id=1, source_target_pairs={{0,16},{16,0},{1,17},{17,1},{2,18},{18,2},{3,19},{19,3},{4,20},{20... | collective-permute-start | bytes 1228808 | tf_op jit(solution)/shard_map/ppermute | solution.py:38
  51.7 10.0 %collective-permute-done.12.refs_1_.refs_17_ = bf16[768,512]{1,0:T(8,128)(2,1)} collective-permute-done((bf16[768,512]{1,0:T(8,128)(2,1)}, bf16[768,512]{1,0:T(8,128)(2,1)}, u32[]{:S(2)}, u32[]{:S(2)}) %collective-permute-start.12) | collective-permute-done | bytes 786464 | tf_op jit(solution)/shard_map/ppermute | solution.py:463
  63.0 1.7 %collective-permute-start.17 = (bf16[768,512]{1,0:T(8,128)(2,1)S(1)}, bf16[768,512]{1,0:T(8,128)(2,1)}, u32[]{:S(2)}, u32[]{:S(2)}) collective-permute-start(bf16[768,512]{1,0:T(8,128)(2,1)S(1)} %copy-done.12), channel_id=1, source_target_pairs={{0,4},{4,0},{8,12},{12,8},{1,5},{5,1},{9,13},{13,9},{2,6},{6,2},{1... | collective-permute-start | bytes 2359304 | tf_op jit(solution)/shard_map/ppermute | solution.py:463
  65.3 1.3 %copy.21 = bf16[1,128,2048]{1,2,0:T(8,128)(2,1)S(1)} copy(bf16[1,128,2048]{2,1,0:T(8,128)(2,1)} %param.21) | data formatting | bytes 1048576 | tf_op args[10]
  67.6 3.7 %all-to-all-start = ((bf16[8,128,256]{2,1,0:T(8,128)(2,1)}), bf16[8,128,256]{2,1,0:T(8,128)(2,1)S(1)}, u32[]{:S(2)}, u32[]{:S(2)}) async-start(bf16[8,128,256]{2,1,0:T(8,128)(2,1)} %fence.7), calls=%async_computation | async-start | bytes 1048576 | tf_op jit(solution)/shard_map/all_to_all | solution.py:495
  71.4 8.6 %project.1.refs_3_ = f32[1024,512]{1,0:T(8,128)} custom-call(s32[2]{0:T(128)} %pad_add_fusion.place.refs_0_, bf16[16,2048]{1,0:T(8,128)(2,1)} %refs_1_.3, bf16[16,1024]{1,0:T(8,128)(2,1)} %refs_2_.3, bf16[128,3200]{1,0:T(8,128)(2,1)} %copy-done, bf16[128,3200]{1,0:T(8,128)(2,1)} %collective-permute-done.1.refs_4_.refs_5_, ...), custom_call_target="tpu_custom_call" | custom-call | flops 2415919104 | bytes 10747904 | tf_op jit(solution)/shard_map/project/pallas_call | solution.py:354
  80.2 2.4 %collective-permute-done.17.refs_23_ = bf16[768,512]{1,0:T(8,128)(2,1)} collective-permute-done((bf16[768,512]{1,0:T(8,128)(2,1)S(1)}, bf16[768,512]{1,0:T(8,128)(2,1)}, u32[]{:S(2)}, u32[]{:S(2)}) %collective-permute-start.17) | collective-permute-done | bytes 786464 | tf_op jit(solution)/shard_map/ppermute | solution.py:463
  82.6 10.6 %attend.1 = (bf16[8,32,384]{2,1,0:T(8,128)(2,1)}, f32[16,384]{1,0:T(8,128)}) custom-call(s32[2]{0:T(128)} %pad_add_fusion.place.refs_0_, bf16[16,2048]{1,0:T(8,128)(2,1)} %refs_1_.3, bf16[16,1024]{1,0:T(8,128)(2,1)} %refs_2_.3, f32[1024,512]{1,0:T(8,128)} %project.1.refs_3_, bf16[128,3200]{1,0:T(8,128)(2,1)} %copy-done, ...), custom_call_target="tpu_custom_call" | custom-call | tf_op jit(solution)/shard_map/attend/pallas_call | solution.py:376
  93.1 9.7 %all_to_all.10.gas = bf16[8,32,384]{2,1,0:T(8,128)(2,1)} all-to-all(bf16[8,32,384]{2,1,0:T(8,128)(2,1)} %get-tuple-element.32), channel_id=1, replica_groups=mesh['groups'=1,'ctx'=2,'z'=4,'y'=2,'c'=2] {'ctx','y','c'}, dimensions={0} | all-to-all | bytes 393216 | tf_op jit(solution)/shard_map/all_to_all | solution.py:605
  102.8 1.6 %sum_pieces.1.refs_0_ = bf16[48,384]{1,0:T(8,128)(2,1)} custom-call(bf16[8,32,384]{2,1,0:T(8,128)(2,1)} %all_to_all.10.gas, f32[16,384]{1,0:T(8,128)} %get-tuple-element.33.gb), custom_call_target="tpu_custom_call" | custom-call | tf_op jit(solution)/shard_map/sum_pieces/pallas_call | solution.py:410
  104.4 2.0 %collective-permute-start.18 = (bf16[48,384]{1,0:T(8,128)(2,1)}, bf16[48,384]{1,0:T(8,128)(2,1)S(1)}, u32[]{:S(2)}, u32[]{:S(2)}) collective-permute-start(bf16[48,384]{1,0:T(8,128)(2,1)} %sum_pieces.1.refs_0_), channel_id=1, source_target_pairs={{0,4},{4,0},{8,12},{12,8},{1,5},{5,1},{9,13},{13,9},{2,6},{6,2},{1... | collective-permute-start | bytes 110600 | tf_op jit(solution)/shard_map/ppermute | solution.py:38
  106.8 2.0 %collective-permute-start.20 = (bf16[48,384]{1,0:T(8,128)(2,1)}, bf16[48,384]{1,0:T(8,128)(2,1)S(1)}, u32[]{:S(2)}, u32[]{:S(2)}) collective-permute-start(bf16[48,384]{1,0:T(8,128)(2,1)} %sum_pieces.1.refs_0_), channel_id=1, source_target_pairs={{0,12},{4,8},{8,4},{12,0},{1,13},{5,9},{9,5},{13,1},{2,14},{6,10},... | collective-permute-start | bytes 110600 | tf_op jit(solution)/shard_map/ppermute | solution.py:38
  108.8 2.9 %collective-permute-done.19.refs_2_ = bf16[48,384]{1,0:T(8,128)(2,1)S(1)} collective-permute-done((bf16[48,384]{1,0:T(8,128)(2,1)}, bf16[48,384]{1,0:T(8,128)(2,1)S(1)}, u32[]{:S(2)}, u32[]{:S(2)}) %collective-permute-start.19) | collective-permute-done | bytes 36896 | tf_op jit(solution)/shard_map/ppermute | solution.py:38
  113.4 1.5 %scale_sum.1.refs_0_ = bf16[48,384]{1,0:T(8,128)(2,1)} custom-call(bf16[48,384]{1,0:T(8,128)(2,1)} %sum_pieces.1.refs_0_, bf16[48,384]{1,0:T(8,128)(2,1)} %copy-done.27, bf16[48,384]{1,0:T(8,128)(2,1)} %copy-done.28, bf16[48,384]{1,0:T(8,128)(2,1)} %copy-done.29), custom_call_target="tpu_custom_call" | custom-call | tf_op jit(solution)/shard_map/scale_sum/pallas_call | solution.py:428
  114.9 1.1 collective-permute-start.22
  116.8 1.1 collective-permute-start.24
  119.5 1.6 %collective-permute-start.27 = (bf16[48,384]{1,0:T(8,128)(2,1)}, bf16[48,384]{1,0:T(8,128)(2,1)S(1)}, u32[]{:S(2)}, u32[]{:S(2)}) collective-permute-start(bf16[48,384]{1,0:T(8,128)(2,1)} %scale_sum.1.refs_0_), channel_id=1, source_target_pairs={{0,19},{1,18},{2,17},{3,16},{16,3},{17,2},{18,1},{19,0},{4,23},{5,... | collective-permute-start | bytes 110600 | tf_op jit(solution)/shard_map/ppermute | solution.py:38
  121.7 1.8 %collective-permute-done.26.refs_6_ = bf16[48,384]{1,0:T(8,128)(2,1)S(1)} collective-permute-done((bf16[48,384]{1,0:T(8,128)(2,1)}, bf16[48,384]{1,0:T(8,128)(2,1)S(1)}, u32[]{:S(2)}, u32[]{:S(2)}) %collective-permute-start.26) | collective-permute-done | bytes 36896 | tf_op jit(solution)/shard_map/ppermute | solution.py:38
  124.7 1.7 %spread.1 = (f32[16,3072]{1,0:T(8,128)}, f32[16,2048]{1,0:T(8,128)}, f32[16,3072]{1,0:T(8,128)}, f32[16,1024]{1,0:T(8,128)}) custom-call(s32[2]{0:T(128)} %pad_add_fusion.place.refs_0_, bf16[48,384]{1,0:T(8,128)(2,1)} %scale_sum.1.refs_0_, bf16[48,384]{1,0:T(8,128)(2,1)} %copy-done.20, bf16[48,384]{1,0:T(8,128)(2,1)} %copy-done.21, ...), custom_call_target="tpu_custom_call" | custom-call | tf_op jit(solution)/shard_map/spread/pallas_call | solution.py:452
  (105 shorter events, 19.7 us)
Async XLA Ops:
  0.6 16.3 %copy-start.2 = (bf16[1,128,3072]{2,1,0:T(8,128)(2,1)S(1)}, bf16[1,128,3072]{2,1,0:T(8,128)(2,1)}, u32[]{:S(2)}) copy-start(bf16[1,128,3072]{2,1,0:T(8,128)(2,1)} %param.11) | copy-start | bytes 2359300
  0.6 16.3 %copy-start.4 = (bf16[3072,16]{0,1:T(8,128)(2,1)S(1)}, bf16[3072,16]{0,1:T(8,128)(2,1)}, u32[]{:S(2)}) copy-start(bf16[3072,16]{0,1:T(8,128)(2,1)} %param.17) | copy-start | bytes 294916
  3.2 2.0 %collective-permute-start = (bf16[2,192,512]{2,1,0:T(8,128)(2,1)}, bf16[2,192,512]{2,1,0:T(8,128)(2,1)S(1)}, u32[]{:S(2)}, u32[]{:S(2)}) collective-permute-start(bf16[2,192,512]{2,1,0:T(8,128)(2,1)} %get-tuple-element.22), channel_id=1, source_target_pairs={{0,1},{1,0},{2,3},{3,2},{4,5},{5,4},{6,7},{7,6},{8,9},{9,8},{10,11... | collective-permute-start | bytes 1179656 | tf_op jit(solution)/shard_map/ppermute | solution.py:38
  8.0 13.3 %collective-permute-start.2 = (bf16[384,512]{1,0:T(8,128)(2,1)}, bf16[384,512]{1,0:T(8,128)(2,1)S(1)}, u32[]{:S(2)}, u32[]{:S(2)}) collective-permute-start(bf16[384,512]{1,0:T(8,128)(2,1)} %get-tuple-element.23.rest_0_), channel_id=1, source_target_pairs={{0,2},{2,0},{1,3},{3,1},{4,6},{6,4},{5,7},{7,5},{8,10},{10,8},{9,1... | collective-permute-start | bytes 1179656 | tf_op jit(solution)/shard_map/ppermute | solution.py:38
  10.9 11.1 %collective-permute-start.3 = (bf16[384,512]{1,0:T(8,128)(2,1)}, bf16[384,512]{1,0:T(8,128)(2,1)S(1)}, u32[]{:S(2)}, u32[]{:S(2)}) collective-permute-start(bf16[384,512]{1,0:T(8,128)(2,1)} %get-tuple-element.26.refs_13_), channel_id=1, source_target_pairs={{0,4},{4,0},{8,12},{12,8},{1,5},{5,1},{9,13},{13,9},{2,6},{6,2},{1... | collective-permute-start | bytes 1179656 | tf_op jit(solution)/shard_map/ppermute | solution.py:463
  12.5 9.5 %collective-permute-start.4 = (bf16[384,512]{1,0:T(8,128)(2,1)}, bf16[384,512]{1,0:T(8,128)(2,1)}, u32[]{:S(2)}, u32[]{:S(2)}) collective-permute-start(bf16[384,512]{1,0:T(8,128)(2,1)} %get-tuple-element.26.refs_13_), channel_id=1, source_target_pairs={{0,0},{4,8},{8,4},{12,12},{1,1},{5,9},{9,5},{13,13},{2,2},{6,10},{... | collective-permute-start | bytes 1179656 | tf_op jit(solution)/shard_map/ppermute | solution.py:467
  19.8 31.7 %copy-start = (bf16[128,3200]{1,0:T(8,128)(2,1)}, bf16[128,3200]{1,0:T(8,128)(2,1)S(1)}, u32[]{:S(2)}) copy-start(bf16[128,3200]{1,0:T(8,128)(2,1)S(1)} %get-tuple-element.24.refs_3_.refs_4_) | copy-start | bytes 2457604
  19.8 26.8 %collective-permute-start.6 = (bf16[128,3200]{1,0:T(8,128)(2,1)S(1)}, bf16[128,3200]{1,0:T(8,128)(2,1)S(1)}, u32[]{:S(2)}, u32[]{:S(2)}) collective-permute-start(bf16[128,3200]{1,0:T(8,128)(2,1)S(1)} %get-tuple-element.24.refs_3_.refs_4_), channel_id=1, source_target_pairs={{0,16},{16,0},{1,17},{17,1},{2,18},{18,2},{3,19},{19,3},{4,20},{20... | collective-permute-start | bytes 2457608 | tf_op jit(solution)/shard_map/ppermute | solution.py:38
  22.7 26.4 %collective-permute-start.5 = (bf16[128,3200]{1,0:T(8,128)(2,1)}, bf16[128,3200]{1,0:T(8,128)(2,1)S(1)}, u32[]{:S(2)}, u32[]{:S(2)}) collective-permute-start(bf16[128,3200]{1,0:T(8,128)(2,1)} %fence.4), channel_id=1, source_target_pairs={{0,2},{2,0},{1,3},{3,1},{4,6},{6,4},{5,7},{7,5},{8,10},{10,8},{9,1... | collective-permute-start | bytes 2457608 | tf_op jit(solution)/shard_map/ppermute | solution.py:38
  23.2 7.7 %collective-permute-start.10 = (bf16[384,512]{1,0:T(8,128)(2,1)}, bf16[384,512]{1,0:T(8,128)(2,1)S(1)}, u32[]{:S(2)}, u32[]{:S(2)}) collective-permute-start(bf16[384,512]{1,0:T(8,128)(2,1)} %copy-done.15), channel_id=1, source_target_pairs={{0,0},{4,8},{8,4},{12,12},{1,1},{5,9},{9,5},{13,13},{2,2},{6,10},{... | collective-permute-start | bytes 1179656 | tf_op jit(solution)/shard_map/ppermute | solution.py:467
  24.8 13.7 %collective-permute-start.9 = (bf16[384,512]{1,0:T(8,128)(2,1)}, bf16[384,512]{1,0:T(8,128)(2,1)S(1)}, u32[]{:S(2)}, u32[]{:S(2)}) collective-permute-start(bf16[384,512]{1,0:T(8,128)(2,1)} %copy-done.15), channel_id=1, source_target_pairs={{0,4},{4,0},{8,12},{12,8},{1,5},{5,1},{9,13},{13,9},{2,6},{6,2},{1... | collective-permute-start | bytes 1179656 | tf_op jit(solution)/shard_map/ppermute | solution.py:463
  41.9 9.6 %collective-permute-start.11 = (bf16[768,512]{1,0:T(8,128)(2,1)}, bf16[768,512]{1,0:T(8,128)(2,1)S(1)}, u32[]{:S(2)}, u32[]{:S(2)}) collective-permute-start(bf16[768,512]{1,0:T(8,128)(2,1)} %get-tuple-element.27.refs_15_.refs_1_), channel_id=1, source_target_pairs={{0,0},{4,8},{8,4},{12,12},{1,1},{5,9},{9,5},{13,13},{2,2},{6,10},{... | collective-permute-start | bytes 2359304 | tf_op jit(solution)/shard_map/ppermute | solution.py:467
  43.7 18.1 %collective-permute-start.12 = (bf16[768,512]{1,0:T(8,128)(2,1)}, bf16[768,512]{1,0:T(8,128)(2,1)}, u32[]{:S(2)}, u32[]{:S(2)}) collective-permute-start(bf16[768,512]{1,0:T(8,128)(2,1)} %get-tuple-element.28.refs_22_), channel_id=1, source_target_pairs={{0,4},{4,0},{8,12},{12,8},{1,5},{5,1},{9,13},{13,9},{2,6},{6,2},{1... | collective-permute-start | bytes 2359304 | tf_op jit(solution)/shard_map/ppermute | solution.py:463
  47.6 14.2 %collective-permute-start.7 = (bf16[64,3200]{1,0:T(8,128)(2,1)}, bf16[64,3200]{1,0:T(8,128)(2,1)S(1)}, u32[]{:S(2)}, u32[]{:S(2)}) collective-permute-start(bf16[64,3200]{1,0:T(8,128)(2,1)} %slice.8), channel_id=1, source_target_pairs={{0,2},{2,0},{1,3},{3,1},{4,6},{6,4},{5,7},{7,5},{8,10},{10,8},{9,1... | collective-permute-start | bytes 1228808 | tf_op jit(solution)/shard_map/ppermute | solution.py:38
  49.1 15.7 %collective-permute-start.14 = (bf16[128,3200]{1,0:T(8,128)(2,1)}, bf16[128,3200]{1,0:T(8,128)(2,1)S(1)}, u32[]{:S(2)}, u32[]{:S(2)}) collective-permute-start(bf16[128,3200]{1,0:T(8,128)(2,1)} %copy-done.13), channel_id=1, source_target_pairs={{0,1},{1,0},{2,3},{3,2},{4,5},{5,4},{6,7},{7,6},{8,9},{9,8},{10,11... | collective-permute-start | bytes 2457608 | tf_op jit(solution)/shard_map/ppermute | solution.py:38
  49.9 12.2 %collective-permute-start.8 = (bf16[64,3200]{1,0:T(8,128)(2,1)}, bf16[64,3200]{1,0:T(8,128)(2,1)}, u32[]{:S(2)}, u32[]{:S(2)}) collective-permute-start(bf16[64,3200]{1,0:T(8,128)(2,1)} %slice.9), channel_id=1, source_target_pairs={{0,16},{16,0},{1,17},{17,1},{2,18},{18,2},{3,19},{19,3},{4,20},{20... | collective-permute-start | bytes 1228808 | tf_op jit(solution)/shard_map/ppermute | solution.py:38
  51.4 19.9 %collective-permute-start.1 = (bf16[128,3200]{1,0:T(8,128)(2,1)S(1)}, bf16[128,3200]{1,0:T(8,128)(2,1)}, u32[]{:S(2)}, u32[]{:S(2)}) collective-permute-start(bf16[128,3200]{1,0:T(8,128)(2,1)S(1)} %get-tuple-element.24.refs_3_.refs_4_), channel_id=1, source_target_pairs={{0,1},{1,0},{2,3},{3,2},{4,5},{5,4},{6,7},{7,6},{8,9},{9,8},{10,11... | collective-permute-start | bytes 2457608 | tf_op jit(solution)/shard_map/ppermute | solution.py:38
  62.5 8.9 %collective-permute-start.13 = (bf16[128,3200]{1,0:T(8,128)(2,1)}, bf16[128,3200]{1,0:T(8,128)(2,1)}, u32[]{:S(2)}, u32[]{:S(2)}) collective-permute-start(bf16[128,3200]{1,0:T(8,128)(2,1)} %get-tuple-element.29.refs_5_.refs_6_), channel_id=1, source_target_pairs={{0,1},{1,0},{2,3},{3,2},{4,5},{5,4},{6,7},{7,6},{8,9},{9,8},{10,11... | collective-permute-start | bytes 2457608 | tf_op jit(solution)/shard_map/ppermute | solution.py:38
  63.0 19.5 %collective-permute-start.17 = (bf16[768,512]{1,0:T(8,128)(2,1)S(1)}, bf16[768,512]{1,0:T(8,128)(2,1)}, u32[]{:S(2)}, u32[]{:S(2)}) collective-permute-start(bf16[768,512]{1,0:T(8,128)(2,1)S(1)} %copy-done.12), channel_id=1, source_target_pairs={{0,4},{4,0},{8,12},{12,8},{1,5},{5,1},{9,13},{13,9},{2,6},{6,2},{1... | collective-permute-start | bytes 2359304 | tf_op jit(solution)/shard_map/ppermute | solution.py:463
  64.8 6.6 %collective-permute-start.15 = (bf16[64,3200]{1,0:T(8,128)(2,1)}, bf16[64,3200]{1,0:T(8,128)(2,1)}, u32[]{:S(2)}, u32[]{:S(2)}) collective-permute-start(bf16[64,3200]{1,0:T(8,128)(2,1)} %get-tuple-element.30.refs_9_.refs_10_), channel_id=1, source_target_pairs={{0,1},{1,0},{2,3},{3,2},{4,5},{5,4},{6,7},{7,6},{8,9},{9,8},{10,11... | collective-permute-start | bytes 1228808 | tf_op jit(solution)/shard_map/ppermute | solution.py:38
  64.8 6.6 %collective-permute-start.16 = (bf16[64,3200]{1,0:T(8,128)(2,1)}, bf16[64,3200]{1,0:T(8,128)(2,1)}, u32[]{:S(2)}, u32[]{:S(2)}) collective-permute-start(bf16[64,3200]{1,0:T(8,128)(2,1)} %get-tuple-element.31.refs_10_.refs_11_), channel_id=1, source_target_pairs={{0,1},{1,0},{2,3},{3,2},{4,5},{5,4},{6,7},{7,6},{8,9},{9,8},{10,11... | collective-permute-start | bytes 1228808 | tf_op jit(solution)/shard_map/ppermute | solution.py:38
  67.6 12.6 %all-to-all-start = ((bf16[8,128,256]{2,1,0:T(8,128)(2,1)}), bf16[8,128,256]{2,1,0:T(8,128)(2,1)S(1)}, u32[]{:S(2)}, u32[]{:S(2)}) async-start(bf16[8,128,256]{2,1,0:T(8,128)(2,1)} %fence.7), calls=%async_computation | async-start | bytes 1048576 | tf_op jit(solution)/shard_map/all_to_all | solution.py:495
  104.4 4.4 %collective-permute-start.18 = (bf16[48,384]{1,0:T(8,128)(2,1)}, bf16[48,384]{1,0:T(8,128)(2,1)S(1)}, u32[]{:S(2)}, u32[]{:S(2)}) collective-permute-start(bf16[48,384]{1,0:T(8,128)(2,1)} %sum_pieces.1.refs_0_), channel_id=1, source_target_pairs={{0,4},{4,0},{8,12},{12,8},{1,5},{5,1},{9,13},{13,9},{2,6},{6,2},{1... | collective-permute-start | bytes 110600 | tf_op jit(solution)/shard_map/ppermute | solution.py:38
  106.4 5.4 %collective-permute-start.19 = (bf16[48,384]{1,0:T(8,128)(2,1)}, bf16[48,384]{1,0:T(8,128)(2,1)S(1)}, u32[]{:S(2)}, u32[]{:S(2)}) collective-permute-start(bf16[48,384]{1,0:T(8,128)(2,1)} %sum_pieces.1.refs_0_), channel_id=1, source_target_pairs={{0,8},{4,12},{8,0},{12,4},{1,9},{5,13},{9,1},{13,5},{2,10},{6,14},... | collective-permute-start | bytes 110600 | tf_op jit(solution)/shard_map/ppermute | solution.py:38
  106.8 6.0 %collective-permute-start.20 = (bf16[48,384]{1,0:T(8,128)(2,1)}, bf16[48,384]{1,0:T(8,128)(2,1)S(1)}, u32[]{:S(2)}, u32[]{:S(2)}) collective-permute-start(bf16[48,384]{1,0:T(8,128)(2,1)} %sum_pieces.1.refs_0_), channel_id=1, source_target_pairs={{0,12},{4,8},{8,4},{12,0},{1,13},{5,9},{9,5},{13,1},{2,14},{6,10},... | collective-permute-start | bytes 110600 | tf_op jit(solution)/shard_map/ppermute | solution.py:38
  114.9 3.5 %collective-permute-start.21 = (bf16[48,384]{1,0:T(8,128)(2,1)}, bf16[48,384]{1,0:T(8,128)(2,1)S(1)}, u32[]{:S(2)}, u32[]{:S(2)}) collective-permute-start(bf16[48,384]{1,0:T(8,128)(2,1)} %scale_sum.1.refs_0_), channel_id=1, source_target_pairs={{0,1},{1,0},{2,3},{3,2},{16,17},{17,16},{18,19},{19,18},{4,5},{5,4... | collective-permute-start | bytes 110600 | tf_op jit(solution)/shard_map/ppermute | solution.py:38
  114.9 4.6 %collective-permute-start.22 = (bf16[48,384]{1,0:T(8,128)(2,1)}, bf16[48,384]{1,0:T(8,128)(2,1)S(1)}, u32[]{:S(2)}, u32[]{:S(2)}) collective-permute-start(bf16[48,384]{1,0:T(8,128)(2,1)} %scale_sum.1.refs_0_), channel_id=1, source_target_pairs={{0,2},{1,3},{2,0},{3,1},{16,18},{17,19},{18,16},{19,17},{4,6},{5,7... | collective-permute-start | bytes 110600 | tf_op jit(solution)/shard_map/ppermute | solution.py:38
  116.0 5.1 %collective-permute-start.23 = (bf16[48,384]{1,0:T(8,128)(2,1)}, bf16[48,384]{1,0:T(8,128)(2,1)S(1)}, u32[]{:S(2)}, u32[]{:S(2)}) collective-permute-start(bf16[48,384]{1,0:T(8,128)(2,1)} %scale_sum.1.refs_0_), channel_id=1, source_target_pairs={{0,3},{1,2},{2,1},{3,0},{16,19},{17,18},{18,17},{19,16},{4,7},{5,6... | collective-permute-start | bytes 110600 | tf_op jit(solution)/shard_map/ppermute | solution.py:38
  116.8 4.4 %collective-permute-start.24 = (bf16[48,384]{1,0:T(8,128)(2,1)}, bf16[48,384]{1,0:T(8,128)(2,1)S(1)}, u32[]{:S(2)}, u32[]{:S(2)}) collective-permute-start(bf16[48,384]{1,0:T(8,128)(2,1)} %scale_sum.1.refs_0_), channel_id=1, source_target_pairs={{0,16},{1,17},{2,18},{3,19},{16,0},{17,1},{18,2},{19,3},{4,20},{5,... | collective-permute-start | bytes 110600 | tf_op jit(solution)/shard_map/ppermute | solution.py:38
  117.9 3.8 %collective-permute-start.25 = (bf16[48,384]{1,0:T(8,128)(2,1)}, bf16[48,384]{1,0:T(8,128)(2,1)S(1)}, u32[]{:S(2)}, u32[]{:S(2)}) collective-permute-start(bf16[48,384]{1,0:T(8,128)(2,1)} %scale_sum.1.refs_0_), channel_id=1, source_target_pairs={{0,17},{1,16},{2,19},{3,18},{16,1},{17,0},{18,3},{19,2},{4,21},{5,... | collective-permute-start | bytes 110600 | tf_op jit(solution)/shard_map/ppermute | solution.py:38
  118.4 5.1 %collective-permute-start.26 = (bf16[48,384]{1,0:T(8,128)(2,1)}, bf16[48,384]{1,0:T(8,128)(2,1)S(1)}, u32[]{:S(2)}, u32[]{:S(2)}) collective-permute-start(bf16[48,384]{1,0:T(8,128)(2,1)} %scale_sum.1.refs_0_), channel_id=1, source_target_pairs={{0,18},{1,19},{2,16},{3,17},{16,2},{17,3},{18,0},{19,1},{4,22},{5,... | collective-permute-start | bytes 110600 | tf_op jit(solution)/shard_map/ppermute | solution.py:38
  119.5 4.5 %collective-permute-start.27 = (bf16[48,384]{1,0:T(8,128)(2,1)}, bf16[48,384]{1,0:T(8,128)(2,1)S(1)}, u32[]{:S(2)}, u32[]{:S(2)}) collective-permute-start(bf16[48,384]{1,0:T(8,128)(2,1)} %scale_sum.1.refs_0_), channel_id=1, source_target_pairs={{0,19},{1,18},{2,17},{3,16},{16,3},{17,2},{18,1},{19,0},{4,23},{5,... | collective-permute-start | bytes 110600 | tf_op jit(solution)/shard_map/ppermute | solution.py:38
  (27 other events, 118.2 us)

commit v4 on v2

--- a/solution.py
+++ b/solution.py
@@ -21,6 +21,7 @@
 ANY = pl.BlockSpec(memory_space=pl.ANY)
 VMEM = pl.BlockSpec(memory_space=pltpu.VMEM)
 SMEM = pl.BlockSpec(memory_space=pltpu.SMEM)
+PARAMS = pltpu.CompilerParams(vmem_limit_bytes=60 * 2**20)
 
 NT = (((1,), (1,)), ((), ()))
 TN = (((0,), (0,)), ((), ()))
@@ -37,22 +38,19 @@
     return lax.ppermute(value, axes, [(i, i ^ distance) for i in range(count)])
 
 
-def pack_weights_kernel(heads, place, qw, kw, vw, out):
-    group = heads * HEAD_SIZE
-    for index in range(out.shape[0]):
-        mine = (place[0] // 4) * 4 + index
-        for src, at, wide in ((qw, 0, group), (kw, group, HEAD_SIZE), (vw, group + HEAD_SIZE, HEAD_SIZE)):
-            out[index, :, at : at + wide] = src[:, pl.ds(pl.multiple_of(mine * wide, wide), wide)]
-
-
-def pack_weights(place, qw, kw, vw, heads):
-    return pl.pallas_call(
-        functools.partial(pack_weights_kernel, heads),
-        out_shape=jax.ShapeDtypeStruct((4, qw.shape[0], (heads + 2) * HEAD_SIZE), qw.dtype),
-        in_specs=[SMEM, VMEM, VMEM, VMEM],
-        out_specs=VMEM,
-        name="pack_weights",
-    )(place, qw, kw, vw)
+def pack_weights(mine, qw, kw, vw, heads):
+    def columns(owner):
+        wide = heads * HEAD_SIZE
+        parts = [lax.dynamic_slice_in_dim(qw, owner * wide, wide, 1)]
+        parts += [lax.dynamic_slice_in_dim(w, owner * HEAD_SIZE, HEAD_SIZE, 1) for w in (kw, vw)]
+        return jnp.concatenate(parts, 1)
+
+    return [jnp.stack([columns(mine ^ (2 * chip + core)) for chip in range(2)]) for core in range(2)]
+
+
+def join_rows(core, kept, got):
+    first, second = jnp.where(core == 0, kept, got), jnp.where(core == 0, got, kept)
+    return [jnp.concatenate([first[chip], second[chip]], 0) for chip in range(2)]
 
 
 def fence_kernel(*refs):
@@ -67,12 +65,12 @@
         in_specs=[ANY] * (count + len(earlier)),
         out_specs=[ANY] * count,
         input_output_aliases={i: i for i in range(count)},
+        compiler_params=PARAMS,
         name="fence",
     )(*values, *earlier)
 
 
-def norm_kernel(tokens, trace, gain, down_q, down_v, *rest):
-    out = rest[-1]
+def norm_kernel(copies, tokens, trace, gain, down_q, down_v, *rest):
     flt = tokens[...].astype(jnp.float32)
     meansq = jnp.mean(flt * flt, axis=-1, keepdims=True)
     normed = (flt * lax.rsqrt(meansq + EPS) * gain[...].astype(jnp.float32)[None, :]).astype(jnp.bfloat16)
@@ -85,18 +83,19 @@
     ids = jnp.sum(jnp.where(diagonal, trace[...].astype(jnp.float32), 0.0), axis=1, keepdims=True)
     filler = jnp.zeros((rows, LANES - 2 * rank - 1), jnp.float32)
     extra = jnp.concatenate([low_q, low_v, ids, filler], 1).astype(jnp.bfloat16)
-    out[:, :feats] = normed
-    out[:, feats:] = extra
-
-
-def norm_tokens(tokens, trace, gain, down_q, down_v, *earlier):
+    for out in rest[-copies:]:
+        out[:, :feats] = normed
+        out[:, feats:] = extra
+
+
+def norm_tokens(tokens, trace, gain, down_q, down_v, copies, *earlier):
     rows, feats = tokens.shape
     return pl.pallas_call(
-        norm_kernel,
-        out_shape=jax.ShapeDtypeStruct((rows, feats + LANES), jnp.bfloat16),
+        functools.partial(norm_kernel, copies),
+        out_shape=[jax.ShapeDtypeStruct((rows, feats + LANES), jnp.bfloat16)] * copies,
         in_specs=[VMEM] * 5 + [ANY] * len(earlier),
-        out_specs=VMEM,
-        compiler_params=pltpu.CompilerParams(vmem_limit_bytes=32 * 2**20),
+        out_specs=[VMEM] * copies,
+        compiler_params=pltpu.CompilerParams(vmem_limit_bytes=16 * 2**20),
         name="norm_tokens",
     )(tokens, trace, gain, down_q, down_v, *earlier)
 
@@ -117,13 +116,6 @@
             self.waits.append((sequence, copy))
             self.count += 1
 
-    def add_either(self, condition, first, second, target):
-        copies = [pltpu.make_async_copy(src, target, self.sems.at[self.count]) for src in (first, second)]
-        pl.when(condition)(copies[0].start)
-        pl.when(jnp.logical_not(condition))(copies[1].start)
-        self.waits.append((0, copies[0]))
-        self.count += 1
-
     def wait(self, sequence):
         for needed, copy in self.waits:
             if needed == sequence:
@@ -139,14 +131,14 @@
     rank, group = up_q.shape[0], heads * HEAD_SIZE
     depth = plan["depth"]
 
-    loads, at = Loads(sems), 0
-    for index, (_, condition, sources) in enumerate(shards):
-        target = w_all.at[pl.ds(index * depth, depth), :]
-        if condition is None:
-            loads.add(place, [((lambda p, i=index: i * depth, 0, None), w_refs[at])], w_all)
-        else:
-            loads.add_either(condition(place), w_refs[at], w_refs[at + 1], target)
-        at += len(sources)
+    loads = Loads(sems)
+    for index, (_, chunks) in enumerate(shards):
+        for number, part, at in chunks:
+            piece = (lambda p, at=at, index=index: index * depth + at(p), 0, None)
+            src = w_refs[number]
+            rows = src.shape[0]
+            src = src.at[slice(*part.indices(rows))]
+            loads.add(place, [(piece, src)], w_all)
     loads.add(place, list(zip(plan["x"], x_refs)), x_all)
 
     mine = place[0]
@@ -162,7 +154,7 @@
         loads.wait(index)
         rows = pl.ds(index * seq, seq)
         total = dot(x_all[rows, feats:], ups)
-        for number, (offset, _, _) in enumerate(shards):
+        for number, (offset, _) in enumerate(shards):
             columns = pl.ds(pl.multiple_of(offset(place), LANES), depth)
             total = total + dot(x_all[rows, columns], w_all[number * depth : (number + 1) * depth])
         out[rows, :] = total
@@ -172,8 +164,9 @@
     n_x, n_g, last = len(plan["x"]), len(plan["g"]), plan["last"]
     place, up_q, up_v, base = refs[:4]
     x_refs, g_refs = refs[4 : 4 + n_x], refs[4 + n_x : 4 + n_x + n_g]
-    w_refs, rest = refs[4 + n_x + n_g : -8], refs[-8:]
-    ga_out, gb_out, x_all, g_all, w_all, base_all, pulls, sems = rest
+    n_out = 7 + plan["cores"]
+    w_refs, rest = refs[4 + n_x + n_g : -n_out], refs[-n_out:]
+    ga_outs, (gb_out, x_all, g_all, w_all, base_all, pulls, sems) = rest[:-7], rest[-7:]
 
     feats, heads, seq, window, depth = (plan[k] for k in ("feats", "heads", "seq", "window", "depth"))
     rank, parts = up_q.shape[0], plan["parts"]
@@ -182,11 +175,6 @@
     sequences = tokens // seq
 
     loads = Loads(sems)
-    if last is not None:
-        offset, condition = last
-        copy = pltpu.make_async_copy(w_refs[0], w_all, sems.at[loads.count])
-        loads.count += 1
-        pl.when(condition(place))(copy.start)
     for index in range(sequences):
         rows = pl.ds(index * seq, seq)
         copy_base = pltpu.make_async_copy(base.at[rows, :], base_all.at[rows, :], sems.at[loads.count])
@@ -197,12 +185,10 @@
             chosen = [(piece, src) for piece, src in zip(pieces, sources) if piece[1] == index]
             loads.add(place, chosen, target)
     if last is not None:
-
-        @pl.when(jnp.logical_not(condition(place)))
-        def _():
-            w_all[...] = w_refs[1][...]
-
-        pl.when(condition(place))(copy.wait)
+        offset, chunks = last
+        for part, at in chunks:
+            value = w_refs[0][part, :]
+            w_all[pl.ds(pl.multiple_of(at(place), 16), value.shape[0]), :] = value
 
     mine = place[0]
     uq = up_q[:, pl.ds(pl.multiple_of(mine * group, group), group)]
@@ -266,23 +252,28 @@
     gb_out[:, :group] = sums[:rank, :group]
     gb_out[:, group:] = sums[rank : 2 * rank, group : group + HEAD_SIZE] + sums[rank : 2 * rank, group + HEAD_SIZE :]
     part = feats // parts
-    for index in range(parts):
-        piece = dot(pulls[...], x_all[:, index * part : (index + 1) * part])
-        ga_out[index, :rank] = piece[:rank].astype(ga_out.dtype)
-        ga_out[index, rank:] = (piece[rank : 2 * rank] + piece[2 * rank :]).astype(ga_out.dtype)
+    for core, out in enumerate(ga_outs):
+        for index in range(out.shape[0]):
+            piece = dot(pulls[...], x_all[:, index * part : (index + 1) * part])
+            out[index, :rank] = piece[:rank].astype(out.dtype)
+            out[index, rank:] = (piece[rank : 2 * rank] + piece[2 * rank :]).astype(out.dtype)
 
 
 def attend(place, up_q, up_v, gathered, plan):
     feats, heads, tokens, parts, seq = (plan[k] for k in ("feats", "heads", "tokens", "parts", "seq"))
-    rank = up_q.shape[0]
+    rank, cores = up_q.shape[0], plan["cores"]
     wide = (heads + 2) * HEAD_SIZE
     x_plan, x_arrays = zip(*gathered["x"])
     g_plan, g_arrays = zip(*gathered["g"])
-    shards = gathered["w"]
-    w_arrays = [array for _, _, sources in shards for array in sources]
-    depth = w_arrays[0].shape[0]
+    w_arrays, shards = [], []
+    for offset, chunks in gathered["w"]:
+        shards.append((offset, []))
+        for array, part, at in chunks:
+            index = next((i for i, known in enumerate(w_arrays) if known is array), len(w_arrays))
+            w_arrays += [array] if index == len(w_arrays) else []
+            shards[-1][1].append((index, part, at))
+    depth = w_arrays[-1].shape[0]
     plan = dict(plan, x=x_plan, g=g_plan, shards=shards, depth=depth)
-    params = pltpu.CompilerParams(vmem_limit_bytes=60 * 2**20)
     base = pl.pallas_call(
         functools.partial(project_kernel, plan),
         out_shape=jax.ShapeDtypeStruct((tokens, wide), jnp.float32),
@@ -291,60 +282,71 @@
         scratch_shapes=[
             pltpu.VMEM((tokens, feats + LANES), jnp.bfloat16),
             pltpu.VMEM((len(shards) * depth, wide), jnp.bfloat16),
-            pltpu.SemaphoreType.DMA((len(x_arrays) + len(shards),)),
+            pltpu.SemaphoreType.DMA((len(x_arrays) + 2 * len(shards),)),
         ],
-        compiler_params=params,
-        cost_estimate=pl.CostEstimate(
-            flops=2 * tokens * len(shards) * depth * wide,
-            bytes_accessed=2 * tokens * feats + 2 * len(shards) * depth * wide + 4 * tokens * wide,
-            transcendentals=0,
-        ),
+        cost_estimate=pl.CostEstimate(flops=0, bytes_accessed=0, transcendentals=0),
+        compiler_params=PARAMS,
         name="project",
     )(place, up_q, up_v, *x_arrays, *w_arrays)
 
-    offset, condition, sources = gathered["last"] or (None, None, [])
-    plan["last"] = None if offset is None else (offset, condition)
+    offset, chunks = gathered["last"] or (None, [])
+    plan["last"] = None if offset is None else (offset, [chunk[1:] for chunk in chunks])
+    last = [chunks[0][0]] if chunks else []
     return pl.pallas_call(
         functools.partial(attend_kernel, plan),
-        out_shape=[
-            jax.ShapeDtypeStruct((parts, 2 * rank, feats // parts), jnp.bfloat16),
-            jax.ShapeDtypeStruct((rank, (heads + 1) * HEAD_SIZE), jnp.float32),
-        ],
+        out_shape=[jax.ShapeDtypeStruct((parts // cores, 2 * rank, feats // parts), jnp.bfloat16)] * cores
+        + [jax.ShapeDtypeStruct((rank, (heads + 1) * HEAD_SIZE), jnp.float32)],
         in_specs=[SMEM, VMEM, VMEM]
         + [ANY] * (1 + len(x_arrays) + len(g_arrays))
-        + [ANY, VMEM][: len(sources)],
-        out_specs=[VMEM] * 2,
+        + [VMEM] * len(last),
+        out_specs=[VMEM] * (cores + 1),
         scratch_shapes=[
             pltpu.VMEM((tokens, feats + LANES), jnp.bfloat16),
             pltpu.VMEM((tokens, heads * HEAD_SIZE), jnp.bfloat16),
-            pltpu.VMEM((depth, wide) if sources else (16, LANES), jnp.bfloat16),
+            pltpu.VMEM((depth, wide) if last else (16, LANES), jnp.bfloat16),
             pltpu.VMEM((tokens, wide), jnp.float32),
             pltpu.VMEM((3 * rank, tokens), jnp.bfloat16),
-            pltpu.SemaphoreType.DMA((1 + tokens // seq + len(x_arrays) + len(g_arrays),)),
+            pltpu.SemaphoreType.DMA((tokens // seq + len(x_arrays) + len(g_arrays),)),
         ],
-        compiler_params=params,
+        compiler_params=PARAMS,
         name="attend",
-    )(place, up_q, up_v, base, *x_arrays, *g_arrays, *sources)
-
-
-def sum_kernel(gas, gb, out):
-    total = gas[0].astype(jnp.float32)
-    for index in range(1, gas.shape[0]):
-        total = total + gas[index].astype(jnp.float32)
+    )(place, up_q, up_v, base, *x_arrays, *g_arrays, *last)
+
+
+def add_kernel(kept, got, *outs):
+    for index, out in enumerate(outs):
+        out[...] = (kept[index].astype(jnp.float32) + got[index].astype(jnp.float32)).astype(out.dtype)
+
+
+def add_pieces(kept, got):
+    return pl.pallas_call(
+        add_kernel,
+        out_shape=[jax.ShapeDtypeStruct(kept.shape[1:], kept.dtype)] * kept.shape[0],
+        in_specs=[VMEM] * 2,
+        out_specs=[VMEM] * kept.shape[0],
+        name="add_pieces",
+    )(kept, got)
+
+
+def sum_kernel(gb, *refs):
+    gas, out = refs[:-1], refs[-1]
+    total = gas[0][...].astype(jnp.float32)
+    for ref in gas[1:]:
+        total = total + ref[...].astype(jnp.float32)
     rows = total.shape[0]
     out[:rows] = total.astype(out.dtype)
     out[rows:] = gb[...].astype(out.dtype)
 
 
 def sum_pieces(gas, gb):
-    _, rows, wide = gas.shape
+    rows, wide = gas[0].shape
     return pl.pallas_call(
         sum_kernel,
         out_shape=jax.ShapeDtypeStruct((rows + gb.shape[0], wide), jnp.bfloat16),
-        in_specs=[VMEM] * 2,
+        in_specs=[VMEM] * (1 + len(gas)),
         out_specs=VMEM,
         name="sum_pieces",
-    )(gas, gb)
+    )(gb, *gas)
 
 
 def scale_kernel(coefficient, *refs):
@@ -387,62 +389,66 @@
     )(place, *pieces)
 
 
-def outer_pairs(value):
-    return lax.ppermute(value, "z", [(0, 1), (1, 0), (2, 3), (3, 2)])
-
-
-def inner_pairs(value):
-    return lax.ppermute(value, "z", [(0, 0), (1, 2), (2, 1), (3, 3)])
-
-
-def is_inner(p):
-    return (p[1] == 1) | (p[1] == 2)
-
-
-def is_outer(p):
-    return (p[1] == 0) | (p[1] == 3)
+def ringed(value):
+    return lax.ppermute(value, "z", [(0, 1), (1, 3), (3, 2), (2, 0)])
 
 
 def paired_gather(place, qw, kw, vw, heads, norm_args, gradient):
     shard, rows = qw.shape[0], norm_args[0].shape[0]
-    packed = pack_weights(place, qw, kw, vw, heads)
-    own = lax.all_to_all(packed, ("y", "c"), 0, 0, tiled=True).reshape(4 * shard, -1)
-    normed = norm_tokens(*norm_args, packed)
-
-    c_tokens = swapped(normed, ("c",), 1)
-    x_tokens = swapped(normed, ("ctx",), 1)
-    (later,) = fence((norm_tokens(*norm_args, normed),), own, c_tokens)
+    mine = lax.axis_index(GROUP)
+    kept, given = pack_weights(mine, qw, kw, vw, heads)
+    near, beside = join_rows(lax.axis_index("c"), kept, swapped(given, ("c",), 1))
+    far = swapped(beside, ("y",), 1)
+    normed, later = norm_tokens(*norm_args, 2, beside)
+    c_tokens, x_tokens = swapped(normed, ("c",), 1), swapped(normed, ("ctx",), 1)
+    (far,) = fence((far,), normed)
+    near_1 = ringed(near)
+    later, gradient = fence((later, gradient), far, near_1)
     y_tokens = swapped(later, ("y",), 1)
-    hop_2, hop_1 = inner_pairs(own), outer_pairs(own)
-    xc_tokens, xy_tokens = swapped(x_tokens, ("c",), 1), swapped(x_tokens, ("y",), 1)
-
-    hop_4, hop_3 = inner_pairs(hop_1), outer_pairs(hop_2)
+    hop_1 = jnp.concatenate([near_1, ringed(far)], 0)
+
+    hop_2 = ringed(hop_1)
+    half = rows // 2
+    far_low, far_high = swapped(x_tokens[:half], ("y",), 1), swapped(y_tokens[half:], ("ctx",), 1)
+    xc_tokens = swapped(x_tokens, ("c",), 1)
     (gradient,) = fence((gradient,), hop_1, xc_tokens)
     gradient = lax.all_to_all(gradient, GROUP, 0, 0, tiled=True)
-    yc_tokens = swapped(y_tokens, ("c",), 1)
-
-    hop_5 = outer_pairs(hop_4)
-    (xy_tokens,) = fence((xy_tokens,), hop_3, hop_4, yc_tokens)
-    xyc_tokens = swapped(xy_tokens, ("c",), 1)
+
+    hop_3 = ringed(hop_2)
+    (y_tokens,) = fence((y_tokens,), hop_2)
+    yc_tokens, farc_low, farc_high = (swapped(value, ("c",), 1) for value in (y_tokens, far_low, far_high))
 
     def weight_columns(back):
-        return lambda p: (p[1] ^ back) * 4 * shard
-
-    def token_rows(step):
-        return lambda p: (step & 3) * 2 * rows + ((p[0] >> 2) ^ (step >> 2)) * rows
+        def columns(p):
+            at = (p[1] ^ (p[1] >> 1)) - back + 4 & 3
+            return (at ^ (at >> 1)) * 4 * shard
+
+        return columns
+
+    def token_rows(step, skip=0):
+        return lambda p: (step & 3) * 2 * rows + ((p[0] >> 2) ^ (step >> 2)) * rows + skip
 
     def source(step):
         return lambda p: p[0] ^ step
 
-    tokens = (normed, c_tokens, y_tokens, yc_tokens, x_tokens, xc_tokens, xy_tokens, xyc_tokens)
+    size = 2 * shard
+
+    def ordered(first, second):
+        return [
+            (first, slice(0, size), lambda p: (p[0] & 2) * shard),
+            (second, slice(-size, None), lambda p: (2 - (p[0] & 2)) * shard),
+        ]
+
+    pieces = [(0, 0, normed), (1, 0, c_tokens), (2, 0, y_tokens), (3, 0, yc_tokens), (4, 0, x_tokens)]
+    pieces += [(5, 0, xc_tokens), (6, 0, far_low), (6, half, far_high), (7, 0, farc_low), (7, half, farc_high)]
     return {
         "w": [
-            (weight_columns(0), None, [own]),
-            (weight_columns(1), None, [hop_1]),
-            (weight_columns(2), is_inner, [hop_4, hop_3]),
+            (weight_columns(0), ordered(near, far)),
+            (weight_columns(1), ordered(hop_1, hop_1)),
+            (weight_columns(2), ordered(hop_2, hop_2)),
         ],
-        "last": (weight_columns(3), is_inner, [hop_2, hop_5]),
-        "x": [((token_rows(step), step & 3, None), value) for step, value in enumerate(tokens)],
+        "last": (weight_columns(3), ordered(hop_3, hop_3)),
+        "x": [((token_rows(step, skip), step & 3, None), value) for step, skip, value in pieces],
         "g": [((token_rows(step), step & 3, source(step)), gradient) for step in range(8)],
     }
 
@@ -492,12 +498,12 @@
         columns = lax.dynamic_slice_in_dim(columns, lax.axis_index("ctx") * per, per, 0)
         columns = lax.all_to_all(columns, ("y", "c"), 0, 0, tiled=True).reshape(per * shard, -1)
         weights = lax.all_gather(columns, "z", axis=0, tiled=True)
-        normed = lax.all_gather(norm_tokens(*norm_args), ("y", "c", "ctx"), axis=0, tiled=True)
+        normed = lax.all_gather(norm_tokens(*norm_args, 1)[0], ("y", "c", "ctx"), axis=0, tiled=True)
         gradient = lax.all_to_all(gradient, GROUP, 0, 0, tiled=True)
         gradient = gradient.reshape(sizes[0], per, rows, group)
         gradient = jnp.moveaxis(gradient, 0, 1).reshape(parts * rows, group)
         gathered = {
-            "w": [(lambda p: 0, None, [weights])],
+            "w": [(lambda p: 0, [(weights, slice(None), lambda p: 0)])],
             "last": None,
             "x": [((lambda p: 0, 0, None), normed)],
             "g": [((lambda p: 0, 0, None), gradient)],
@@ -510,17 +516,22 @@
         "window": 2 * rows,
         "tokens": parts * rows,
         "parts": parts,
+        "cores": 1,
     }
-    ga, gb = attend(place, query_up_weight, value_up_weight, gathered, plan)
+    *ga, gb = attend(place, query_up_weight, value_up_weight, gathered, plan)
 
     coefficient = ADAPTER_NAME / math.sqrt(parts * shards * rows)
-    mixed = sum_pieces(lax.all_to_all(ga, GROUP, 0, 0, tiled=True), gb)
+    pieces = lax.all_to_all(ga[0], GROUP, 0, 0, tiled=True)
+    mixed = jnp.concatenate([jnp.sum(pieces.astype(jnp.float32), 0), gb], 0).astype(jnp.bfloat16)
     if shards & (shards - 1) == 0 and shards <= 4:
         mixed = [mixed] + [swapped(mixed, ("z",), step) for step in range(1, shards)]
     else:
         mixed = [lax.psum(mixed.astype(jnp.float32), "z")]
-    scaled = scale_sum(mixed, coefficient)
-    scaled = [scaled] + [swapped(scaled, GROUP, step) for step in range(1, parts)]
+    scaled = (sum(piece.astype(jnp.float32) for piece in mixed) * coefficient).astype(jnp.bfloat16)
+    chips = ("ctx", "y")
+    scaled = [scaled] + [swapped(scaled, chips, step) for step in range(1, sizes[0] * sizes[1])]
+    if sizes[2] == 2:
+        scaled = [piece for value in scaled for piece in (value, swapped(value, ("c",), 1))]
     shapes = ((rank, feats), (rank, heads_kv * group), (rank, feats), (rank, heads_kv * HEAD_SIZE))
     aq, bq, av, bv = spread(place, scaled, rank, group, shapes)
     return aq.T, bq, av.T, bv

time: 134 us -> 113 us (0.84)
  blocking collectives: 9.68 us -> 0 us
  starting transfers between devices: 33.4 us -> 27.4 us
  Pallas kernels: 28 us -> 22.7 us
  waiting for transfers between devices: 50.9 us -> 48.5 us
  local copies, waits for them, and re-layouts: 9.35 us -> 11.1 us
    all_to_all x1 -> x0, blocking collectives: 9.68 us -> none  [on_device(): mixed = sum_pieces(lax.all_to_all(ga, GROUP, 0, 0, tiled=True), gb)]
    ppermute x5 -> x4, waiting for transfers between devices: 8.93 us -> 15.3 us  [ringed(): return lax.ppermute(value, 'z', [(0, 1), (1, 3), (3, 2), (2, 0)])]
    ppermute x5 -> x4, starting transfers between devices: 10.9 us -> 5.09 us  [ringed(): return lax.ppermute(value, 'z', [(0, 1), (1, 3), (3, 2), (2, 0)])]
    ppermute x17 -> x21, waiting for transfers between devices: 33.9 us -> 28.3 us  [swapped(): return lax.ppermute(value, axes, [(i, i ^ distance) for i in range(count)])]
    pallas_call x5 -> x1, Pallas kernels: 7.17 us -> 1.78 us  [norm_tokens(): pl.pallas_call(functools.partial(norm_kernel, copies), out_shape=[jax.Sha...]
    all_to_all x1, waiting for transfers between devices: 8.08 us -> 4.84 us  [on_device(): pieces = lax.all_to_all(ga[0], GROUP, 0, 0, tiled=True)]
    unnamed x59 -> x54, local copies, waits for them, and re-layouts: 8.36 us -> 6.26 us
    dynamic_slice x0 -> x2, local copies, waits for them, and re-layouts: none -> 2.1 us  [the longest x1 1.08 us: columns(): parts = [lax.dynamic_slice_in_dim(qw, owner * wide, wide, 1)]]
  transfers between devices with their start and end apart: 24 -> 27, of which waited for: 11 -> 17; matrix products, arithmetic and copies ran while one was open for 2% -> 5% of each run, Pallas kernels for 7% -> 9%
where the time goes in v4:
time: 113 us; the launch traced here: 112 us
  waiting for transfers between devices  48.5 us (43%)
  starting transfers between devices  27.4 us (24%)
  Pallas kernels  22.7 us (20%)
  local copies, waits for them, and re-layouts  11.1 us (10%)
  other arithmetic  1.69 us (1%)
    ppermute x21, waiting for transfers between devices, swapped(): return lax.ppermute(value, axes, [(i, i ^ distance) for i in range(count)])  28.3 us
    ppermute x21, starting transfers between devices, swapped(): return lax.ppermute(value, axes, [(i, i ^ distance) for i in range(count)])  15.4 us
    ppermute x4, waiting for transfers between devices, ringed(): return lax.ppermute(value, 'z', [(0, 1), (1, 3), (3, 2), (2, 0)])  15.3 us
    pallas_call x1, Pallas kernels, attend(): pl.pallas_call(functools.partial(attend_kernel, plan), out_shape=[jax.Sha...  10.5 us
    pallas_call x1, Pallas kernels, attend(): pl.pallas_call(functools.partial(project_kernel, plan), out_shape=jax.Sha...  8.61 us
    unnamed x54, local copies, waits for them, and re-layouts  6.26 us
    ppermute x4, starting transfers between devices, ringed(): return lax.ppermute(value, 'z', [(0, 1), (1, 3), (3, 2), (2, 0)])  5.09 us
    all_to_all x1, waiting for transfers between devices, on_device(): pieces = lax.all_to_all(ga[0], GROUP, 0, 0, tiled=True)  4.84 us
  transfers between devices with their start and end apart: 27, of which 17 were waited for; matrix products, arithmetic and copies ran while one was open for 5% of the time, Pallas kernels for 9%

profile of v4, /device:TPU:0, one launch (start us, length us, event | category | flops | bytes accessed | tf_op | source)
XLA Modules:
  0.0 112.4 jit_solution(11833474146233581901)
XLA Ops:
  0.7 1.1 constant_dynamic-slice_fusion.11
  1.8 1.0 constant_dynamic-slice_fusion.9
  3.5 1.2 %collective-permute-done = bf16[2,192,512]{2,1,0:T(8,128)(2,1)S(1)} collective-permute-done((bf16[2,192,512]{2,1,0:T(8,128)(2,1)S(1)}, bf16[2,192,512]{2,1,0:T(8,128)(2,1)S(1)}, u32[]{:S(2)}, u32[]{:S(2)}) %collective-permute-start) | collective-permute-done | bytes 393248 | tf_op jit(solution)/shard_map/ppermute | solution.py:38
  4.9 3.0 %collective-permute-start.2 = (bf16[384,512]{1,0:T(8,128)(2,1)S(1)}, bf16[384,512]{1,0:T(8,128)(2,1)S(1)}, u32[]{:S(2)}, u32[]{:S(2)}) collective-permute-start(bf16[384,512]{1,0:T(8,128)(2,1)S(1)} %pad_maximum_fusion.2.rest_0_), channel_id=1, source_target_pairs={{0,2},{2,0},{1,3},{3,1},{4,6},{6,4},{5,7},{7,5},{8,10},{10,8},{9,1... | collective-permute-start | bytes 1179656 | tf_op jit(solution)/shard_map/ppermute | solution.py:38
  7.9 1.8 %norm_tokens.1 = (bf16[128,3200]{1,0:T(8,128)(2,1)}, bf16[128,3200]{1,0:T(8,128)(2,1)S(1)}) custom-call(bf16[128,3072]{1,0:T(8,128)(2,1)S(1)} %bitcast.25, s32[1,128]{1,0:T(1,128)S(1)} %copy-done.5, bf16[3072]{0:T(1024)(128)(2,1)S(1)} %copy-done.4, bf16[16,3072]{1,0:T(8,128)(2,1)S(1)} %bitcast.26, bf16[16,3072]{1,0:T(8,128)(2,1)S(1)} %bitcast.27, ...), custom_call_target="tpu_custom_call" | custom-call | tf_op jit(solution)/shard_map/norm_tokens/pallas_call | solution.py:93
  10.6 1.5 %collective-permute-start.8 = (bf16[128,3200]{1,0:T(8,128)(2,1)}, bf16[128,3200]{1,0:T(8,128)(2,1)S(1)}, u32[]{:S(2)}, u32[]{:S(2)}) collective-permute-start(bf16[128,3200]{1,0:T(8,128)(2,1)} %get-tuple-element.14.refs_1_.refs_3_.refs_4_), channel_id=1, source_target_pairs={{0,16},{16,0},{1,17},{17,1},{2,18},{18,2},{3,19},{19,3},{4,20},{20... | collective-permute-start | bytes 2457608 | tf_op jit(solution)/shard_map/ppermute | solution.py:38
  12.1 1.6 %collective-permute-start.3 = (bf16[384,512]{1,0:T(8,128)(2,1)S(1)}, bf16[384,512]{1,0:T(8,128)(2,1)S(1)}, u32[]{:S(2)}, u32[]{:S(2)}) collective-permute-start(bf16[384,512]{1,0:T(8,128)(2,1)S(1)} %pad_maximum_fusion.3.refs_13_), channel_id=1, source_target_pairs={{0,4},{4,12},{12,8},{8,0},{1,5},{5,13},{13,9},{9,1},{2,6},{6,14},{... | collective-permute-start | bytes 1179656 | tf_op jit(solution)/shard_map/ppermute | solution.py:393
  13.8 3.5 %collective-permute-done.2.refs_0_ = bf16[384,512]{1,0:T(8,128)(2,1)S(1)} collective-permute-done((bf16[384,512]{1,0:T(8,128)(2,1)S(1)}, bf16[384,512]{1,0:T(8,128)(2,1)S(1)}, u32[]{:S(2)}, u32[]{:S(2)}) %collective-permute-start.2) | collective-permute-done | bytes 393248 | tf_op jit(solution)/shard_map/ppermute | solution.py:38
  18.1 1.8 %collective-permute-start.5 = (bf16[384,512]{1,0:T(8,128)(2,1)}, bf16[384,512]{1,0:T(8,128)(2,1)S(1)}, u32[]{:S(2)}, u32[]{:S(2)}) collective-permute-start(bf16[384,512]{1,0:T(8,128)(2,1)} %fence.4.refs_2_.refs_14_), channel_id=1, source_target_pairs={{0,4},{4,12},{12,8},{8,0},{1,5},{5,13},{13,9},{9,1},{2,6},{6,14},{... | collective-permute-start | bytes 1179656 | tf_op jit(solution)/shard_map/ppermute | solution.py:393
  20.1 1.0 copy.21
  21.2 3.9 %collective-permute-done.3.refs_3_ = bf16[384,512]{1,0:T(8,128)(2,1)S(1)} collective-permute-done((bf16[384,512]{1,0:T(8,128)(2,1)S(1)}, bf16[384,512]{1,0:T(8,128)(2,1)S(1)}, u32[]{:S(2)}, u32[]{:S(2)}) %collective-permute-start.3) | collective-permute-done | bytes 393248 | tf_op jit(solution)/shard_map/ppermute | solution.py:393
  26.3 1.0 constant_dynamic-update-slice_fusion.1
  27.3 4.8 %collective-permute-done.5 = bf16[384,512]{1,0:T(8,128)(2,1)S(1)} collective-permute-done((bf16[384,512]{1,0:T(8,128)(2,1)}, bf16[384,512]{1,0:T(8,128)(2,1)S(1)}, u32[]{:S(2)}, u32[]{:S(2)}) %collective-permute-start.5) | collective-permute-done | bytes 393248 | tf_op jit(solution)/shard_map/ppermute | solution.py:393
  32.2 0.9 collective-permute-start.6
  34.9 12.4 %collective-permute-done.4.refs_0_ = bf16[128,3200]{1,0:T(8,128)(2,1)S(1)} collective-permute-done((bf16[128,3200]{1,0:T(8,128)(2,1)}, bf16[128,3200]{1,0:T(8,128)(2,1)S(1)}, u32[]{:S(2)}, u32[]{:S(2)}) %collective-permute-start.4) | collective-permute-done | bytes 819232 | tf_op jit(solution)/shard_map/ppermute | solution.py:38
  48.6 2.7 %collective-permute-done.6.refs_1_.refs_16_ = bf16[768,512]{1,0:T(8,128)(2,1)} collective-permute-done((bf16[768,512]{1,0:T(8,128)(2,1)S(1)}, bf16[768,512]{1,0:T(8,128)(2,1)}, u32[]{:S(2)}, u32[]{:S(2)}) %collective-permute-start.6) | collective-permute-done | bytes 786464 | tf_op jit(solution)/shard_map/ppermute | solution.py:393
  52.3 3.5 %all-to-all-start = ((bf16[8,128,256]{2,1,0:T(8,128)(2,1)}), bf16[8,128,256]{2,1,0:T(8,128)(2,1)S(1)}, u32[]{:S(2)}, u32[]{:S(2)}) async-start(bf16[8,128,256]{2,1,0:T(8,128)(2,1)} %fence.7), calls=%async_computation | async-start | bytes 1048576 | tf_op jit(solution)/shard_map/all_to_all | solution.py:415
  60.1 8.6 %project.1.refs_3_ = f32[1024,512]{1,0:T(8,128)} custom-call(s32[2]{0:T(128)} %pad_add_fusion.refs_0_.place, bf16[16,2048]{1,0:T(8,128)(2,1)} %refs_1_.3, bf16[16,1024]{1,0:T(8,128)(2,1)} %refs_2_.3, bf16[128,3200]{1,0:T(8,128)(2,1)} %get-tuple-element.14.refs_1_.refs_3_.refs_4_, bf16[128,3200]{1,0:T(8,128)(2,1)} %collective-permute-done.1.refs_4_.refs_5_, ...), custom_call_target="tpu_custom_call" | custom-call | tf_op jit(solution)/shard_map/project/pallas_call | solution.py:277
  68.8 3.8 %collective-permute-done.14.refs_22_ = bf16[768,512]{1,0:T(8,128)(2,1)} collective-permute-done((bf16[768,512]{1,0:T(8,128)(2,1)}, bf16[768,512]{1,0:T(8,128)(2,1)}, u32[]{:S(2)}, u32[]{:S(2)}) %collective-permute-start.14) | collective-permute-done | bytes 786464 | tf_op jit(solution)/shard_map/ppermute | solution.py:393
  72.5 10.5 %attend.1 = (bf16[8,32,384]{2,1,0:T(8,128)(2,1)}, f32[16,384]{1,0:T(8,128)}) custom-call(s32[2]{0:T(128)} %pad_add_fusion.refs_0_.place, bf16[16,2048]{1,0:T(8,128)(2,1)} %refs_1_.3, bf16[16,1024]{1,0:T(8,128)(2,1)} %refs_2_.3, f32[1024,512]{1,0:T(8,128)} %project.1.refs_3_, bf16[128,3200]{1,0:T(8,128)(2,1)} %get-tuple-element.14.refs_1_.refs_3_.refs_4_, ...), custom_call_target="tpu_custom_call" | custom-call | tf_op jit(solution)/shard_map/attend/pallas_call | solution.py:295
  83.1 3.4 %all-to-all-start.1 = ((bf16[8,32,384]{2,1,0:T(8,128)(2,1)}), bf16[8,32,384]{2,1,0:T(8,128)(2,1)S(1)}, u32[]{:S(2)}, u32[]{:S(2)}) async-start(bf16[8,32,384]{2,1,0:T(8,128)(2,1)} %get-tuple-element.18), calls=%async_computation.1 | async-start | bytes 393216 | tf_op jit(solution)/shard_map/all_to_all | solution.py:524
  87.2 4.8 %all-to-all-done.1 = bf16[8,32,384]{2,1,0:T(8,128)(2,1)S(1)} async-done(((bf16[8,32,384]{2,1,0:T(8,128)(2,1)}), bf16[8,32,384]{2,1,0:T(8,128)(2,1)S(1)}, u32[]{:S(2)}, u32[]{:S(2)}) %all-to-all-start.1) | async-done | bytes 196640 | tf_op jit(solution)/shard_map/all_to_all | solution.py:524
  92.1 1.1 collective-permute-start.15
  93.2 3.1 %collective-permute-start.16 = (bf16[48,384]{1,0:T(8,128)(2,1)S(1)}, bf16[48,384]{1,0:T(8,128)(2,1)S(1)}, u32[]{:S(2)}, u32[]{:S(2)}) collective-permute-start(bf16[48,384]{1,0:T(8,128)(2,1)S(1)} %pad_maximum_fusion.4), channel_id=1, source_target_pairs={{0,8},{4,12},{8,0},{12,4},{1,9},{5,13},{9,1},{13,5},{2,10},{6,14},... | collective-permute-start | bytes 110600 | tf_op jit(solution)/shard_map/ppermute | solution.py:38
  96.6 2.4 %collective-permute-done.16 = bf16[48,384]{1,0:T(8,128)(2,1)S(1)} collective-permute-done((bf16[48,384]{1,0:T(8,128)(2,1)S(1)}, bf16[48,384]{1,0:T(8,128)(2,1)S(1)}, u32[]{:S(2)}, u32[]{:S(2)}) %collective-permute-start.16) | collective-permute-done | bytes 36896 | tf_op jit(solution)/shard_map/ppermute | solution.py:38
  98.9 3.2 %collective-permute-done.17 = bf16[48,384]{1,0:T(8,128)(2,1)S(1)} collective-permute-done((bf16[48,384]{1,0:T(8,128)(2,1)S(1)}, bf16[48,384]{1,0:T(8,128)(2,1)S(1)}, u32[]{:S(2)}, u32[]{:S(2)}) %collective-permute-start.17) | collective-permute-done | bytes 36896 | tf_op jit(solution)/shard_map/ppermute | solution.py:38
  102.1 1.2 %collective-permute-start.19 = (bf16[48,384]{1,0:T(8,128)(2,1)S(1)}, bf16[48,384]{1,0:T(8,128)(2,1)S(1)}, u32[]{:S(2)}, u32[]{:S(2)}) collective-permute-start(bf16[48,384]{1,0:T(8,128)(2,1)S(1)} %multiply_convert_fusion.refs_0_), channel_id=1, source_target_pairs={{0,2},{2,0},{16,18},{18,16},{1,3},{3,1},{17,19},{19,17},{4,6},{6,4... | collective-permute-start | bytes 110600 | tf_op jit(solution)/shard_map/ppermute | solution.py:38
  103.9 1.8 %collective-permute-start.23 = (bf16[48,384]{1,0:T(8,128)(2,1)S(1)}, bf16[48,384]{1,0:T(8,128)(2,1)S(1)}, u32[]{:S(2)}, u32[]{:S(2)}) collective-permute-start(bf16[48,384]{1,0:T(8,128)(2,1)S(1)} %multiply_convert_fusion.refs_0_), channel_id=1, source_target_pairs={{0,18},{2,16},{16,2},{18,0},{1,19},{3,17},{17,3},{19,1},{4,22},{6,... | collective-permute-start | bytes 110600 | tf_op jit(solution)/shard_map/ppermute | solution.py:38
  106.2 1.1 collective-permute-done.21.refs_4_
  107.3 1.4 %collective-permute-done.23.refs_6_ = bf16[48,384]{1,0:T(8,128)(2,1)S(1)} collective-permute-done((bf16[48,384]{1,0:T(8,128)(2,1)S(1)}, bf16[48,384]{1,0:T(8,128)(2,1)S(1)}, u32[]{:S(2)}, u32[]{:S(2)}) %collective-permute-start.23) | collective-permute-done | bytes 36896 | tf_op jit(solution)/shard_map/ppermute | solution.py:38
  108.8 1.2 %collective-permute-done.24.refs_7_ = bf16[48,384]{1,0:T(8,128)(2,1)S(1)} collective-permute-done((bf16[48,384]{1,0:T(8,128)(2,1)S(1)}, bf16[48,384]{1,0:T(8,128)(2,1)S(1)}, u32[]{:S(2)}, u32[]{:S(2)}) %collective-permute-start.24) | collective-permute-done | bytes 36896 | tf_op jit(solution)/shard_map/ppermute | solution.py:38
  110.6 1.7 %spread.1 = (f32[16,3072]{1,0:T(8,128)}, f32[16,2048]{1,0:T(8,128)}, f32[16,3072]{1,0:T(8,128)}, f32[16,1024]{1,0:T(8,128)}) custom-call(s32[2]{0:T(128)} %pad_add_fusion.refs_0_.place, bf16[48,384]{1,0:T(8,128)(2,1)} %copy-done.18, bf16[48,384]{1,0:T(8,128)(2,1)} %copy-done.22, bf16[48,384]{1,0:T(8,128)(2,1)} %copy-done.19, bf16[48,384]{1,0:T(8,128)(2,1)} %copy-done.23, ...), custom_call_target="tpu_custom_call" | custom-call | tf_op jit(solution)/shard_map/spread/pallas_call | solution.py:383
  (105 shorter events, 15.1 us)
Async XLA Ops:
  2.9 1.9 %collective-permute-start = (bf16[2,192,512]{2,1,0:T(8,128)(2,1)S(1)}, bf16[2,192,512]{2,1,0:T(8,128)(2,1)S(1)}, u32[]{:S(2)}, u32[]{:S(2)}) collective-permute-start(bf16[2,192,512]{2,1,0:T(8,128)(2,1)S(1)} %pad_maximum_fusion.1), channel_id=1, source_target_pairs={{0,1},{1,0},{2,3},{3,2},{4,5},{5,4},{6,7},{7,6},{8,9},{9,8},{10,11... | collective-permute-start | bytes 1179656 | tf_op jit(solution)/shard_map/ppermute | solution.py:38
  4.9 15.0 %copy-start.17 = (bf16[1,128,2048]{2,1,0:T(8,128)(2,1)S(1)}, bf16[1,128,2048]{2,1,0:T(8,128)(2,1)}, u32[]{:S(2)}) copy-start(bf16[1,128,2048]{2,1,0:T(8,128)(2,1)} %param.21) | copy-start | bytes 1572868
  4.9 12.4 %collective-permute-start.2 = (bf16[384,512]{1,0:T(8,128)(2,1)S(1)}, bf16[384,512]{1,0:T(8,128)(2,1)S(1)}, u32[]{:S(2)}, u32[]{:S(2)}) collective-permute-start(bf16[384,512]{1,0:T(8,128)(2,1)S(1)} %pad_maximum_fusion.2.rest_0_), channel_id=1, source_target_pairs={{0,2},{2,0},{1,3},{3,1},{4,6},{6,4},{5,7},{7,5},{8,10},{10,8},{9,1... | collective-permute-start | bytes 1179656 | tf_op jit(solution)/shard_map/ppermute | solution.py:38
  10.6 22.5 %collective-permute-start.8 = (bf16[128,3200]{1,0:T(8,128)(2,1)}, bf16[128,3200]{1,0:T(8,128)(2,1)S(1)}, u32[]{:S(2)}, u32[]{:S(2)}) collective-permute-start(bf16[128,3200]{1,0:T(8,128)(2,1)} %get-tuple-element.14.refs_1_.refs_3_.refs_4_), channel_id=1, source_target_pairs={{0,16},{16,0},{1,17},{17,1},{2,18},{18,2},{3,19},{19,3},{4,20},{20... | collective-permute-start | bytes 2457608 | tf_op jit(solution)/shard_map/ppermute | solution.py:38
  12.1 13.7 %copy-start.15 = (bf16[384,512]{1,0:T(8,128)(2,1)}, bf16[384,512]{1,0:T(8,128)(2,1)S(1)}, u32[]{:S(2)}) copy-start(bf16[384,512]{1,0:T(8,128)(2,1)S(1)} %pad_maximum_fusion.3.refs_13_) | copy-start | bytes 1179652
  12.1 13.0 %collective-permute-start.3 = (bf16[384,512]{1,0:T(8,128)(2,1)S(1)}, bf16[384,512]{1,0:T(8,128)(2,1)S(1)}, u32[]{:S(2)}, u32[]{:S(2)}) collective-permute-start(bf16[384,512]{1,0:T(8,128)(2,1)S(1)} %pad_maximum_fusion.3.refs_13_), channel_id=1, source_target_pairs={{0,4},{4,12},{12,8},{8,0},{1,5},{5,13},{13,9},{9,1},{2,6},{6,14},{... | collective-permute-start | bytes 1179656 | tf_op jit(solution)/shard_map/ppermute | solution.py:393
  18.1 14.0 %collective-permute-start.5 = (bf16[384,512]{1,0:T(8,128)(2,1)}, bf16[384,512]{1,0:T(8,128)(2,1)S(1)}, u32[]{:S(2)}, u32[]{:S(2)}) collective-permute-start(bf16[384,512]{1,0:T(8,128)(2,1)} %fence.4.refs_2_.refs_14_), channel_id=1, source_target_pairs={{0,4},{4,12},{12,8},{8,0},{1,5},{5,13},{13,9},{9,1},{2,6},{6,14},{... | collective-permute-start | bytes 1179656 | tf_op jit(solution)/shard_map/ppermute | solution.py:393
  25.9 21.4 %collective-permute-start.4 = (bf16[128,3200]{1,0:T(8,128)(2,1)}, bf16[128,3200]{1,0:T(8,128)(2,1)S(1)}, u32[]{:S(2)}, u32[]{:S(2)}) collective-permute-start(bf16[128,3200]{1,0:T(8,128)(2,1)} %get-tuple-element.16), channel_id=1, source_target_pairs={{0,2},{2,0},{1,3},{3,1},{4,6},{6,4},{5,7},{7,5},{8,10},{10,8},{9,1... | collective-permute-start | bytes 2457608 | tf_op jit(solution)/shard_map/ppermute | solution.py:38
  32.1 19.9 %copy-start.10 = (bf16[768,512]{1,0:T(8,128)(2,1)}, bf16[768,512]{1,0:T(8,128)(2,1)S(1)}, u32[]{:S(2)}) copy-start(bf16[768,512]{1,0:T(8,128)(2,1)S(1)} %constant_dynamic-update-slice_fusion.refs_15_.refs_1_) | copy-start | bytes 2359300
  32.2 19.2 %collective-permute-start.6 = (bf16[768,512]{1,0:T(8,128)(2,1)S(1)}, bf16[768,512]{1,0:T(8,128)(2,1)}, u32[]{:S(2)}, u32[]{:S(2)}) collective-permute-start(bf16[768,512]{1,0:T(8,128)(2,1)S(1)} %constant_dynamic-update-slice_fusion.refs_15_.refs_1_), channel_id=1, source_target_pairs={{0,4},{4,12},{12,8},{8,0},{1,5},{5,13},{13,9},{9,1},{2,6},{6,14},{... | collective-permute-start | bytes 2359304 | tf_op jit(solution)/shard_map/ppermute | solution.py:393
  33.1 19.2 %copy-start.9 = (bf16[128,3200]{1,0:T(8,128)(2,1)}, bf16[128,3200]{1,0:T(8,128)(2,1)S(1)}, u32[]{:S(2)}) copy-start(bf16[128,3200]{1,0:T(8,128)(2,1)S(1)} %collective-permute-done.8.refs_7_.refs_8_) | copy-start | bytes 2457604
  33.1 18.2 %collective-permute-start.9 = (bf16[128,3200]{1,0:T(8,128)(2,1)S(1)}, bf16[128,3200]{1,0:T(8,128)(2,1)S(1)}, u32[]{:S(2)}, u32[]{:S(2)}) collective-permute-start(bf16[128,3200]{1,0:T(8,128)(2,1)S(1)} %collective-permute-done.8.refs_7_.refs_8_), channel_id=1, source_target_pairs={{0,1},{1,0},{2,3},{3,2},{4,5},{5,4},{6,7},{7,6},{8,9},{9,8},{10,11... | collective-permute-start | bytes 2457608 | tf_op jit(solution)/shard_map/ppermute | solution.py:38
  33.1 23.9 %collective-permute-start.1 = (bf16[128,3200]{1,0:T(8,128)(2,1)}, bf16[128,3200]{1,0:T(8,128)(2,1)}, u32[]{:S(2)}, u32[]{:S(2)}) collective-permute-start(bf16[128,3200]{1,0:T(8,128)(2,1)} %get-tuple-element.14.refs_1_.refs_3_.refs_4_), channel_id=1, source_target_pairs={{0,1},{1,0},{2,3},{3,2},{4,5},{5,4},{6,7},{7,6},{8,9},{9,8},{10,11... | collective-permute-start | bytes 2457608 | tf_op jit(solution)/shard_map/ppermute | solution.py:38
  34.4 21.4 %collective-permute-start.10 = (bf16[64,3200]{1,0:T(8,128)(2,1)}, bf16[64,3200]{1,0:T(8,128)(2,1)}, u32[]{:S(2)}, u32[]{:S(2)}) collective-permute-start(bf16[64,3200]{1,0:T(8,128)(2,1)} %slice.28), channel_id=1, source_target_pairs={{0,2},{2,0},{1,3},{3,1},{4,6},{6,4},{5,7},{7,5},{8,10},{10,8},{9,1... | collective-permute-start | bytes 1228808 | tf_op jit(solution)/shard_map/ppermute | solution.py:38
  48.1 8.3 %collective-permute-start.11 = (bf16[64,3200]{1,0:T(8,128)(2,1)}, bf16[64,3200]{1,0:T(8,128)(2,1)}, u32[]{:S(2)}, u32[]{:S(2)}) collective-permute-start(bf16[64,3200]{1,0:T(8,128)(2,1)} %slice.29), channel_id=1, source_target_pairs={{0,16},{16,0},{1,17},{17,1},{2,18},{18,2},{3,19},{19,3},{4,20},{20... | collective-permute-start | bytes 1228808 | tf_op jit(solution)/shard_map/ppermute | solution.py:38
  51.3 7.1 %collective-permute-start.7 = (bf16[128,3200]{1,0:T(8,128)(2,1)}, bf16[128,3200]{1,0:T(8,128)(2,1)S(1)}, u32[]{:S(2)}, u32[]{:S(2)}) collective-permute-start(bf16[128,3200]{1,0:T(8,128)(2,1)} %fence.6.refs_5_.refs_6_), channel_id=1, source_target_pairs={{0,1},{1,0},{2,3},{3,2},{4,5},{5,4},{6,7},{7,6},{8,9},{9,8},{10,11... | collective-permute-start | bytes 2457608 | tf_op jit(solution)/shard_map/ppermute | solution.py:38
  51.4 21.2 %collective-permute-start.14 = (bf16[768,512]{1,0:T(8,128)(2,1)}, bf16[768,512]{1,0:T(8,128)(2,1)}, u32[]{:S(2)}, u32[]{:S(2)}) collective-permute-start(bf16[768,512]{1,0:T(8,128)(2,1)} %collective-permute-done.6.refs_1_.refs_16_), channel_id=1, source_target_pairs={{0,4},{4,12},{12,8},{8,0},{1,5},{5,13},{13,9},{9,1},{2,6},{6,14},{... | collective-permute-start | bytes 2359304 | tf_op jit(solution)/shard_map/ppermute | solution.py:393
  52.3 16.5 %all-to-all-start = ((bf16[8,128,256]{2,1,0:T(8,128)(2,1)}), bf16[8,128,256]{2,1,0:T(8,128)(2,1)S(1)}, u32[]{:S(2)}, u32[]{:S(2)}) async-start(bf16[8,128,256]{2,1,0:T(8,128)(2,1)} %fence.7), calls=%async_computation | async-start | bytes 1048576 | tf_op jit(solution)/shard_map/all_to_all | solution.py:415
  55.8 2.1 %collective-permute-start.12 = (bf16[64,3200]{1,0:T(8,128)(2,1)}, bf16[64,3200]{1,0:T(8,128)(2,1)S(1)}, u32[]{:S(2)}, u32[]{:S(2)}) collective-permute-start(bf16[64,3200]{1,0:T(8,128)(2,1)} %collective-permute-done.10.refs_9_.refs_10_), channel_id=1, source_target_pairs={{0,1},{1,0},{2,3},{3,2},{4,5},{5,4},{6,7},{7,6},{8,9},{9,8},{10,11... | collective-permute-start | bytes 1228808 | tf_op jit(solution)/shard_map/ppermute | solution.py:38
  56.4 2.1 %collective-permute-start.13 = (bf16[64,3200]{1,0:T(8,128)(2,1)}, bf16[64,3200]{1,0:T(8,128)(2,1)S(1)}, u32[]{:S(2)}, u32[]{:S(2)}) collective-permute-start(bf16[64,3200]{1,0:T(8,128)(2,1)} %collective-permute-done.11.refs_10_.refs_11_), channel_id=1, source_target_pairs={{0,1},{1,0},{2,3},{3,2},{4,5},{5,4},{6,7},{7,6},{8,9},{9,8},{10,11... | collective-permute-start | bytes 1228808 | tf_op jit(solution)/shard_map/ppermute | solution.py:38
  83.1 9.0 %all-to-all-start.1 = ((bf16[8,32,384]{2,1,0:T(8,128)(2,1)}), bf16[8,32,384]{2,1,0:T(8,128)(2,1)S(1)}, u32[]{:S(2)}, u32[]{:S(2)}) async-start(bf16[8,32,384]{2,1,0:T(8,128)(2,1)} %get-tuple-element.18), calls=%async_computation.1 | async-start | bytes 393216 | tf_op jit(solution)/shard_map/all_to_all | solution.py:524
  92.1 4.5 %collective-permute-start.15 = (bf16[48,384]{1,0:T(8,128)(2,1)S(1)}, bf16[48,384]{1,0:T(8,128)(2,1)S(1)}, u32[]{:S(2)}, u32[]{:S(2)}) collective-permute-start(bf16[48,384]{1,0:T(8,128)(2,1)S(1)} %pad_maximum_fusion.4), channel_id=1, source_target_pairs={{0,4},{4,0},{8,12},{12,8},{1,5},{5,1},{9,13},{13,9},{2,6},{6,2},{1... | collective-permute-start | bytes 110600 | tf_op jit(solution)/shard_map/ppermute | solution.py:38
  93.2 5.7 %collective-permute-start.16 = (bf16[48,384]{1,0:T(8,128)(2,1)S(1)}, bf16[48,384]{1,0:T(8,128)(2,1)S(1)}, u32[]{:S(2)}, u32[]{:S(2)}) collective-permute-start(bf16[48,384]{1,0:T(8,128)(2,1)S(1)} %pad_maximum_fusion.4), channel_id=1, source_target_pairs={{0,8},{4,12},{8,0},{12,4},{1,9},{5,13},{9,1},{13,5},{2,10},{6,14},... | collective-permute-start | bytes 110600 | tf_op jit(solution)/shard_map/ppermute | solution.py:38
  96.3 5.8 %collective-permute-start.17 = (bf16[48,384]{1,0:T(8,128)(2,1)S(1)}, bf16[48,384]{1,0:T(8,128)(2,1)S(1)}, u32[]{:S(2)}, u32[]{:S(2)}) collective-permute-start(bf16[48,384]{1,0:T(8,128)(2,1)S(1)} %pad_maximum_fusion.4), channel_id=1, source_target_pairs={{0,12},{4,8},{8,4},{12,0},{1,13},{5,9},{9,5},{13,1},{2,14},{6,10},... | collective-permute-start | bytes 110600 | tf_op jit(solution)/shard_map/ppermute | solution.py:38
  102.1 7.8 %copy-start.18 = (bf16[48,384]{1,0:T(8,128)(2,1)}, bf16[48,384]{1,0:T(8,128)(2,1)S(1)}, u32[]{:S(2)}) copy-start(bf16[48,384]{1,0:T(8,128)(2,1)S(1)} %multiply_convert_fusion.refs_0_) | copy-start | bytes 110596
  102.1 4.0 %collective-permute-start.19 = (bf16[48,384]{1,0:T(8,128)(2,1)S(1)}, bf16[48,384]{1,0:T(8,128)(2,1)S(1)}, u32[]{:S(2)}, u32[]{:S(2)}) collective-permute-start(bf16[48,384]{1,0:T(8,128)(2,1)S(1)} %multiply_convert_fusion.refs_0_), channel_id=1, source_target_pairs={{0,2},{2,0},{16,18},{18,16},{1,3},{3,1},{17,19},{19,17},{4,6},{6,4... | collective-permute-start | bytes 110600 | tf_op jit(solution)/shard_map/ppermute | solution.py:38
  103.3 4.0 %collective-permute-start.21 = (bf16[48,384]{1,0:T(8,128)(2,1)S(1)}, bf16[48,384]{1,0:T(8,128)(2,1)S(1)}, u32[]{:S(2)}, u32[]{:S(2)}) collective-permute-start(bf16[48,384]{1,0:T(8,128)(2,1)S(1)} %multiply_convert_fusion.refs_0_), channel_id=1, source_target_pairs={{0,16},{2,18},{16,0},{18,2},{1,17},{3,19},{17,1},{19,3},{4,20},{6,... | collective-permute-start | bytes 110600 | tf_op jit(solution)/shard_map/ppermute | solution.py:38
  103.9 4.9 %collective-permute-start.23 = (bf16[48,384]{1,0:T(8,128)(2,1)S(1)}, bf16[48,384]{1,0:T(8,128)(2,1)S(1)}, u32[]{:S(2)}, u32[]{:S(2)}) collective-permute-start(bf16[48,384]{1,0:T(8,128)(2,1)S(1)} %multiply_convert_fusion.refs_0_), channel_id=1, source_target_pairs={{0,18},{2,16},{16,2},{18,0},{1,19},{3,17},{17,3},{19,1},{4,22},{6,... | collective-permute-start | bytes 110600 | tf_op jit(solution)/shard_map/ppermute | solution.py:38
  105.7 3.1 %collective-permute-start.18 = (bf16[48,384]{1,0:T(8,128)(2,1)S(1)}, bf16[48,384]{1,0:T(8,128)(2,1)S(1)}, u32[]{:S(2)}, u32[]{:S(2)}) collective-permute-start(bf16[48,384]{1,0:T(8,128)(2,1)S(1)} %multiply_convert_fusion.refs_0_), channel_id=1, source_target_pairs={{0,1},{1,0},{2,3},{3,2},{4,5},{5,4},{6,7},{7,6},{8,9},{9,8},{10,11... | collective-permute-start | bytes 110600 | tf_op jit(solution)/shard_map/ppermute | solution.py:38
  106.1 2.6 %collective-permute-start.20 = (bf16[48,384]{1,0:T(8,128)(2,1)S(1)}, bf16[48,384]{1,0:T(8,128)(2,1)S(1)}, u32[]{:S(2)}, u32[]{:S(2)}) collective-permute-start(bf16[48,384]{1,0:T(8,128)(2,1)S(1)} %collective-permute-done.19.refs_2_), channel_id=1, source_target_pairs={{0,1},{1,0},{2,3},{3,2},{4,5},{5,4},{6,7},{7,6},{8,9},{9,8},{10,11... | collective-permute-start | bytes 110600 | tf_op jit(solution)/shard_map/ppermute | solution.py:38
  107.3 1.5 %collective-permute-start.22 = (bf16[48,384]{1,0:T(8,128)(2,1)S(1)}, bf16[48,384]{1,0:T(8,128)(2,1)S(1)}, u32[]{:S(2)}, u32[]{:S(2)}) collective-permute-start(bf16[48,384]{1,0:T(8,128)(2,1)S(1)} %collective-permute-done.21.refs_4_), channel_id=1, source_target_pairs={{0,1},{1,0},{2,3},{3,2},{4,5},{5,4},{6,7},{7,6},{8,9},{9,8},{10,11... | collective-permute-start | bytes 110600 | tf_op jit(solution)/shard_map/ppermute | solution.py:38
  108.7 1.2 %collective-permute-start.24 = (bf16[48,384]{1,0:T(8,128)(2,1)S(1)}, bf16[48,384]{1,0:T(8,128)(2,1)S(1)}, u32[]{:S(2)}, u32[]{:S(2)}) collective-permute-start(bf16[48,384]{1,0:T(8,128)(2,1)S(1)} %collective-permute-done.23.refs_6_), channel_id=1, source_target_pairs={{0,1},{1,0},{2,3},{3,2},{4,5},{5,4},{6,7},{7,6},{8,9},{9,8},{10,11... | collective-permute-start | bytes 110600 | tf_op jit(solution)/shard_map/ppermute | solution.py:38
  (21 other events, 47.8 us)

commit v5 on v4

--- a/solution.py
+++ b/solution.py
@@ -21,7 +21,7 @@
 ANY = pl.BlockSpec(memory_space=pl.ANY)
 VMEM = pl.BlockSpec(memory_space=pltpu.VMEM)
 SMEM = pl.BlockSpec(memory_space=pltpu.SMEM)
-PARAMS = pltpu.CompilerParams(vmem_limit_bytes=60 * 2**20)
+PARAMS = pltpu.CompilerParams(vmem_limit_bytes=63 * 2**20)
 
 NT = (((1,), (1,)), ((), ()))
 TN = (((0,), (0,)), ((), ()))
@@ -29,6 +29,10 @@
 
 def dot(a, b, dims=(((1,), (0,)), ((), ()))):
     return lax.dot_general(a, b, dims, preferred_element_type=jnp.float32)
+
+
+def add_wide(first, second):
+    return first.astype(jnp.float32) + second.astype(jnp.float32)
 
 
 def swapped(value, axes, distance):
@@ -57,7 +61,7 @@
     pass
 
 
-def fence(values, *earlier):
+def fence(values, *earlier, wait_us=0):
     count = len(values)
     return pl.pallas_call(
         fence_kernel,
@@ -65,6 +69,9 @@
         in_specs=[ANY] * (count + len(earlier)),
         out_specs=[ANY] * count,
         input_output_aliases={i: i for i in range(count)},
+        cost_estimate=pl.CostEstimate(
+            flops=wait_us * 10**9, bytes_accessed=wait_us * 3 * 10**6, transcendentals=0
+        ),
         compiler_params=PARAMS,
         name="fence",
     )(*values, *earlier)
@@ -102,7 +109,7 @@
 
 class Loads:
     def __init__(self, sems):
-        self.sems, self.count, self.waits = sems, 0, []
+        self.sems, self.copies = sems, []
 
     def add(self, place, pieces, target):
         for piece, src in pieces:
@@ -111,13 +118,18 @@
             rows = src.shape[-2]
             if choice is not None and len(src.shape) == 3:
                 src = src.at[choice(place)]
-            copy = pltpu.make_async_copy(src, target.at[pl.ds(begin, rows), :], self.sems.at[self.count])
-            copy.start()
-            self.waits.append((sequence, copy))
-            self.count += 1
+            self.add_copy(sequence, src, target.at[pl.ds(begin, rows), :])
+
+    def add_copy(self, sequence, src, target):
+        self.copies.append((sequence, pltpu.make_async_copy(src, target, self.sems.at[len(self.copies)])))
+
+    def start(self, sequence):
+        for needed, copy in self.copies:
+            if needed == sequence:
+                copy.start()
 
     def wait(self, sequence):
-        for needed, copy in self.waits:
+        for needed, copy in self.copies:
             if needed == sequence:
                 copy.wait()
 
@@ -140,6 +152,7 @@
             src = src.at[slice(*part.indices(rows))]
             loads.add(place, [(piece, src)], w_all)
     loads.add(place, list(zip(plan["x"], x_refs)), x_all)
+    loads.start(0)
 
     mine = place[0]
     uq = up_q[:, pl.ds(pl.multiple_of(mine * group, group), group)]
@@ -151,6 +164,7 @@
     ups = jnp.concatenate([top, low, pad], 0).astype(jnp.bfloat16)
 
     for index in range(x_all.shape[0] // seq):
+        loads.start(index + 1)
         loads.wait(index)
         rows = pl.ds(index * seq, seq)
         total = dot(x_all[rows, feats:], ups)
@@ -164,9 +178,8 @@
     n_x, n_g, last = len(plan["x"]), len(plan["g"]), plan["last"]
     place, up_q, up_v, base = refs[:4]
     x_refs, g_refs = refs[4 : 4 + n_x], refs[4 + n_x : 4 + n_x + n_g]
-    n_out = 7 + plan["cores"]
-    w_refs, rest = refs[4 + n_x + n_g : -n_out], refs[-n_out:]
-    ga_outs, (gb_out, x_all, g_all, w_all, base_all, pulls, sems) = rest[:-7], rest[-7:]
+    w_refs, rest = refs[4 + n_x + n_g : -8], refs[-8:]
+    ga_out, gb_out, x_all, g_all, w_all, base_all, pulls, sems = rest
 
     feats, heads, seq, window, depth = (plan[k] for k in ("feats", "heads", "seq", "window", "depth"))
     rank, parts = up_q.shape[0], plan["parts"]
@@ -177,28 +190,28 @@
     loads = Loads(sems)
     for index in range(sequences):
         rows = pl.ds(index * seq, seq)
-        copy_base = pltpu.make_async_copy(base.at[rows, :], base_all.at[rows, :], sems.at[loads.count])
-        copy_base.start()
-        loads.waits.append((index, copy_base))
-        loads.count += 1
+        loads.add_copy(index, base.at[rows, :], base_all.at[rows, :])
         for pieces, sources, target in ((plan["x"], x_refs, x_all), (plan["g"], g_refs, g_all)):
             chosen = [(piece, src) for piece, src in zip(pieces, sources) if piece[1] == index]
             loads.add(place, chosen, target)
     if last is not None:
         offset, chunks = last
         for part, at in chunks:
-            value = w_refs[0][part, :]
-            w_all[pl.ds(pl.multiple_of(at(place), 16), value.shape[0]), :] = value
+            src = w_refs[0].at[slice(*part.indices(depth))]
+            target = w_all.at[pl.ds(pl.multiple_of(at(place), 16), src.shape[0]), :]
+            loads.add_copy(0, src, target)
+    loads.start(0)
 
     mine = place[0]
     uq = up_q[:, pl.ds(pl.multiple_of(mine * group, group), group)]
     uv = up_v[:, pl.ds(pl.multiple_of(mine * HEAD_SIZE, HEAD_SIZE), HEAD_SIZE)]
     id_row = jnp.where(lax.broadcasted_iota(jnp.int32, (8, LANES), 1) == 2 * rank, 1.0, 0.0).astype(jnp.bfloat16)
-    span = min(seq, window)
+    span = plan["span"]
     blocks = seq // span
     sums = jnp.zeros((LANES, group + 2 * HEAD_SIZE), jnp.float32)
 
     for index in range(sequences):
+        loads.start(index + 1)
         loads.wait(index)
         rows = pl.ds(index * seq, seq)
         qkv = base_all[rows, :]
@@ -212,34 +225,35 @@
         keys = qkv[:, group : group + HEAD_SIZE]
         values = qkv[:, group + HEAD_SIZE :]
         grads = g_all[rows, :]
-        dq_parts = [[] for _ in range(heads)]
-        dv_parts = [None] * blocks
+        dq_parts, dv_parts = [], [None] * blocks
         for block in range(blocks):
             lo, hi = block * span, (block + 1) * span
-            back = max(0, lo - span)
+            back = max(0, lo - window)
             kb, vb = keys[back:hi], values[back:hi]
             shape = (span, hi - back)
             pos_q = lax.broadcasted_iota(jnp.int32, shape, 0) + lo
             pos_k = lax.broadcasted_iota(jnp.int32, shape, 1) + back
             mask = (pos_k <= pos_q) & (pos_k > pos_q - window)
             mask = mask & (ids_query[lo:hi] == ids_key[:, back:hi])
-            for head in range(heads):
-                cols = slice(head * HEAD_SIZE, (head + 1) * HEAD_SIZE)
-                q, g = qkv[lo:hi, cols], grads[lo:hi, cols]
-                t = jnp.tanh(dot(q, kb, NT) * (QSCALE / CAP))
-                expo = jnp.where(mask, jnp.exp(CAP * t), 0.0)
-                weights = expo / jnp.sum(expo, axis=-1, keepdims=True)
-                weights16 = weights.astype(jnp.bfloat16)
-                dweight = dot(g, vb, NT)
-                delta = jnp.sum(weights16.astype(jnp.float32) * dweight, axis=-1, keepdims=True)
-                dscore = (weights * (dweight - delta) * (1.0 - t * t) * QSCALE).astype(jnp.bfloat16)
-                dq_parts[head].append(dot(dscore, kb).astype(jnp.bfloat16))
-                dv = dot(weights16, g, TN)
-                for at in range(back // span, block + 1):
-                    piece = dv[at * span - back : (at + 1) * span - back]
-                    dv_parts[at] = piece if dv_parts[at] is None else dv_parts[at] + piece
-        dq = jnp.concatenate([jnp.concatenate(some, 0) for some in dq_parts], 1)
-        dv = jnp.concatenate(dv_parts, 0)
+            masks = jnp.concatenate([jnp.where(mask, 1.0, 0.0)] * heads, 0)
+            q, g = (
+                jnp.concatenate([x[lo:hi, h * HEAD_SIZE : (h + 1) * HEAD_SIZE] for h in range(heads)], 0)
+                for x in (qkv, grads)
+            )
+            t = jnp.tanh(dot(q, kb, NT) * (QSCALE / CAP))
+            dweight = dot(g, vb, NT)
+            expo = masks * jnp.exp2((CAP * math.log2(math.e)) * t)
+            share = 1.0 / jnp.sum(expo, axis=-1, keepdims=True)
+            weights = expo * share
+            delta = jnp.sum(expo * dweight, axis=-1, keepdims=True) * share
+            dscore = (weights * (dweight - delta) * (1.0 - t * t)).astype(jnp.bfloat16)
+            dq = (dot(dscore, kb) * QSCALE).astype(jnp.bfloat16)
+            dq_parts.append(jnp.concatenate([dq[h * span : (h + 1) * span] for h in range(heads)], 1))
+            dv = dot(weights.astype(jnp.bfloat16), g, TN)
+            for at in range(back // span, block + 1):
+                piece = dv[at * span - back : (at + 1) * span - back]
+                dv_parts[at] = piece if dv_parts[at] is None else dv_parts[at] + piece
+        dq, dv = jnp.concatenate(dq_parts, 0), jnp.concatenate(dv_parts, 0)
         dv_hi = dv.astype(jnp.bfloat16)
         dv_lo = (dv - dv_hi.astype(jnp.float32)).astype(jnp.bfloat16)
         pull_q = dot(uq, dq, NT)
@@ -252,16 +266,15 @@
     gb_out[:, :group] = sums[:rank, :group]
     gb_out[:, group:] = sums[rank : 2 * rank, group : group + HEAD_SIZE] + sums[rank : 2 * rank, group + HEAD_SIZE :]
     part = feats // parts
-    for core, out in enumerate(ga_outs):
-        for index in range(out.shape[0]):
-            piece = dot(pulls[...], x_all[:, index * part : (index + 1) * part])
-            out[index, :rank] = piece[:rank].astype(out.dtype)
-            out[index, rank:] = (piece[rank : 2 * rank] + piece[2 * rank :]).astype(out.dtype)
+    for index in range(parts):
+        piece = dot(pulls[...], x_all[:, index * part : (index + 1) * part])
+        ga_out[index, :rank] = piece[:rank].astype(ga_out.dtype)
+        ga_out[index, rank:] = (piece[rank : 2 * rank] + piece[2 * rank :]).astype(ga_out.dtype)
 
 
 def attend(place, up_q, up_v, gathered, plan):
     feats, heads, tokens, parts, seq = (plan[k] for k in ("feats", "heads", "tokens", "parts", "seq"))
-    rank, cores = up_q.shape[0], plan["cores"]
+    rank = up_q.shape[0]
     wide = (heads + 2) * HEAD_SIZE
     x_plan, x_arrays = zip(*gathered["x"])
     g_plan, g_arrays = zip(*gathered["g"])
@@ -294,76 +307,25 @@
     last = [chunks[0][0]] if chunks else []
     return pl.pallas_call(
         functools.partial(attend_kernel, plan),
-        out_shape=[jax.ShapeDtypeStruct((parts // cores, 2 * rank, feats // parts), jnp.bfloat16)] * cores
-        + [jax.ShapeDtypeStruct((rank, (heads + 1) * HEAD_SIZE), jnp.float32)],
+        out_shape=[
+            jax.ShapeDtypeStruct((parts, 2 * rank, feats // parts), jnp.bfloat16),
+            jax.ShapeDtypeStruct((rank, (heads + 1) * HEAD_SIZE), jnp.float32),
+        ],
         in_specs=[SMEM, VMEM, VMEM]
         + [ANY] * (1 + len(x_arrays) + len(g_arrays))
-        + [VMEM] * len(last),
-        out_specs=[VMEM] * (cores + 1),
+        + [ANY] * len(last),
+        out_specs=[VMEM] * 2,
         scratch_shapes=[
             pltpu.VMEM((tokens, feats + LANES), jnp.bfloat16),
             pltpu.VMEM((tokens, heads * HEAD_SIZE), jnp.bfloat16),
             pltpu.VMEM((depth, wide) if last else (16, LANES), jnp.bfloat16),
             pltpu.VMEM((tokens, wide), jnp.float32),
             pltpu.VMEM((3 * rank, tokens), jnp.bfloat16),
-            pltpu.SemaphoreType.DMA((tokens // seq + len(x_arrays) + len(g_arrays),)),
+            pltpu.SemaphoreType.DMA((len(chunks) + tokens // seq + len(x_arrays) + len(g_arrays),)),
         ],
         compiler_params=PARAMS,
         name="attend",
     )(place, up_q, up_v, base, *x_arrays, *g_arrays, *last)
-
-
-def add_kernel(kept, got, *outs):
-    for index, out in enumerate(outs):
-        out[...] = (kept[index].astype(jnp.float32) + got[index].astype(jnp.float32)).astype(out.dtype)
-
-
-def add_pieces(kept, got):
-    return pl.pallas_call(
-        add_kernel,
-        out_shape=[jax.ShapeDtypeStruct(kept.shape[1:], kept.dtype)] * kept.shape[0],
-        in_specs=[VMEM] * 2,
-        out_specs=[VMEM] * kept.shape[0],
-        name="add_pieces",
-    )(kept, got)
-
-
-def sum_kernel(gb, *refs):
-    gas, out = refs[:-1], refs[-1]
-    total = gas[0][...].astype(jnp.float32)
-    for ref in gas[1:]:
-        total = total + ref[...].astype(jnp.float32)
-    rows = total.shape[0]
-    out[:rows] = total.astype(out.dtype)
-    out[rows:] = gb[...].astype(out.dtype)
-
-
-def sum_pieces(gas, gb):
-    rows, wide = gas[0].shape
-    return pl.pallas_call(
-        sum_kernel,
-        out_shape=jax.ShapeDtypeStruct((rows + gb.shape[0], wide), jnp.bfloat16),
-        in_specs=[VMEM] * (1 + len(gas)),
-        out_specs=VMEM,
-        name="sum_pieces",
-    )(gb, *gas)
-
-
-def scale_kernel(coefficient, *refs):
-    total = refs[0][...].astype(jnp.float32)
-    for ref in refs[1:-1]:
-        total = total + ref[...].astype(jnp.float32)
-    refs[-1][...] = (total * coefficient).astype(refs[-1].dtype)
-
-
-def scale_sum(pieces, coefficient):
-    return pl.pallas_call(
-        functools.partial(scale_kernel, coefficient),
-        out_shape=jax.ShapeDtypeStruct(pieces[0].shape, jnp.bfloat16),
-        in_specs=[VMEM] * len(pieces),
-        out_specs=VMEM,
-        name="scale_sum",
-    )(*pieces)
 
 
 def spread_kernel(rank, group, place, *refs):
@@ -401,8 +363,7 @@
     far = swapped(beside, ("y",), 1)
     normed, later = norm_tokens(*norm_args, 2, beside)
     c_tokens, x_tokens = swapped(normed, ("c",), 1), swapped(normed, ("ctx",), 1)
-    (far,) = fence((far,), normed)
-    near_1 = ringed(near)
+    (near_1,) = fence((ringed(near),), wait_us=6)
     later, gradient = fence((later, gradient), far, near_1)
     y_tokens = swapped(later, ("y",), 1)
     hop_1 = jnp.concatenate([near_1, ringed(far)], 0)
@@ -514,20 +475,21 @@
         "heads": heads,
         "seq": sizes[0] * rows,
         "window": 2 * rows,
+        "span": min(sizes[0], 2) * rows,
         "tokens": parts * rows,
         "parts": parts,
-        "cores": 1,
     }
-    *ga, gb = attend(place, query_up_weight, value_up_weight, gathered, plan)
+    ga, gb = attend(place, query_up_weight, value_up_weight, gathered, plan)
 
     coefficient = ADAPTER_NAME / math.sqrt(parts * shards * rows)
-    pieces = lax.all_to_all(ga[0], GROUP, 0, 0, tiled=True)
-    mixed = jnp.concatenate([jnp.sum(pieces.astype(jnp.float32), 0), gb], 0).astype(jnp.bfloat16)
-    if shards & (shards - 1) == 0 and shards <= 4:
-        mixed = [mixed] + [swapped(mixed, ("z",), step) for step in range(1, shards)]
+    part = jnp.sum(lax.all_to_all(ga, GROUP, 0, 0, tiled=True).astype(jnp.float32), 0)
+    mixed = jnp.concatenate([part, gb], 0).astype(jnp.bfloat16)
+    if paired:
+        for step in (1, 2):
+            mixed = add_wide(mixed, swapped(mixed, ("z",), step)).astype(jnp.bfloat16)
     else:
-        mixed = [lax.psum(mixed.astype(jnp.float32), "z")]
-    scaled = (sum(piece.astype(jnp.float32) for piece in mixed) * coefficient).astype(jnp.bfloat16)
+        mixed = lax.psum(mixed.astype(jnp.float32), "z")
+    scaled = (mixed.astype(jnp.float32) * coefficient).astype(jnp.bfloat16)
     chips = ("ctx", "y")
     scaled = [scaled] + [swapped(scaled, chips, step) for step in range(1, sizes[0] * sizes[1])]
     if sizes[2] == 2:

time: 113 us -> 110 us (0.973)
  local copies, waits for them, and re-layouts: 11.1 us -> 8.62 us
  Pallas kernels: 22.7 us -> 20.4 us
  other arithmetic: 1.69 us -> 3.52 us
  waiting for transfers between devices: 48.5 us -> 47.1 us
    ppermute x21 -> x20, waiting for transfers between devices: 28.3 us -> 22.5 us  [swapped(): return lax.ppermute(value, axes, [(i, i ^ distance) for i in range(count)])]
    ppermute x4, waiting for transfers between devices: 15.3 us -> 19.7 us  [ringed(): return lax.ppermute(value, 'z', [(0, 1), (1, 3), (3, 2), (2, 0)])]
    unnamed x54 -> x35, local copies, waits for them, and re-layouts: 6.26 us -> 2.87 us
    concatenate x1 -> x2, other arithmetic: 0.01 us -> 1.17 us  [the longest x1 1.17 us: paired_gather(): hop_1 = jnp.concatenate([near_1, ringed(far)], 0)]
    ppermute x21 -> x20, starting transfers between devices: 15.4 us -> 16.1 us  [swapped(): return lax.ppermute(value, axes, [(i, i ^ distance) for i in range(count)])]
  transfers between devices with their start and end apart: 27 -> 26, of which waited for: 17 -> 16; matrix products, arithmetic and copies ran while one was open for 5% -> 8% of each run, Pallas kernels for 9% -> 8%
where the time goes in v5:
time: 110 us; the launch traced here: 109 us
  waiting for transfers between devices  47.1 us (43%)
  starting transfers between devices  28.1 us (26%)
  Pallas kernels  20.4 us (19%)
  local copies, waits for them, and re-layouts  8.62 us (8%)
  other arithmetic  3.52 us (3%)
    ppermute x20, waiting for transfers between devices, swapped(): return lax.ppermute(value, axes, [(i, i ^ distance) for i in range(count)])  22.5 us
    ppermute x4, waiting for transfers between devices, ringed(): return lax.ppermute(value, 'z', [(0, 1), (1, 3), (3, 2), (2, 0)])  19.7 us
    ppermute x20, starting transfers between devices, swapped(): return lax.ppermute(value, axes, [(i, i ^ distance) for i in range(count)])  16.1 us
    pallas_call x1, Pallas kernels, attend(): pl.pallas_call(functools.partial(attend_kernel, plan), out_shape=[jax.Sha...  9.53 us
    pallas_call x1, Pallas kernels, attend(): pl.pallas_call(functools.partial(project_kernel, plan), out_shape=jax.Sha...  8.28 us
    all_to_all x1, waiting for transfers between devices, on_device(): lax.all_to_all(ga, GROUP, 0, 0, tiled=True).astype(jnp.float32)  4.84 us
    ppermute x4, starting transfers between devices, ringed(): return lax.ppermute(value, 'z', [(0, 1), (1, 3), (3, 2), (2, 0)])  4.39 us
    all_to_all x1, starting transfers between devices, paired_gather(): gradient = lax.all_to_all(gradient, GROUP, 0, 0, tiled=True)  4.14 us
  transfers between devices with their start and end apart: 26, of which 16 were waited for; matrix products, arithmetic and copies ran while one was open for 8% of the time, Pallas kernels for 8%

profile of v5, /device:TPU:0, one launch (start us, length us, event | category | flops | bytes accessed | tf_op | source)
XLA Modules:
  0.0 108.7 jit_solution(15380288005254587716)
XLA Ops:
  0.7 1.1 constant_dynamic-slice_fusion.11
  1.8 1.0 constant_dynamic-slice_fusion.9
  3.4 1.3 %collective-permute-done = bf16[2,192,512]{2,1,0:T(8,128)(2,1)S(1)} collective-permute-done((bf16[2,192,512]{2,1,0:T(8,128)(2,1)S(1)}, bf16[2,192,512]{2,1,0:T(8,128)(2,1)S(1)}, u32[]{:S(2)}, u32[]{:S(2)}) %collective-permute-start) | collective-permute-done | bytes 393248 | tf_op jit(solution)/shard_map/ppermute | solution.py:42
  5.0 3.0 %collective-permute-start.2 = (bf16[384,512]{1,0:T(8,128)(2,1)S(1)}, bf16[384,512]{1,0:T(8,128)(2,1)}, u32[]{:S(2)}, u32[]{:S(2)}) collective-permute-start(bf16[384,512]{1,0:T(8,128)(2,1)S(1)} %pad_maximum_fusion.3.rest_0_), channel_id=1, source_target_pairs={{0,2},{2,0},{1,3},{3,1},{4,6},{6,4},{5,7},{7,5},{8,10},{10,8},{9,1... | collective-permute-start | bytes 1179656 | tf_op jit(solution)/shard_map/ppermute | solution.py:42
  8.7 1.6 %collective-permute-start.3 = (bf16[384,512]{1,0:T(8,128)(2,1)}, bf16[384,512]{1,0:T(8,128)(2,1)}, u32[]{:S(2)}, u32[]{:S(2)}) collective-permute-start(bf16[384,512]{1,0:T(8,128)(2,1)} %pad_maximum_fusion.4.refs_13_), channel_id=1, source_target_pairs={{0,4},{4,12},{12,8},{8,0},{1,5},{5,13},{13,9},{9,1},{2,6},{6,14},{... | collective-permute-start | bytes 1179656 | tf_op jit(solution)/shard_map/ppermute | solution.py:355
  11.2 1.6 %collective-permute-start.8 = (bf16[128,3200]{1,0:T(8,128)(2,1)S(1)}, bf16[128,3200]{1,0:T(8,128)(2,1)}, u32[]{:S(2)}, u32[]{:S(2)}) collective-permute-start(bf16[128,3200]{1,0:T(8,128)(2,1)S(1)} %get-tuple-element.14.refs_3_.refs_4_), channel_id=1, source_target_pairs={{0,16},{16,0},{1,17},{17,1},{2,18},{18,2},{3,19},{19,3},{4,20},{20... | collective-permute-start | bytes 2457608 | tf_op jit(solution)/shard_map/ppermute | solution.py:42
  12.8 1.3 %copy.20 = bf16[1,128,2048]{1,2,0:T(8,128)(2,1)S(1)} copy(bf16[1,128,2048]{2,1,0:T(8,128)(2,1)} %param.21) | data formatting | bytes 1048576 | tf_op args[10]
  15.1 2.3 %collective-permute-done.2.refs_2_.refs_14_ = bf16[384,512]{1,0:T(8,128)(2,1)} collective-permute-done((bf16[384,512]{1,0:T(8,128)(2,1)S(1)}, bf16[384,512]{1,0:T(8,128)(2,1)}, u32[]{:S(2)}, u32[]{:S(2)}) %collective-permute-start.2) | collective-permute-done | bytes 393248 | tf_op jit(solution)/shard_map/ppermute | solution.py:42
  17.5 1.8 %collective-permute-start.5 = (bf16[384,512]{1,0:T(8,128)(2,1)}, bf16[384,512]{1,0:T(8,128)(2,1)}, u32[]{:S(2)}, u32[]{:S(2)}) collective-permute-start(bf16[384,512]{1,0:T(8,128)(2,1)} %collective-permute-done.2.refs_2_.refs_14_), channel_id=1, source_target_pairs={{0,4},{4,12},{12,8},{8,0},{1,5},{5,13},{13,9},{9,1},{2,6},{6,14},{... | collective-permute-start | bytes 1179656 | tf_op jit(solution)/shard_map/ppermute | solution.py:355
  19.3 1.6 %collective-permute-done.3.refs_0_ = bf16[384,512]{1,0:T(8,128)(2,1)} collective-permute-done((bf16[384,512]{1,0:T(8,128)(2,1)}, bf16[384,512]{1,0:T(8,128)(2,1)}, u32[]{:S(2)}, u32[]{:S(2)}) %collective-permute-start.3) | collective-permute-done | bytes 393248 | tf_op jit(solution)/shard_map/ppermute | solution.py:355
  21.3 8.1 %collective-permute-done.5 = bf16[384,512]{1,0:T(8,128)(2,1)} collective-permute-done((bf16[384,512]{1,0:T(8,128)(2,1)}, bf16[384,512]{1,0:T(8,128)(2,1)}, u32[]{:S(2)}, u32[]{:S(2)}) %collective-permute-start.5) | collective-permute-done | bytes 393248 | tf_op jit(solution)/shard_map/ppermute | solution.py:355
  29.3 1.2 %pad_maximum_fusion.refs_15_.refs_1_ = bf16[768,512]{1,0:T(8,128)(2,1)S(1)} fusion(bf16[384,512]{1,0:T(8,128)(2,1)} %collective-permute-done.5, bf16[384,512]{1,0:T(8,128)(2,1)} %fence.4.refs_3_), kind=kLoop, calls=%fused_computation | loop fusion | flops 1572864 | bytes 1572864 | tf_op jit(solution)/shard_map/concatenate | solution.py:369
  31.8 1.8 %slice.28 = bf16[64,3200]{1,0:T(8,128)(2,1)} slice(bf16[128,3200]{1,0:T(8,128)(2,1)} %collective-permute-done.8.refs_7_.refs_8_), slice={[0:64], [0:3200]} | slice | bytes 819200 | tf_op jit(solution)/shard_map/slice | solution.py:373
  33.6 1.5 %collective-permute-start.10 = (bf16[64,3200]{1,0:T(8,128)(2,1)}, bf16[64,3200]{1,0:T(8,128)(2,1)}, u32[]{:S(2)}, u32[]{:S(2)}) collective-permute-start(bf16[64,3200]{1,0:T(8,128)(2,1)} %slice.28), channel_id=1, source_target_pairs={{0,2},{2,0},{1,3},{3,1},{4,6},{6,4},{5,7},{7,5},{8,10},{10,8},{9,1... | collective-permute-start | bytes 1228808 | tf_op jit(solution)/shard_map/ppermute | solution.py:42
  35.1 7.1 %collective-permute-done.4.refs_0_ = bf16[128,3200]{1,0:T(8,128)(2,1)S(1)} collective-permute-done((bf16[128,3200]{1,0:T(8,128)(2,1)}, bf16[128,3200]{1,0:T(8,128)(2,1)S(1)}, u32[]{:S(2)}, u32[]{:S(2)}) %collective-permute-start.4) | collective-permute-done | bytes 819232 | tf_op jit(solution)/shard_map/ppermute | solution.py:42
  43.9 1.5 %collective-permute-start.11 = (bf16[64,3200]{1,0:T(8,128)(2,1)}, bf16[64,3200]{1,0:T(8,128)(2,1)}, u32[]{:S(2)}, u32[]{:S(2)}) collective-permute-start(bf16[64,3200]{1,0:T(8,128)(2,1)} %slice.29), channel_id=1, source_target_pairs={{0,16},{16,0},{1,17},{17,1},{2,18},{18,2},{3,19},{19,3},{4,20},{20... | collective-permute-start | bytes 1228808 | tf_op jit(solution)/shard_map/ppermute | solution.py:42
  45.4 4.4 %collective-permute-done.6.refs_1_.refs_16_ = bf16[768,512]{1,0:T(8,128)(2,1)} collective-permute-done((bf16[768,512]{1,0:T(8,128)(2,1)S(1)}, bf16[768,512]{1,0:T(8,128)(2,1)}, u32[]{:S(2)}, u32[]{:S(2)}) %collective-permute-start.6) | collective-permute-done | bytes 786464 | tf_op jit(solution)/shard_map/ppermute | solution.py:355
  50.0 4.1 %all-to-all-start = ((bf16[8,128,256]{2,1,0:T(8,128)(2,1)}), bf16[8,128,256]{2,1,0:T(8,128)(2,1)}, u32[]{:S(2)}, u32[]{:S(2)}) async-start(bf16[8,128,256]{2,1,0:T(8,128)(2,1)} %fence.7), calls=%async_computation | async-start | bytes 1048576 | tf_op jit(solution)/shard_map/all_to_all | solution.py:376
  56.9 8.3 %project.1.refs_3_ = f32[1024,512]{1,0:T(8,128)} custom-call(s32[2]{0:T(128)} %pad_add_fusion.refs_0_.place, bf16[16,2048]{1,0:T(8,128)(2,1)} %refs_1_.3, bf16[16,1024]{1,0:T(8,128)(2,1)} %refs_2_.3, bf16[128,3200]{1,0:T(8,128)(2,1)} %copy-done, bf16[128,3200]{1,0:T(8,128)(2,1)} %collective-permute-done.1.refs_4_.refs_5_, ...), custom_call_target="tpu_custom_call" | custom-call | tf_op jit(solution)/shard_map/project/pallas_call | solution.py:290
  65.2 5.7 %collective-permute-done.14.refs_22_ = bf16[768,512]{1,0:T(8,128)(2,1)} collective-permute-done((bf16[768,512]{1,0:T(8,128)(2,1)}, bf16[768,512]{1,0:T(8,128)(2,1)}, u32[]{:S(2)}, u32[]{:S(2)}) %collective-permute-start.14) | collective-permute-done | bytes 786464 | tf_op jit(solution)/shard_map/ppermute | solution.py:355
  70.9 9.5 %attend.1 = (bf16[8,32,384]{2,1,0:T(8,128)(2,1)}, f32[16,384]{1,0:T(8,128)}) custom-call(s32[2]{0:T(128)} %pad_add_fusion.refs_0_.place, bf16[16,2048]{1,0:T(8,128)(2,1)} %refs_1_.3, bf16[16,1024]{1,0:T(8,128)(2,1)} %refs_2_.3, f32[1024,512]{1,0:T(8,128)} %project.1.refs_3_, bf16[128,3200]{1,0:T(8,128)(2,1)} %copy-done, ...), custom_call_target="tpu_custom_call" | custom-call | tf_op jit(solution)/shard_map/attend/pallas_call | solution.py:308
  80.4 3.4 %all-to-all-start.1 = ((bf16[8,32,384]{2,1,0:T(8,128)(2,1)}), bf16[8,32,384]{2,1,0:T(8,128)(2,1)S(1)}, u32[]{:S(2)}, u32[]{:S(2)}) async-start(bf16[8,32,384]{2,1,0:T(8,128)(2,1)} %get-tuple-element.18), calls=%async_computation.1 | async-start | bytes 393216 | tf_op jit(solution)/shard_map/all_to_all | solution.py:485
  84.6 4.8 %all-to-all-done.1 = bf16[8,32,384]{2,1,0:T(8,128)(2,1)S(1)} async-done(((bf16[8,32,384]{2,1,0:T(8,128)(2,1)}), bf16[8,32,384]{2,1,0:T(8,128)(2,1)S(1)}, u32[]{:S(2)}, u32[]{:S(2)}) %all-to-all-start.1) | async-done | bytes 196640 | tf_op jit(solution)/shard_map/all_to_all | solution.py:485
  90.3 3.2 %collective-permute-done.15 = bf16[48,384]{1,0:T(8,128)(2,1)S(1)} collective-permute-done((bf16[48,384]{1,0:T(8,128)(2,1)S(1)}, bf16[48,384]{1,0:T(8,128)(2,1)S(1)}, u32[]{:S(2)}, u32[]{:S(2)}) %collective-permute-start.15) | collective-permute-done | bytes 36896 | tf_op jit(solution)/shard_map/ppermute | solution.py:42
  93.5 2.2 %collective-permute-start.16 = (bf16[48,384]{1,0:T(8,128)(2,1)S(1)}, bf16[48,384]{1,0:T(8,128)(2,1)S(1)}, u32[]{:S(2)}, u32[]{:S(2)}) collective-permute-start(bf16[48,384]{1,0:T(8,128)(2,1)S(1)} %add_convert_fusion.1), channel_id=1, source_target_pairs={{0,8},{4,12},{8,0},{12,4},{1,9},{5,13},{9,1},{13,5},{2,10},{6,14},... | collective-permute-start | bytes 110600 | tf_op jit(solution)/shard_map/ppermute | solution.py:42
  95.7 2.8 %collective-permute-done.16 = bf16[48,384]{1,0:T(8,128)(2,1)S(1)} collective-permute-done((bf16[48,384]{1,0:T(8,128)(2,1)S(1)}, bf16[48,384]{1,0:T(8,128)(2,1)S(1)}, u32[]{:S(2)}, u32[]{:S(2)}) %collective-permute-start.16) | collective-permute-done | bytes 36896 | tf_op jit(solution)/shard_map/ppermute | solution.py:42
  98.5 1.2 %collective-permute-start.18 = (bf16[48,384]{1,0:T(8,128)(2,1)S(1)}, bf16[48,384]{1,0:T(8,128)(2,1)S(1)}, u32[]{:S(2)}, u32[]{:S(2)}) collective-permute-start(bf16[48,384]{1,0:T(8,128)(2,1)S(1)} %multiply_convert_fusion.refs_0_), channel_id=1, source_target_pairs={{0,2},{2,0},{16,18},{18,16},{1,3},{3,1},{17,19},{19,17},{4,6},{6,4... | collective-permute-start | bytes 110600 | tf_op jit(solution)/shard_map/ppermute | solution.py:42
  100.2 1.8 %collective-permute-start.22 = (bf16[48,384]{1,0:T(8,128)(2,1)S(1)}, bf16[48,384]{1,0:T(8,128)(2,1)S(1)}, u32[]{:S(2)}, u32[]{:S(2)}) collective-permute-start(bf16[48,384]{1,0:T(8,128)(2,1)S(1)} %multiply_convert_fusion.refs_0_), channel_id=1, source_target_pairs={{0,18},{2,16},{16,2},{18,0},{1,19},{3,17},{17,3},{19,1},{4,22},{6,... | collective-permute-start | bytes 110600 | tf_op jit(solution)/shard_map/ppermute | solution.py:42
  102.6 1.1 %collective-permute-done.20.refs_4_ = bf16[48,384]{1,0:T(8,128)(2,1)S(1)} collective-permute-done((bf16[48,384]{1,0:T(8,128)(2,1)S(1)}, bf16[48,384]{1,0:T(8,128)(2,1)S(1)}, u32[]{:S(2)}, u32[]{:S(2)}) %collective-permute-start.20) | collective-permute-done | bytes 36896 | tf_op jit(solution)/shard_map/ppermute | solution.py:42
  103.7 1.4 %collective-permute-done.22.refs_6_ = bf16[48,384]{1,0:T(8,128)(2,1)S(1)} collective-permute-done((bf16[48,384]{1,0:T(8,128)(2,1)S(1)}, bf16[48,384]{1,0:T(8,128)(2,1)S(1)}, u32[]{:S(2)}, u32[]{:S(2)}) %collective-permute-start.22) | collective-permute-done | bytes 36896 | tf_op jit(solution)/shard_map/ppermute | solution.py:42
  105.2 1.2 %collective-permute-done.23.refs_7_ = bf16[48,384]{1,0:T(8,128)(2,1)S(1)} collective-permute-done((bf16[48,384]{1,0:T(8,128)(2,1)S(1)}, bf16[48,384]{1,0:T(8,128)(2,1)S(1)}, u32[]{:S(2)}, u32[]{:S(2)}) %collective-permute-start.23) | collective-permute-done | bytes 36896 | tf_op jit(solution)/shard_map/ppermute | solution.py:42
  107.0 1.7 %spread.1 = (f32[16,3072]{1,0:T(8,128)}, f32[16,2048]{1,0:T(8,128)}, f32[16,3072]{1,0:T(8,128)}, f32[16,1024]{1,0:T(8,128)}) custom-call(s32[2]{0:T(128)} %pad_add_fusion.refs_0_.place, bf16[48,384]{1,0:T(8,128)(2,1)} %copy-done.9, bf16[48,384]{1,0:T(8,128)(2,1)} %copy-done.13, bf16[48,384]{1,0:T(8,128)(2,1)} %copy-done.10, bf16[48,384]{1,0:T(8,128)(2,1)} %copy-done.14, ...), custom_call_target="tpu_custom_call" | custom-call | tf_op jit(solution)/shard_map/spread/pallas_call | solution.py:345
  (85 shorter events, 13.2 us)
Async XLA Ops:
  2.9 1.9 %collective-permute-start = (bf16[2,192,512]{2,1,0:T(8,128)(2,1)S(1)}, bf16[2,192,512]{2,1,0:T(8,128)(2,1)S(1)}, u32[]{:S(2)}, u32[]{:S(2)}) collective-permute-start(bf16[2,192,512]{2,1,0:T(8,128)(2,1)S(1)} %pad_maximum_fusion.2), channel_id=1, source_target_pairs={{0,1},{1,0},{2,3},{3,2},{4,5},{5,4},{6,7},{7,6},{8,9},{9,8},{10,11... | collective-permute-start | bytes 1179656 | tf_op jit(solution)/shard_map/ppermute | solution.py:42
  4.8 5.5 %copy-start.2 = (bf16[1,128,3072]{2,1,0:T(8,128)(2,1)S(1)}, bf16[1,128,3072]{2,1,0:T(8,128)(2,1)}, u32[]{:S(2)}) copy-start(bf16[1,128,3072]{2,1,0:T(8,128)(2,1)} %param.11) | copy-start | bytes 2359300
  4.8 5.5 %copy-start.3 = (bf16[3072,16]{0,1:T(8,128)(2,1)S(1)}, bf16[3072,16]{0,1:T(8,128)(2,1)}, u32[]{:S(2)}) copy-start(bf16[3072,16]{0,1:T(8,128)(2,1)} %param.17) | copy-start | bytes 294916
  5.0 12.5 %collective-permute-start.2 = (bf16[384,512]{1,0:T(8,128)(2,1)S(1)}, bf16[384,512]{1,0:T(8,128)(2,1)}, u32[]{:S(2)}, u32[]{:S(2)}) collective-permute-start(bf16[384,512]{1,0:T(8,128)(2,1)S(1)} %pad_maximum_fusion.3.rest_0_), channel_id=1, source_target_pairs={{0,2},{2,0},{1,3},{3,1},{4,6},{6,4},{5,7},{7,5},{8,10},{10,8},{9,1... | collective-permute-start | bytes 1179656 | tf_op jit(solution)/shard_map/ppermute | solution.py:42
  8.7 12.1 %collective-permute-start.3 = (bf16[384,512]{1,0:T(8,128)(2,1)}, bf16[384,512]{1,0:T(8,128)(2,1)}, u32[]{:S(2)}, u32[]{:S(2)}) collective-permute-start(bf16[384,512]{1,0:T(8,128)(2,1)} %pad_maximum_fusion.4.refs_13_), channel_id=1, source_target_pairs={{0,4},{4,12},{12,8},{8,0},{1,5},{5,13},{13,9},{9,1},{2,6},{6,14},{... | collective-permute-start | bytes 1179656 | tf_op jit(solution)/shard_map/ppermute | solution.py:355
  11.2 6.3 %copy-start.1 = (bf16[128,3200]{1,0:T(8,128)(2,1)}, bf16[128,3200]{1,0:T(8,128)(2,1)S(1)}, u32[]{:S(2)}) copy-start(bf16[128,3200]{1,0:T(8,128)(2,1)S(1)} %get-tuple-element.15.refs_0_) | copy-start | bytes 2457604
  11.2 20.0 %copy-start = (bf16[128,3200]{1,0:T(8,128)(2,1)}, bf16[128,3200]{1,0:T(8,128)(2,1)S(1)}, u32[]{:S(2)}) copy-start(bf16[128,3200]{1,0:T(8,128)(2,1)S(1)} %get-tuple-element.14.refs_3_.refs_4_) | copy-start | bytes 2457604
  11.2 20.0 %collective-permute-start.8 = (bf16[128,3200]{1,0:T(8,128)(2,1)S(1)}, bf16[128,3200]{1,0:T(8,128)(2,1)}, u32[]{:S(2)}, u32[]{:S(2)}) collective-permute-start(bf16[128,3200]{1,0:T(8,128)(2,1)S(1)} %get-tuple-element.14.refs_3_.refs_4_), channel_id=1, source_target_pairs={{0,16},{16,0},{1,17},{17,1},{2,18},{18,2},{3,19},{19,3},{4,20},{20... | collective-permute-start | bytes 2457608 | tf_op jit(solution)/shard_map/ppermute | solution.py:42
  17.5 11.9 %collective-permute-start.5 = (bf16[384,512]{1,0:T(8,128)(2,1)}, bf16[384,512]{1,0:T(8,128)(2,1)}, u32[]{:S(2)}, u32[]{:S(2)}) collective-permute-start(bf16[384,512]{1,0:T(8,128)(2,1)} %collective-permute-done.2.refs_2_.refs_14_), channel_id=1, source_target_pairs={{0,4},{4,12},{12,8},{8,0},{1,5},{5,13},{13,9},{9,1},{2,6},{6,14},{... | collective-permute-start | bytes 1179656 | tf_op jit(solution)/shard_map/ppermute | solution.py:355
  20.8 21.4 %collective-permute-start.4 = (bf16[128,3200]{1,0:T(8,128)(2,1)}, bf16[128,3200]{1,0:T(8,128)(2,1)S(1)}, u32[]{:S(2)}, u32[]{:S(2)}) collective-permute-start(bf16[128,3200]{1,0:T(8,128)(2,1)} %get-tuple-element.16), channel_id=1, source_target_pairs={{0,2},{2,0},{1,3},{3,1},{4,6},{6,4},{5,7},{7,5},{8,10},{10,8},{9,1... | collective-permute-start | bytes 2457608 | tf_op jit(solution)/shard_map/ppermute | solution.py:42
  30.5 13.4 %copy-start.8 = (bf16[768,512]{1,0:T(8,128)(2,1)}, bf16[768,512]{1,0:T(8,128)(2,1)S(1)}, u32[]{:S(2)}) copy-start(bf16[768,512]{1,0:T(8,128)(2,1)S(1)} %pad_maximum_fusion.refs_15_.refs_1_) | copy-start | bytes 2359300
  30.5 19.2 %collective-permute-start.6 = (bf16[768,512]{1,0:T(8,128)(2,1)S(1)}, bf16[768,512]{1,0:T(8,128)(2,1)}, u32[]{:S(2)}, u32[]{:S(2)}) collective-permute-start(bf16[768,512]{1,0:T(8,128)(2,1)S(1)} %pad_maximum_fusion.refs_15_.refs_1_), channel_id=1, source_target_pairs={{0,4},{4,12},{12,8},{8,0},{1,5},{5,13},{13,9},{9,1},{2,6},{6,14},{... | collective-permute-start | bytes 2359304 | tf_op jit(solution)/shard_map/ppermute | solution.py:355
  31.3 18.5 %collective-permute-start.9 = (bf16[128,3200]{1,0:T(8,128)(2,1)}, bf16[128,3200]{1,0:T(8,128)(2,1)}, u32[]{:S(2)}, u32[]{:S(2)}) collective-permute-start(bf16[128,3200]{1,0:T(8,128)(2,1)} %collective-permute-done.8.refs_7_.refs_8_), channel_id=1, source_target_pairs={{0,1},{1,0},{2,3},{3,2},{4,5},{5,4},{6,7},{7,6},{8,9},{9,8},{10,11... | collective-permute-start | bytes 2457608 | tf_op jit(solution)/shard_map/ppermute | solution.py:42
  31.3 24.0 %collective-permute-start.1 = (bf16[128,3200]{1,0:T(8,128)(2,1)S(1)}, bf16[128,3200]{1,0:T(8,128)(2,1)}, u32[]{:S(2)}, u32[]{:S(2)}) collective-permute-start(bf16[128,3200]{1,0:T(8,128)(2,1)S(1)} %get-tuple-element.14.refs_3_.refs_4_), channel_id=1, source_target_pairs={{0,1},{1,0},{2,3},{3,2},{4,5},{5,4},{6,7},{7,6},{8,9},{9,8},{10,11... | collective-permute-start | bytes 2457608 | tf_op jit(solution)/shard_map/ppermute | solution.py:42
  33.6 20.6 %collective-permute-start.10 = (bf16[64,3200]{1,0:T(8,128)(2,1)}, bf16[64,3200]{1,0:T(8,128)(2,1)}, u32[]{:S(2)}, u32[]{:S(2)}) collective-permute-start(bf16[64,3200]{1,0:T(8,128)(2,1)} %slice.28), channel_id=1, source_target_pairs={{0,2},{2,0},{1,3},{3,1},{4,6},{6,4},{5,7},{7,5},{8,10},{10,8},{9,1... | collective-permute-start | bytes 1228808 | tf_op jit(solution)/shard_map/ppermute | solution.py:42
  43.9 10.7 %collective-permute-start.11 = (bf16[64,3200]{1,0:T(8,128)(2,1)}, bf16[64,3200]{1,0:T(8,128)(2,1)}, u32[]{:S(2)}, u32[]{:S(2)}) collective-permute-start(bf16[64,3200]{1,0:T(8,128)(2,1)} %slice.29), channel_id=1, source_target_pairs={{0,16},{16,0},{1,17},{17,1},{2,18},{18,2},{3,19},{19,3},{4,20},{20... | collective-permute-start | bytes 1228808 | tf_op jit(solution)/shard_map/ppermute | solution.py:42
  49.7 7.2 %collective-permute-start.7 = (bf16[128,3200]{1,0:T(8,128)(2,1)}, bf16[128,3200]{1,0:T(8,128)(2,1)}, u32[]{:S(2)}, u32[]{:S(2)}) collective-permute-start(bf16[128,3200]{1,0:T(8,128)(2,1)} %fence.6.refs_5_.refs_6_), channel_id=1, source_target_pairs={{0,1},{1,0},{2,3},{3,2},{4,5},{5,4},{6,7},{7,6},{8,9},{9,8},{10,11... | collective-permute-start | bytes 2457608 | tf_op jit(solution)/shard_map/ppermute | solution.py:42
  49.7 21.2 %collective-permute-start.14 = (bf16[768,512]{1,0:T(8,128)(2,1)}, bf16[768,512]{1,0:T(8,128)(2,1)}, u32[]{:S(2)}, u32[]{:S(2)}) collective-permute-start(bf16[768,512]{1,0:T(8,128)(2,1)} %collective-permute-done.6.refs_1_.refs_16_), channel_id=1, source_target_pairs={{0,4},{4,12},{12,8},{8,0},{1,5},{5,13},{13,9},{9,1},{2,6},{6,14},{... | collective-permute-start | bytes 2359304 | tf_op jit(solution)/shard_map/ppermute | solution.py:355
  50.0 15.2 %all-to-all-start = ((bf16[8,128,256]{2,1,0:T(8,128)(2,1)}), bf16[8,128,256]{2,1,0:T(8,128)(2,1)}, u32[]{:S(2)}, u32[]{:S(2)}) async-start(bf16[8,128,256]{2,1,0:T(8,128)(2,1)} %fence.7), calls=%async_computation | async-start | bytes 1048576 | tf_op jit(solution)/shard_map/all_to_all | solution.py:376
  54.2 2.2 %collective-permute-start.12 = (bf16[64,3200]{1,0:T(8,128)(2,1)}, bf16[64,3200]{1,0:T(8,128)(2,1)}, u32[]{:S(2)}, u32[]{:S(2)}) collective-permute-start(bf16[64,3200]{1,0:T(8,128)(2,1)} %collective-permute-done.10.refs_9_.refs_10_), channel_id=1, source_target_pairs={{0,1},{1,0},{2,3},{3,2},{4,5},{5,4},{6,7},{7,6},{8,9},{9,8},{10,11... | collective-permute-start | bytes 1228808 | tf_op jit(solution)/shard_map/ppermute | solution.py:42
  54.5 2.4 %collective-permute-start.13 = (bf16[64,3200]{1,0:T(8,128)(2,1)}, bf16[64,3200]{1,0:T(8,128)(2,1)}, u32[]{:S(2)}, u32[]{:S(2)}) collective-permute-start(bf16[64,3200]{1,0:T(8,128)(2,1)} %collective-permute-done.11.refs_10_.refs_11_), channel_id=1, source_target_pairs={{0,1},{1,0},{2,3},{3,2},{4,5},{5,4},{6,7},{7,6},{8,9},{9,8},{10,11... | collective-permute-start | bytes 1228808 | tf_op jit(solution)/shard_map/ppermute | solution.py:42
  80.4 9.0 %all-to-all-start.1 = ((bf16[8,32,384]{2,1,0:T(8,128)(2,1)}), bf16[8,32,384]{2,1,0:T(8,128)(2,1)S(1)}, u32[]{:S(2)}, u32[]{:S(2)}) async-start(bf16[8,32,384]{2,1,0:T(8,128)(2,1)} %get-tuple-element.18), calls=%async_computation.1 | async-start | bytes 393216 | tf_op jit(solution)/shard_map/all_to_all | solution.py:485
  89.5 4.0 %collective-permute-start.15 = (bf16[48,384]{1,0:T(8,128)(2,1)S(1)}, bf16[48,384]{1,0:T(8,128)(2,1)S(1)}, u32[]{:S(2)}, u32[]{:S(2)}) collective-permute-start(bf16[48,384]{1,0:T(8,128)(2,1)S(1)} %pad_maximum_fusion.5), channel_id=1, source_target_pairs={{0,4},{4,0},{8,12},{12,8},{1,5},{5,1},{9,13},{13,9},{2,6},{6,2},{1... | collective-permute-start | bytes 110600 | tf_op jit(solution)/shard_map/ppermute | solution.py:42
  93.5 4.9 %collective-permute-start.16 = (bf16[48,384]{1,0:T(8,128)(2,1)S(1)}, bf16[48,384]{1,0:T(8,128)(2,1)S(1)}, u32[]{:S(2)}, u32[]{:S(2)}) collective-permute-start(bf16[48,384]{1,0:T(8,128)(2,1)S(1)} %add_convert_fusion.1), channel_id=1, source_target_pairs={{0,8},{4,12},{8,0},{12,4},{1,9},{5,13},{9,1},{13,5},{2,10},{6,14},... | collective-permute-start | bytes 110600 | tf_op jit(solution)/shard_map/ppermute | solution.py:42
  98.5 7.8 %copy-start.9 = (bf16[48,384]{1,0:T(8,128)(2,1)}, bf16[48,384]{1,0:T(8,128)(2,1)S(1)}, u32[]{:S(2)}) copy-start(bf16[48,384]{1,0:T(8,128)(2,1)S(1)} %multiply_convert_fusion.refs_0_) | copy-start | bytes 110596
  98.5 4.0 %collective-permute-start.18 = (bf16[48,384]{1,0:T(8,128)(2,1)S(1)}, bf16[48,384]{1,0:T(8,128)(2,1)S(1)}, u32[]{:S(2)}, u32[]{:S(2)}) collective-permute-start(bf16[48,384]{1,0:T(8,128)(2,1)S(1)} %multiply_convert_fusion.refs_0_), channel_id=1, source_target_pairs={{0,2},{2,0},{16,18},{18,16},{1,3},{3,1},{17,19},{19,17},{4,6},{6,4... | collective-permute-start | bytes 110600 | tf_op jit(solution)/shard_map/ppermute | solution.py:42
  99.7 4.0 %collective-permute-start.20 = (bf16[48,384]{1,0:T(8,128)(2,1)S(1)}, bf16[48,384]{1,0:T(8,128)(2,1)S(1)}, u32[]{:S(2)}, u32[]{:S(2)}) collective-permute-start(bf16[48,384]{1,0:T(8,128)(2,1)S(1)} %multiply_convert_fusion.refs_0_), channel_id=1, source_target_pairs={{0,16},{2,18},{16,0},{18,2},{1,17},{3,19},{17,1},{19,3},{4,20},{6,... | collective-permute-start | bytes 110600 | tf_op jit(solution)/shard_map/ppermute | solution.py:42
  100.2 4.9 %collective-permute-start.22 = (bf16[48,384]{1,0:T(8,128)(2,1)S(1)}, bf16[48,384]{1,0:T(8,128)(2,1)S(1)}, u32[]{:S(2)}, u32[]{:S(2)}) collective-permute-start(bf16[48,384]{1,0:T(8,128)(2,1)S(1)} %multiply_convert_fusion.refs_0_), channel_id=1, source_target_pairs={{0,18},{2,16},{16,2},{18,0},{1,19},{3,17},{17,3},{19,1},{4,22},{6,... | collective-permute-start | bytes 110600 | tf_op jit(solution)/shard_map/ppermute | solution.py:42
  102.0 3.1 %collective-permute-start.17 = (bf16[48,384]{1,0:T(8,128)(2,1)S(1)}, bf16[48,384]{1,0:T(8,128)(2,1)S(1)}, u32[]{:S(2)}, u32[]{:S(2)}) collective-permute-start(bf16[48,384]{1,0:T(8,128)(2,1)S(1)} %multiply_convert_fusion.refs_0_), channel_id=1, source_target_pairs={{0,1},{1,0},{2,3},{3,2},{4,5},{5,4},{6,7},{7,6},{8,9},{9,8},{10,11... | collective-permute-start | bytes 110600 | tf_op jit(solution)/shard_map/ppermute | solution.py:42
  102.5 2.6 %collective-permute-start.19 = (bf16[48,384]{1,0:T(8,128)(2,1)S(1)}, bf16[48,384]{1,0:T(8,128)(2,1)S(1)}, u32[]{:S(2)}, u32[]{:S(2)}) collective-permute-start(bf16[48,384]{1,0:T(8,128)(2,1)S(1)} %collective-permute-done.18.refs_2_), channel_id=1, source_target_pairs={{0,1},{1,0},{2,3},{3,2},{4,5},{5,4},{6,7},{7,6},{8,9},{9,8},{10,11... | collective-permute-start | bytes 110600 | tf_op jit(solution)/shard_map/ppermute | solution.py:42
  103.7 1.5 %collective-permute-start.21 = (bf16[48,384]{1,0:T(8,128)(2,1)S(1)}, bf16[48,384]{1,0:T(8,128)(2,1)S(1)}, u32[]{:S(2)}, u32[]{:S(2)}) collective-permute-start(bf16[48,384]{1,0:T(8,128)(2,1)S(1)} %collective-permute-done.20.refs_4_), channel_id=1, source_target_pairs={{0,1},{1,0},{2,3},{3,2},{4,5},{5,4},{6,7},{7,6},{8,9},{9,8},{10,11... | collective-permute-start | bytes 110600 | tf_op jit(solution)/shard_map/ppermute | solution.py:42
  105.1 1.2 %collective-permute-start.23 = (bf16[48,384]{1,0:T(8,128)(2,1)S(1)}, bf16[48,384]{1,0:T(8,128)(2,1)S(1)}, u32[]{:S(2)}, u32[]{:S(2)}) collective-permute-start(bf16[48,384]{1,0:T(8,128)(2,1)S(1)} %collective-permute-done.22.refs_6_), channel_id=1, source_target_pairs={{0,1},{1,0},{2,3},{3,2},{4,5},{5,4},{6,7},{7,6},{8,9},{9,8},{10,11... | collective-permute-start | bytes 110600 | tf_op jit(solution)/shard_map/ppermute | solution.py:42
  (11 other events, 29.2 us)

commit v6 on v5

--- a/solution.py
+++ b/solution.py
@@ -72,7 +72,7 @@
         cost_estimate=pl.CostEstimate(
             flops=wait_us * 10**9, bytes_accessed=wait_us * 3 * 10**6, transcendentals=0
         ),
-        compiler_params=PARAMS,
+        compiler_params=pltpu.CompilerParams(vmem_limit_bytes=60 * 2**20),
         name="fence",
     )(*values, *earlier)
 
@@ -328,29 +328,6 @@
     )(place, up_q, up_v, base, *x_arrays, *g_arrays, *last)
 
 
-def spread_kernel(rank, group, place, *refs):
-    pieces, (aq, bq, av, bv) = refs[:-4], refs[-4:]
-    wide = pieces[0].shape[1]
-    for step, ref in enumerate(pieces):
-        mine = place[0] ^ step
-        value = ref[...].astype(jnp.float32)
-        at = pl.ds(pl.multiple_of(mine * wide, LANES), wide)
-        aq[:, at] = value[:rank]
-        av[:, at] = value[rank : 2 * rank]
-        bq[:, pl.ds(pl.multiple_of(mine * group, LANES), group)] = value[2 * rank :, :group]
-        bv[:, pl.ds(pl.multiple_of(mine * HEAD_SIZE, LANES), HEAD_SIZE)] = value[2 * rank :, group:]
-
-
-def spread(place, pieces, rank, group, shapes):
-    return pl.pallas_call(
-        functools.partial(spread_kernel, rank, group),
-        out_shape=[jax.ShapeDtypeStruct(shape, jnp.float32) for shape in shapes],
-        in_specs=[SMEM] + [VMEM] * len(pieces),
-        out_specs=[VMEM] * 4,
-        name="spread",
-    )(place, *pieces)
-
-
 def ringed(value):
     return lax.ppermute(value, "z", [(0, 1), (1, 3), (3, 2), (2, 0)])
 
@@ -494,8 +471,19 @@
     scaled = [scaled] + [swapped(scaled, chips, step) for step in range(1, sizes[0] * sizes[1])]
     if sizes[2] == 2:
         scaled = [piece for value in scaled for piece in (value, swapped(value, ("c",), 1))]
-    shapes = ((rank, feats), (rank, heads_kv * group), (rank, feats), (rank, heads_kv * HEAD_SIZE))
-    aq, bq, av, bv = spread(place, scaled, rank, group, shapes)
+    for bit in range(parts.bit_length() - 1):
+        one = (mine >> bit) & 1 == 1
+        scaled = [jnp.where(one, scaled[at ^ (1 << bit)], scaled[at]) for at in range(parts)]
+    scaled = [value.astype(jnp.float32) for value in scaled]
+    aq, av, bq, bv = (
+        jnp.concatenate([value[rows_of, columns] for value in scaled], 1)
+        for rows_of, columns in (
+            (slice(0, rank), slice(None)),
+            (slice(rank, 2 * rank), slice(None)),
+            (slice(2 * rank, None), slice(0, group)),
+            (slice(2 * rank, None), slice(group, None)),
+        )
+    )
     return aq.T, bq, av.T, bv
 
 

time: 110 us -> 109 us (level)
  Pallas kernels: 20.4 us -> 18.7 us
  local copies, waits for them, and re-layouts: 8.62 us -> 10.2 us
    pallas_call x1 -> x0, Pallas kernels: 1.75 us -> none  [spread(): pl.pallas_call(functools.partial(spread_kernel, rank, group), out_shape=[...]
    unnamed x35 -> x58, local copies, waits for them, and re-layouts: 2.87 us -> 3.59 us
  transfers between devices with their start and end apart: 26 -> 26, of which waited for: 16 -> 16; matrix products, arithmetic and copies ran while one was open for 8% -> 7% of each run, Pallas kernels for 8% -> 8%
where the time goes in v6:
time: 109 us; the launch traced here: 108 us
  waiting for transfers between devices  46.3 us (42%)
  starting transfers between devices  28.8 us (26%)
  Pallas kernels  18.7 us (17%)
  local copies, waits for them, and re-layouts  10.2 us (9%)
  other arithmetic  2.76 us (3%)
  between operations  1.23 us (1%)
    ppermute x20, waiting for transfers between devices, swapped(): return lax.ppermute(value, axes, [(i, i ^ distance) for i in range(count)])  22.4 us
    ppermute x4, waiting for transfers between devices, ringed(): return lax.ppermute(value, 'z', [(0, 1), (1, 3), (3, 2), (2, 0)])  19 us
    ppermute x20, starting transfers between devices, swapped(): return lax.ppermute(value, axes, [(i, i ^ distance) for i in range(count)])  16.8 us
    pallas_call x1, Pallas kernels, attend(): pl.pallas_call(functools.partial(attend_kernel, plan), out_shape=[jax.Sha...  9.53 us
    pallas_call x1, Pallas kernels, attend(): pl.pallas_call(functools.partial(project_kernel, plan), out_shape=jax.Sha...  8.29 us
    all_to_all x1, waiting for transfers between devices, on_device(): lax.all_to_all(ga, GROUP, 0, 0, tiled=True).astype(jnp.float32)  4.84 us
    ppermute x4, starting transfers between devices, ringed(): return lax.ppermute(value, 'z', [(0, 1), (1, 3), (3, 2), (2, 0)])  4.45 us
    all_to_all x1, starting transfers between devices, paired_gather(): gradient = lax.all_to_all(gradient, GROUP, 0, 0, tiled=True)  4.15 us
  transfers between devices with their start and end apart: 26, of which 16 were waited for; matrix products, arithmetic and copies ran while one was open for 7% of the time, Pallas kernels for 8%

profile of v6, /device:TPU:0, one launch (start us, length us, event | category | flops | bytes accessed | tf_op | source)
XLA Modules:
  0.0 108.0 jit_solution(13147869857402012872)
XLA Ops:
  0.7 0.9 constant_dynamic-slice_fusion.10
  2.5 1.1 %constant_dynamic-slice_fusion.11 = (bf16[192,256]{1,0:T(8,128)(2,1)S(1)}, bf16[192,256]{1,0:T(8,128)(2,1)S(1)}, bf16[192,256]{1,0:T(8,128)(2,1)S(1)}, bf16[192,256]{1,0:T(8,128)(2,1)S(1)}) fusion(bf16[192,2048]{1,0:T(8,128)(2,1)} %param.14, s32[]{:T(128)S(6)} %select_n.148, s32[]{:T(128)S(6)} %select_n.150, s32[]{:T(128)S(6)} %select_n.154, s32[]{:T(128)S(6)} %select_n.152), kind=kLoop, calls=%fused_computation.86 | loop fusion | bytes 786448 | tf_op jit(solution)/shard_map/dynamic_slice | solution.py:48
  4.3 1.3 %collective-permute-done = bf16[2,192,512]{2,1,0:T(8,128)(2,1)S(1)} collective-permute-done((bf16[2,192,512]{2,1,0:T(8,128)(2,1)S(1)}, bf16[2,192,512]{2,1,0:T(8,128)(2,1)S(1)}, u32[]{:S(2)}, u32[]{:S(2)}) %collective-permute-start) | collective-permute-done | bytes 393248 | tf_op jit(solution)/shard_map/ppermute | solution.py:42
  5.8 3.0 %collective-permute-start.2 = (bf16[384,512]{1,0:T(8,128)(2,1)S(1)}, bf16[384,512]{1,0:T(8,128)(2,1)S(1)}, u32[]{:S(2)}, u32[]{:S(2)}) collective-permute-start(bf16[384,512]{1,0:T(8,128)(2,1)S(1)} %pad_maximum_fusion.3.rest_0_), channel_id=1, source_target_pairs={{0,2},{2,0},{1,3},{3,1},{4,6},{6,4},{5,7},{7,5},{8,10},{10,8},{9,1... | collective-permute-start | bytes 1179656 | tf_op jit(solution)/shard_map/ppermute | solution.py:42
  8.8 1.6 %collective-permute-start.3 = (bf16[384,512]{1,0:T(8,128)(2,1)S(1)}, bf16[384,512]{1,0:T(8,128)(2,1)}, u32[]{:S(2)}, u32[]{:S(2)}) collective-permute-start(bf16[384,512]{1,0:T(8,128)(2,1)S(1)} %pad_maximum_fusion.4.refs_13_), channel_id=1, source_target_pairs={{0,4},{4,12},{12,8},{8,0},{1,5},{5,13},{13,9},{9,1},{2,6},{6,14},{... | collective-permute-start | bytes 1179656 | tf_op jit(solution)/shard_map/ppermute | solution.py:332
  11.3 1.6 %collective-permute-start.8 = (bf16[128,3200]{1,0:T(8,128)(2,1)S(1)}, bf16[128,3200]{1,0:T(8,128)(2,1)}, u32[]{:S(2)}, u32[]{:S(2)}) collective-permute-start(bf16[128,3200]{1,0:T(8,128)(2,1)S(1)} %get-tuple-element.10.refs_3_.refs_4_), channel_id=1, source_target_pairs={{0,16},{16,0},{1,17},{17,1},{2,18},{18,2},{3,19},{19,3},{4,20},{20... | collective-permute-start | bytes 2457608 | tf_op jit(solution)/shard_map/ppermute | solution.py:42
  12.9 1.3 %copy.20 = bf16[1,128,2048]{1,2,0:T(8,128)(2,1)S(1)} copy(bf16[1,128,2048]{2,1,0:T(8,128)(2,1)} %param.21) | data formatting | bytes 1048576 | tf_op args[10]
  14.2 1.0 copy.21
  15.2 2.9 %collective-permute-done.2.refs_2_.refs_14_ = bf16[384,512]{1,0:T(8,128)(2,1)S(1)} collective-permute-done((bf16[384,512]{1,0:T(8,128)(2,1)S(1)}, bf16[384,512]{1,0:T(8,128)(2,1)S(1)}, u32[]{:S(2)}, u32[]{:S(2)}) %collective-permute-start.2) | collective-permute-done | bytes 393248 | tf_op jit(solution)/shard_map/ppermute | solution.py:42
  18.1 1.8 %collective-permute-start.5 = (bf16[384,512]{1,0:T(8,128)(2,1)S(1)}, bf16[384,512]{1,0:T(8,128)(2,1)S(1)}, u32[]{:S(2)}, u32[]{:S(2)}) collective-permute-start(bf16[384,512]{1,0:T(8,128)(2,1)S(1)} %collective-permute-done.2.refs_2_.refs_14_), channel_id=1, source_target_pairs={{0,4},{4,12},{12,8},{8,0},{1,5},{5,13},{13,9},{9,1},{2,6},{6,14},{... | collective-permute-start | bytes 1179656 | tf_op jit(solution)/shard_map/ppermute | solution.py:332
  21.6 8.2 %collective-permute-done.5 = bf16[384,512]{1,0:T(8,128)(2,1)S(1)} collective-permute-done((bf16[384,512]{1,0:T(8,128)(2,1)S(1)}, bf16[384,512]{1,0:T(8,128)(2,1)S(1)}, u32[]{:S(2)}, u32[]{:S(2)}) %collective-permute-start.5) | collective-permute-done | bytes 393248 | tf_op jit(solution)/shard_map/ppermute | solution.py:332
  29.8 1.0 pad_maximum_fusion.refs_15_.refs_1_
  32.1 1.8 %slice.156 = bf16[64,3200]{1,0:T(8,128)(2,1)} slice(bf16[128,3200]{1,0:T(8,128)(2,1)} %collective-permute-done.8.refs_7_.refs_8_), slice={[0:64], [0:3200]} | slice | bytes 819200 | tf_op jit(solution)/shard_map/slice | solution.py:350
  33.9 1.5 %collective-permute-start.10 = (bf16[64,3200]{1,0:T(8,128)(2,1)}, bf16[64,3200]{1,0:T(8,128)(2,1)}, u32[]{:S(2)}, u32[]{:S(2)}) collective-permute-start(bf16[64,3200]{1,0:T(8,128)(2,1)} %slice.156), channel_id=1, source_target_pairs={{0,2},{2,0},{1,3},{3,1},{4,6},{6,4},{5,7},{7,5},{8,10},{10,8},{9,1... | collective-permute-start | bytes 1228808 | tf_op jit(solution)/shard_map/ppermute | solution.py:42
  35.4 6.7 %collective-permute-done.4.refs_0_ = bf16[128,3200]{1,0:T(8,128)(2,1)S(1)} collective-permute-done((bf16[128,3200]{1,0:T(8,128)(2,1)}, bf16[128,3200]{1,0:T(8,128)(2,1)S(1)}, u32[]{:S(2)}, u32[]{:S(2)}) %collective-permute-start.4) | collective-permute-done | bytes 819232 | tf_op jit(solution)/shard_map/ppermute | solution.py:42
  43.0 1.5 %collective-permute-start.11 = (bf16[64,3200]{1,0:T(8,128)(2,1)}, bf16[64,3200]{1,0:T(8,128)(2,1)}, u32[]{:S(2)}, u32[]{:S(2)}) collective-permute-start(bf16[64,3200]{1,0:T(8,128)(2,1)} %slice.157), channel_id=1, source_target_pairs={{0,16},{16,0},{1,17},{17,1},{2,18},{18,2},{3,19},{19,3},{4,20},{20... | collective-permute-start | bytes 1228808 | tf_op jit(solution)/shard_map/ppermute | solution.py:42
  44.5 5.7 %collective-permute-done.6.refs_1_.refs_16_ = bf16[768,512]{1,0:T(8,128)(2,1)} collective-permute-done((bf16[768,512]{1,0:T(8,128)(2,1)S(1)}, bf16[768,512]{1,0:T(8,128)(2,1)}, u32[]{:S(2)}, u32[]{:S(2)}) %collective-permute-start.6) | collective-permute-done | bytes 786464 | tf_op jit(solution)/shard_map/ppermute | solution.py:332
  51.1 4.2 %all-to-all-start = ((bf16[8,128,256]{2,1,0:T(8,128)(2,1)}), bf16[8,128,256]{2,1,0:T(8,128)(2,1)}, u32[]{:S(2)}, u32[]{:S(2)}) async-start(bf16[8,128,256]{2,1,0:T(8,128)(2,1)} %fence.7), calls=%async_computation | async-start | bytes 1048576 | tf_op jit(solution)/shard_map/all_to_all | solution.py:353
  56.5 0.9 collective-permute-done.12.refs_11_.refs_12_
  58.8 8.3 %project.1.refs_3_ = f32[1024,512]{1,0:T(8,128)} custom-call(s32[2]{0:T(128)} %pad_add_fusion.refs_0_, bf16[16,2048]{1,0:T(8,128)(2,1)} %refs_1_.3, bf16[16,1024]{1,0:T(8,128)(2,1)} %refs_2_.3, bf16[128,3200]{1,0:T(8,128)(2,1)} %copy-done, bf16[128,3200]{1,0:T(8,128)(2,1)} %collective-permute-done.1.refs_4_.refs_5_, bf16[128,3200]{1,0:T(8,128)(2,1)} %fence.6.refs_5_.refs_6_, ...), custom_call_target="tpu_custom_call" | custom-call | tf_op jit(solution)/shard_map/project/pallas_call | solution.py:290
  67.1 4.3 %collective-permute-done.14.refs_22_ = bf16[768,512]{1,0:T(8,128)(2,1)} collective-permute-done((bf16[768,512]{1,0:T(8,128)(2,1)}, bf16[768,512]{1,0:T(8,128)(2,1)}, u32[]{:S(2)}, u32[]{:S(2)}) %collective-permute-start.14) | collective-permute-done | bytes 786464 | tf_op jit(solution)/shard_map/ppermute | solution.py:332
  71.4 9.5 %attend.1 = (bf16[8,32,384]{2,1,0:T(8,128)(2,1)}, f32[16,384]{1,0:T(8,128)}) custom-call(s32[2]{0:T(128)} %pad_add_fusion.refs_0_, bf16[16,2048]{1,0:T(8,128)(2,1)} %refs_1_.3, bf16[16,1024]{1,0:T(8,128)(2,1)} %refs_2_.3, f32[1024,512]{1,0:T(8,128)} %project.1.refs_3_, bf16[128,3200]{1,0:T(8,128)(2,1)} %copy-done, ...), custom_call_target="tpu_custom_call" | custom-call | tf_op jit(solution)/shard_map/attend/pallas_call | solution.py:308
  80.9 3.4 %all-to-all-start.1 = ((bf16[8,32,384]{2,1,0:T(8,128)(2,1)}), bf16[8,32,384]{2,1,0:T(8,128)(2,1)S(1)}, u32[]{:S(2)}, u32[]{:S(2)}) async-start(bf16[8,32,384]{2,1,0:T(8,128)(2,1)} %get-tuple-element.14), calls=%async_computation.1 | async-start | bytes 393216 | tf_op jit(solution)/shard_map/all_to_all | solution.py:462
  85.1 4.8 %all-to-all-done.1 = bf16[8,32,384]{2,1,0:T(8,128)(2,1)S(1)} async-done(((bf16[8,32,384]{2,1,0:T(8,128)(2,1)}), bf16[8,32,384]{2,1,0:T(8,128)(2,1)S(1)}, u32[]{:S(2)}, u32[]{:S(2)}) %all-to-all-start.1) | async-done | bytes 196640 | tf_op jit(solution)/shard_map/all_to_all | solution.py:462
  90.8 3.2 %collective-permute-done.15 = bf16[48,384]{1,0:T(8,128)(2,1)S(1)} collective-permute-done((bf16[48,384]{1,0:T(8,128)(2,1)S(1)}, bf16[48,384]{1,0:T(8,128)(2,1)S(1)}, u32[]{:S(2)}, u32[]{:S(2)}) %collective-permute-start.15) | collective-permute-done | bytes 36896 | tf_op jit(solution)/shard_map/ppermute | solution.py:42
  94.0 2.2 %collective-permute-start.16 = (bf16[48,384]{1,0:T(8,128)(2,1)S(1)}, bf16[48,384]{1,0:T(8,128)(2,1)S(1)}, u32[]{:S(2)}, u32[]{:S(2)}) collective-permute-start(bf16[48,384]{1,0:T(8,128)(2,1)S(1)} %add_convert_fusion.1), channel_id=1, source_target_pairs={{0,8},{4,12},{8,0},{12,4},{1,9},{5,13},{9,1},{13,5},{2,10},{6,14},... | collective-permute-start | bytes 110600 | tf_op jit(solution)/shard_map/ppermute | solution.py:42
  96.2 2.8 %collective-permute-done.16 = bf16[48,384]{1,0:T(8,128)(2,1)S(1)} collective-permute-done((bf16[48,384]{1,0:T(8,128)(2,1)S(1)}, bf16[48,384]{1,0:T(8,128)(2,1)S(1)}, u32[]{:S(2)}, u32[]{:S(2)}) %collective-permute-start.16) | collective-permute-done | bytes 36896 | tf_op jit(solution)/shard_map/ppermute | solution.py:42
  99.0 1.2 %collective-permute-start.17 = (bf16[48,384]{1,0:T(8,128)(2,1)S(1)}, bf16[48,384]{1,0:T(8,128)(2,1)S(1)}, u32[]{:S(2)}, u32[]{:S(2)}) collective-permute-start(bf16[48,384]{1,0:T(8,128)(2,1)S(1)} %multiply_convert_fusion), channel_id=1, source_target_pairs={{0,18},{2,16},{16,2},{18,0},{1,19},{3,17},{17,3},{19,1},{4,22},{6,... | collective-permute-start | bytes 110600 | tf_op jit(solution)/shard_map/ppermute | solution.py:42
  100.2 1.5 %collective-permute-start.19 = (bf16[48,384]{1,0:T(8,128)(2,1)S(1)}, bf16[48,384]{1,0:T(8,128)(2,1)S(1)}, u32[]{:S(2)}, u32[]{:S(2)}) collective-permute-start(bf16[48,384]{1,0:T(8,128)(2,1)S(1)} %multiply_convert_fusion), channel_id=1, source_target_pairs={{0,16},{2,18},{16,0},{18,2},{1,17},{3,19},{17,1},{19,3},{4,20},{6,... | collective-permute-start | bytes 110600 | tf_op jit(solution)/shard_map/ppermute | solution.py:42
  102.5 1.4 %collective-permute-done.17 = bf16[48,384]{1,0:T(8,128)(2,1)S(1)} collective-permute-done((bf16[48,384]{1,0:T(8,128)(2,1)S(1)}, bf16[48,384]{1,0:T(8,128)(2,1)S(1)}, u32[]{:S(2)}, u32[]{:S(2)}) %collective-permute-start.17) | collective-permute-done | bytes 36896 | tf_op jit(solution)/shard_map/ppermute | solution.py:42
  104.4 1.2 %collective-permute-done.21 = bf16[48,384]{1,0:T(8,128)(2,1)S(1)} collective-permute-done((bf16[48,384]{1,0:T(8,128)(2,1)S(1)}, bf16[48,384]{1,0:T(8,128)(2,1)S(1)}, u32[]{:S(2)}, u32[]{:S(2)}) %collective-permute-start.21) | collective-permute-done | bytes 36896 | tf_op jit(solution)/shard_map/ppermute | solution.py:42
  105.6 1.2 %collective-permute-done.22 = bf16[48,384]{1,0:T(8,128)(2,1)S(1)} collective-permute-done((bf16[48,384]{1,0:T(8,128)(2,1)S(1)}, bf16[48,384]{1,0:T(8,128)(2,1)S(1)}, u32[]{:S(2)}, u32[]{:S(2)}) %collective-permute-start.22) | collective-permute-done | bytes 36896 | tf_op jit(solution)/shard_map/ppermute | solution.py:42
  (113 shorter events, 13.7 us)
Async XLA Ops:
  3.7 1.9 %collective-permute-start = (bf16[2,192,512]{2,1,0:T(8,128)(2,1)S(1)}, bf16[2,192,512]{2,1,0:T(8,128)(2,1)S(1)}, u32[]{:S(2)}, u32[]{:S(2)}) collective-permute-start(bf16[2,192,512]{2,1,0:T(8,128)(2,1)S(1)} %pad_maximum_fusion.2), channel_id=1, source_target_pairs={{0,1},{1,0},{2,3},{3,2},{4,5},{5,4},{6,7},{7,6},{8,9},{9,8},{10,11... | collective-permute-start | bytes 1179656 | tf_op jit(solution)/shard_map/ppermute | solution.py:42
  5.6 4.8 %copy-start.2 = (bf16[1,128,3072]{2,1,0:T(8,128)(2,1)S(1)}, bf16[1,128,3072]{2,1,0:T(8,128)(2,1)}, u32[]{:S(2)}) copy-start(bf16[1,128,3072]{2,1,0:T(8,128)(2,1)} %param.11) | copy-start | bytes 2359300
  5.8 12.4 %collective-permute-start.2 = (bf16[384,512]{1,0:T(8,128)(2,1)S(1)}, bf16[384,512]{1,0:T(8,128)(2,1)S(1)}, u32[]{:S(2)}, u32[]{:S(2)}) collective-permute-start(bf16[384,512]{1,0:T(8,128)(2,1)S(1)} %pad_maximum_fusion.3.rest_0_), channel_id=1, source_target_pairs={{0,2},{2,0},{1,3},{3,1},{4,6},{6,4},{5,7},{7,5},{8,10},{10,8},{9,1... | collective-permute-start | bytes 1179656 | tf_op jit(solution)/shard_map/ppermute | solution.py:42
  8.8 6.5 %copy-start.13 = (bf16[384,512]{1,0:T(8,128)(2,1)}, bf16[384,512]{1,0:T(8,128)(2,1)S(1)}, u32[]{:S(2)}) copy-start(bf16[384,512]{1,0:T(8,128)(2,1)S(1)} %pad_maximum_fusion.4.refs_13_) | copy-start | bytes 1179652
  8.8 11.9 %collective-permute-start.3 = (bf16[384,512]{1,0:T(8,128)(2,1)S(1)}, bf16[384,512]{1,0:T(8,128)(2,1)}, u32[]{:S(2)}, u32[]{:S(2)}) collective-permute-start(bf16[384,512]{1,0:T(8,128)(2,1)S(1)} %pad_maximum_fusion.4.refs_13_), channel_id=1, source_target_pairs={{0,4},{4,12},{12,8},{8,0},{1,5},{5,13},{13,9},{9,1},{2,6},{6,14},{... | collective-permute-start | bytes 1179656 | tf_op jit(solution)/shard_map/ppermute | solution.py:332
  11.3 9.4 %copy-start.1 = (bf16[128,3200]{1,0:T(8,128)(2,1)}, bf16[128,3200]{1,0:T(8,128)(2,1)S(1)}, u32[]{:S(2)}) copy-start(bf16[128,3200]{1,0:T(8,128)(2,1)S(1)} %get-tuple-element.11.refs_0_) | copy-start | bytes 2457604
  11.3 20.3 %copy-start = (bf16[128,3200]{1,0:T(8,128)(2,1)}, bf16[128,3200]{1,0:T(8,128)(2,1)S(1)}, u32[]{:S(2)}) copy-start(bf16[128,3200]{1,0:T(8,128)(2,1)S(1)} %get-tuple-element.10.refs_3_.refs_4_) | copy-start | bytes 2457604
  11.3 20.3 %collective-permute-start.8 = (bf16[128,3200]{1,0:T(8,128)(2,1)S(1)}, bf16[128,3200]{1,0:T(8,128)(2,1)}, u32[]{:S(2)}, u32[]{:S(2)}) collective-permute-start(bf16[128,3200]{1,0:T(8,128)(2,1)S(1)} %get-tuple-element.10.refs_3_.refs_4_), channel_id=1, source_target_pairs={{0,16},{16,0},{1,17},{17,1},{2,18},{18,2},{3,19},{19,3},{4,20},{20... | collective-permute-start | bytes 2457608 | tf_op jit(solution)/shard_map/ppermute | solution.py:42
  18.1 11.7 %collective-permute-start.5 = (bf16[384,512]{1,0:T(8,128)(2,1)S(1)}, bf16[384,512]{1,0:T(8,128)(2,1)S(1)}, u32[]{:S(2)}, u32[]{:S(2)}) collective-permute-start(bf16[384,512]{1,0:T(8,128)(2,1)S(1)} %collective-permute-done.2.refs_2_.refs_14_), channel_id=1, source_target_pairs={{0,4},{4,12},{12,8},{8,0},{1,5},{5,13},{13,9},{9,1},{2,6},{6,14},{... | collective-permute-start | bytes 1179656 | tf_op jit(solution)/shard_map/ppermute | solution.py:332
  20.7 21.5 %collective-permute-start.4 = (bf16[128,3200]{1,0:T(8,128)(2,1)}, bf16[128,3200]{1,0:T(8,128)(2,1)S(1)}, u32[]{:S(2)}, u32[]{:S(2)}) collective-permute-start(bf16[128,3200]{1,0:T(8,128)(2,1)} %get-tuple-element.12), channel_id=1, source_target_pairs={{0,2},{2,0},{1,3},{3,1},{4,6},{6,4},{5,7},{7,5},{8,10},{10,8},{9,1... | collective-permute-start | bytes 2457608 | tf_op jit(solution)/shard_map/ppermute | solution.py:42
  30.9 19.4 %copy-start.9 = (bf16[768,512]{1,0:T(8,128)(2,1)}, bf16[768,512]{1,0:T(8,128)(2,1)S(1)}, u32[]{:S(2)}) copy-start(bf16[768,512]{1,0:T(8,128)(2,1)S(1)} %pad_maximum_fusion.refs_15_.refs_1_) | copy-start | bytes 2359300
  30.9 19.3 %collective-permute-start.6 = (bf16[768,512]{1,0:T(8,128)(2,1)S(1)}, bf16[768,512]{1,0:T(8,128)(2,1)}, u32[]{:S(2)}, u32[]{:S(2)}) collective-permute-start(bf16[768,512]{1,0:T(8,128)(2,1)S(1)} %pad_maximum_fusion.refs_15_.refs_1_), channel_id=1, source_target_pairs={{0,4},{4,12},{12,8},{8,0},{1,5},{5,13},{13,9},{9,1},{2,6},{6,14},{... | collective-permute-start | bytes 2359304 | tf_op jit(solution)/shard_map/ppermute | solution.py:332
  31.6 18.6 %collective-permute-start.9 = (bf16[128,3200]{1,0:T(8,128)(2,1)}, bf16[128,3200]{1,0:T(8,128)(2,1)S(1)}, u32[]{:S(2)}, u32[]{:S(2)}) collective-permute-start(bf16[128,3200]{1,0:T(8,128)(2,1)} %collective-permute-done.8.refs_7_.refs_8_), channel_id=1, source_target_pairs={{0,1},{1,0},{2,3},{3,2},{4,5},{5,4},{6,7},{7,6},{8,9},{9,8},{10,11... | collective-permute-start | bytes 2457608 | tf_op jit(solution)/shard_map/ppermute | solution.py:42
  31.6 24.9 %collective-permute-start.1 = (bf16[128,3200]{1,0:T(8,128)(2,1)S(1)}, bf16[128,3200]{1,0:T(8,128)(2,1)}, u32[]{:S(2)}, u32[]{:S(2)}) collective-permute-start(bf16[128,3200]{1,0:T(8,128)(2,1)S(1)} %get-tuple-element.10.refs_3_.refs_4_), channel_id=1, source_target_pairs={{0,1},{1,0},{2,3},{3,2},{4,5},{5,4},{6,7},{7,6},{8,9},{9,8},{10,11... | collective-permute-start | bytes 2457608 | tf_op jit(solution)/shard_map/ppermute | solution.py:42
  33.9 21.4 %collective-permute-start.10 = (bf16[64,3200]{1,0:T(8,128)(2,1)}, bf16[64,3200]{1,0:T(8,128)(2,1)}, u32[]{:S(2)}, u32[]{:S(2)}) collective-permute-start(bf16[64,3200]{1,0:T(8,128)(2,1)} %slice.156), channel_id=1, source_target_pairs={{0,2},{2,0},{1,3},{3,1},{4,6},{6,4},{5,7},{7,5},{8,10},{10,8},{9,1... | collective-permute-start | bytes 1228808 | tf_op jit(solution)/shard_map/ppermute | solution.py:42
  42.2 8.0 %copy-start.7 = (bf16[128,3200]{1,0:T(8,128)(2,1)}, bf16[128,3200]{1,0:T(8,128)(2,1)S(1)}, u32[]{:S(2)}) copy-start(bf16[128,3200]{1,0:T(8,128)(2,1)S(1)} %collective-permute-done.4.refs_0_) | copy-start | bytes 2457604
  43.0 12.8 %collective-permute-start.11 = (bf16[64,3200]{1,0:T(8,128)(2,1)}, bf16[64,3200]{1,0:T(8,128)(2,1)}, u32[]{:S(2)}, u32[]{:S(2)}) collective-permute-start(bf16[64,3200]{1,0:T(8,128)(2,1)} %slice.157), channel_id=1, source_target_pairs={{0,16},{16,0},{1,17},{17,1},{2,18},{18,2},{3,19},{19,3},{4,20},{20... | collective-permute-start | bytes 1228808 | tf_op jit(solution)/shard_map/ppermute | solution.py:42
  50.2 7.8 %collective-permute-start.7 = (bf16[128,3200]{1,0:T(8,128)(2,1)}, bf16[128,3200]{1,0:T(8,128)(2,1)}, u32[]{:S(2)}, u32[]{:S(2)}) collective-permute-start(bf16[128,3200]{1,0:T(8,128)(2,1)} %fence.6.refs_5_.refs_6_), channel_id=1, source_target_pairs={{0,1},{1,0},{2,3},{3,2},{4,5},{5,4},{6,7},{7,6},{8,9},{9,8},{10,11... | collective-permute-start | bytes 2457608 | tf_op jit(solution)/shard_map/ppermute | solution.py:42
  50.2 21.2 %collective-permute-start.14 = (bf16[768,512]{1,0:T(8,128)(2,1)}, bf16[768,512]{1,0:T(8,128)(2,1)}, u32[]{:S(2)}, u32[]{:S(2)}) collective-permute-start(bf16[768,512]{1,0:T(8,128)(2,1)} %collective-permute-done.6.refs_1_.refs_16_), channel_id=1, source_target_pairs={{0,4},{4,12},{12,8},{8,0},{1,5},{5,13},{13,9},{9,1},{2,6},{6,14},{... | collective-permute-start | bytes 2359304 | tf_op jit(solution)/shard_map/ppermute | solution.py:332
  51.1 15.9 %all-to-all-start = ((bf16[8,128,256]{2,1,0:T(8,128)(2,1)}), bf16[8,128,256]{2,1,0:T(8,128)(2,1)}, u32[]{:S(2)}, u32[]{:S(2)}) async-start(bf16[8,128,256]{2,1,0:T(8,128)(2,1)} %fence.7), calls=%async_computation | async-start | bytes 1048576 | tf_op jit(solution)/shard_map/all_to_all | solution.py:353
  55.3 2.1 %collective-permute-start.12 = (bf16[64,3200]{1,0:T(8,128)(2,1)}, bf16[64,3200]{1,0:T(8,128)(2,1)S(1)}, u32[]{:S(2)}, u32[]{:S(2)}) collective-permute-start(bf16[64,3200]{1,0:T(8,128)(2,1)} %collective-permute-done.10.refs_9_.refs_10_), channel_id=1, source_target_pairs={{0,1},{1,0},{2,3},{3,2},{4,5},{5,4},{6,7},{7,6},{8,9},{9,8},{10,11... | collective-permute-start | bytes 1228808 | tf_op jit(solution)/shard_map/ppermute | solution.py:42
  55.8 2.2 %collective-permute-start.13 = (bf16[64,3200]{1,0:T(8,128)(2,1)}, bf16[64,3200]{1,0:T(8,128)(2,1)S(1)}, u32[]{:S(2)}, u32[]{:S(2)}) collective-permute-start(bf16[64,3200]{1,0:T(8,128)(2,1)} %collective-permute-done.11.refs_10_.refs_11_), channel_id=1, source_target_pairs={{0,1},{1,0},{2,3},{3,2},{4,5},{5,4},{6,7},{7,6},{8,9},{9,8},{10,11... | collective-permute-start | bytes 1228808 | tf_op jit(solution)/shard_map/ppermute | solution.py:42
  80.9 9.0 %all-to-all-start.1 = ((bf16[8,32,384]{2,1,0:T(8,128)(2,1)}), bf16[8,32,384]{2,1,0:T(8,128)(2,1)S(1)}, u32[]{:S(2)}, u32[]{:S(2)}) async-start(bf16[8,32,384]{2,1,0:T(8,128)(2,1)} %get-tuple-element.14), calls=%async_computation.1 | async-start | bytes 393216 | tf_op jit(solution)/shard_map/all_to_all | solution.py:462
  90.0 4.0 %collective-permute-start.15 = (bf16[48,384]{1,0:T(8,128)(2,1)S(1)}, bf16[48,384]{1,0:T(8,128)(2,1)S(1)}, u32[]{:S(2)}, u32[]{:S(2)}) collective-permute-start(bf16[48,384]{1,0:T(8,128)(2,1)S(1)} %pad_maximum_fusion.5), channel_id=1, source_target_pairs={{0,4},{4,0},{8,12},{12,8},{1,5},{5,1},{9,13},{13,9},{2,6},{6,2},{1... | collective-permute-start | bytes 110600 | tf_op jit(solution)/shard_map/ppermute | solution.py:42
  94.0 4.9 %collective-permute-start.16 = (bf16[48,384]{1,0:T(8,128)(2,1)S(1)}, bf16[48,384]{1,0:T(8,128)(2,1)S(1)}, u32[]{:S(2)}, u32[]{:S(2)}) collective-permute-start(bf16[48,384]{1,0:T(8,128)(2,1)S(1)} %add_convert_fusion.1), channel_id=1, source_target_pairs={{0,8},{4,12},{8,0},{12,4},{1,9},{5,13},{9,1},{13,5},{2,10},{6,14},... | collective-permute-start | bytes 110600 | tf_op jit(solution)/shard_map/ppermute | solution.py:42
  99.0 4.9 %collective-permute-start.17 = (bf16[48,384]{1,0:T(8,128)(2,1)S(1)}, bf16[48,384]{1,0:T(8,128)(2,1)S(1)}, u32[]{:S(2)}, u32[]{:S(2)}) collective-permute-start(bf16[48,384]{1,0:T(8,128)(2,1)S(1)} %multiply_convert_fusion), channel_id=1, source_target_pairs={{0,18},{2,16},{16,2},{18,0},{1,19},{3,17},{17,3},{19,1},{4,22},{6,... | collective-permute-start | bytes 110600 | tf_op jit(solution)/shard_map/ppermute | solution.py:42
  100.2 4.0 %collective-permute-start.19 = (bf16[48,384]{1,0:T(8,128)(2,1)S(1)}, bf16[48,384]{1,0:T(8,128)(2,1)S(1)}, u32[]{:S(2)}, u32[]{:S(2)}) collective-permute-start(bf16[48,384]{1,0:T(8,128)(2,1)S(1)} %multiply_convert_fusion), channel_id=1, source_target_pairs={{0,16},{2,18},{16,0},{18,2},{1,17},{3,19},{17,1},{19,3},{4,20},{6,... | collective-permute-start | bytes 110600 | tf_op jit(solution)/shard_map/ppermute | solution.py:42
  101.6 4.0 %collective-permute-start.21 = (bf16[48,384]{1,0:T(8,128)(2,1)S(1)}, bf16[48,384]{1,0:T(8,128)(2,1)S(1)}, u32[]{:S(2)}, u32[]{:S(2)}) collective-permute-start(bf16[48,384]{1,0:T(8,128)(2,1)S(1)} %multiply_convert_fusion), channel_id=1, source_target_pairs={{0,2},{2,0},{16,18},{18,16},{1,3},{3,1},{17,19},{19,17},{4,6},{6,4... | collective-permute-start | bytes 110600 | tf_op jit(solution)/shard_map/ppermute | solution.py:42
  102.5 3.1 %collective-permute-start.23 = (bf16[48,384]{1,0:T(8,128)(2,1)S(1)}, bf16[48,384]{1,0:T(8,128)(2,1)S(1)}, u32[]{:S(2)}, u32[]{:S(2)}) collective-permute-start(bf16[48,384]{1,0:T(8,128)(2,1)S(1)} %multiply_convert_fusion), channel_id=1, source_target_pairs={{0,1},{1,0},{2,3},{3,2},{4,5},{5,4},{6,7},{7,6},{8,9},{9,8},{10,11... | collective-permute-start | bytes 110600 | tf_op jit(solution)/shard_map/ppermute | solution.py:42
  103.9 1.7 %collective-permute-start.18 = (bf16[48,384]{1,0:T(8,128)(2,1)S(1)}, bf16[48,384]{1,0:T(8,128)(2,1)S(1)}, u32[]{:S(2)}, u32[]{:S(2)}) collective-permute-start(bf16[48,384]{1,0:T(8,128)(2,1)S(1)} %collective-permute-done.17), channel_id=1, source_target_pairs={{0,1},{1,0},{2,3},{3,2},{4,5},{5,4},{6,7},{7,6},{8,9},{9,8},{10,11... | collective-permute-start | bytes 110600 | tf_op jit(solution)/shard_map/ppermute | solution.py:42
  104.1 1.5 %collective-permute-start.20 = (bf16[48,384]{1,0:T(8,128)(2,1)S(1)}, bf16[48,384]{1,0:T(8,128)(2,1)S(1)}, u32[]{:S(2)}, u32[]{:S(2)}) collective-permute-start(bf16[48,384]{1,0:T(8,128)(2,1)S(1)} %collective-permute-done.19), channel_id=1, source_target_pairs={{0,1},{1,0},{2,3},{3,2},{4,5},{5,4},{6,7},{7,6},{8,9},{9,8},{10,11... | collective-permute-start | bytes 110600 | tf_op jit(solution)/shard_map/ppermute | solution.py:42
  105.6 1.2 %collective-permute-start.22 = (bf16[48,384]{1,0:T(8,128)(2,1)S(1)}, bf16[48,384]{1,0:T(8,128)(2,1)S(1)}, u32[]{:S(2)}, u32[]{:S(2)}) collective-permute-start(bf16[48,384]{1,0:T(8,128)(2,1)S(1)} %collective-permute-done.21), channel_id=1, source_target_pairs={{0,1},{1,0},{2,3},{3,2},{4,5},{5,4},{6,7},{7,6},{8,9},{9,8},{10,11... | collective-permute-start | bytes 110600 | tf_op jit(solution)/shard_map/ppermute | solution.py:42
  (12 other events, 26.8 us)

commit v7 on v6

--- a/solution.py
+++ b/solution.py
@@ -329,7 +329,9 @@
 
 
 def ringed(value):
-    return lax.ppermute(value, "z", [(0, 1), (1, 3), (3, 2), (2, 0)])
+    steps = ((0, 1), (1, 3), (3, 2), (2, 0))
+    pairs = [(2 * a, 2 * b) for a, b in steps] + [(2 * b + 1, 2 * a + 1) for a, b in steps]
+    return lax.ppermute(value, ("z", "c"), pairs)
 
 
 def paired_gather(place, qw, kw, vw, heads, norm_args, gradient):
@@ -358,7 +360,7 @@
 
     def weight_columns(back):
         def columns(p):
-            at = (p[1] ^ (p[1] >> 1)) - back + 4 & 3
+            at = (p[1] ^ (p[1] >> 1)) - back * (1 - 2 * (p[0] & 1)) + 4 & 3
             return (at ^ (at >> 1)) * 4 * shard
 
         return columns

time: 109 us -> 109 us (level)
  starting transfers between devices: 28.8 us -> 32.1 us
  waiting for transfers between devices: 46.3 us -> 43.8 us
    ppermute x20, waiting for transfers between devices: 22.4 us -> 20.5 us  [swapped(): return lax.ppermute(value, axes, [(i, i ^ distance) for i in range(count)])]
    ppermute x4, starting transfers between devices: 4.45 us -> 6.08 us  [ringed(): return lax.ppermute(value, ('z', 'c'), pairs)]
    ppermute x20, starting transfers between devices: 16.8 us -> 18.2 us  [swapped(): return lax.ppermute(value, axes, [(i, i ^ distance) for i in range(count)])]
where the time goes in v7:
time: 109 us; the launch traced here: 108 us
  waiting for transfers between devices  43.8 us (40%)
  starting transfers between devices  32.1 us (29%)
  Pallas kernels  18.7 us (17%)
  local copies, waits for them, and re-layouts  9.59 us (9%)
  other arithmetic  2.76 us (3%)
  between operations  1.22 us (1%)
    ppermute x20, waiting for transfers between devices, swapped(): return lax.ppermute(value, axes, [(i, i ^ distance) for i in range(count)])  20.5 us
    ppermute x4, waiting for transfers between devices, ringed(): return lax.ppermute(value, ('z', 'c'), pairs)  18.3 us
    ppermute x20, starting transfers between devices, swapped(): return lax.ppermute(value, axes, [(i, i ^ distance) for i in range(count)])  18.2 us
    pallas_call x1, Pallas kernels, attend(): pl.pallas_call(functools.partial(attend_kernel, plan), out_shape=[jax.Sha...  9.52 us
    pallas_call x1, Pallas kernels, attend(): pl.pallas_call(functools.partial(project_kernel, plan), out_shape=jax.Sha...  8.29 us
    ppermute x4, starting transfers between devices, ringed(): return lax.ppermute(value, ('z', 'c'), pairs)  6.08 us
    all_to_all x1, waiting for transfers between devices, on_device(): lax.all_to_all(ga, GROUP, 0, 0, tiled=True).astype(jnp.float32)  4.91 us
    all_to_all x1, starting transfers between devices, paired_gather(): gradient = lax.all_to_all(gradient, GROUP, 0, 0, tiled=True)  4.16 us
  transfers between devices with their start and end apart: 26, of which 16 were waited for; matrix products, arithmetic and copies ran while one was open for 7% of the time, Pallas kernels for 8%

profile of v7, /device:TPU:0, one launch (start us, length us, event | category | flops | bytes accessed | tf_op | source)
XLA Modules:
  0.0 108.1 jit_solution(3639622115573618905)
XLA Ops:
  2.5 1.1 constant_dynamic-slice_fusion.11
  4.3 1.3 %collective-permute-done = bf16[2,192,512]{2,1,0:T(8,128)(2,1)S(1)} collective-permute-done((bf16[2,192,512]{2,1,0:T(8,128)(2,1)S(1)}, bf16[2,192,512]{2,1,0:T(8,128)(2,1)S(1)}, u32[]{:S(2)}, u32[]{:S(2)}) %collective-permute-start) | collective-permute-done | bytes 393248 | tf_op jit(solution)/shard_map/ppermute | solution.py:42
  5.8 3.0 %collective-permute-start.2 = (bf16[384,512]{1,0:T(8,128)(2,1)S(1)}, bf16[384,512]{1,0:T(8,128)(2,1)S(1)}, u32[]{:S(2)}, u32[]{:S(2)}) collective-permute-start(bf16[384,512]{1,0:T(8,128)(2,1)S(1)} %pad_maximum_fusion.3.rest_0_), channel_id=1, source_target_pairs={{0,2},{2,0},{1,3},{3,1},{4,6},{6,4},{5,7},{7,5},{8,10},{10,8},{9,1... | collective-permute-start | bytes 1179656 | tf_op jit(solution)/shard_map/ppermute | solution.py:42
  8.8 1.6 %collective-permute-start.3 = (bf16[384,512]{1,0:T(8,128)(2,1)S(1)}, bf16[384,512]{1,0:T(8,128)(2,1)}, u32[]{:S(2)}, u32[]{:S(2)}) collective-permute-start(bf16[384,512]{1,0:T(8,128)(2,1)S(1)} %pad_maximum_fusion.4.refs_13_), channel_id=1, source_target_pairs={{0,4},{4,12},{12,8},{8,0},{5,1},{13,5},{9,13},{1,9},{2,6},{6,14},{... | collective-permute-start | bytes 1179656 | tf_op jit(solution)/shard_map/ppermute | solution.py:334
  11.3 1.6 %collective-permute-start.8 = (bf16[128,3200]{1,0:T(8,128)(2,1)S(1)}, bf16[128,3200]{1,0:T(8,128)(2,1)}, u32[]{:S(2)}, u32[]{:S(2)}) collective-permute-start(bf16[128,3200]{1,0:T(8,128)(2,1)S(1)} %get-tuple-element.10.refs_3_.refs_4_), channel_id=1, source_target_pairs={{0,16},{16,0},{1,17},{17,1},{2,18},{18,2},{3,19},{19,3},{4,20},{20... | collective-permute-start | bytes 2457608 | tf_op jit(solution)/shard_map/ppermute | solution.py:42
  12.9 1.3 %copy.20 = bf16[1,128,2048]{1,2,0:T(8,128)(2,1)S(1)} copy(bf16[1,128,2048]{2,1,0:T(8,128)(2,1)} %param.21) | data formatting | bytes 1048576 | tf_op args[10]
  15.2 2.9 %collective-permute-done.2.refs_2_.refs_14_ = bf16[384,512]{1,0:T(8,128)(2,1)S(1)} collective-permute-done((bf16[384,512]{1,0:T(8,128)(2,1)S(1)}, bf16[384,512]{1,0:T(8,128)(2,1)S(1)}, u32[]{:S(2)}, u32[]{:S(2)}) %collective-permute-start.2) | collective-permute-done | bytes 393248 | tf_op jit(solution)/shard_map/ppermute | solution.py:42
  18.1 1.8 %collective-permute-start.5 = (bf16[384,512]{1,0:T(8,128)(2,1)S(1)}, bf16[384,512]{1,0:T(8,128)(2,1)S(1)}, u32[]{:S(2)}, u32[]{:S(2)}) collective-permute-start(bf16[384,512]{1,0:T(8,128)(2,1)S(1)} %collective-permute-done.2.refs_2_.refs_14_), channel_id=1, source_target_pairs={{0,4},{4,12},{12,8},{8,0},{5,1},{13,5},{9,13},{1,9},{2,6},{6,14},{... | collective-permute-start | bytes 1179656 | tf_op jit(solution)/shard_map/ppermute | solution.py:334
  19.9 1.9 %collective-permute-done.3.refs_0_ = bf16[384,512]{1,0:T(8,128)(2,1)} collective-permute-done((bf16[384,512]{1,0:T(8,128)(2,1)S(1)}, bf16[384,512]{1,0:T(8,128)(2,1)}, u32[]{:S(2)}, u32[]{:S(2)}) %collective-permute-start.3) | collective-permute-done | bytes 393248 | tf_op jit(solution)/shard_map/ppermute | solution.py:334
  22.1 8.7 %collective-permute-done.5 = bf16[384,512]{1,0:T(8,128)(2,1)S(1)} collective-permute-done((bf16[384,512]{1,0:T(8,128)(2,1)S(1)}, bf16[384,512]{1,0:T(8,128)(2,1)S(1)}, u32[]{:S(2)}, u32[]{:S(2)}) %collective-permute-start.5) | collective-permute-done | bytes 393248 | tf_op jit(solution)/shard_map/ppermute | solution.py:334
  30.7 1.0 pad_maximum_fusion.refs_15_.refs_1_
  33.0 1.8 %slice.156 = bf16[64,3200]{1,0:T(8,128)(2,1)} slice(bf16[128,3200]{1,0:T(8,128)(2,1)} %collective-permute-done.8.refs_7_.refs_8_), slice={[0:64], [0:3200]} | slice | bytes 819200 | tf_op jit(solution)/shard_map/slice | solution.py:352
  34.8 1.5 %collective-permute-start.10 = (bf16[64,3200]{1,0:T(8,128)(2,1)}, bf16[64,3200]{1,0:T(8,128)(2,1)}, u32[]{:S(2)}, u32[]{:S(2)}) collective-permute-start(bf16[64,3200]{1,0:T(8,128)(2,1)} %slice.156), channel_id=1, source_target_pairs={{0,2},{2,0},{1,3},{3,1},{4,6},{6,4},{5,7},{7,5},{8,10},{10,8},{9,1... | collective-permute-start | bytes 1228808 | tf_op jit(solution)/shard_map/ppermute | solution.py:42
  36.3 7.0 %collective-permute-done.4.refs_0_ = bf16[128,3200]{1,0:T(8,128)(2,1)S(1)} collective-permute-done((bf16[128,3200]{1,0:T(8,128)(2,1)}, bf16[128,3200]{1,0:T(8,128)(2,1)S(1)}, u32[]{:S(2)}, u32[]{:S(2)}) %collective-permute-start.4) | collective-permute-done | bytes 819232 | tf_op jit(solution)/shard_map/ppermute | solution.py:42
  44.1 1.5 %collective-permute-start.11 = (bf16[64,3200]{1,0:T(8,128)(2,1)}, bf16[64,3200]{1,0:T(8,128)(2,1)}, u32[]{:S(2)}, u32[]{:S(2)}) collective-permute-start(bf16[64,3200]{1,0:T(8,128)(2,1)} %slice.157), channel_id=1, source_target_pairs={{0,16},{16,0},{1,17},{17,1},{2,18},{18,2},{3,19},{19,3},{4,20},{20... | collective-permute-start | bytes 1228808 | tf_op jit(solution)/shard_map/ppermute | solution.py:42
  45.6 4.8 %collective-permute-done.6.refs_1_.refs_16_ = bf16[768,512]{1,0:T(8,128)(2,1)} collective-permute-done((bf16[768,512]{1,0:T(8,128)(2,1)S(1)}, bf16[768,512]{1,0:T(8,128)(2,1)}, u32[]{:S(2)}, u32[]{:S(2)}) %collective-permute-start.6) | collective-permute-done | bytes 786464 | tf_op jit(solution)/shard_map/ppermute | solution.py:334
  50.5 1.9 %collective-permute-start.14 = (bf16[768,512]{1,0:T(8,128)(2,1)}, bf16[768,512]{1,0:T(8,128)(2,1)}, u32[]{:S(2)}, u32[]{:S(2)}) collective-permute-start(bf16[768,512]{1,0:T(8,128)(2,1)} %collective-permute-done.6.refs_1_.refs_16_), channel_id=1, source_target_pairs={{0,4},{4,12},{12,8},{8,0},{5,1},{13,5},{9,13},{1,9},{2,6},{6,14},{... | collective-permute-start | bytes 2359304 | tf_op jit(solution)/shard_map/ppermute | solution.py:334
  52.4 4.2 %all-to-all-start = ((bf16[8,128,256]{2,1,0:T(8,128)(2,1)}), bf16[8,128,256]{2,1,0:T(8,128)(2,1)}, u32[]{:S(2)}, u32[]{:S(2)}) async-start(bf16[8,128,256]{2,1,0:T(8,128)(2,1)} %fence.7), calls=%async_computation | async-start | bytes 1048576 | tf_op jit(solution)/shard_map/all_to_all | solution.py:355
  60.0 8.3 %project.1.refs_3_ = f32[1024,512]{1,0:T(8,128)} custom-call(s32[2]{0:T(128)} %pad_add_fusion.refs_0_, bf16[16,2048]{1,0:T(8,128)(2,1)} %refs_1_.3, bf16[16,1024]{1,0:T(8,128)(2,1)} %refs_2_.3, bf16[128,3200]{1,0:T(8,128)(2,1)} %copy-done, bf16[128,3200]{1,0:T(8,128)(2,1)} %collective-permute-done.1.refs_4_.refs_5_, bf16[128,3200]{1,0:T(8,128)(2,1)} %fence.6.refs_5_.refs_6_, ...), custom_call_target="tpu_custom_call" | custom-call | tf_op jit(solution)/shard_map/project/pallas_call | solution.py:290
  68.3 3.0 %collective-permute-done.14.refs_22_ = bf16[768,512]{1,0:T(8,128)(2,1)} collective-permute-done((bf16[768,512]{1,0:T(8,128)(2,1)}, bf16[768,512]{1,0:T(8,128)(2,1)}, u32[]{:S(2)}, u32[]{:S(2)}) %collective-permute-start.14) | collective-permute-done | bytes 786464 | tf_op jit(solution)/shard_map/ppermute | solution.py:334
  71.2 9.5 %attend.1 = (bf16[8,32,384]{2,1,0:T(8,128)(2,1)}, f32[16,384]{1,0:T(8,128)}) custom-call(s32[2]{0:T(128)} %pad_add_fusion.refs_0_, bf16[16,2048]{1,0:T(8,128)(2,1)} %refs_1_.3, bf16[16,1024]{1,0:T(8,128)(2,1)} %refs_2_.3, f32[1024,512]{1,0:T(8,128)} %project.1.refs_3_, bf16[128,3200]{1,0:T(8,128)(2,1)} %copy-done, ...), custom_call_target="tpu_custom_call" | custom-call | tf_op jit(solution)/shard_map/attend/pallas_call | solution.py:308
  80.8 3.6 %all-to-all-start.1 = ((bf16[8,32,384]{2,1,0:T(8,128)(2,1)}), bf16[8,32,384]{2,1,0:T(8,128)(2,1)S(1)}, u32[]{:S(2)}, u32[]{:S(2)}) async-start(bf16[8,32,384]{2,1,0:T(8,128)(2,1)} %get-tuple-element.14), calls=%async_computation.1 | async-start | bytes 393216 | tf_op jit(solution)/shard_map/all_to_all | solution.py:464
  85.1 4.9 %all-to-all-done.1 = bf16[8,32,384]{2,1,0:T(8,128)(2,1)S(1)} async-done(((bf16[8,32,384]{2,1,0:T(8,128)(2,1)}), bf16[8,32,384]{2,1,0:T(8,128)(2,1)S(1)}, u32[]{:S(2)}, u32[]{:S(2)}) %all-to-all-start.1) | async-done | bytes 196640 | tf_op jit(solution)/shard_map/all_to_all | solution.py:464
  90.1 2.1 %collective-permute-start.15 = (bf16[48,384]{1,0:T(8,128)(2,1)S(1)}, bf16[48,384]{1,0:T(8,128)(2,1)S(1)}, u32[]{:S(2)}, u32[]{:S(2)}) collective-permute-start(bf16[48,384]{1,0:T(8,128)(2,1)S(1)} %pad_maximum_fusion.5), channel_id=1, source_target_pairs={{0,4},{4,0},{8,12},{12,8},{1,5},{5,1},{9,13},{13,9},{2,6},{6,2},{1... | collective-permute-start | bytes 110600 | tf_op jit(solution)/shard_map/ppermute | solution.py:42
  92.2 1.9 %collective-permute-done.15 = bf16[48,384]{1,0:T(8,128)(2,1)S(1)} collective-permute-done((bf16[48,384]{1,0:T(8,128)(2,1)S(1)}, bf16[48,384]{1,0:T(8,128)(2,1)S(1)}, u32[]{:S(2)}, u32[]{:S(2)}) %collective-permute-start.15) | collective-permute-done | bytes 36896 | tf_op jit(solution)/shard_map/ppermute | solution.py:42
  94.1 2.9 %collective-permute-start.16 = (bf16[48,384]{1,0:T(8,128)(2,1)S(1)}, bf16[48,384]{1,0:T(8,128)(2,1)S(1)}, u32[]{:S(2)}, u32[]{:S(2)}) collective-permute-start(bf16[48,384]{1,0:T(8,128)(2,1)S(1)} %add_convert_fusion.1), channel_id=1, source_target_pairs={{0,8},{4,12},{8,0},{12,4},{1,9},{5,13},{9,1},{13,5},{2,10},{6,14},... | collective-permute-start | bytes 110600 | tf_op jit(solution)/shard_map/ppermute | solution.py:42
  97.1 2.0 %collective-permute-done.16 = bf16[48,384]{1,0:T(8,128)(2,1)S(1)} collective-permute-done((bf16[48,384]{1,0:T(8,128)(2,1)S(1)}, bf16[48,384]{1,0:T(8,128)(2,1)S(1)}, u32[]{:S(2)}, u32[]{:S(2)}) %collective-permute-start.16) | collective-permute-done | bytes 36896 | tf_op jit(solution)/shard_map/ppermute | solution.py:42
  99.1 1.2 %collective-permute-start.17 = (bf16[48,384]{1,0:T(8,128)(2,1)S(1)}, bf16[48,384]{1,0:T(8,128)(2,1)S(1)}, u32[]{:S(2)}, u32[]{:S(2)}) collective-permute-start(bf16[48,384]{1,0:T(8,128)(2,1)S(1)} %multiply_convert_fusion), channel_id=1, source_target_pairs={{0,18},{2,16},{16,2},{18,0},{1,19},{3,17},{17,3},{19,1},{4,22},{6,... | collective-permute-start | bytes 110600 | tf_op jit(solution)/shard_map/ppermute | solution.py:42
  100.3 1.5 %collective-permute-start.19 = (bf16[48,384]{1,0:T(8,128)(2,1)S(1)}, bf16[48,384]{1,0:T(8,128)(2,1)S(1)}, u32[]{:S(2)}, u32[]{:S(2)}) collective-permute-start(bf16[48,384]{1,0:T(8,128)(2,1)S(1)} %multiply_convert_fusion), channel_id=1, source_target_pairs={{0,16},{2,18},{16,0},{18,2},{1,17},{3,19},{17,1},{19,3},{4,20},{6,... | collective-permute-start | bytes 110600 | tf_op jit(solution)/shard_map/ppermute | solution.py:42
  102.6 1.4 %collective-permute-done.17 = bf16[48,384]{1,0:T(8,128)(2,1)S(1)} collective-permute-done((bf16[48,384]{1,0:T(8,128)(2,1)S(1)}, bf16[48,384]{1,0:T(8,128)(2,1)S(1)}, u32[]{:S(2)}, u32[]{:S(2)}) %collective-permute-start.17) | collective-permute-done | bytes 36896 | tf_op jit(solution)/shard_map/ppermute | solution.py:42
  104.5 1.2 %collective-permute-done.21 = bf16[48,384]{1,0:T(8,128)(2,1)S(1)} collective-permute-done((bf16[48,384]{1,0:T(8,128)(2,1)S(1)}, bf16[48,384]{1,0:T(8,128)(2,1)S(1)}, u32[]{:S(2)}, u32[]{:S(2)}) %collective-permute-start.21) | collective-permute-done | bytes 36896 | tf_op jit(solution)/shard_map/ppermute | solution.py:42
  105.7 1.2 %collective-permute-done.22 = bf16[48,384]{1,0:T(8,128)(2,1)S(1)} collective-permute-done((bf16[48,384]{1,0:T(8,128)(2,1)S(1)}, bf16[48,384]{1,0:T(8,128)(2,1)S(1)}, u32[]{:S(2)}, u32[]{:S(2)}) %collective-permute-start.22) | collective-permute-done | bytes 36896 | tf_op jit(solution)/shard_map/ppermute | solution.py:42
  (113 shorter events, 13.4 us)
Async XLA Ops:
  3.7 1.9 %collective-permute-start = (bf16[2,192,512]{2,1,0:T(8,128)(2,1)S(1)}, bf16[2,192,512]{2,1,0:T(8,128)(2,1)S(1)}, u32[]{:S(2)}, u32[]{:S(2)}) collective-permute-start(bf16[2,192,512]{2,1,0:T(8,128)(2,1)S(1)} %pad_maximum_fusion.2), channel_id=1, source_target_pairs={{0,1},{1,0},{2,3},{3,2},{4,5},{5,4},{6,7},{7,6},{8,9},{9,8},{10,11... | collective-permute-start | bytes 1179656 | tf_op jit(solution)/shard_map/ppermute | solution.py:42
  5.6 4.8 %copy-start.2 = (bf16[1,128,3072]{2,1,0:T(8,128)(2,1)S(1)}, bf16[1,128,3072]{2,1,0:T(8,128)(2,1)}, u32[]{:S(2)}) copy-start(bf16[1,128,3072]{2,1,0:T(8,128)(2,1)} %param.11) | copy-start | bytes 2359300
  5.8 12.4 %collective-permute-start.2 = (bf16[384,512]{1,0:T(8,128)(2,1)S(1)}, bf16[384,512]{1,0:T(8,128)(2,1)S(1)}, u32[]{:S(2)}, u32[]{:S(2)}) collective-permute-start(bf16[384,512]{1,0:T(8,128)(2,1)S(1)} %pad_maximum_fusion.3.rest_0_), channel_id=1, source_target_pairs={{0,2},{2,0},{1,3},{3,1},{4,6},{6,4},{5,7},{7,5},{8,10},{10,8},{9,1... | collective-permute-start | bytes 1179656 | tf_op jit(solution)/shard_map/ppermute | solution.py:42
  8.8 6.5 %copy-start.13 = (bf16[384,512]{1,0:T(8,128)(2,1)}, bf16[384,512]{1,0:T(8,128)(2,1)S(1)}, u32[]{:S(2)}) copy-start(bf16[384,512]{1,0:T(8,128)(2,1)S(1)} %pad_maximum_fusion.4.refs_13_) | copy-start | bytes 1179652
  8.8 13.1 %collective-permute-start.3 = (bf16[384,512]{1,0:T(8,128)(2,1)S(1)}, bf16[384,512]{1,0:T(8,128)(2,1)}, u32[]{:S(2)}, u32[]{:S(2)}) collective-permute-start(bf16[384,512]{1,0:T(8,128)(2,1)S(1)} %pad_maximum_fusion.4.refs_13_), channel_id=1, source_target_pairs={{0,4},{4,12},{12,8},{8,0},{5,1},{13,5},{9,13},{1,9},{2,6},{6,14},{... | collective-permute-start | bytes 1179656 | tf_op jit(solution)/shard_map/ppermute | solution.py:334
  11.3 10.5 %copy-start.1 = (bf16[128,3200]{1,0:T(8,128)(2,1)}, bf16[128,3200]{1,0:T(8,128)(2,1)S(1)}, u32[]{:S(2)}) copy-start(bf16[128,3200]{1,0:T(8,128)(2,1)S(1)} %get-tuple-element.11.refs_0_) | copy-start | bytes 2457604
  11.3 21.2 %copy-start = (bf16[128,3200]{1,0:T(8,128)(2,1)}, bf16[128,3200]{1,0:T(8,128)(2,1)S(1)}, u32[]{:S(2)}) copy-start(bf16[128,3200]{1,0:T(8,128)(2,1)S(1)} %get-tuple-element.10.refs_3_.refs_4_) | copy-start | bytes 2457604
  11.3 21.2 %collective-permute-start.8 = (bf16[128,3200]{1,0:T(8,128)(2,1)S(1)}, bf16[128,3200]{1,0:T(8,128)(2,1)}, u32[]{:S(2)}, u32[]{:S(2)}) collective-permute-start(bf16[128,3200]{1,0:T(8,128)(2,1)S(1)} %get-tuple-element.10.refs_3_.refs_4_), channel_id=1, source_target_pairs={{0,16},{16,0},{1,17},{17,1},{2,18},{18,2},{3,19},{19,3},{4,20},{20... | collective-permute-start | bytes 2457608 | tf_op jit(solution)/shard_map/ppermute | solution.py:42
  18.1 12.6 %collective-permute-start.5 = (bf16[384,512]{1,0:T(8,128)(2,1)S(1)}, bf16[384,512]{1,0:T(8,128)(2,1)S(1)}, u32[]{:S(2)}, u32[]{:S(2)}) collective-permute-start(bf16[384,512]{1,0:T(8,128)(2,1)S(1)} %collective-permute-done.2.refs_2_.refs_14_), channel_id=1, source_target_pairs={{0,4},{4,12},{12,8},{8,0},{5,1},{13,5},{9,13},{1,9},{2,6},{6,14},{... | collective-permute-start | bytes 1179656 | tf_op jit(solution)/shard_map/ppermute | solution.py:334
  21.8 21.5 %collective-permute-start.4 = (bf16[128,3200]{1,0:T(8,128)(2,1)}, bf16[128,3200]{1,0:T(8,128)(2,1)S(1)}, u32[]{:S(2)}, u32[]{:S(2)}) collective-permute-start(bf16[128,3200]{1,0:T(8,128)(2,1)} %get-tuple-element.12), channel_id=1, source_target_pairs={{0,2},{2,0},{1,3},{3,1},{4,6},{6,4},{5,7},{7,5},{8,10},{10,8},{9,1... | collective-permute-start | bytes 2457608 | tf_op jit(solution)/shard_map/ppermute | solution.py:42
  31.8 18.7 %copy-start.9 = (bf16[768,512]{1,0:T(8,128)(2,1)}, bf16[768,512]{1,0:T(8,128)(2,1)S(1)}, u32[]{:S(2)}) copy-start(bf16[768,512]{1,0:T(8,128)(2,1)S(1)} %pad_maximum_fusion.refs_15_.refs_1_) | copy-start | bytes 2359300
  31.8 18.6 %collective-permute-start.6 = (bf16[768,512]{1,0:T(8,128)(2,1)S(1)}, bf16[768,512]{1,0:T(8,128)(2,1)}, u32[]{:S(2)}, u32[]{:S(2)}) collective-permute-start(bf16[768,512]{1,0:T(8,128)(2,1)S(1)} %pad_maximum_fusion.refs_15_.refs_1_), channel_id=1, source_target_pairs={{0,4},{4,12},{12,8},{8,0},{5,1},{13,5},{9,13},{1,9},{2,6},{6,14},{... | collective-permute-start | bytes 2359304 | tf_op jit(solution)/shard_map/ppermute | solution.py:334
  32.5 17.9 %collective-permute-start.9 = (bf16[128,3200]{1,0:T(8,128)(2,1)}, bf16[128,3200]{1,0:T(8,128)(2,1)S(1)}, u32[]{:S(2)}, u32[]{:S(2)}) collective-permute-start(bf16[128,3200]{1,0:T(8,128)(2,1)} %collective-permute-done.8.refs_7_.refs_8_), channel_id=1, source_target_pairs={{0,1},{1,0},{2,3},{3,2},{4,5},{5,4},{6,7},{7,6},{8,9},{9,8},{10,11... | collective-permute-start | bytes 2457608 | tf_op jit(solution)/shard_map/ppermute | solution.py:42
  32.5 25.2 %collective-permute-start.1 = (bf16[128,3200]{1,0:T(8,128)(2,1)S(1)}, bf16[128,3200]{1,0:T(8,128)(2,1)}, u32[]{:S(2)}, u32[]{:S(2)}) collective-permute-start(bf16[128,3200]{1,0:T(8,128)(2,1)S(1)} %get-tuple-element.10.refs_3_.refs_4_), channel_id=1, source_target_pairs={{0,1},{1,0},{2,3},{3,2},{4,5},{5,4},{6,7},{7,6},{8,9},{9,8},{10,11... | collective-permute-start | bytes 2457608 | tf_op jit(solution)/shard_map/ppermute | solution.py:42
  34.8 21.8 %collective-permute-start.10 = (bf16[64,3200]{1,0:T(8,128)(2,1)}, bf16[64,3200]{1,0:T(8,128)(2,1)}, u32[]{:S(2)}, u32[]{:S(2)}) collective-permute-start(bf16[64,3200]{1,0:T(8,128)(2,1)} %slice.156), channel_id=1, source_target_pairs={{0,2},{2,0},{1,3},{3,1},{4,6},{6,4},{5,7},{7,5},{8,10},{10,8},{9,1... | collective-permute-start | bytes 1228808 | tf_op jit(solution)/shard_map/ppermute | solution.py:42
  43.3 7.1 %copy-start.7 = (bf16[128,3200]{1,0:T(8,128)(2,1)}, bf16[128,3200]{1,0:T(8,128)(2,1)S(1)}, u32[]{:S(2)}) copy-start(bf16[128,3200]{1,0:T(8,128)(2,1)S(1)} %collective-permute-done.4.refs_0_) | copy-start | bytes 2457604
  44.1 12.8 %collective-permute-start.11 = (bf16[64,3200]{1,0:T(8,128)(2,1)}, bf16[64,3200]{1,0:T(8,128)(2,1)}, u32[]{:S(2)}, u32[]{:S(2)}) collective-permute-start(bf16[64,3200]{1,0:T(8,128)(2,1)} %slice.157), channel_id=1, source_target_pairs={{0,16},{16,0},{1,17},{17,1},{2,18},{18,2},{3,19},{19,3},{4,20},{20... | collective-permute-start | bytes 1228808 | tf_op jit(solution)/shard_map/ppermute | solution.py:42
  50.4 8.7 %collective-permute-start.7 = (bf16[128,3200]{1,0:T(8,128)(2,1)}, bf16[128,3200]{1,0:T(8,128)(2,1)}, u32[]{:S(2)}, u32[]{:S(2)}) collective-permute-start(bf16[128,3200]{1,0:T(8,128)(2,1)} %fence.6.refs_5_.refs_6_), channel_id=1, source_target_pairs={{0,1},{1,0},{2,3},{3,2},{4,5},{5,4},{6,7},{7,6},{8,9},{9,8},{10,11... | collective-permute-start | bytes 2457608 | tf_op jit(solution)/shard_map/ppermute | solution.py:42
  50.5 20.8 %collective-permute-start.14 = (bf16[768,512]{1,0:T(8,128)(2,1)}, bf16[768,512]{1,0:T(8,128)(2,1)}, u32[]{:S(2)}, u32[]{:S(2)}) collective-permute-start(bf16[768,512]{1,0:T(8,128)(2,1)} %collective-permute-done.6.refs_1_.refs_16_), channel_id=1, source_target_pairs={{0,4},{4,12},{12,8},{8,0},{5,1},{13,5},{9,13},{1,9},{2,6},{6,14},{... | collective-permute-start | bytes 2359304 | tf_op jit(solution)/shard_map/ppermute | solution.py:334
  52.4 15.9 %all-to-all-start = ((bf16[8,128,256]{2,1,0:T(8,128)(2,1)}), bf16[8,128,256]{2,1,0:T(8,128)(2,1)}, u32[]{:S(2)}, u32[]{:S(2)}) async-start(bf16[8,128,256]{2,1,0:T(8,128)(2,1)} %fence.7), calls=%async_computation | async-start | bytes 1048576 | tf_op jit(solution)/shard_map/all_to_all | solution.py:355
  56.6 2.0 %collective-permute-start.12 = (bf16[64,3200]{1,0:T(8,128)(2,1)}, bf16[64,3200]{1,0:T(8,128)(2,1)S(1)}, u32[]{:S(2)}, u32[]{:S(2)}) collective-permute-start(bf16[64,3200]{1,0:T(8,128)(2,1)} %collective-permute-done.10.refs_9_.refs_10_), channel_id=1, source_target_pairs={{0,1},{1,0},{2,3},{3,2},{4,5},{5,4},{6,7},{7,6},{8,9},{9,8},{10,11... | collective-permute-start | bytes 1228808 | tf_op jit(solution)/shard_map/ppermute | solution.py:42
  56.9 2.2 %collective-permute-start.13 = (bf16[64,3200]{1,0:T(8,128)(2,1)}, bf16[64,3200]{1,0:T(8,128)(2,1)S(1)}, u32[]{:S(2)}, u32[]{:S(2)}) collective-permute-start(bf16[64,3200]{1,0:T(8,128)(2,1)} %collective-permute-done.11.refs_10_.refs_11_), channel_id=1, source_target_pairs={{0,1},{1,0},{2,3},{3,2},{4,5},{5,4},{6,7},{7,6},{8,9},{9,8},{10,11... | collective-permute-start | bytes 1228808 | tf_op jit(solution)/shard_map/ppermute | solution.py:42
  80.8 9.3 %all-to-all-start.1 = ((bf16[8,32,384]{2,1,0:T(8,128)(2,1)}), bf16[8,32,384]{2,1,0:T(8,128)(2,1)S(1)}, u32[]{:S(2)}, u32[]{:S(2)}) async-start(bf16[8,32,384]{2,1,0:T(8,128)(2,1)} %get-tuple-element.14), calls=%async_computation.1 | async-start | bytes 393216 | tf_op jit(solution)/shard_map/all_to_all | solution.py:464
  90.1 4.0 %collective-permute-start.15 = (bf16[48,384]{1,0:T(8,128)(2,1)S(1)}, bf16[48,384]{1,0:T(8,128)(2,1)S(1)}, u32[]{:S(2)}, u32[]{:S(2)}) collective-permute-start(bf16[48,384]{1,0:T(8,128)(2,1)S(1)} %pad_maximum_fusion.5), channel_id=1, source_target_pairs={{0,4},{4,0},{8,12},{12,8},{1,5},{5,1},{9,13},{13,9},{2,6},{6,2},{1... | collective-permute-start | bytes 110600 | tf_op jit(solution)/shard_map/ppermute | solution.py:42
  94.1 4.9 %collective-permute-start.16 = (bf16[48,384]{1,0:T(8,128)(2,1)S(1)}, bf16[48,384]{1,0:T(8,128)(2,1)S(1)}, u32[]{:S(2)}, u32[]{:S(2)}) collective-permute-start(bf16[48,384]{1,0:T(8,128)(2,1)S(1)} %add_convert_fusion.1), channel_id=1, source_target_pairs={{0,8},{4,12},{8,0},{12,4},{1,9},{5,13},{9,1},{13,5},{2,10},{6,14},... | collective-permute-start | bytes 110600 | tf_op jit(solution)/shard_map/ppermute | solution.py:42
  99.1 4.9 %collective-permute-start.17 = (bf16[48,384]{1,0:T(8,128)(2,1)S(1)}, bf16[48,384]{1,0:T(8,128)(2,1)S(1)}, u32[]{:S(2)}, u32[]{:S(2)}) collective-permute-start(bf16[48,384]{1,0:T(8,128)(2,1)S(1)} %multiply_convert_fusion), channel_id=1, source_target_pairs={{0,18},{2,16},{16,2},{18,0},{1,19},{3,17},{17,3},{19,1},{4,22},{6,... | collective-permute-start | bytes 110600 | tf_op jit(solution)/shard_map/ppermute | solution.py:42
  100.3 4.0 %collective-permute-start.19 = (bf16[48,384]{1,0:T(8,128)(2,1)S(1)}, bf16[48,384]{1,0:T(8,128)(2,1)S(1)}, u32[]{:S(2)}, u32[]{:S(2)}) collective-permute-start(bf16[48,384]{1,0:T(8,128)(2,1)S(1)} %multiply_convert_fusion), channel_id=1, source_target_pairs={{0,16},{2,18},{16,0},{18,2},{1,17},{3,19},{17,1},{19,3},{4,20},{6,... | collective-permute-start | bytes 110600 | tf_op jit(solution)/shard_map/ppermute | solution.py:42
  101.7 4.0 %collective-permute-start.21 = (bf16[48,384]{1,0:T(8,128)(2,1)S(1)}, bf16[48,384]{1,0:T(8,128)(2,1)S(1)}, u32[]{:S(2)}, u32[]{:S(2)}) collective-permute-start(bf16[48,384]{1,0:T(8,128)(2,1)S(1)} %multiply_convert_fusion), channel_id=1, source_target_pairs={{0,2},{2,0},{16,18},{18,16},{1,3},{3,1},{17,19},{19,17},{4,6},{6,4... | collective-permute-start | bytes 110600 | tf_op jit(solution)/shard_map/ppermute | solution.py:42
  102.6 3.1 %collective-permute-start.23 = (bf16[48,384]{1,0:T(8,128)(2,1)S(1)}, bf16[48,384]{1,0:T(8,128)(2,1)S(1)}, u32[]{:S(2)}, u32[]{:S(2)}) collective-permute-start(bf16[48,384]{1,0:T(8,128)(2,1)S(1)} %multiply_convert_fusion), channel_id=1, source_target_pairs={{0,1},{1,0},{2,3},{3,2},{4,5},{5,4},{6,7},{7,6},{8,9},{9,8},{10,11... | collective-permute-start | bytes 110600 | tf_op jit(solution)/shard_map/ppermute | solution.py:42
  104.0 1.7 %collective-permute-start.18 = (bf16[48,384]{1,0:T(8,128)(2,1)S(1)}, bf16[48,384]{1,0:T(8,128)(2,1)S(1)}, u32[]{:S(2)}, u32[]{:S(2)}) collective-permute-start(bf16[48,384]{1,0:T(8,128)(2,1)S(1)} %collective-permute-done.17), channel_id=1, source_target_pairs={{0,1},{1,0},{2,3},{3,2},{4,5},{5,4},{6,7},{7,6},{8,9},{9,8},{10,11... | collective-permute-start | bytes 110600 | tf_op jit(solution)/shard_map/ppermute | solution.py:42
  104.2 1.5 %collective-permute-start.20 = (bf16[48,384]{1,0:T(8,128)(2,1)S(1)}, bf16[48,384]{1,0:T(8,128)(2,1)S(1)}, u32[]{:S(2)}, u32[]{:S(2)}) collective-permute-start(bf16[48,384]{1,0:T(8,128)(2,1)S(1)} %collective-permute-done.19), channel_id=1, source_target_pairs={{0,1},{1,0},{2,3},{3,2},{4,5},{5,4},{6,7},{7,6},{8,9},{9,8},{10,11... | collective-permute-start | bytes 110600 | tf_op jit(solution)/shard_map/ppermute | solution.py:42
  105.7 1.2 %collective-permute-start.22 = (bf16[48,384]{1,0:T(8,128)(2,1)S(1)}, bf16[48,384]{1,0:T(8,128)(2,1)S(1)}, u32[]{:S(2)}, u32[]{:S(2)}) collective-permute-start(bf16[48,384]{1,0:T(8,128)(2,1)S(1)} %collective-permute-done.21), channel_id=1, source_target_pairs={{0,1},{1,0},{2,3},{3,2},{4,5},{5,4},{6,7},{7,6},{8,9},{9,8},{10,11... | collective-permute-start | bytes 110600 | tf_op jit(solution)/shard_map/ppermute | solution.py:42
  (12 other events, 28.9 us)

commit v8 on v6

--- a/solution.py
+++ b/solution.py
@@ -267,7 +267,9 @@
     gb_out[:, group:] = sums[rank : 2 * rank, group : group + HEAD_SIZE] + sums[rank : 2 * rank, group + HEAD_SIZE :]
     part = feats // parts
     for index in range(parts):
-        piece = dot(pulls[...], x_all[:, index * part : (index + 1) * part])
+        if index % 2 == 0:
+            pair = dot(pulls[...], x_all[:, index * part : min(index + 2, parts) * part])
+        piece = pair[:, (index % 2) * part : (index % 2 + 1) * part]
         ga_out[index, :rank] = piece[:rank].astype(ga_out.dtype)
         ga_out[index, rank:] = (piece[rank : 2 * rank] + piece[2 * rank :]).astype(ga_out.dtype)
 

time: 109 us -> 109 us (level)
  no operation moved by 1% of the time
where the time goes in v8:
time: 109 us; the launch traced here: 108 us
  waiting for transfers between devices  46.3 us (42%)
  starting transfers between devices  28.8 us (26%)
  Pallas kernels  18.8 us (17%)
  local copies, waits for them, and re-layouts  10.2 us (9%)
  other arithmetic  2.76 us (3%)
  between operations  1.23 us (1%)
    ppermute x20, waiting for transfers between devices, swapped(): return lax.ppermute(value, axes, [(i, i ^ distance) for i in range(count)])  22.4 us
    ppermute x4, waiting for transfers between devices, ringed(): return lax.ppermute(value, 'z', [(0, 1), (1, 3), (3, 2), (2, 0)])  19 us
    ppermute x20, starting transfers between devices, swapped(): return lax.ppermute(value, axes, [(i, i ^ distance) for i in range(count)])  16.8 us
    pallas_call x1, Pallas kernels, attend(): pl.pallas_call(functools.partial(attend_kernel, plan), out_shape=[jax.Sha...  9.67 us
    pallas_call x1, Pallas kernels, attend(): pl.pallas_call(functools.partial(project_kernel, plan), out_shape=jax.Sha...  8.29 us
    all_to_all x1, waiting for transfers between devices, on_device(): lax.all_to_all(ga, GROUP, 0, 0, tiled=True).astype(jnp.float32)  4.84 us
    ppermute x4, starting transfers between devices, ringed(): return lax.ppermute(value, 'z', [(0, 1), (1, 3), (3, 2), (2, 0)])  4.45 us
    all_to_all x1, starting transfers between devices, paired_gather(): gradient = lax.all_to_all(gradient, GROUP, 0, 0, tiled=True)  4.15 us
  transfers between devices with their start and end apart: 26, of which 16 were waited for; matrix products, arithmetic and copies ran while one was open for 7% of the time, Pallas kernels for 8%

profile of v8, /device:TPU:0, one launch (start us, length us, event | category | flops | bytes accessed | tf_op | source)
XLA Modules:
  0.0 108.1 jit_solution(10662271523463360176)
XLA Ops:
  0.7 0.9 constant_dynamic-slice_fusion.10
  2.5 1.1 constant_dynamic-slice_fusion.11
  4.3 1.3 %collective-permute-done = bf16[2,192,512]{2,1,0:T(8,128)(2,1)S(1)} collective-permute-done((bf16[2,192,512]{2,1,0:T(8,128)(2,1)S(1)}, bf16[2,192,512]{2,1,0:T(8,128)(2,1)S(1)}, u32[]{:S(2)}, u32[]{:S(2)}) %collective-permute-start) | collective-permute-done | bytes 393248 | tf_op jit(solution)/shard_map/ppermute | solution.py:42
  5.8 3.0 %collective-permute-start.2 = (bf16[384,512]{1,0:T(8,128)(2,1)S(1)}, bf16[384,512]{1,0:T(8,128)(2,1)S(1)}, u32[]{:S(2)}, u32[]{:S(2)}) collective-permute-start(bf16[384,512]{1,0:T(8,128)(2,1)S(1)} %pad_maximum_fusion.3.rest_0_), channel_id=1, source_target_pairs={{0,2},{2,0},{1,3},{3,1},{4,6},{6,4},{5,7},{7,5},{8,10},{10,8},{9,1... | collective-permute-start | bytes 1179656 | tf_op jit(solution)/shard_map/ppermute | solution.py:42
  8.8 1.6 %collective-permute-start.3 = (bf16[384,512]{1,0:T(8,128)(2,1)S(1)}, bf16[384,512]{1,0:T(8,128)(2,1)}, u32[]{:S(2)}, u32[]{:S(2)}) collective-permute-start(bf16[384,512]{1,0:T(8,128)(2,1)S(1)} %pad_maximum_fusion.4.refs_13_), channel_id=1, source_target_pairs={{0,4},{4,12},{12,8},{8,0},{1,5},{5,13},{13,9},{9,1},{2,6},{6,14},{... | collective-permute-start | bytes 1179656 | tf_op jit(solution)/shard_map/ppermute | solution.py:334
  11.3 1.6 %collective-permute-start.8 = (bf16[128,3200]{1,0:T(8,128)(2,1)S(1)}, bf16[128,3200]{1,0:T(8,128)(2,1)}, u32[]{:S(2)}, u32[]{:S(2)}) collective-permute-start(bf16[128,3200]{1,0:T(8,128)(2,1)S(1)} %get-tuple-element.10.refs_3_.refs_4_), channel_id=1, source_target_pairs={{0,16},{16,0},{1,17},{17,1},{2,18},{18,2},{3,19},{19,3},{4,20},{20... | collective-permute-start | bytes 2457608 | tf_op jit(solution)/shard_map/ppermute | solution.py:42
  12.9 1.3 %copy.20 = bf16[1,128,2048]{1,2,0:T(8,128)(2,1)S(1)} copy(bf16[1,128,2048]{2,1,0:T(8,128)(2,1)} %param.21) | data formatting | bytes 1048576 | tf_op args[10]
  14.2 1.0 copy.21
  15.2 2.9 %collective-permute-done.2.refs_2_.refs_14_ = bf16[384,512]{1,0:T(8,128)(2,1)S(1)} collective-permute-done((bf16[384,512]{1,0:T(8,128)(2,1)S(1)}, bf16[384,512]{1,0:T(8,128)(2,1)S(1)}, u32[]{:S(2)}, u32[]{:S(2)}) %collective-permute-start.2) | collective-permute-done | bytes 393248 | tf_op jit(solution)/shard_map/ppermute | solution.py:42
  18.1 1.8 %collective-permute-start.5 = (bf16[384,512]{1,0:T(8,128)(2,1)S(1)}, bf16[384,512]{1,0:T(8,128)(2,1)S(1)}, u32[]{:S(2)}, u32[]{:S(2)}) collective-permute-start(bf16[384,512]{1,0:T(8,128)(2,1)S(1)} %collective-permute-done.2.refs_2_.refs_14_), channel_id=1, source_target_pairs={{0,4},{4,12},{12,8},{8,0},{1,5},{5,13},{13,9},{9,1},{2,6},{6,14},{... | collective-permute-start | bytes 1179656 | tf_op jit(solution)/shard_map/ppermute | solution.py:334
  21.6 8.2 %collective-permute-done.5 = bf16[384,512]{1,0:T(8,128)(2,1)S(1)} collective-permute-done((bf16[384,512]{1,0:T(8,128)(2,1)S(1)}, bf16[384,512]{1,0:T(8,128)(2,1)S(1)}, u32[]{:S(2)}, u32[]{:S(2)}) %collective-permute-start.5) | collective-permute-done | bytes 393248 | tf_op jit(solution)/shard_map/ppermute | solution.py:334
  29.8 1.0 pad_maximum_fusion.refs_15_.refs_1_
  32.1 1.8 %slice.156 = bf16[64,3200]{1,0:T(8,128)(2,1)} slice(bf16[128,3200]{1,0:T(8,128)(2,1)} %collective-permute-done.8.refs_7_.refs_8_), slice={[0:64], [0:3200]} | slice | bytes 819200 | tf_op jit(solution)/shard_map/slice | solution.py:352
  33.9 1.5 %collective-permute-start.10 = (bf16[64,3200]{1,0:T(8,128)(2,1)}, bf16[64,3200]{1,0:T(8,128)(2,1)}, u32[]{:S(2)}, u32[]{:S(2)}) collective-permute-start(bf16[64,3200]{1,0:T(8,128)(2,1)} %slice.156), channel_id=1, source_target_pairs={{0,2},{2,0},{1,3},{3,1},{4,6},{6,4},{5,7},{7,5},{8,10},{10,8},{9,1... | collective-permute-start | bytes 1228808 | tf_op jit(solution)/shard_map/ppermute | solution.py:42
  35.4 6.7 %collective-permute-done.4.refs_0_ = bf16[128,3200]{1,0:T(8,128)(2,1)S(1)} collective-permute-done((bf16[128,3200]{1,0:T(8,128)(2,1)}, bf16[128,3200]{1,0:T(8,128)(2,1)S(1)}, u32[]{:S(2)}, u32[]{:S(2)}) %collective-permute-start.4) | collective-permute-done | bytes 819232 | tf_op jit(solution)/shard_map/ppermute | solution.py:42
  43.0 1.5 %collective-permute-start.11 = (bf16[64,3200]{1,0:T(8,128)(2,1)}, bf16[64,3200]{1,0:T(8,128)(2,1)}, u32[]{:S(2)}, u32[]{:S(2)}) collective-permute-start(bf16[64,3200]{1,0:T(8,128)(2,1)} %slice.157), channel_id=1, source_target_pairs={{0,16},{16,0},{1,17},{17,1},{2,18},{18,2},{3,19},{19,3},{4,20},{20... | collective-permute-start | bytes 1228808 | tf_op jit(solution)/shard_map/ppermute | solution.py:42
  44.5 5.7 %collective-permute-done.6.refs_1_.refs_16_ = bf16[768,512]{1,0:T(8,128)(2,1)} collective-permute-done((bf16[768,512]{1,0:T(8,128)(2,1)S(1)}, bf16[768,512]{1,0:T(8,128)(2,1)}, u32[]{:S(2)}, u32[]{:S(2)}) %collective-permute-start.6) | collective-permute-done | bytes 786464 | tf_op jit(solution)/shard_map/ppermute | solution.py:334
  51.1 4.2 %all-to-all-start = ((bf16[8,128,256]{2,1,0:T(8,128)(2,1)}), bf16[8,128,256]{2,1,0:T(8,128)(2,1)}, u32[]{:S(2)}, u32[]{:S(2)}) async-start(bf16[8,128,256]{2,1,0:T(8,128)(2,1)} %fence.7), calls=%async_computation | async-start | bytes 1048576 | tf_op jit(solution)/shard_map/all_to_all | solution.py:355
  56.5 0.9 collective-permute-done.12.refs_11_.refs_12_
  58.8 8.3 %project.1.refs_3_ = f32[1024,512]{1,0:T(8,128)} custom-call(s32[2]{0:T(128)} %pad_add_fusion.refs_0_, bf16[16,2048]{1,0:T(8,128)(2,1)} %refs_1_.3, bf16[16,1024]{1,0:T(8,128)(2,1)} %refs_2_.3, bf16[128,3200]{1,0:T(8,128)(2,1)} %copy-done, bf16[128,3200]{1,0:T(8,128)(2,1)} %collective-permute-done.1.refs_4_.refs_5_, bf16[128,3200]{1,0:T(8,128)(2,1)} %fence.6.refs_5_.refs_6_, ...), custom_call_target="tpu_custom_call" | custom-call | tf_op jit(solution)/shard_map/project/pallas_call | solution.py:292
  67.1 4.3 %collective-permute-done.14.refs_22_ = bf16[768,512]{1,0:T(8,128)(2,1)} collective-permute-done((bf16[768,512]{1,0:T(8,128)(2,1)}, bf16[768,512]{1,0:T(8,128)(2,1)}, u32[]{:S(2)}, u32[]{:S(2)}) %collective-permute-start.14) | collective-permute-done | bytes 786464 | tf_op jit(solution)/shard_map/ppermute | solution.py:334
  71.4 9.7 %attend.1 = (bf16[8,32,384]{2,1,0:T(8,128)(2,1)}, f32[16,384]{1,0:T(8,128)}) custom-call(s32[2]{0:T(128)} %pad_add_fusion.refs_0_, bf16[16,2048]{1,0:T(8,128)(2,1)} %refs_1_.3, bf16[16,1024]{1,0:T(8,128)(2,1)} %refs_2_.3, f32[1024,512]{1,0:T(8,128)} %project.1.refs_3_, bf16[128,3200]{1,0:T(8,128)(2,1)} %copy-done, ...), custom_call_target="tpu_custom_call" | custom-call | tf_op jit(solution)/shard_map/attend/pallas_call | solution.py:310
  81.1 3.4 %all-to-all-start.1 = ((bf16[8,32,384]{2,1,0:T(8,128)(2,1)}), bf16[8,32,384]{2,1,0:T(8,128)(2,1)S(1)}, u32[]{:S(2)}, u32[]{:S(2)}) async-start(bf16[8,32,384]{2,1,0:T(8,128)(2,1)} %get-tuple-element.14), calls=%async_computation.1 | async-start | bytes 393216 | tf_op jit(solution)/shard_map/all_to_all | solution.py:464
  85.2 4.8 %all-to-all-done.1 = bf16[8,32,384]{2,1,0:T(8,128)(2,1)S(1)} async-done(((bf16[8,32,384]{2,1,0:T(8,128)(2,1)}), bf16[8,32,384]{2,1,0:T(8,128)(2,1)S(1)}, u32[]{:S(2)}, u32[]{:S(2)}) %all-to-all-start.1) | async-done | bytes 196640 | tf_op jit(solution)/shard_map/all_to_all | solution.py:464
  90.9 3.2 %collective-permute-done.15 = bf16[48,384]{1,0:T(8,128)(2,1)S(1)} collective-permute-done((bf16[48,384]{1,0:T(8,128)(2,1)S(1)}, bf16[48,384]{1,0:T(8,128)(2,1)S(1)}, u32[]{:S(2)}, u32[]{:S(2)}) %collective-permute-start.15) | collective-permute-done | bytes 36896 | tf_op jit(solution)/shard_map/ppermute | solution.py:42
  94.2 2.2 %collective-permute-start.16 = (bf16[48,384]{1,0:T(8,128)(2,1)S(1)}, bf16[48,384]{1,0:T(8,128)(2,1)S(1)}, u32[]{:S(2)}, u32[]{:S(2)}) collective-permute-start(bf16[48,384]{1,0:T(8,128)(2,1)S(1)} %add_convert_fusion.1), channel_id=1, source_target_pairs={{0,8},{4,12},{8,0},{12,4},{1,9},{5,13},{9,1},{13,5},{2,10},{6,14},... | collective-permute-start | bytes 110600 | tf_op jit(solution)/shard_map/ppermute | solution.py:42
  96.3 2.8 %collective-permute-done.16 = bf16[48,384]{1,0:T(8,128)(2,1)S(1)} collective-permute-done((bf16[48,384]{1,0:T(8,128)(2,1)S(1)}, bf16[48,384]{1,0:T(8,128)(2,1)S(1)}, u32[]{:S(2)}, u32[]{:S(2)}) %collective-permute-start.16) | collective-permute-done | bytes 36896 | tf_op jit(solution)/shard_map/ppermute | solution.py:42
  99.1 1.2 %collective-permute-start.17 = (bf16[48,384]{1,0:T(8,128)(2,1)S(1)}, bf16[48,384]{1,0:T(8,128)(2,1)S(1)}, u32[]{:S(2)}, u32[]{:S(2)}) collective-permute-start(bf16[48,384]{1,0:T(8,128)(2,1)S(1)} %multiply_convert_fusion), channel_id=1, source_target_pairs={{0,18},{2,16},{16,2},{18,0},{1,19},{3,17},{17,3},{19,1},{4,22},{6,... | collective-permute-start | bytes 110600 | tf_op jit(solution)/shard_map/ppermute | solution.py:42
  100.3 1.5 %collective-permute-start.19 = (bf16[48,384]{1,0:T(8,128)(2,1)S(1)}, bf16[48,384]{1,0:T(8,128)(2,1)S(1)}, u32[]{:S(2)}, u32[]{:S(2)}) collective-permute-start(bf16[48,384]{1,0:T(8,128)(2,1)S(1)} %multiply_convert_fusion), channel_id=1, source_target_pairs={{0,16},{2,18},{16,0},{18,2},{1,17},{3,19},{17,1},{19,3},{4,20},{6,... | collective-permute-start | bytes 110600 | tf_op jit(solution)/shard_map/ppermute | solution.py:42
  102.7 1.4 %collective-permute-done.17 = bf16[48,384]{1,0:T(8,128)(2,1)S(1)} collective-permute-done((bf16[48,384]{1,0:T(8,128)(2,1)S(1)}, bf16[48,384]{1,0:T(8,128)(2,1)S(1)}, u32[]{:S(2)}, u32[]{:S(2)}) %collective-permute-start.17) | collective-permute-done | bytes 36896 | tf_op jit(solution)/shard_map/ppermute | solution.py:42
  104.6 1.2 %collective-permute-done.21 = bf16[48,384]{1,0:T(8,128)(2,1)S(1)} collective-permute-done((bf16[48,384]{1,0:T(8,128)(2,1)S(1)}, bf16[48,384]{1,0:T(8,128)(2,1)S(1)}, u32[]{:S(2)}, u32[]{:S(2)}) %collective-permute-start.21) | collective-permute-done | bytes 36896 | tf_op jit(solution)/shard_map/ppermute | solution.py:42
  105.8 1.2 %collective-permute-done.22 = bf16[48,384]{1,0:T(8,128)(2,1)S(1)} collective-permute-done((bf16[48,384]{1,0:T(8,128)(2,1)S(1)}, bf16[48,384]{1,0:T(8,128)(2,1)S(1)}, u32[]{:S(2)}, u32[]{:S(2)}) %collective-permute-start.22) | collective-permute-done | bytes 36896 | tf_op jit(solution)/shard_map/ppermute | solution.py:42
  (113 shorter events, 13.7 us)
Async XLA Ops:
  3.7 1.9 %collective-permute-start = (bf16[2,192,512]{2,1,0:T(8,128)(2,1)S(1)}, bf16[2,192,512]{2,1,0:T(8,128)(2,1)S(1)}, u32[]{:S(2)}, u32[]{:S(2)}) collective-permute-start(bf16[2,192,512]{2,1,0:T(8,128)(2,1)S(1)} %pad_maximum_fusion.2), channel_id=1, source_target_pairs={{0,1},{1,0},{2,3},{3,2},{4,5},{5,4},{6,7},{7,6},{8,9},{9,8},{10,11... | collective-permute-start | bytes 1179656 | tf_op jit(solution)/shard_map/ppermute | solution.py:42
  5.6 4.8 %copy-start.2 = (bf16[1,128,3072]{2,1,0:T(8,128)(2,1)S(1)}, bf16[1,128,3072]{2,1,0:T(8,128)(2,1)}, u32[]{:S(2)}) copy-start(bf16[1,128,3072]{2,1,0:T(8,128)(2,1)} %param.11) | copy-start | bytes 2359300
  5.8 12.4 %collective-permute-start.2 = (bf16[384,512]{1,0:T(8,128)(2,1)S(1)}, bf16[384,512]{1,0:T(8,128)(2,1)S(1)}, u32[]{:S(2)}, u32[]{:S(2)}) collective-permute-start(bf16[384,512]{1,0:T(8,128)(2,1)S(1)} %pad_maximum_fusion.3.rest_0_), channel_id=1, source_target_pairs={{0,2},{2,0},{1,3},{3,1},{4,6},{6,4},{5,7},{7,5},{8,10},{10,8},{9,1... | collective-permute-start | bytes 1179656 | tf_op jit(solution)/shard_map/ppermute | solution.py:42
  8.8 6.5 %copy-start.13 = (bf16[384,512]{1,0:T(8,128)(2,1)}, bf16[384,512]{1,0:T(8,128)(2,1)S(1)}, u32[]{:S(2)}) copy-start(bf16[384,512]{1,0:T(8,128)(2,1)S(1)} %pad_maximum_fusion.4.refs_13_) | copy-start | bytes 1179652
  8.8 11.9 %collective-permute-start.3 = (bf16[384,512]{1,0:T(8,128)(2,1)S(1)}, bf16[384,512]{1,0:T(8,128)(2,1)}, u32[]{:S(2)}, u32[]{:S(2)}) collective-permute-start(bf16[384,512]{1,0:T(8,128)(2,1)S(1)} %pad_maximum_fusion.4.refs_13_), channel_id=1, source_target_pairs={{0,4},{4,12},{12,8},{8,0},{1,5},{5,13},{13,9},{9,1},{2,6},{6,14},{... | collective-permute-start | bytes 1179656 | tf_op jit(solution)/shard_map/ppermute | solution.py:334
  11.3 9.4 %copy-start.1 = (bf16[128,3200]{1,0:T(8,128)(2,1)}, bf16[128,3200]{1,0:T(8,128)(2,1)S(1)}, u32[]{:S(2)}) copy-start(bf16[128,3200]{1,0:T(8,128)(2,1)S(1)} %get-tuple-element.11.refs_0_) | copy-start | bytes 2457604
  11.3 20.3 %copy-start = (bf16[128,3200]{1,0:T(8,128)(2,1)}, bf16[128,3200]{1,0:T(8,128)(2,1)S(1)}, u32[]{:S(2)}) copy-start(bf16[128,3200]{1,0:T(8,128)(2,1)S(1)} %get-tuple-element.10.refs_3_.refs_4_) | copy-start | bytes 2457604
  11.3 20.3 %collective-permute-start.8 = (bf16[128,3200]{1,0:T(8,128)(2,1)S(1)}, bf16[128,3200]{1,0:T(8,128)(2,1)}, u32[]{:S(2)}, u32[]{:S(2)}) collective-permute-start(bf16[128,3200]{1,0:T(8,128)(2,1)S(1)} %get-tuple-element.10.refs_3_.refs_4_), channel_id=1, source_target_pairs={{0,16},{16,0},{1,17},{17,1},{2,18},{18,2},{3,19},{19,3},{4,20},{20... | collective-permute-start | bytes 2457608 | tf_op jit(solution)/shard_map/ppermute | solution.py:42
  18.1 11.7 %collective-permute-start.5 = (bf16[384,512]{1,0:T(8,128)(2,1)S(1)}, bf16[384,512]{1,0:T(8,128)(2,1)S(1)}, u32[]{:S(2)}, u32[]{:S(2)}) collective-permute-start(bf16[384,512]{1,0:T(8,128)(2,1)S(1)} %collective-permute-done.2.refs_2_.refs_14_), channel_id=1, source_target_pairs={{0,4},{4,12},{12,8},{8,0},{1,5},{5,13},{13,9},{9,1},{2,6},{6,14},{... | collective-permute-start | bytes 1179656 | tf_op jit(solution)/shard_map/ppermute | solution.py:334
  20.7 21.5 %collective-permute-start.4 = (bf16[128,3200]{1,0:T(8,128)(2,1)}, bf16[128,3200]{1,0:T(8,128)(2,1)S(1)}, u32[]{:S(2)}, u32[]{:S(2)}) collective-permute-start(bf16[128,3200]{1,0:T(8,128)(2,1)} %get-tuple-element.12), channel_id=1, source_target_pairs={{0,2},{2,0},{1,3},{3,1},{4,6},{6,4},{5,7},{7,5},{8,10},{10,8},{9,1... | collective-permute-start | bytes 2457608 | tf_op jit(solution)/shard_map/ppermute | solution.py:42
  30.9 19.4 %copy-start.9 = (bf16[768,512]{1,0:T(8,128)(2,1)}, bf16[768,512]{1,0:T(8,128)(2,1)S(1)}, u32[]{:S(2)}) copy-start(bf16[768,512]{1,0:T(8,128)(2,1)S(1)} %pad_maximum_fusion.refs_15_.refs_1_) | copy-start | bytes 2359300
  30.9 19.3 %collective-permute-start.6 = (bf16[768,512]{1,0:T(8,128)(2,1)S(1)}, bf16[768,512]{1,0:T(8,128)(2,1)}, u32[]{:S(2)}, u32[]{:S(2)}) collective-permute-start(bf16[768,512]{1,0:T(8,128)(2,1)S(1)} %pad_maximum_fusion.refs_15_.refs_1_), channel_id=1, source_target_pairs={{0,4},{4,12},{12,8},{8,0},{1,5},{5,13},{13,9},{9,1},{2,6},{6,14},{... | collective-permute-start | bytes 2359304 | tf_op jit(solution)/shard_map/ppermute | solution.py:334
  31.6 18.6 %collective-permute-start.9 = (bf16[128,3200]{1,0:T(8,128)(2,1)}, bf16[128,3200]{1,0:T(8,128)(2,1)S(1)}, u32[]{:S(2)}, u32[]{:S(2)}) collective-permute-start(bf16[128,3200]{1,0:T(8,128)(2,1)} %collective-permute-done.8.refs_7_.refs_8_), channel_id=1, source_target_pairs={{0,1},{1,0},{2,3},{3,2},{4,5},{5,4},{6,7},{7,6},{8,9},{9,8},{10,11... | collective-permute-start | bytes 2457608 | tf_op jit(solution)/shard_map/ppermute | solution.py:42
  31.6 24.9 %collective-permute-start.1 = (bf16[128,3200]{1,0:T(8,128)(2,1)S(1)}, bf16[128,3200]{1,0:T(8,128)(2,1)}, u32[]{:S(2)}, u32[]{:S(2)}) collective-permute-start(bf16[128,3200]{1,0:T(8,128)(2,1)S(1)} %get-tuple-element.10.refs_3_.refs_4_), channel_id=1, source_target_pairs={{0,1},{1,0},{2,3},{3,2},{4,5},{5,4},{6,7},{7,6},{8,9},{9,8},{10,11... | collective-permute-start | bytes 2457608 | tf_op jit(solution)/shard_map/ppermute | solution.py:42
  33.9 21.4 %collective-permute-start.10 = (bf16[64,3200]{1,0:T(8,128)(2,1)}, bf16[64,3200]{1,0:T(8,128)(2,1)}, u32[]{:S(2)}, u32[]{:S(2)}) collective-permute-start(bf16[64,3200]{1,0:T(8,128)(2,1)} %slice.156), channel_id=1, source_target_pairs={{0,2},{2,0},{1,3},{3,1},{4,6},{6,4},{5,7},{7,5},{8,10},{10,8},{9,1... | collective-permute-start | bytes 1228808 | tf_op jit(solution)/shard_map/ppermute | solution.py:42
  42.2 8.0 %copy-start.7 = (bf16[128,3200]{1,0:T(8,128)(2,1)}, bf16[128,3200]{1,0:T(8,128)(2,1)S(1)}, u32[]{:S(2)}) copy-start(bf16[128,3200]{1,0:T(8,128)(2,1)S(1)} %collective-permute-done.4.refs_0_) | copy-start | bytes 2457604
  43.0 12.8 %collective-permute-start.11 = (bf16[64,3200]{1,0:T(8,128)(2,1)}, bf16[64,3200]{1,0:T(8,128)(2,1)}, u32[]{:S(2)}, u32[]{:S(2)}) collective-permute-start(bf16[64,3200]{1,0:T(8,128)(2,1)} %slice.157), channel_id=1, source_target_pairs={{0,16},{16,0},{1,17},{17,1},{2,18},{18,2},{3,19},{19,3},{4,20},{20... | collective-permute-start | bytes 1228808 | tf_op jit(solution)/shard_map/ppermute | solution.py:42
  50.2 7.8 %collective-permute-start.7 = (bf16[128,3200]{1,0:T(8,128)(2,1)}, bf16[128,3200]{1,0:T(8,128)(2,1)}, u32[]{:S(2)}, u32[]{:S(2)}) collective-permute-start(bf16[128,3200]{1,0:T(8,128)(2,1)} %fence.6.refs_5_.refs_6_), channel_id=1, source_target_pairs={{0,1},{1,0},{2,3},{3,2},{4,5},{5,4},{6,7},{7,6},{8,9},{9,8},{10,11... | collective-permute-start | bytes 2457608 | tf_op jit(solution)/shard_map/ppermute | solution.py:42
  50.2 21.2 %collective-permute-start.14 = (bf16[768,512]{1,0:T(8,128)(2,1)}, bf16[768,512]{1,0:T(8,128)(2,1)}, u32[]{:S(2)}, u32[]{:S(2)}) collective-permute-start(bf16[768,512]{1,0:T(8,128)(2,1)} %collective-permute-done.6.refs_1_.refs_16_), channel_id=1, source_target_pairs={{0,4},{4,12},{12,8},{8,0},{1,5},{5,13},{13,9},{9,1},{2,6},{6,14},{... | collective-permute-start | bytes 2359304 | tf_op jit(solution)/shard_map/ppermute | solution.py:334
  51.1 15.9 %all-to-all-start = ((bf16[8,128,256]{2,1,0:T(8,128)(2,1)}), bf16[8,128,256]{2,1,0:T(8,128)(2,1)}, u32[]{:S(2)}, u32[]{:S(2)}) async-start(bf16[8,128,256]{2,1,0:T(8,128)(2,1)} %fence.7), calls=%async_computation | async-start | bytes 1048576 | tf_op jit(solution)/shard_map/all_to_all | solution.py:355
  55.3 2.1 %collective-permute-start.12 = (bf16[64,3200]{1,0:T(8,128)(2,1)}, bf16[64,3200]{1,0:T(8,128)(2,1)S(1)}, u32[]{:S(2)}, u32[]{:S(2)}) collective-permute-start(bf16[64,3200]{1,0:T(8,128)(2,1)} %collective-permute-done.10.refs_9_.refs_10_), channel_id=1, source_target_pairs={{0,1},{1,0},{2,3},{3,2},{4,5},{5,4},{6,7},{7,6},{8,9},{9,8},{10,11... | collective-permute-start | bytes 1228808 | tf_op jit(solution)/shard_map/ppermute | solution.py:42
  55.8 2.2 %collective-permute-start.13 = (bf16[64,3200]{1,0:T(8,128)(2,1)}, bf16[64,3200]{1,0:T(8,128)(2,1)S(1)}, u32[]{:S(2)}, u32[]{:S(2)}) collective-permute-start(bf16[64,3200]{1,0:T(8,128)(2,1)} %collective-permute-done.11.refs_10_.refs_11_), channel_id=1, source_target_pairs={{0,1},{1,0},{2,3},{3,2},{4,5},{5,4},{6,7},{7,6},{8,9},{9,8},{10,11... | collective-permute-start | bytes 1228808 | tf_op jit(solution)/shard_map/ppermute | solution.py:42
  81.1 9.0 %all-to-all-start.1 = ((bf16[8,32,384]{2,1,0:T(8,128)(2,1)}), bf16[8,32,384]{2,1,0:T(8,128)(2,1)S(1)}, u32[]{:S(2)}, u32[]{:S(2)}) async-start(bf16[8,32,384]{2,1,0:T(8,128)(2,1)} %get-tuple-element.14), calls=%async_computation.1 | async-start | bytes 393216 | tf_op jit(solution)/shard_map/all_to_all | solution.py:464
  90.1 4.0 %collective-permute-start.15 = (bf16[48,384]{1,0:T(8,128)(2,1)S(1)}, bf16[48,384]{1,0:T(8,128)(2,1)S(1)}, u32[]{:S(2)}, u32[]{:S(2)}) collective-permute-start(bf16[48,384]{1,0:T(8,128)(2,1)S(1)} %pad_maximum_fusion.5), channel_id=1, source_target_pairs={{0,4},{4,0},{8,12},{12,8},{1,5},{5,1},{9,13},{13,9},{2,6},{6,2},{1... | collective-permute-start | bytes 110600 | tf_op jit(solution)/shard_map/ppermute | solution.py:42
  94.2 4.9 %collective-permute-start.16 = (bf16[48,384]{1,0:T(8,128)(2,1)S(1)}, bf16[48,384]{1,0:T(8,128)(2,1)S(1)}, u32[]{:S(2)}, u32[]{:S(2)}) collective-permute-start(bf16[48,384]{1,0:T(8,128)(2,1)S(1)} %add_convert_fusion.1), channel_id=1, source_target_pairs={{0,8},{4,12},{8,0},{12,4},{1,9},{5,13},{9,1},{13,5},{2,10},{6,14},... | collective-permute-start | bytes 110600 | tf_op jit(solution)/shard_map/ppermute | solution.py:42
  99.1 4.9 %collective-permute-start.17 = (bf16[48,384]{1,0:T(8,128)(2,1)S(1)}, bf16[48,384]{1,0:T(8,128)(2,1)S(1)}, u32[]{:S(2)}, u32[]{:S(2)}) collective-permute-start(bf16[48,384]{1,0:T(8,128)(2,1)S(1)} %multiply_convert_fusion), channel_id=1, source_target_pairs={{0,18},{2,16},{16,2},{18,0},{1,19},{3,17},{17,3},{19,1},{4,22},{6,... | collective-permute-start | bytes 110600 | tf_op jit(solution)/shard_map/ppermute | solution.py:42
  100.3 4.0 %collective-permute-start.19 = (bf16[48,384]{1,0:T(8,128)(2,1)S(1)}, bf16[48,384]{1,0:T(8,128)(2,1)S(1)}, u32[]{:S(2)}, u32[]{:S(2)}) collective-permute-start(bf16[48,384]{1,0:T(8,128)(2,1)S(1)} %multiply_convert_fusion), channel_id=1, source_target_pairs={{0,16},{2,18},{16,0},{18,2},{1,17},{3,19},{17,1},{19,3},{4,20},{6,... | collective-permute-start | bytes 110600 | tf_op jit(solution)/shard_map/ppermute | solution.py:42
  101.8 4.0 %collective-permute-start.21 = (bf16[48,384]{1,0:T(8,128)(2,1)S(1)}, bf16[48,384]{1,0:T(8,128)(2,1)S(1)}, u32[]{:S(2)}, u32[]{:S(2)}) collective-permute-start(bf16[48,384]{1,0:T(8,128)(2,1)S(1)} %multiply_convert_fusion), channel_id=1, source_target_pairs={{0,2},{2,0},{16,18},{18,16},{1,3},{3,1},{17,19},{19,17},{4,6},{6,4... | collective-permute-start | bytes 110600 | tf_op jit(solution)/shard_map/ppermute | solution.py:42
  102.7 3.1 %collective-permute-start.23 = (bf16[48,384]{1,0:T(8,128)(2,1)S(1)}, bf16[48,384]{1,0:T(8,128)(2,1)S(1)}, u32[]{:S(2)}, u32[]{:S(2)}) collective-permute-start(bf16[48,384]{1,0:T(8,128)(2,1)S(1)} %multiply_convert_fusion), channel_id=1, source_target_pairs={{0,1},{1,0},{2,3},{3,2},{4,5},{5,4},{6,7},{7,6},{8,9},{9,8},{10,11... | collective-permute-start | bytes 110600 | tf_op jit(solution)/shard_map/ppermute | solution.py:42
  104.0 1.7 %collective-permute-start.18 = (bf16[48,384]{1,0:T(8,128)(2,1)S(1)}, bf16[48,384]{1,0:T(8,128)(2,1)S(1)}, u32[]{:S(2)}, u32[]{:S(2)}) collective-permute-start(bf16[48,384]{1,0:T(8,128)(2,1)S(1)} %collective-permute-done.17), channel_id=1, source_target_pairs={{0,1},{1,0},{2,3},{3,2},{4,5},{5,4},{6,7},{7,6},{8,9},{9,8},{10,11... | collective-permute-start | bytes 110600 | tf_op jit(solution)/shard_map/ppermute | solution.py:42
  104.3 1.5 %collective-permute-start.20 = (bf16[48,384]{1,0:T(8,128)(2,1)S(1)}, bf16[48,384]{1,0:T(8,128)(2,1)S(1)}, u32[]{:S(2)}, u32[]{:S(2)}) collective-permute-start(bf16[48,384]{1,0:T(8,128)(2,1)S(1)} %collective-permute-done.19), channel_id=1, source_target_pairs={{0,1},{1,0},{2,3},{3,2},{4,5},{5,4},{6,7},{7,6},{8,9},{9,8},{10,11... | collective-permute-start | bytes 110600 | tf_op jit(solution)/shard_map/ppermute | solution.py:42
  105.7 1.2 %collective-permute-start.22 = (bf16[48,384]{1,0:T(8,128)(2,1)S(1)}, bf16[48,384]{1,0:T(8,128)(2,1)S(1)}, u32[]{:S(2)}, u32[]{:S(2)}) collective-permute-start(bf16[48,384]{1,0:T(8,128)(2,1)S(1)} %collective-permute-done.21), channel_id=1, source_target_pairs={{0,1},{1,0},{2,3},{3,2},{4,5},{5,4},{6,7},{7,6},{8,9},{9,8},{10,11... | collective-permute-start | bytes 110600 | tf_op jit(solution)/shard_map/ppermute | solution.py:42
  (12 other events, 26.8 us)
